TPU v7x, 32 devices: a whole 2x2x4 slice. The times are simulated.
32 devices in a mesh: tm: 4 (over x, core), gy: 2 (over y), gx: 4 (over z).
Axes of the slice: x: 2, y: 2, z: 4, core: 2. Of those that a mesh axis runs over, the one named last changes fastest.
Arguments:
- initial_state: float32 [2, 8, 64, 128], P(None, 'gy', 'gx'), may hold values from 0 to 1
- slice_guess: float32 [4, 2, 8, 64, 128], P('tm', None, 'gy', 'gx'), may hold values from 0 to 1
- feed_rate: float32 [8, 64, 128], P('gy', 'gx'), may hold values from 0.02 to 0.2
- kill_rate: float32 [8, 64, 128], P('gy', 'gx'), may hold values from 0.03 to 0.12
Outputs:
- final_states: float32 [4, 2, 8, 64, 128], P('tm', None, 'gy', 'gx')
All inputs are finite; a program needn't handle non-finite values.
Results may differ from a plain program's by a relative error of at most 0.0001.
Values sent between devices are 32-bit elements; how exact they have to be, the bound alone decides.
No kernel may reach another device: no remote copies, remote signals or barrier semaphores. Data moves between devices by JAX's collectives and lax.ppermute only.
A program may use at most 64 MiB of HBM per device.

v0:
```python
import functools

import jax
import jax.numpy as jnp
from jax import lax
from jax.experimental import pallas as pl
from jax.experimental.pallas import tpu as pltpu
from jax.sharding import PartitionSpec as P

ITERS = 3
DIFF_U = 0.2
DIFF_V = 0.1
HALF_STEP = 0.5
WEIGHTS = ((5.0 / 24.0, 8.0 / 24.0, -1.0 / 24.0), (-1.0 / 24.0, 8.0 / 24.0, 5.0 / 24.0))

AXES = ("tm", "gy", "gx")
HALO = 5
RATE_HALO = 4
PACK = 6


def shifted(value, by_tm, by_gy, by_gx):
    n_tm, n_gy, n_gx = (lax.axis_size(axis) for axis in AXES)
    pairs = []
    for t in range(n_tm):
        for y in range(n_gy):
            for x in range(n_gx):
                target = ((t + by_tm) % n_tm * n_gy + (y + by_gy) % n_gy) * n_gx + (x + by_gx) % n_gx
                pairs.append(((t * n_gy + y) * n_gx + x, target))
    return lax.ppermute(value, AXES, pairs)


def near(row, distance, axis):
    size = row.shape[axis]
    return pltpu.roll(row, distance % size, axis) + pltpu.roll(row, -distance % size, axis)


def rates_of(state, feed, feed_kill, spacing):
    scale = 1.0 / (spacing * spacing)

    @functools.cache
    def at(r):
        (u, v), (ub, vb), (ua, va) = state(r), state(r - 1), state(r + 1)
        around_u = (ub + ua) + near(u, int(spacing), 0) + near(u, int(spacing), 1)
        around_v = (vb + va) + near(v, int(spacing), 0) + near(v, int(spacing), 1)
        reaction = u * (v * v)
        rate_u = (DIFF_U * scale) * around_u + feed(r) - (6.0 * DIFF_U * scale + feed(r)) * u - reaction
        rate_v = (DIFF_V * scale) * around_v - (6.0 * DIFF_V * scale + feed_kill(r)) * v + reaction
        return rate_u, rate_v

    return at


def half_sum(low, high):
    x, z = low.shape
    total = low + high
    total = total + pltpu.roll(total, z - 1, 1)
    total = total + pltpu.roll(total, x - 1, 0)
    return 0.125 * total


def restricted(state):
    @functools.cache
    def at(c):
        return tuple(half_sum(a, b) for a, b in zip(state(2 * c), state(2 * c + 1)))

    return at


def spread(row):
    even_x = lax.broadcasted_iota(jnp.int32, row.shape, 0) % 2 == 0
    even_z = lax.broadcasted_iota(jnp.int32, row.shape, 1) % 2 == 0
    row = jnp.where(even_z, row, pltpu.roll(row, 1, 1))
    return jnp.where(even_x, row, pltpu.roll(row, 1, 0))


def quadrature(values, interval):
    def at(r):
        zero, one, two = (value(r) for value in values)
        w = WEIGHTS[interval]
        return tuple(w[0] * a + w[1] * b + w[2] * c for a, b, c in zip(zero, one, two))

    return at


def iteration(start, feed, kill, old_rates):
    feed_kill = functools.cache(lambda r: feed(r) + kill(r))
    coarse_feed = functools.cache(lambda c: half_sum(feed(2 * c), feed(2 * c + 1)))
    coarse_sum = functools.cache(lambda c: half_sum(feed_kill(2 * c), feed_kill(2 * c + 1)))

    def stepped(state, rate, interval):
        @functools.cache
        def at(r):
            out = [s + HALF_STEP * f for s, f in zip(state(r), rate(r))]
            if old_rates is not None:
                integral = quadrature(old_rates, interval)(r)
                old = old_rates[interval](r)
                out = [o + (q - HALF_STEP * f) for o, q, f in zip(out, integral, old)]
            return tuple(out)

        return at

    fine = lambda state: rates_of(state, feed, feed_kill, 1.0)
    coarse = lambda state: rates_of(state, coarse_feed, coarse_sum, 2.0)
    rate_zero = fine(start)
    node_one = stepped(start, rate_zero, 0)
    rate_one = fine(node_one)
    node_two = stepped(node_one, rate_one, 1)
    rate_two = fine(node_two)
    fresh = (rate_zero, rate_one, rate_two)
    rest_zero, rest_one, rest_two = restricted(start), restricted(node_one), restricted(node_two)
    rest_integral = [restricted(quadrature(fresh, interval)) for interval in (0, 1)]
    coarse_start = rest_zero

    def coarse_stepped(state, rate, rest_rate, integral):
        @functools.cache
        def at(c):
            return tuple(
                s + HALF_STEP * (f - g) + q for s, f, g, q in zip(state(c), rate(c), rest_rate(c), integral(c))
            )

        return at

    coarse_one = coarse_stepped(coarse_start, coarse(coarse_start), coarse(rest_zero), rest_integral[0])
    coarse_two = coarse_stepped(coarse_one, coarse(coarse_one), coarse(rest_one), rest_integral[1])

    def corrected(node, coarse_node, rest):
        change = functools.cache(lambda c: tuple(spread(w - m) for w, m in zip(coarse_node(c), rest(c))))

        @functools.cache
        def at(r):
            return tuple(n + d for n, d in zip(node(r), change(r // 2)))

        return at

    return rate_zero, corrected(node_one, coarse_one, rest_one), corrected(node_two, coarse_two, rest_two)


def rows_of(ref, width, first):
    @functools.cache
    def at(r):
        assert 0 <= (r - first) * width < ref.shape[1]
        return tuple(ref[field, pl.ds((r - first) * width, width), :] for field in range(2))

    return at


def pack_kernel(last_ref, initial_ref, guess_ref, feed_ref, kill_ref, state_ref, all_ref, low_ref, high_ref):
    _, n_x, n_y, _ = initial_ref.shape
    is_last = last_ref[0] == 1
    for x in range(n_x):
        rows = pl.ds(x, n_y, stride=n_x)
        for field in range(2):
            tile = jnp.where(is_last, initial_ref[field, x], guess_ref[field, x])
            state_ref[field, rows, :] = tile
            all_ref[field, rows, :] = tile
        all_ref[2, rows, :] = feed_ref[x]
        all_ref[3, rows, :] = kill_ref[x]
    for field in range(4):
        low_ref[field] = all_ref[field, pl.ds(0, PACK * n_x), :]
        high_ref[field] = all_ref[field, pl.ds((n_y - PACK) * n_x, PACK * n_x), :]


def first_kernel(n_gy, n_x, n_y, *refs):
    state_ref, local_ref = refs[:2]
    others, lows, highs = refs[2 : 1 + n_gy], refs[1 + n_gy : 1 + 2 * n_gy], refs[1 + 2 * n_gy : 1 + 3 * n_gy]
    start_ref, params_ref, zero_ref, one_ref, two_ref, two_low, two_high, low_ref, high_ref = refs[1 + 3 * n_gy :]
    width = n_gy * n_x

    def collect(out_ref, field, source_field, middles):
        for gy in range(n_gy):
            pieces = [(-PACK, lows[gy], PACK), (0, middles[gy], n_y), (n_y, highs[gy], PACK)]
            for first, ref, count in pieces:
                for k in range(count):
                    if -HALO <= first + k < n_y + HALO:
                        place = pl.ds((first + k + HALO) * width + gy * n_x, n_x)
                        out_ref[field, place, :] = ref[source_field, pl.ds(k * n_x, n_x), :]

    for field in range(2):
        collect(start_ref, field, field, [state_ref, *others])
        collect(params_ref, field, 2 + field, [local_ref, *others])
    start = rows_of(start_ref, width, -HALO)
    params = rows_of(params_ref, width, -HALO)
    results = iteration(start, lambda r: params(r)[0], lambda r: params(r)[1], None)
    write_nodes(results, width, n_y, zero_ref, one_ref, two_ref, two_low, two_high, low_ref, high_ref)


def write_nodes(results, width, n_y, zero_ref, one_ref, two_ref, two_low, two_high, low_ref, high_ref):
    rate_zero, node_one, node_two = results
    for r in range(-RATE_HALO, n_y + RATE_HALO):
        if 0 <= r < n_y:
            place = pl.ds(r * width, width)
            for field, (one, two) in enumerate(zip(node_one(r), node_two(r))):
                one_ref[field, place, :] = one
                two_ref[field, place, :] = two
                for edge, pair_ref, edge_ref in ((0, two_low, low_ref), (n_y - HALO, two_high, high_ref)):
                    if edge <= r < edge + HALO:
                        beside = pl.ds((r - edge) * width, width)
                        pair_ref[field, beside, :] = two
                        edge_ref[field, beside, :] = one
                        edge_ref[2 + field, beside, :] = two
        for field, zero in enumerate(rate_zero(r)):
            zero_ref[field, pl.ds((r + RATE_HALO) * width, width), :] = zero


def later_kernel(
    width, n_y, out_x, first_ref, start_ref, params_ref, zero_ref, one_ref, two_ref, got_ref, got_low, got_high, low_ref, high_ref, *outs
):
    is_first = first_ref[0] == 1
    params = rows_of(params_ref, width, -HALO)
    feed, kill = (lambda r: params(r)[0]), (lambda r: params(r)[1])
    kept = rows_of(start_ref, width, -HALO)
    sources = [rows_of(got_low, width, -HALO), rows_of(got_ref, width, 0), rows_of(got_high, width, n_y)]

    def pick(r):
        return 0 if r < 0 else 1 if r < n_y else 2

    @functools.cache
    def start(r):
        return tuple(jnp.where(is_first, a, b) for a, b in zip(kept(r), sources[pick(r)](r)))

    def own(tile_ref, offset):
        pieces = [
            rows_of(low_ref.at[pl.ds(offset, 2)], width, -HALO),
            rows_of(tile_ref, width, 0),
            rows_of(high_ref.at[pl.ds(offset, 2)], width, n_y),
        ]
        return lambda r: pieces[pick(r)](r)

    old_zero = rows_of(zero_ref, width, -RATE_HALO)
    feed_kill = functools.cache(lambda r: feed(r) + kill(r))
    old_one, old_two = (rates_of(own(ref, offset), feed, feed_kill, 1.0) for ref, offset in ((one_ref, 0), (two_ref, 2)))
    results = iteration(start, feed, kill, (old_zero, old_one, old_two))
    if out_x is None:
        write_nodes(results, width, n_y, *outs)
    else:
        out_ref, scratch = outs
        for r in range(n_y):
            for field, value in enumerate(results[2](r)):
                scratch[field, pl.ds(r * width, width), :] = value
        for x in range(out_x):
            for field in range(2):
                out_ref[field, x] = scratch[field, pl.ds(x, n_y, stride=width), :]


def call(kernel, name, n_scalars, operands, shapes, scratch=()):
    specs = [pl.BlockSpec(memory_space=pltpu.SMEM)] * n_scalars
    specs += [pl.BlockSpec(memory_space=pltpu.VMEM)] * (len(operands) - n_scalars)
    return pl.pallas_call(
        kernel,
        name=name,
        out_shape=[jax.ShapeDtypeStruct(shape, jnp.float32) for shape in shapes],
        in_specs=specs,
        out_specs=[pl.BlockSpec(memory_space=pltpu.VMEM)] * len(shapes),
        scratch_shapes=scratch,
        compiler_params=pltpu.CompilerParams(vmem_limit_bytes=32 * 1024 * 1024),
    )(*operands)


def shards(initial_state, slice_guess, feed_rate, kill_rate):
    n_gy, n_tm = lax.axis_size("gy"), lax.axis_size("tm")
    _, n_x, n_y, n_z = initial_state.shape
    width = n_gy * n_x
    place = lax.axis_index("tm")
    is_first = (place == 0).astype(jnp.int32)[None]
    is_last = (place == n_tm - 1).astype(jnp.int32)[None]

    state, local, low, high = call(
        pack_kernel,
        "pack",
        1,
        (is_last, initial_state, slice_guess[0], feed_rate, kill_rate),
        [(2, n_y * n_x, n_z), (4, n_y * n_x, n_z), (4, PACK * n_x, n_z), (4, PACK * n_x, n_z)],
    )
    got = [shifted(state, 1, 0, 0), local]
    got += [shifted(local, 1, -gy, 0) for gy in range(1, n_gy)]
    got += [shifted(high, 1, -gy, 1) for gy in range(n_gy)]
    got += [shifted(low, 1, -gy, -1) for gy in range(n_gy)]

    tile, edge = (2, n_y * width, n_z), (2, HALO * width, n_z)
    node_shapes = [(2, (n_y + 2 * RATE_HALO) * width, n_z), tile, tile, edge, edge, (4, *edge[1:]), (4, *edge[1:])]
    window = (2, (n_y + 2 * HALO) * width, n_z)
    start, params, *nodes = call(
        functools.partial(first_kernel, n_gy, n_x, n_y), "first", 0, got, [window, window, *node_shapes]
    )
    for sweep_index in range(1, ITERS):
        zero, one, two, two_low, two_high, low, high = nodes
        got = [shifted(two, 1, 0, 0), shifted(two_high, 1, 0, 1), shifted(two_low, 1, 0, -1)]
        got += [shifted(high, 0, 0, 1), shifted(low, 0, 0, -1)]
        done = sweep_index + 1 == ITERS
        nodes = call(
            functools.partial(later_kernel, width, n_y, n_x if done else None),
            "last" if done else "later",
            1,
            (is_first, start, params, zero, one, two, *got),
            [initial_state.shape] if done else node_shapes,
            [pltpu.VMEM(tile, jnp.float32)] if done else (),
        )
    return nodes[0][None]


def solution(mesh):
    in_specs = (
        P(None, "gy", "gx", None),
        P("tm", None, "gy", "gx", None),
        P("gy", "gx", None),
        P("gy", "gx", None),
    )
    out_specs = P("tm", None, "gy", "gx", None)
    return jax.shard_map(shards, mesh=mesh, in_specs=in_specs, out_specs=out_specs, check_vma=False)
```

profile of v0, /device:TPU:0, one launch (start us, length us, event | category | flops | bytes accessed | tf_op | source)
XLA Modules:
  0.0 44.7 jit_solution(12329477737593312195)
XLA Ops:
  0.0 0.0 copy-start
  0.0 0.8 %copy-done = f32[2,4,16,128]{3,2,1,0:T(8,128)S(1)} copy-done((f32[2,4,16,128]{3,2,1,0:T(8,128)S(1)}, f32[2,4,16,128]{3,2,1,0:T(8,128)}, u32[]{:S(2)}) %copy-start) | copy-done | bytes 65560
  0.8 0.0 copy-start.1
  0.8 0.8 %copy-done.1 = f32[1,2,4,16,128]{4,3,2,1,0:T(8,128)S(1)} copy-done((f32[1,2,4,16,128]{4,3,2,1,0:T(8,128)S(1)}, f32[1,2,4,16,128]{4,3,2,1,0:T(8,128)}, u32[]{:S(2)}) %copy-start.1) | copy-done | bytes 65560
  1.7 0.0 copy-start.2
  1.7 0.8 %copy-done.2 = f32[4,16,128]{2,1,0:T(8,128)S(1)} copy-done((f32[4,16,128]{2,1,0:T(8,128)S(1)}, f32[4,16,128]{2,1,0:T(8,128)}, u32[]{:S(2)}) %copy-start.2) | copy-done | bytes 32792
  2.4 0.0 copy-start.3
  2.4 0.8 %copy-done.3 = f32[4,16,128]{2,1,0:T(8,128)S(1)} copy-done((f32[4,16,128]{2,1,0:T(8,128)S(1)}, f32[4,16,128]{2,1,0:T(8,128)}, u32[]{:S(2)}) %copy-start.3) | copy-done | bytes 32792
  3.2 2.5 %collective-permute-start.1 = (f32[4,64,128]{2,1,0:T(8,128)S(1)}, f32[4,64,128]{2,1,0:T(8,128)S(1)}, u32[]{:S(2)}, u32[]{:S(2)}) collective-permute-start(f32[4,64,128]{2,1,0:T(8,128)S(1)} %get-tuple-element.26.refs_1_), channel_id=1, source_target_pairs={{0,12},{1,13},{2,14},{3,15},{4,8},{5,9},{6,10},{7,11},{8,20},{9,21... | collective-permute-start | bytes 393224 | tf_op jit(solution)/shard_map/ppermute | solution.py:30
  5.7 2.7 %collective-permute-start.3 = (f32[4,24,128]{2,1,0:T(8,128)S(1)}, f32[4,24,128]{2,1,0:T(8,128)S(1)}, u32[]{:S(2)}, u32[]{:S(2)}) collective-permute-start(f32[4,24,128]{2,1,0:T(8,128)S(1)} %get-tuple-element.27), channel_id=1, source_target_pairs={{0,13},{1,14},{2,15},{3,12},{4,9},{5,10},{6,11},{7,8},{8,21},{9,22... | collective-permute-start | bytes 147464 | tf_op jit(solution)/shard_map/ppermute | solution.py:30
  8.4 0.0 collective-permute-start
  8.4 1.8 %collective-permute-start.2 = (f32[4,24,128]{2,1,0:T(8,128)S(1)}, f32[4,24,128]{2,1,0:T(8,128)S(1)}, u32[]{:S(2)}, u32[]{:S(2)}) collective-permute-start(f32[4,24,128]{2,1,0:T(8,128)S(1)} %get-tuple-element.27), channel_id=1, source_target_pairs={{0,9},{1,10},{2,11},{3,8},{4,13},{5,14},{6,15},{7,12},{8,17},{9,18... | collective-permute-start | bytes 147464 | tf_op jit(solution)/shard_map/ppermute | solution.py:30
  10.2 2.6 %collective-permute-start.5 = (f32[4,24,128]{2,1,0:T(8,128)S(1)}, f32[4,24,128]{2,1,0:T(8,128)S(1)}, u32[]{:S(2)}, u32[]{:S(2)}) collective-permute-start(f32[4,24,128]{2,1,0:T(8,128)S(1)} %get-tuple-element.28), channel_id=1, source_target_pairs={{0,15},{1,12},{2,13},{3,14},{4,11},{5,8},{6,9},{7,10},{8,23},{9,20... | collective-permute-start | bytes 147464 | tf_op jit(solution)/shard_map/ppermute | solution.py:30
  12.9 0.0 collective-permute-done.3.refs_4_
  12.9 2.5 %collective-permute-start.4 = (f32[4,24,128]{2,1,0:T(8,128)S(1)}, f32[4,24,128]{2,1,0:T(8,128)S(1)}, u32[]{:S(2)}, u32[]{:S(2)}) collective-permute-start(f32[4,24,128]{2,1,0:T(8,128)S(1)} %get-tuple-element.28), channel_id=1, source_target_pairs={{0,11},{1,8},{2,9},{3,10},{4,15},{5,12},{6,13},{7,14},{8,19},{9,16... | collective-permute-start | bytes 147464 | tf_op jit(solution)/shard_map/ppermute | solution.py:30
  15.4 0.0 collective-permute-done.2.refs_3_
  15.4 1.6 %collective-permute-done.5.refs_6_ = f32[4,24,128]{2,1,0:T(8,128)S(1)} collective-permute-done((f32[4,24,128]{2,1,0:T(8,128)S(1)}, f32[4,24,128]{2,1,0:T(8,128)S(1)}, u32[]{:S(2)}, u32[]{:S(2)}) %collective-permute-start.5) | collective-permute-done | bytes 49184 | tf_op jit(solution)/shard_map/ppermute | solution.py:30
  17.0 0.5 %collective-permute-done.4.refs_5_ = f32[4,24,128]{2,1,0:T(8,128)S(1)} collective-permute-done((f32[4,24,128]{2,1,0:T(8,128)S(1)}, f32[4,24,128]{2,1,0:T(8,128)S(1)}, u32[]{:S(2)}, u32[]{:S(2)}) %collective-permute-start.4) | collective-permute-done | bytes 49184 | tf_op jit(solution)/shard_map/ppermute | solution.py:30
  17.5 0.0 collective-permute-done.refs_0_
  17.5 0.0 collective-permute-done.1.refs_2_
  17.5 1.2 %first.1 = (f32[2,208,128]{2,1,0:T(8,128)S(1)}, f32[2,208,128]{2,1,0:T(8,128)S(1)}, f32[2,192,128]{2,1,0:T(8,128)S(1)}, f32[2,128,128]{2,1,0:T(8,128)S(1)}, f32[...) custom-call(f32[2,64,128]{2,1,0:T(8,128)S(1)} %collective-permute-do, ...), custom_call_target="tpu_custom_call" | custom-call | tf_op jit(solution)/shard_map/first/pallas_call | solution.py:249
  18.7 0.6 %collective-permute-start.6 = (f32[2,128,128]{2,1,0:T(8,128)S(1)}, f32[2,128,128]{2,1,0:T(8,128)S(1)}, u32[]{:S(2)}, u32[]{:S(2)}) collective-permute-start(f32[2,128,128]{2,1,0:T(8,128)S(1)} %get-tuple-element.33.two_ref), channel_id=1, source_target_pairs={{0,8},{1,9},{2,10},{3,11},{4,12},{5,13},{6,14},{7,15},{8,16},{9,17... | collective-permute-start | bytes 393224 | tf_op jit(solution)/shard_map/ppermute | solution.py:30
  19.3 0.8 %collective-permute-start.9 = (f32[4,40,128]{2,1,0:T(8,128)S(1)}, f32[4,40,128]{2,1,0:T(8,128)S(1)}, u32[]{:S(2)}, u32[]{:S(2)}) collective-permute-start(f32[4,40,128]{2,1,0:T(8,128)S(1)} %get-tuple-element.36), channel_id=1, source_target_pairs={{0,1},{1,2},{2,3},{3,0},{4,5},{5,6},{6,7},{7,4},{8,9},{9,10},{10,1... | collective-permute-start | bytes 245768 | tf_op jit(solution)/shard_map/ppermute | solution.py:30
  20.1 3.1 %collective-permute-start.10 = (f32[4,40,128]{2,1,0:T(8,128)S(1)}, f32[4,40,128]{2,1,0:T(8,128)S(1)}, u32[]{:S(2)}, u32[]{:S(2)}) collective-permute-start(f32[4,40,128]{2,1,0:T(8,128)S(1)} %get-tuple-element.37), channel_id=1, source_target_pairs={{0,3},{1,0},{2,1},{3,2},{4,7},{5,4},{6,5},{7,6},{8,11},{9,8},{10,9... | collective-permute-start | bytes 245768 | tf_op jit(solution)/shard_map/ppermute | solution.py:30
  23.1 0.0 collective-permute-start.7
  23.1 4.5 %collective-permute-start.8 = (f32[2,40,128]{2,1,0:T(8,128)S(1)}, f32[2,40,128]{2,1,0:T(8,128)S(1)}, u32[]{:S(2)}, u32[]{:S(2)}) collective-permute-start(f32[2,40,128]{2,1,0:T(8,128)S(1)} %get-tuple-element.35), channel_id=1, source_target_pairs={{0,11},{1,8},{2,9},{3,10},{4,15},{5,12},{6,13},{7,14},{8,19},{9,16... | collective-permute-start | bytes 122888 | tf_op jit(solution)/shard_map/ppermute | solution.py:30
  27.7 2.0 %collective-permute-done.7.got_low = f32[2,40,128]{2,1,0:T(8,128)S(1)} collective-permute-done((f32[2,40,128]{2,1,0:T(8,128)S(1)}, f32[2,40,128]{2,1,0:T(8,128)S(1)}, u32[]{:S(2)}, u32[]{:S(2)}) %collective-permute-start.7) | collective-permute-done | bytes 40992 | tf_op jit(solution)/shard_map/ppermute | solution.py:30
  29.7 0.0 collective-permute-done.8.got_high
  29.7 0.0 collective-permute-done.9.low_ref
  29.7 0.0 collective-permute-done.10.high_ref
  29.7 0.0 collective-permute-done.6.got_ref
  29.7 1.9 %later.1 = (f32[2,192,128]{2,1,0:T(8,128)S(1)}, f32[2,128,128]{2,1,0:T(8,128)S(1)}, f32[2,128,128]{2,1,0:T(8,128)S(1)}, f32[2,40,128]{2,1,0:T(8,128)S(1)}, f32[2...) custom-call(s32[1]{0:T(128)} %bitcast.first_ref, ...), custom_call_target="tpu_custom_call" | custom-call | tf_op jit(solution)/shard_map/later/pallas_call | solution.py:249
  31.6 0.3 collective-permute-start.11
  32.0 0.7 %collective-permute-start.14 = (f32[4,40,128]{2,1,0:T(8,128)S(1)}, f32[4,40,128]{2,1,0:T(8,128)S(1)}, u32[]{:S(2)}, u32[]{:S(2)}) collective-permute-start(f32[4,40,128]{2,1,0:T(8,128)S(1)} %get-tuple-element.43), channel_id=1, source_target_pairs={{0,1},{1,2},{2,3},{3,0},{4,5},{5,6},{6,7},{7,4},{8,9},{9,10},{10,1... | collective-permute-start | bytes 245768 | tf_op jit(solution)/shard_map/ppermute | solution.py:30
  32.7 3.4 %collective-permute-start.15 = (f32[4,40,128]{2,1,0:T(8,128)S(1)}, f32[4,40,128]{2,1,0:T(8,128)S(1)}, u32[]{:S(2)}, u32[]{:S(2)}) collective-permute-start(f32[4,40,128]{2,1,0:T(8,128)S(1)} %get-tuple-element.44), channel_id=1, source_target_pairs={{0,3},{1,0},{2,1},{3,2},{4,7},{5,4},{6,5},{7,6},{8,11},{9,8},{10,9... | collective-permute-start | bytes 245768 | tf_op jit(solution)/shard_map/ppermute | solution.py:30
  36.1 0.0 collective-permute-start.12
  36.1 3.7 %collective-permute-start.13 = (f32[2,40,128]{2,1,0:T(8,128)S(1)}, f32[2,40,128]{2,1,0:T(8,128)S(1)}, u32[]{:S(2)}, u32[]{:S(2)}) collective-permute-start(f32[2,40,128]{2,1,0:T(8,128)S(1)} %get-tuple-element.42), channel_id=1, source_target_pairs={{0,11},{1,8},{2,9},{3,10},{4,15},{5,12},{6,13},{7,14},{8,19},{9,16... | collective-permute-start | bytes 122888 | tf_op jit(solution)/shard_map/ppermute | solution.py:30
  39.8 2.5 %collective-permute-done.12.got_low = f32[2,40,128]{2,1,0:T(8,128)S(1)} collective-permute-done((f32[2,40,128]{2,1,0:T(8,128)S(1)}, f32[2,40,128]{2,1,0:T(8,128)S(1)}, u32[]{:S(2)}, u32[]{:S(2)}) %collective-permute-start.12) | collective-permute-done | bytes 40992 | tf_op jit(solution)/shard_map/ppermute | solution.py:30
  42.2 0.0 collective-permute-done.13.got_high
  42.2 0.0 collective-permute-done.14.low_ref
  42.2 0.0 collective-permute-done.15.high_ref
  42.3 0.0 collective-permute-done.11.got_ref
  42.3 2.5 %last.1 = f32[2,4,16,128]{3,2,1,0:T(8,128)} custom-call(s32[1]{0:T(128)} %bitcast.first_ref, f32[2,208,128]{2,1,0:T(8,128)S(1)} %get-tuple-element.29.start_ref, f32[2,208,128]{2,1,0:T(8,128)S(1)} %get-tuple-element.30.params_ref, f32[2,192,128]{2,1,0:T(8,128)S(1)} %get-tuple-element.38.zero_ref, f32[2,128,128]{2,1,0:T(8,128)S(1)} %get-tuple-element.39.one_ref, ...), custom_call_target="tpu_custom_call" | custom-call | tf_op jit(solution)/shard_map/last/pallas_call | solution.py:249
  (1 shorter events, 0.0 us)
Async XLA Ops:
  0.0 0.8 %copy-start = (f32[2,4,16,128]{3,2,1,0:T(8,128)S(1)}, f32[2,4,16,128]{3,2,1,0:T(8,128)}, u32[]{:S(2)}) copy-start(f32[2,4,16,128]{3,2,1,0:T(8,128)} %initial_ref.1) | copy-start | bytes 196612
  0.8 0.8 %copy-start.1 = (f32[1,2,4,16,128]{4,3,2,1,0:T(8,128)S(1)}, f32[1,2,4,16,128]{4,3,2,1,0:T(8,128)}, u32[]{:S(2)}) copy-start(f32[1,2,4,16,128]{4,3,2,1,0:T(8,128)} %param.5) | copy-start | bytes 196612
  1.7 0.8 %copy-start.2 = (f32[4,16,128]{2,1,0:T(8,128)S(1)}, f32[4,16,128]{2,1,0:T(8,128)}, u32[]{:S(2)}) copy-start(f32[4,16,128]{2,1,0:T(8,128)} %feed_ref.1) | copy-start | bytes 98308
  2.4 0.8 %copy-start.3 = (f32[4,16,128]{2,1,0:T(8,128)S(1)}, f32[4,16,128]{2,1,0:T(8,128)}, u32[]{:S(2)}) copy-start(f32[4,16,128]{2,1,0:T(8,128)} %kill_ref.1) | copy-start | bytes 98308
  3.2 14.3 %collective-permute-start.1 = (f32[4,64,128]{2,1,0:T(8,128)S(1)}, f32[4,64,128]{2,1,0:T(8,128)S(1)}, u32[]{:S(2)}, u32[]{:S(2)}) collective-permute-start(f32[4,64,128]{2,1,0:T(8,128)S(1)} %get-tuple-element.26.refs_1_), channel_id=1, source_target_pairs={{0,12},{1,13},{2,14},{3,15},{4,8},{5,9},{6,10},{7,11},{8,20},{9,21... | collective-permute-start | bytes 393224 | tf_op jit(solution)/shard_map/ppermute | solution.py:30
  5.7 7.2 %collective-permute-start.3 = (f32[4,24,128]{2,1,0:T(8,128)S(1)}, f32[4,24,128]{2,1,0:T(8,128)S(1)}, u32[]{:S(2)}, u32[]{:S(2)}) collective-permute-start(f32[4,24,128]{2,1,0:T(8,128)S(1)} %get-tuple-element.27), channel_id=1, source_target_pairs={{0,13},{1,14},{2,15},{3,12},{4,9},{5,10},{6,11},{7,8},{8,21},{9,22... | collective-permute-start | bytes 147464 | tf_op jit(solution)/shard_map/ppermute | solution.py:30
  8.4 9.1 %collective-permute-start = (f32[2,64,128]{2,1,0:T(8,128)S(1)}, f32[2,64,128]{2,1,0:T(8,128)S(1)}, u32[]{:S(2)}, u32[]{:S(2)}) collective-permute-start(f32[2,64,128]{2,1,0:T(8,128)S(1)} %get-tuple-element.25), channel_id=1, source_target_pairs={{0,8},{1,9},{2,10},{3,11},{4,12},{5,13},{6,14},{7,15},{8,16},{9,17... | collective-permute-start | bytes 196616 | tf_op jit(solution)/shard_map/ppermute | solution.py:30
  8.4 7.0 %collective-permute-start.2 = (f32[4,24,128]{2,1,0:T(8,128)S(1)}, f32[4,24,128]{2,1,0:T(8,128)S(1)}, u32[]{:S(2)}, u32[]{:S(2)}) collective-permute-start(f32[4,24,128]{2,1,0:T(8,128)S(1)} %get-tuple-element.27), channel_id=1, source_target_pairs={{0,9},{1,10},{2,11},{3,8},{4,13},{5,14},{6,15},{7,12},{8,17},{9,18... | collective-permute-start | bytes 147464 | tf_op jit(solution)/shard_map/ppermute | solution.py:30
  10.2 6.8 %collective-permute-start.5 = (f32[4,24,128]{2,1,0:T(8,128)S(1)}, f32[4,24,128]{2,1,0:T(8,128)S(1)}, u32[]{:S(2)}, u32[]{:S(2)}) collective-permute-start(f32[4,24,128]{2,1,0:T(8,128)S(1)} %get-tuple-element.28), channel_id=1, source_target_pairs={{0,15},{1,12},{2,13},{3,14},{4,11},{5,8},{6,9},{7,10},{8,23},{9,20... | collective-permute-start | bytes 147464 | tf_op jit(solution)/shard_map/ppermute | solution.py:30
  12.9 4.6 %collective-permute-start.4 = (f32[4,24,128]{2,1,0:T(8,128)S(1)}, f32[4,24,128]{2,1,0:T(8,128)S(1)}, u32[]{:S(2)}, u32[]{:S(2)}) collective-permute-start(f32[4,24,128]{2,1,0:T(8,128)S(1)} %get-tuple-element.28), channel_id=1, source_target_pairs={{0,11},{1,8},{2,9},{3,10},{4,15},{5,12},{6,13},{7,14},{8,19},{9,16... | collective-permute-start | bytes 147464 | tf_op jit(solution)/shard_map/ppermute | solution.py:30
  18.7 11.0 %collective-permute-start.6 = (f32[2,128,128]{2,1,0:T(8,128)S(1)}, f32[2,128,128]{2,1,0:T(8,128)S(1)}, u32[]{:S(2)}, u32[]{:S(2)}) collective-permute-start(f32[2,128,128]{2,1,0:T(8,128)S(1)} %get-tuple-element.33.two_ref), channel_id=1, source_target_pairs={{0,8},{1,9},{2,10},{3,11},{4,12},{5,13},{6,14},{7,15},{8,16},{9,17... | collective-permute-start | bytes 393224 | tf_op jit(solution)/shard_map/ppermute | solution.py:30
  19.3 10.4 %collective-permute-start.9 = (f32[4,40,128]{2,1,0:T(8,128)S(1)}, f32[4,40,128]{2,1,0:T(8,128)S(1)}, u32[]{:S(2)}, u32[]{:S(2)}) collective-permute-start(f32[4,40,128]{2,1,0:T(8,128)S(1)} %get-tuple-element.36), channel_id=1, source_target_pairs={{0,1},{1,2},{2,3},{3,0},{4,5},{5,6},{6,7},{7,4},{8,9},{9,10},{10,1... | collective-permute-start | bytes 245768 | tf_op jit(solution)/shard_map/ppermute | solution.py:30
  20.1 9.6 %collective-permute-start.10 = (f32[4,40,128]{2,1,0:T(8,128)S(1)}, f32[4,40,128]{2,1,0:T(8,128)S(1)}, u32[]{:S(2)}, u32[]{:S(2)}) collective-permute-start(f32[4,40,128]{2,1,0:T(8,128)S(1)} %get-tuple-element.37), channel_id=1, source_target_pairs={{0,3},{1,0},{2,1},{3,2},{4,7},{5,4},{6,5},{7,6},{8,11},{9,8},{10,9... | collective-permute-start | bytes 245768 | tf_op jit(solution)/shard_map/ppermute | solution.py:30
  23.1 6.6 %collective-permute-start.7 = (f32[2,40,128]{2,1,0:T(8,128)S(1)}, f32[2,40,128]{2,1,0:T(8,128)S(1)}, u32[]{:S(2)}, u32[]{:S(2)}) collective-permute-start(f32[2,40,128]{2,1,0:T(8,128)S(1)} %get-tuple-element.34), channel_id=1, source_target_pairs={{0,9},{1,10},{2,11},{3,8},{4,13},{5,14},{6,15},{7,12},{8,17},{9,18... | collective-permute-start | bytes 122888 | tf_op jit(solution)/shard_map/ppermute | solution.py:30
  23.1 6.6 %collective-permute-start.8 = (f32[2,40,128]{2,1,0:T(8,128)S(1)}, f32[2,40,128]{2,1,0:T(8,128)S(1)}, u32[]{:S(2)}, u32[]{:S(2)}) collective-permute-start(f32[2,40,128]{2,1,0:T(8,128)S(1)} %get-tuple-element.35), channel_id=1, source_target_pairs={{0,11},{1,8},{2,9},{3,10},{4,15},{5,12},{6,13},{7,14},{8,19},{9,16... | collective-permute-start | bytes 122888 | tf_op jit(solution)/shard_map/ppermute | solution.py:30
  31.6 10.6 %collective-permute-start.11 = (f32[2,128,128]{2,1,0:T(8,128)S(1)}, f32[2,128,128]{2,1,0:T(8,128)S(1)}, u32[]{:S(2)}, u32[]{:S(2)}) collective-permute-start(f32[2,128,128]{2,1,0:T(8,128)S(1)} %get-tuple-element.40.two_ref), channel_id=1, source_target_pairs={{0,8},{1,9},{2,10},{3,11},{4,12},{5,13},{6,14},{7,15},{8,16},{9,17... | collective-permute-start | bytes 393224 | tf_op jit(solution)/shard_map/ppermute | solution.py:30
  32.0 10.3 %collective-permute-start.14 = (f32[4,40,128]{2,1,0:T(8,128)S(1)}, f32[4,40,128]{2,1,0:T(8,128)S(1)}, u32[]{:S(2)}, u32[]{:S(2)}) collective-permute-start(f32[4,40,128]{2,1,0:T(8,128)S(1)} %get-tuple-element.43), channel_id=1, source_target_pairs={{0,1},{1,2},{2,3},{3,0},{4,5},{5,6},{6,7},{7,4},{8,9},{9,10},{10,1... | collective-permute-start | bytes 245768 | tf_op jit(solution)/shard_map/ppermute | solution.py:30
  32.7 9.6 %collective-permute-start.15 = (f32[4,40,128]{2,1,0:T(8,128)S(1)}, f32[4,40,128]{2,1,0:T(8,128)S(1)}, u32[]{:S(2)}, u32[]{:S(2)}) collective-permute-start(f32[4,40,128]{2,1,0:T(8,128)S(1)} %get-tuple-element.44), channel_id=1, source_target_pairs={{0,3},{1,0},{2,1},{3,2},{4,7},{5,4},{6,5},{7,6},{8,11},{9,8},{10,9... | collective-permute-start | bytes 245768 | tf_op jit(solution)/shard_map/ppermute | solution.py:30
  36.1 6.2 %collective-permute-start.12 = (f32[2,40,128]{2,1,0:T(8,128)S(1)}, f32[2,40,128]{2,1,0:T(8,128)S(1)}, u32[]{:S(2)}, u32[]{:S(2)}) collective-permute-start(f32[2,40,128]{2,1,0:T(8,128)S(1)} %get-tuple-element.41), channel_id=1, source_target_pairs={{0,9},{1,10},{2,11},{3,8},{4,13},{5,14},{6,15},{7,12},{8,17},{9,18... | collective-permute-start | bytes 122888 | tf_op jit(solution)/shard_map/ppermute | solution.py:30
  36.1 6.2 %collective-permute-start.13 = (f32[2,40,128]{2,1,0:T(8,128)S(1)}, f32[2,40,128]{2,1,0:T(8,128)S(1)}, u32[]{:S(2)}, u32[]{:S(2)}) collective-permute-start(f32[2,40,128]{2,1,0:T(8,128)S(1)} %get-tuple-element.42), channel_id=1, source_target_pairs={{0,11},{1,8},{2,9},{3,10},{4,15},{5,12},{6,13},{7,14},{8,19},{9,16... | collective-permute-start | bytes 122888 | tf_op jit(solution)/shard_map/ppermute | solution.py:30
where the time goes:
time: 45.1 us; the launch traced here: 44.7 us
  starting transfers between devices  29.2 us (65%)
  waiting for transfers between devices  6.62 us (15%)
  Pallas kernels  5.62 us (12%)
  local copies, waits for them, and re-layouts  3.19 us (7%)
    ppermute x16, starting transfers between devices, shifted(): return lax.ppermute(value, AXES, pairs)  29.2 us
    ppermute x16, waiting for transfers between devices, shifted(): return lax.ppermute(value, AXES, pairs)  6.62 us
    pallas_call x4, Pallas kernels, call(): pl.pallas_call(kernel, name=name, out_shape=[jax.ShapeDtypeStruct(shape,...  5.62 us
    unnamed x8, local copies, waits for them, and re-layouts  3.19 us
  transfers between devices with their start and end apart: 16, of which 4 were waited for; matrix products, arithmetic and copies ran while one was open for 0% of the time, Pallas kernels for 0%

commit v1 on v0

--- a/solution.py
+++ b/solution.py
@@ -145,9 +145,16 @@
     return at
 
 
-def pack_kernel(last_ref, initial_ref, guess_ref, feed_ref, kill_ref, state_ref, all_ref, low_ref, high_ref):
+def pack_kernel(last_ref, initial_hbm, guess_hbm, feed_hbm, kill_hbm, state_ref, all_ref, low_ref, high_ref, *scratch):
+    initial_ref, guess_ref, feed_ref, kill_ref, arrived = scratch
     _, n_x, n_y, _ = initial_ref.shape
     is_last = last_ref[0] == 1
+    pairs = ((initial_hbm, initial_ref), (guess_hbm, guess_ref), (feed_hbm, feed_ref), (kill_hbm, kill_ref))
+    copies = [pltpu.make_async_copy(src, dst, arrived.at[i]) for i, (src, dst) in enumerate(pairs)]
+    for copy in copies:
+        copy.start()
+    for copy in copies:
+        copy.wait()
     for x in range(n_x):
         rows = pl.ds(x, n_y, stride=n_x)
         for field in range(2):
@@ -243,9 +250,9 @@
                 out_ref[field, x] = scratch[field, pl.ds(x, n_y, stride=width), :]
 
 
-def call(kernel, name, n_scalars, operands, shapes, scratch=()):
+def call(kernel, name, n_scalars, operands, shapes, scratch=(), space=pltpu.VMEM):
     specs = [pl.BlockSpec(memory_space=pltpu.SMEM)] * n_scalars
-    specs += [pl.BlockSpec(memory_space=pltpu.VMEM)] * (len(operands) - n_scalars)
+    specs += [pl.BlockSpec(memory_space=space)] * (len(operands) - n_scalars)
     return pl.pallas_call(
         kernel,
         name=name,
@@ -271,6 +278,9 @@
         1,
         (is_last, initial_state, slice_guess[0], feed_rate, kill_rate),
         [(2, n_y * n_x, n_z), (4, n_y * n_x, n_z), (4, PACK * n_x, n_z), (4, PACK * n_x, n_z)],
+        [pltpu.VMEM(a.shape, jnp.float32) for a in (initial_state, slice_guess[0], feed_rate, kill_rate)]
+        + [pltpu.SemaphoreType.DMA((4,))],
+        pltpu.HBM,
     )
     got = [shifted(state, 1, 0, 0), local]
     got += [shifted(local, 1, -gy, 0) for gy in range(1, n_gy)]

time: 45.1 us -> 45.3 us (level)
  no operation moved by 1% of the time
where the time goes in v1:
time: 45.3 us; the launch traced here: 45 us
  starting transfers between devices  29.2 us (64%)
  waiting for transfers between devices  6.62 us (15%)
  Pallas kernels  5.88 us (13%)
  local copies, waits for them, and re-layouts  3.19 us (7%)
    ppermute x16, starting transfers between devices, shifted(): return lax.ppermute(value, AXES, pairs)  29.2 us
    ppermute x16, waiting for transfers between devices, shifted(): return lax.ppermute(value, AXES, pairs)  6.62 us
    pallas_call x4, Pallas kernels, call(): pl.pallas_call(kernel, name=name, out_shape=[jax.ShapeDtypeStruct(shape,...  5.88 us
    unnamed x8, local copies, waits for them, and re-layouts  3.19 us
  transfers between devices with their start and end apart: 16, of which 4 were waited for; matrix products, arithmetic and copies ran while one was open for 0% of the time, Pallas kernels for 0%

profile of v1, /device:TPU:0, one launch (start us, length us, event | category | flops | bytes accessed | tf_op | source)
XLA Modules:
  0.0 45.0 jit_solution(15580689735011003080)
XLA Ops:
  0.0 0.0 copy-start
  0.0 0.8 %copy-done = f32[2,4,16,128]{3,2,1,0:T(8,128)S(1)} copy-done((f32[2,4,16,128]{3,2,1,0:T(8,128)S(1)}, f32[2,4,16,128]{3,2,1,0:T(8,128)}, u32[]{:S(2)}) %copy-start) | copy-done | bytes 65560
  0.8 0.0 copy-start.1
  0.8 0.8 %copy-done.1 = f32[1,2,4,16,128]{4,3,2,1,0:T(8,128)S(1)} copy-done((f32[1,2,4,16,128]{4,3,2,1,0:T(8,128)S(1)}, f32[1,2,4,16,128]{4,3,2,1,0:T(8,128)}, u32[]{:S(2)}) %copy-start.1) | copy-done | bytes 65560
  1.7 0.0 copy-start.2
  1.7 0.8 %copy-done.2 = f32[4,16,128]{2,1,0:T(8,128)S(1)} copy-done((f32[4,16,128]{2,1,0:T(8,128)S(1)}, f32[4,16,128]{2,1,0:T(8,128)}, u32[]{:S(2)}) %copy-start.2) | copy-done | bytes 32792
  2.4 0.0 copy-start.3
  2.4 0.8 %copy-done.3 = f32[4,16,128]{2,1,0:T(8,128)S(1)} copy-done((f32[4,16,128]{2,1,0:T(8,128)S(1)}, f32[4,16,128]{2,1,0:T(8,128)}, u32[]{:S(2)}) %copy-start.3) | copy-done | bytes 32792
  3.2 0.3 pack.1
  3.5 2.5 %collective-permute-start.1 = (f32[4,64,128]{2,1,0:T(8,128)S(1)}, f32[4,64,128]{2,1,0:T(8,128)S(1)}, u32[]{:S(2)}, u32[]{:S(2)}) collective-permute-start(f32[4,64,128]{2,1,0:T(8,128)S(1)} %get-tuple-element.26.refs_1_), channel_id=1, source_target_pairs={{0,12},{1,13},{2,14},{3,15},{4,8},{5,9},{6,10},{7,11},{8,20},{9,21... | collective-permute-start | bytes 393224 | tf_op jit(solution)/shard_map/ppermute | solution.py:30
  6.0 2.7 %collective-permute-start.3 = (f32[4,24,128]{2,1,0:T(8,128)S(1)}, f32[4,24,128]{2,1,0:T(8,128)S(1)}, u32[]{:S(2)}, u32[]{:S(2)}) collective-permute-start(f32[4,24,128]{2,1,0:T(8,128)S(1)} %get-tuple-element.27), channel_id=1, source_target_pairs={{0,13},{1,14},{2,15},{3,12},{4,9},{5,10},{6,11},{7,8},{8,21},{9,22... | collective-permute-start | bytes 147464 | tf_op jit(solution)/shard_map/ppermute | solution.py:30
  8.7 0.0 collective-permute-start
  8.7 1.8 %collective-permute-start.2 = (f32[4,24,128]{2,1,0:T(8,128)S(1)}, f32[4,24,128]{2,1,0:T(8,128)S(1)}, u32[]{:S(2)}, u32[]{:S(2)}) collective-permute-start(f32[4,24,128]{2,1,0:T(8,128)S(1)} %get-tuple-element.27), channel_id=1, source_target_pairs={{0,9},{1,10},{2,11},{3,8},{4,13},{5,14},{6,15},{7,12},{8,17},{9,18... | collective-permute-start | bytes 147464 | tf_op jit(solution)/shard_map/ppermute | solution.py:30
  10.5 2.6 %collective-permute-start.5 = (f32[4,24,128]{2,1,0:T(8,128)S(1)}, f32[4,24,128]{2,1,0:T(8,128)S(1)}, u32[]{:S(2)}, u32[]{:S(2)}) collective-permute-start(f32[4,24,128]{2,1,0:T(8,128)S(1)} %get-tuple-element.28), channel_id=1, source_target_pairs={{0,15},{1,12},{2,13},{3,14},{4,11},{5,8},{6,9},{7,10},{8,23},{9,20... | collective-permute-start | bytes 147464 | tf_op jit(solution)/shard_map/ppermute | solution.py:30
  13.2 0.0 collective-permute-done.3.refs_4_
  13.2 2.5 %collective-permute-start.4 = (f32[4,24,128]{2,1,0:T(8,128)S(1)}, f32[4,24,128]{2,1,0:T(8,128)S(1)}, u32[]{:S(2)}, u32[]{:S(2)}) collective-permute-start(f32[4,24,128]{2,1,0:T(8,128)S(1)} %get-tuple-element.28), channel_id=1, source_target_pairs={{0,11},{1,8},{2,9},{3,10},{4,15},{5,12},{6,13},{7,14},{8,19},{9,16... | collective-permute-start | bytes 147464 | tf_op jit(solution)/shard_map/ppermute | solution.py:30
  15.7 0.0 collective-permute-done.2.refs_3_
  15.7 1.6 %collective-permute-done.5.refs_6_ = f32[4,24,128]{2,1,0:T(8,128)S(1)} collective-permute-done((f32[4,24,128]{2,1,0:T(8,128)S(1)}, f32[4,24,128]{2,1,0:T(8,128)S(1)}, u32[]{:S(2)}, u32[]{:S(2)}) %collective-permute-start.5) | collective-permute-done | bytes 49184 | tf_op jit(solution)/shard_map/ppermute | solution.py:30
  17.3 0.5 %collective-permute-done.4.refs_5_ = f32[4,24,128]{2,1,0:T(8,128)S(1)} collective-permute-done((f32[4,24,128]{2,1,0:T(8,128)S(1)}, f32[4,24,128]{2,1,0:T(8,128)S(1)}, u32[]{:S(2)}, u32[]{:S(2)}) %collective-permute-start.4) | collective-permute-done | bytes 49184 | tf_op jit(solution)/shard_map/ppermute | solution.py:30
  17.8 0.0 collective-permute-done.refs_0_
  17.8 0.0 collective-permute-done.1.refs_2_
  17.8 1.2 %first.1 = (f32[2,208,128]{2,1,0:T(8,128)S(1)}, f32[2,208,128]{2,1,0:T(8,128)S(1)}, f32[2,192,128]{2,1,0:T(8,128)S(1)}, f32[2,128,128]{2,1,0:T(8,128)S(1)}, f32[...) custom-call(f32[2,64,128]{2,1,0:T(8,128)S(1)} %collective-permute-do, ...), custom_call_target="tpu_custom_call" | custom-call | tf_op jit(solution)/shard_map/first/pallas_call | solution.py:256
  19.0 0.6 %collective-permute-start.6 = (f32[2,128,128]{2,1,0:T(8,128)S(1)}, f32[2,128,128]{2,1,0:T(8,128)S(1)}, u32[]{:S(2)}, u32[]{:S(2)}) collective-permute-start(f32[2,128,128]{2,1,0:T(8,128)S(1)} %get-tuple-element.33.two_ref), channel_id=1, source_target_pairs={{0,8},{1,9},{2,10},{3,11},{4,12},{5,13},{6,14},{7,15},{8,16},{9,17... | collective-permute-start | bytes 393224 | tf_op jit(solution)/shard_map/ppermute | solution.py:30
  19.6 0.8 %collective-permute-start.9 = (f32[4,40,128]{2,1,0:T(8,128)S(1)}, f32[4,40,128]{2,1,0:T(8,128)S(1)}, u32[]{:S(2)}, u32[]{:S(2)}) collective-permute-start(f32[4,40,128]{2,1,0:T(8,128)S(1)} %get-tuple-element.36), channel_id=1, source_target_pairs={{0,1},{1,2},{2,3},{3,0},{4,5},{5,6},{6,7},{7,4},{8,9},{9,10},{10,1... | collective-permute-start | bytes 245768 | tf_op jit(solution)/shard_map/ppermute | solution.py:30
  20.3 3.1 %collective-permute-start.10 = (f32[4,40,128]{2,1,0:T(8,128)S(1)}, f32[4,40,128]{2,1,0:T(8,128)S(1)}, u32[]{:S(2)}, u32[]{:S(2)}) collective-permute-start(f32[4,40,128]{2,1,0:T(8,128)S(1)} %get-tuple-element.37), channel_id=1, source_target_pairs={{0,3},{1,0},{2,1},{3,2},{4,7},{5,4},{6,5},{7,6},{8,11},{9,8},{10,9... | collective-permute-start | bytes 245768 | tf_op jit(solution)/shard_map/ppermute | solution.py:30
  23.4 0.0 collective-permute-start.7
  23.4 4.5 %collective-permute-start.8 = (f32[2,40,128]{2,1,0:T(8,128)S(1)}, f32[2,40,128]{2,1,0:T(8,128)S(1)}, u32[]{:S(2)}, u32[]{:S(2)}) collective-permute-start(f32[2,40,128]{2,1,0:T(8,128)S(1)} %get-tuple-element.35), channel_id=1, source_target_pairs={{0,11},{1,8},{2,9},{3,10},{4,15},{5,12},{6,13},{7,14},{8,19},{9,16... | collective-permute-start | bytes 122888 | tf_op jit(solution)/shard_map/ppermute | solution.py:30
  27.9 2.0 %collective-permute-done.7.got_low = f32[2,40,128]{2,1,0:T(8,128)S(1)} collective-permute-done((f32[2,40,128]{2,1,0:T(8,128)S(1)}, f32[2,40,128]{2,1,0:T(8,128)S(1)}, u32[]{:S(2)}, u32[]{:S(2)}) %collective-permute-start.7) | collective-permute-done | bytes 40992 | tf_op jit(solution)/shard_map/ppermute | solution.py:30
  30.0 0.0 collective-permute-done.8.got_high
  30.0 0.0 collective-permute-done.9.low_ref
  30.0 0.0 collective-permute-done.10.high_ref
  30.0 0.0 collective-permute-done.6.got_ref
  30.0 1.9 %later.1 = (f32[2,192,128]{2,1,0:T(8,128)S(1)}, f32[2,128,128]{2,1,0:T(8,128)S(1)}, f32[2,128,128]{2,1,0:T(8,128)S(1)}, f32[2,40,128]{2,1,0:T(8,128)S(1)}, f32[2...) custom-call(s32[1]{0:T(128)} %bitcast.first_ref, ...), custom_call_target="tpu_custom_call" | custom-call | tf_op jit(solution)/shard_map/later/pallas_call | solution.py:256
  31.9 0.3 collective-permute-start.11
  32.2 0.7 %collective-permute-start.14 = (f32[4,40,128]{2,1,0:T(8,128)S(1)}, f32[4,40,128]{2,1,0:T(8,128)S(1)}, u32[]{:S(2)}, u32[]{:S(2)}) collective-permute-start(f32[4,40,128]{2,1,0:T(8,128)S(1)} %get-tuple-element.43), channel_id=1, source_target_pairs={{0,1},{1,2},{2,3},{3,0},{4,5},{5,6},{6,7},{7,4},{8,9},{9,10},{10,1... | collective-permute-start | bytes 245768 | tf_op jit(solution)/shard_map/ppermute | solution.py:30
  32.9 3.4 %collective-permute-start.15 = (f32[4,40,128]{2,1,0:T(8,128)S(1)}, f32[4,40,128]{2,1,0:T(8,128)S(1)}, u32[]{:S(2)}, u32[]{:S(2)}) collective-permute-start(f32[4,40,128]{2,1,0:T(8,128)S(1)} %get-tuple-element.44), channel_id=1, source_target_pairs={{0,3},{1,0},{2,1},{3,2},{4,7},{5,4},{6,5},{7,6},{8,11},{9,8},{10,9... | collective-permute-start | bytes 245768 | tf_op jit(solution)/shard_map/ppermute | solution.py:30
  36.3 0.0 collective-permute-start.12
  36.3 3.7 %collective-permute-start.13 = (f32[2,40,128]{2,1,0:T(8,128)S(1)}, f32[2,40,128]{2,1,0:T(8,128)S(1)}, u32[]{:S(2)}, u32[]{:S(2)}) collective-permute-start(f32[2,40,128]{2,1,0:T(8,128)S(1)} %get-tuple-element.42), channel_id=1, source_target_pairs={{0,11},{1,8},{2,9},{3,10},{4,15},{5,12},{6,13},{7,14},{8,19},{9,16... | collective-permute-start | bytes 122888 | tf_op jit(solution)/shard_map/ppermute | solution.py:30
  40.0 2.5 %collective-permute-done.12.got_low = f32[2,40,128]{2,1,0:T(8,128)S(1)} collective-permute-done((f32[2,40,128]{2,1,0:T(8,128)S(1)}, f32[2,40,128]{2,1,0:T(8,128)S(1)}, u32[]{:S(2)}, u32[]{:S(2)}) %collective-permute-start.12) | collective-permute-done | bytes 40992 | tf_op jit(solution)/shard_map/ppermute | solution.py:30
  42.5 0.0 collective-permute-done.13.got_high
  42.5 0.0 collective-permute-done.14.low_ref
  42.5 0.0 collective-permute-done.15.high_ref
  42.5 0.0 collective-permute-done.11.got_ref
  42.5 2.5 %last.1 = f32[2,4,16,128]{3,2,1,0:T(8,128)} custom-call(s32[1]{0:T(128)} %bitcast.first_ref, f32[2,208,128]{2,1,0:T(8,128)S(1)} %get-tuple-element.29.start_ref, f32[2,208,128]{2,1,0:T(8,128)S(1)} %get-tuple-element.30.params_ref, f32[2,192,128]{2,1,0:T(8,128)S(1)} %get-tuple-element.38.zero_ref, f32[2,128,128]{2,1,0:T(8,128)S(1)} %get-tuple-element.39.one_ref, ...), custom_call_target="tpu_custom_call" | custom-call | tf_op jit(solution)/shard_map/last/pallas_call | solution.py:256
Async XLA Ops:
  0.0 0.8 %copy-start = (f32[2,4,16,128]{3,2,1,0:T(8,128)S(1)}, f32[2,4,16,128]{3,2,1,0:T(8,128)}, u32[]{:S(2)}) copy-start(f32[2,4,16,128]{3,2,1,0:T(8,128)} %initial_hbm.1) | copy-start | bytes 196612
  0.8 0.8 %copy-start.1 = (f32[1,2,4,16,128]{4,3,2,1,0:T(8,128)S(1)}, f32[1,2,4,16,128]{4,3,2,1,0:T(8,128)}, u32[]{:S(2)}) copy-start(f32[1,2,4,16,128]{4,3,2,1,0:T(8,128)} %param.5) | copy-start | bytes 196612
  1.7 0.8 %copy-start.2 = (f32[4,16,128]{2,1,0:T(8,128)S(1)}, f32[4,16,128]{2,1,0:T(8,128)}, u32[]{:S(2)}) copy-start(f32[4,16,128]{2,1,0:T(8,128)} %feed_hbm.1) | copy-start | bytes 98308
  2.4 0.8 %copy-start.3 = (f32[4,16,128]{2,1,0:T(8,128)S(1)}, f32[4,16,128]{2,1,0:T(8,128)}, u32[]{:S(2)}) copy-start(f32[4,16,128]{2,1,0:T(8,128)} %kill_hbm.1) | copy-start | bytes 98308
  3.5 14.3 %collective-permute-start.1 = (f32[4,64,128]{2,1,0:T(8,128)S(1)}, f32[4,64,128]{2,1,0:T(8,128)S(1)}, u32[]{:S(2)}, u32[]{:S(2)}) collective-permute-start(f32[4,64,128]{2,1,0:T(8,128)S(1)} %get-tuple-element.26.refs_1_), channel_id=1, source_target_pairs={{0,12},{1,13},{2,14},{3,15},{4,8},{5,9},{6,10},{7,11},{8,20},{9,21... | collective-permute-start | bytes 393224 | tf_op jit(solution)/shard_map/ppermute | solution.py:30
  6.0 7.2 %collective-permute-start.3 = (f32[4,24,128]{2,1,0:T(8,128)S(1)}, f32[4,24,128]{2,1,0:T(8,128)S(1)}, u32[]{:S(2)}, u32[]{:S(2)}) collective-permute-start(f32[4,24,128]{2,1,0:T(8,128)S(1)} %get-tuple-element.27), channel_id=1, source_target_pairs={{0,13},{1,14},{2,15},{3,12},{4,9},{5,10},{6,11},{7,8},{8,21},{9,22... | collective-permute-start | bytes 147464 | tf_op jit(solution)/shard_map/ppermute | solution.py:30
  8.7 9.1 %collective-permute-start = (f32[2,64,128]{2,1,0:T(8,128)S(1)}, f32[2,64,128]{2,1,0:T(8,128)S(1)}, u32[]{:S(2)}, u32[]{:S(2)}) collective-permute-start(f32[2,64,128]{2,1,0:T(8,128)S(1)} %get-tuple-element.25), channel_id=1, source_target_pairs={{0,8},{1,9},{2,10},{3,11},{4,12},{5,13},{6,14},{7,15},{8,16},{9,17... | collective-permute-start | bytes 196616 | tf_op jit(solution)/shard_map/ppermute | solution.py:30
  8.7 7.0 %collective-permute-start.2 = (f32[4,24,128]{2,1,0:T(8,128)S(1)}, f32[4,24,128]{2,1,0:T(8,128)S(1)}, u32[]{:S(2)}, u32[]{:S(2)}) collective-permute-start(f32[4,24,128]{2,1,0:T(8,128)S(1)} %get-tuple-element.27), channel_id=1, source_target_pairs={{0,9},{1,10},{2,11},{3,8},{4,13},{5,14},{6,15},{7,12},{8,17},{9,18... | collective-permute-start | bytes 147464 | tf_op jit(solution)/shard_map/ppermute | solution.py:30
  10.5 6.8 %collective-permute-start.5 = (f32[4,24,128]{2,1,0:T(8,128)S(1)}, f32[4,24,128]{2,1,0:T(8,128)S(1)}, u32[]{:S(2)}, u32[]{:S(2)}) collective-permute-start(f32[4,24,128]{2,1,0:T(8,128)S(1)} %get-tuple-element.28), channel_id=1, source_target_pairs={{0,15},{1,12},{2,13},{3,14},{4,11},{5,8},{6,9},{7,10},{8,23},{9,20... | collective-permute-start | bytes 147464 | tf_op jit(solution)/shard_map/ppermute | solution.py:30
  13.2 4.6 %collective-permute-start.4 = (f32[4,24,128]{2,1,0:T(8,128)S(1)}, f32[4,24,128]{2,1,0:T(8,128)S(1)}, u32[]{:S(2)}, u32[]{:S(2)}) collective-permute-start(f32[4,24,128]{2,1,0:T(8,128)S(1)} %get-tuple-element.28), channel_id=1, source_target_pairs={{0,11},{1,8},{2,9},{3,10},{4,15},{5,12},{6,13},{7,14},{8,19},{9,16... | collective-permute-start | bytes 147464 | tf_op jit(solution)/shard_map/ppermute | solution.py:30
  19.0 11.0 %collective-permute-start.6 = (f32[2,128,128]{2,1,0:T(8,128)S(1)}, f32[2,128,128]{2,1,0:T(8,128)S(1)}, u32[]{:S(2)}, u32[]{:S(2)}) collective-permute-start(f32[2,128,128]{2,1,0:T(8,128)S(1)} %get-tuple-element.33.two_ref), channel_id=1, source_target_pairs={{0,8},{1,9},{2,10},{3,11},{4,12},{5,13},{6,14},{7,15},{8,16},{9,17... | collective-permute-start | bytes 393224 | tf_op jit(solution)/shard_map/ppermute | solution.py:30
  19.6 10.4 %collective-permute-start.9 = (f32[4,40,128]{2,1,0:T(8,128)S(1)}, f32[4,40,128]{2,1,0:T(8,128)S(1)}, u32[]{:S(2)}, u32[]{:S(2)}) collective-permute-start(f32[4,40,128]{2,1,0:T(8,128)S(1)} %get-tuple-element.36), channel_id=1, source_target_pairs={{0,1},{1,2},{2,3},{3,0},{4,5},{5,6},{6,7},{7,4},{8,9},{9,10},{10,1... | collective-permute-start | bytes 245768 | tf_op jit(solution)/shard_map/ppermute | solution.py:30
  20.3 9.6 %collective-permute-start.10 = (f32[4,40,128]{2,1,0:T(8,128)S(1)}, f32[4,40,128]{2,1,0:T(8,128)S(1)}, u32[]{:S(2)}, u32[]{:S(2)}) collective-permute-start(f32[4,40,128]{2,1,0:T(8,128)S(1)} %get-tuple-element.37), channel_id=1, source_target_pairs={{0,3},{1,0},{2,1},{3,2},{4,7},{5,4},{6,5},{7,6},{8,11},{9,8},{10,9... | collective-permute-start | bytes 245768 | tf_op jit(solution)/shard_map/ppermute | solution.py:30
  23.4 6.6 %collective-permute-start.7 = (f32[2,40,128]{2,1,0:T(8,128)S(1)}, f32[2,40,128]{2,1,0:T(8,128)S(1)}, u32[]{:S(2)}, u32[]{:S(2)}) collective-permute-start(f32[2,40,128]{2,1,0:T(8,128)S(1)} %get-tuple-element.34), channel_id=1, source_target_pairs={{0,9},{1,10},{2,11},{3,8},{4,13},{5,14},{6,15},{7,12},{8,17},{9,18... | collective-permute-start | bytes 122888 | tf_op jit(solution)/shard_map/ppermute | solution.py:30
  23.4 6.6 %collective-permute-start.8 = (f32[2,40,128]{2,1,0:T(8,128)S(1)}, f32[2,40,128]{2,1,0:T(8,128)S(1)}, u32[]{:S(2)}, u32[]{:S(2)}) collective-permute-start(f32[2,40,128]{2,1,0:T(8,128)S(1)} %get-tuple-element.35), channel_id=1, source_target_pairs={{0,11},{1,8},{2,9},{3,10},{4,15},{5,12},{6,13},{7,14},{8,19},{9,16... | collective-permute-start | bytes 122888 | tf_op jit(solution)/shard_map/ppermute | solution.py:30
  31.9 10.6 %collective-permute-start.11 = (f32[2,128,128]{2,1,0:T(8,128)S(1)}, f32[2,128,128]{2,1,0:T(8,128)S(1)}, u32[]{:S(2)}, u32[]{:S(2)}) collective-permute-start(f32[2,128,128]{2,1,0:T(8,128)S(1)} %get-tuple-element.40.two_ref), channel_id=1, source_target_pairs={{0,8},{1,9},{2,10},{3,11},{4,12},{5,13},{6,14},{7,15},{8,16},{9,17... | collective-permute-start | bytes 393224 | tf_op jit(solution)/shard_map/ppermute | solution.py:30
  32.2 10.3 %collective-permute-start.14 = (f32[4,40,128]{2,1,0:T(8,128)S(1)}, f32[4,40,128]{2,1,0:T(8,128)S(1)}, u32[]{:S(2)}, u32[]{:S(2)}) collective-permute-start(f32[4,40,128]{2,1,0:T(8,128)S(1)} %get-tuple-element.43), channel_id=1, source_target_pairs={{0,1},{1,2},{2,3},{3,0},{4,5},{5,6},{6,7},{7,4},{8,9},{9,10},{10,1... | collective-permute-start | bytes 245768 | tf_op jit(solution)/shard_map/ppermute | solution.py:30
  32.9 9.6 %collective-permute-start.15 = (f32[4,40,128]{2,1,0:T(8,128)S(1)}, f32[4,40,128]{2,1,0:T(8,128)S(1)}, u32[]{:S(2)}, u32[]{:S(2)}) collective-permute-start(f32[4,40,128]{2,1,0:T(8,128)S(1)} %get-tuple-element.44), channel_id=1, source_target_pairs={{0,3},{1,0},{2,1},{3,2},{4,7},{5,4},{6,5},{7,6},{8,11},{9,8},{10,9... | collective-permute-start | bytes 245768 | tf_op jit(solution)/shard_map/ppermute | solution.py:30
  36.3 6.2 %collective-permute-start.12 = (f32[2,40,128]{2,1,0:T(8,128)S(1)}, f32[2,40,128]{2,1,0:T(8,128)S(1)}, u32[]{:S(2)}, u32[]{:S(2)}) collective-permute-start(f32[2,40,128]{2,1,0:T(8,128)S(1)} %get-tuple-element.41), channel_id=1, source_target_pairs={{0,9},{1,10},{2,11},{3,8},{4,13},{5,14},{6,15},{7,12},{8,17},{9,18... | collective-permute-start | bytes 122888 | tf_op jit(solution)/shard_map/ppermute | solution.py:30
  36.3 6.2 %collective-permute-start.13 = (f32[2,40,128]{2,1,0:T(8,128)S(1)}, f32[2,40,128]{2,1,0:T(8,128)S(1)}, u32[]{:S(2)}, u32[]{:S(2)}) collective-permute-start(f32[2,40,128]{2,1,0:T(8,128)S(1)} %get-tuple-element.42), channel_id=1, source_target_pairs={{0,11},{1,8},{2,9},{3,10},{4,15},{5,12},{6,13},{7,14},{8,19},{9,16... | collective-permute-start | bytes 122888 | tf_op jit(solution)/shard_map/ppermute | solution.py:30

commit v2 on v0

--- a/solution.py
+++ b/solution.py
@@ -145,20 +145,15 @@
     return at
 
 
-def pack_kernel(last_ref, initial_ref, guess_ref, feed_ref, kill_ref, state_ref, all_ref, low_ref, high_ref):
-    _, n_x, n_y, _ = initial_ref.shape
-    is_last = last_ref[0] == 1
-    for x in range(n_x):
-        rows = pl.ds(x, n_y, stride=n_x)
-        for field in range(2):
-            tile = jnp.where(is_last, initial_ref[field, x], guess_ref[field, x])
-            state_ref[field, rows, :] = tile
-            all_ref[field, rows, :] = tile
-        all_ref[2, rows, :] = feed_ref[x]
-        all_ref[3, rows, :] = kill_ref[x]
-    for field in range(4):
+def pack_kernel(tiles_ref, state_ref, all_ref, low_ref, high_ref):
+    n_fields, n_x, n_y, _ = tiles_ref.shape
+    for field in range(n_fields):
+        for x in range(n_x):
+            all_ref[field, pl.ds(x, n_y, stride=n_x), :] = tiles_ref[field, x]
         low_ref[field] = all_ref[field, pl.ds(0, PACK * n_x), :]
         high_ref[field] = all_ref[field, pl.ds((n_y - PACK) * n_x, PACK * n_x), :]
+    for field in range(2):
+        state_ref[field] = all_ref[field]
 
 
 def first_kernel(n_gy, n_x, n_y, *refs):
@@ -263,13 +258,13 @@
     width = n_gy * n_x
     place = lax.axis_index("tm")
     is_first = (place == 0).astype(jnp.int32)[None]
-    is_last = (place == n_tm - 1).astype(jnp.int32)[None]
-
+
+    sent = jnp.where(place == n_tm - 1, initial_state, slice_guess[0])
     state, local, low, high = call(
         pack_kernel,
         "pack",
-        1,
-        (is_last, initial_state, slice_guess[0], feed_rate, kill_rate),
+        0,
+        (jnp.concatenate([sent, feed_rate[None], kill_rate[None]]),),
         [(2, n_y * n_x, n_z), (4, n_y * n_x, n_z), (4, PACK * n_x, n_z), (4, PACK * n_x, n_z)],
     )
     got = [shifted(state, 1, 0, 0), local]

time: 45.1 us -> 42.6 us (0.945)
  local copies, waits for them, and re-layouts: 3.19 us -> 0.01 us
  other arithmetic: 0 us -> 0.87 us
    unnamed x8 -> x4, local copies, waits for them, and re-layouts: 3.19 us -> 0.01 us
    select_n x0 -> x1, other arithmetic: none -> 0.86 us  [shards(): sent = jnp.where(place == n_tm - 1, initial_state, slice_guess[0])]
where the time goes in v2:
time: 42.6 us; the launch traced here: 42.5 us
  starting transfers between devices  29.3 us (69%)
  waiting for transfers between devices  6.63 us (16%)
  Pallas kernels  5.62 us (13%)
  other arithmetic  0.87 us (2%)
    ppermute x16, starting transfers between devices, shifted(): return lax.ppermute(value, AXES, pairs)  29.3 us
    ppermute x16, waiting for transfers between devices, shifted(): return lax.ppermute(value, AXES, pairs)  6.63 us
    pallas_call x4, Pallas kernels, call(): pl.pallas_call(kernel, name=name, out_shape=[jax.ShapeDtypeStruct(shape,...  5.62 us
    select_n x1, other arithmetic, shards(): sent = jnp.where(place == n_tm - 1, initial_state, slice_guess[0])  0.86 us
  transfers between devices with their start and end apart: 16, of which 4 were waited for; matrix products, arithmetic and copies ran while one was open for 0% of the time, Pallas kernels for 0%

profile of v2, /device:TPU:0, one launch (start us, length us, event | category | flops | bytes accessed | tf_op | source)
XLA Modules:
  0.0 42.5 jit_solution(5820236739354275363)
XLA Ops:
  0.0 0.0 copy-start
  0.0 0.0 copy-start.1
  0.0 0.9 %bitcast_select_fusion = f32[2,4,16,128]{3,2,1,0:T(8,128)S(1)} fusion(f32[2,4,16,128]{3,2,1,0:T(8,128)} %param.4, f32[1,2,4,16,128]{4,3,2,1,0:T(8,128)} %param.5, pred[]{:T(512)S(6)} %eq.7), kind=kLoop, calls=%fused_computation.1 | loop fusion | flops 16384 | bytes 196609 | tf_op jit(solution)/shard_map/jit(_where)/select_n | solution.py:262
  0.9 0.0 copy-done
  0.9 0.0 copy-done.1
  0.9 2.5 %collective-permute-start.1 = (f32[4,64,128]{2,1,0:T(8,128)S(1)}, f32[4,64,128]{2,1,0:T(8,128)S(1)}, u32[]{:S(2)}, u32[]{:S(2)}) collective-permute-start(f32[4,64,128]{2,1,0:T(8,128)S(1)} %get-tuple-element.26.refs_1_), channel_id=1, source_target_pairs={{0,12},{1,13},{2,14},{3,15},{4,8},{5,9},{6,10},{7,11},{8,20},{9,21... | collective-permute-start | bytes 393224 | tf_op jit(solution)/shard_map/ppermute | solution.py:30
  3.4 2.7 %collective-permute-start.3 = (f32[4,24,128]{2,1,0:T(8,128)S(1)}, f32[4,24,128]{2,1,0:T(8,128)S(1)}, u32[]{:S(2)}, u32[]{:S(2)}) collective-permute-start(f32[4,24,128]{2,1,0:T(8,128)S(1)} %get-tuple-element.27), channel_id=1, source_target_pairs={{0,13},{1,14},{2,15},{3,12},{4,9},{5,10},{6,11},{7,8},{8,21},{9,22... | collective-permute-start | bytes 147464 | tf_op jit(solution)/shard_map/ppermute | solution.py:30
  6.1 0.0 collective-permute-start
  6.1 1.8 %collective-permute-start.2 = (f32[4,24,128]{2,1,0:T(8,128)S(1)}, f32[4,24,128]{2,1,0:T(8,128)S(1)}, u32[]{:S(2)}, u32[]{:S(2)}) collective-permute-start(f32[4,24,128]{2,1,0:T(8,128)S(1)} %get-tuple-element.27), channel_id=1, source_target_pairs={{0,9},{1,10},{2,11},{3,8},{4,13},{5,14},{6,15},{7,12},{8,17},{9,18... | collective-permute-start | bytes 147464 | tf_op jit(solution)/shard_map/ppermute | solution.py:30
  8.0 2.6 %collective-permute-start.5 = (f32[4,24,128]{2,1,0:T(8,128)S(1)}, f32[4,24,128]{2,1,0:T(8,128)S(1)}, u32[]{:S(2)}, u32[]{:S(2)}) collective-permute-start(f32[4,24,128]{2,1,0:T(8,128)S(1)} %get-tuple-element.28), channel_id=1, source_target_pairs={{0,15},{1,12},{2,13},{3,14},{4,11},{5,8},{6,9},{7,10},{8,23},{9,20... | collective-permute-start | bytes 147464 | tf_op jit(solution)/shard_map/ppermute | solution.py:30
  10.6 0.0 collective-permute-done.3.refs_4_
  10.6 2.5 %collective-permute-start.4 = (f32[4,24,128]{2,1,0:T(8,128)S(1)}, f32[4,24,128]{2,1,0:T(8,128)S(1)}, u32[]{:S(2)}, u32[]{:S(2)}) collective-permute-start(f32[4,24,128]{2,1,0:T(8,128)S(1)} %get-tuple-element.28), channel_id=1, source_target_pairs={{0,11},{1,8},{2,9},{3,10},{4,15},{5,12},{6,13},{7,14},{8,19},{9,16... | collective-permute-start | bytes 147464 | tf_op jit(solution)/shard_map/ppermute | solution.py:30
  13.1 0.0 collective-permute-done.2.refs_3_
  13.1 1.6 %collective-permute-done.5.refs_6_ = f32[4,24,128]{2,1,0:T(8,128)S(1)} collective-permute-done((f32[4,24,128]{2,1,0:T(8,128)S(1)}, f32[4,24,128]{2,1,0:T(8,128)S(1)}, u32[]{:S(2)}, u32[]{:S(2)}) %collective-permute-start.5) | collective-permute-done | bytes 49184 | tf_op jit(solution)/shard_map/ppermute | solution.py:30
  14.7 0.5 %collective-permute-done.4.refs_5_ = f32[4,24,128]{2,1,0:T(8,128)S(1)} collective-permute-done((f32[4,24,128]{2,1,0:T(8,128)S(1)}, f32[4,24,128]{2,1,0:T(8,128)S(1)}, u32[]{:S(2)}, u32[]{:S(2)}) %collective-permute-start.4) | collective-permute-done | bytes 49184 | tf_op jit(solution)/shard_map/ppermute | solution.py:30
  15.2 0.0 collective-permute-done.refs_0_
  15.2 0.0 collective-permute-done.1.refs_2_
  15.2 1.2 %first.1 = (f32[2,208,128]{2,1,0:T(8,128)S(1)}, f32[2,208,128]{2,1,0:T(8,128)S(1)}, f32[2,192,128]{2,1,0:T(8,128)S(1)}, f32[2,128,128]{2,1,0:T(8,128)S(1)}, f32[...) custom-call(f32[2,64,128]{2,1,0:T(8,128)S(1)} %collective-permute-do, ...), custom_call_target="tpu_custom_call" | custom-call | tf_op jit(solution)/shard_map/first/pallas_call | solution.py:244
  16.4 0.6 %collective-permute-start.6 = (f32[2,128,128]{2,1,0:T(8,128)S(1)}, f32[2,128,128]{2,1,0:T(8,128)S(1)}, u32[]{:S(2)}, u32[]{:S(2)}) collective-permute-start(f32[2,128,128]{2,1,0:T(8,128)S(1)} %get-tuple-element.33.two_ref), channel_id=1, source_target_pairs={{0,8},{1,9},{2,10},{3,11},{4,12},{5,13},{6,14},{7,15},{8,16},{9,17... | collective-permute-start | bytes 393224 | tf_op jit(solution)/shard_map/ppermute | solution.py:30
  17.0 0.8 %collective-permute-start.9 = (f32[4,40,128]{2,1,0:T(8,128)S(1)}, f32[4,40,128]{2,1,0:T(8,128)S(1)}, u32[]{:S(2)}, u32[]{:S(2)}) collective-permute-start(f32[4,40,128]{2,1,0:T(8,128)S(1)} %get-tuple-element.36), channel_id=1, source_target_pairs={{0,1},{1,2},{2,3},{3,0},{4,5},{5,6},{6,7},{7,4},{8,9},{9,10},{10,1... | collective-permute-start | bytes 245768 | tf_op jit(solution)/shard_map/ppermute | solution.py:30
  17.8 3.1 %collective-permute-start.10 = (f32[4,40,128]{2,1,0:T(8,128)S(1)}, f32[4,40,128]{2,1,0:T(8,128)S(1)}, u32[]{:S(2)}, u32[]{:S(2)}) collective-permute-start(f32[4,40,128]{2,1,0:T(8,128)S(1)} %get-tuple-element.37), channel_id=1, source_target_pairs={{0,3},{1,0},{2,1},{3,2},{4,7},{5,4},{6,5},{7,6},{8,11},{9,8},{10,9... | collective-permute-start | bytes 245768 | tf_op jit(solution)/shard_map/ppermute | solution.py:30
  20.9 0.0 collective-permute-start.7
  20.9 4.5 %collective-permute-start.8 = (f32[2,40,128]{2,1,0:T(8,128)S(1)}, f32[2,40,128]{2,1,0:T(8,128)S(1)}, u32[]{:S(2)}, u32[]{:S(2)}) collective-permute-start(f32[2,40,128]{2,1,0:T(8,128)S(1)} %get-tuple-element.35), channel_id=1, source_target_pairs={{0,11},{1,8},{2,9},{3,10},{4,15},{5,12},{6,13},{7,14},{8,19},{9,16... | collective-permute-start | bytes 122888 | tf_op jit(solution)/shard_map/ppermute | solution.py:30
  25.4 2.0 %collective-permute-done.7.got_low = f32[2,40,128]{2,1,0:T(8,128)S(1)} collective-permute-done((f32[2,40,128]{2,1,0:T(8,128)S(1)}, f32[2,40,128]{2,1,0:T(8,128)S(1)}, u32[]{:S(2)}, u32[]{:S(2)}) %collective-permute-start.7) | collective-permute-done | bytes 40992 | tf_op jit(solution)/shard_map/ppermute | solution.py:30
  27.4 0.0 collective-permute-done.8.got_high
  27.4 0.0 collective-permute-done.9.low_ref
  27.4 0.0 collective-permute-done.10.high_ref
  27.4 0.0 collective-permute-done.6.got_ref
  27.4 1.9 %later.1 = (f32[2,192,128]{2,1,0:T(8,128)S(1)}, f32[2,128,128]{2,1,0:T(8,128)S(1)}, f32[2,128,128]{2,1,0:T(8,128)S(1)}, f32[2,40,128]{2,1,0:T(8,128)S(1)}, f32[2...) custom-call(s32[1]{0:T(128)} %bitcast.first_ref, ...), custom_call_target="tpu_custom_call" | custom-call | tf_op jit(solution)/shard_map/later/pallas_call | solution.py:244
  29.4 0.3 collective-permute-start.11
  29.7 0.7 %collective-permute-start.14 = (f32[4,40,128]{2,1,0:T(8,128)S(1)}, f32[4,40,128]{2,1,0:T(8,128)S(1)}, u32[]{:S(2)}, u32[]{:S(2)}) collective-permute-start(f32[4,40,128]{2,1,0:T(8,128)S(1)} %get-tuple-element.43), channel_id=1, source_target_pairs={{0,1},{1,2},{2,3},{3,0},{4,5},{5,6},{6,7},{7,4},{8,9},{9,10},{10,1... | collective-permute-start | bytes 245768 | tf_op jit(solution)/shard_map/ppermute | solution.py:30
  30.4 3.4 %collective-permute-start.15 = (f32[4,40,128]{2,1,0:T(8,128)S(1)}, f32[4,40,128]{2,1,0:T(8,128)S(1)}, u32[]{:S(2)}, u32[]{:S(2)}) collective-permute-start(f32[4,40,128]{2,1,0:T(8,128)S(1)} %get-tuple-element.44), channel_id=1, source_target_pairs={{0,3},{1,0},{2,1},{3,2},{4,7},{5,4},{6,5},{7,6},{8,11},{9,8},{10,9... | collective-permute-start | bytes 245768 | tf_op jit(solution)/shard_map/ppermute | solution.py:30
  33.8 0.0 collective-permute-start.12
  33.8 3.7 %collective-permute-start.13 = (f32[2,40,128]{2,1,0:T(8,128)S(1)}, f32[2,40,128]{2,1,0:T(8,128)S(1)}, u32[]{:S(2)}, u32[]{:S(2)}) collective-permute-start(f32[2,40,128]{2,1,0:T(8,128)S(1)} %get-tuple-element.42), channel_id=1, source_target_pairs={{0,11},{1,8},{2,9},{3,10},{4,15},{5,12},{6,13},{7,14},{8,19},{9,16... | collective-permute-start | bytes 122888 | tf_op jit(solution)/shard_map/ppermute | solution.py:30
  37.5 2.5 %collective-permute-done.12.got_low = f32[2,40,128]{2,1,0:T(8,128)S(1)} collective-permute-done((f32[2,40,128]{2,1,0:T(8,128)S(1)}, f32[2,40,128]{2,1,0:T(8,128)S(1)}, u32[]{:S(2)}, u32[]{:S(2)}) %collective-permute-start.12) | collective-permute-done | bytes 40992 | tf_op jit(solution)/shard_map/ppermute | solution.py:30
  40.0 0.0 collective-permute-done.13.got_high
  40.0 0.0 collective-permute-done.14.low_ref
  40.0 0.0 collective-permute-done.15.high_ref
  40.0 0.0 collective-permute-done.11.got_ref
  40.0 2.5 %last.1 = f32[2,4,16,128]{3,2,1,0:T(8,128)} custom-call(s32[1]{0:T(128)} %bitcast.first_ref, f32[2,208,128]{2,1,0:T(8,128)S(1)} %get-tuple-element.29.start_ref, f32[2,208,128]{2,1,0:T(8,128)S(1)} %get-tuple-element.30.params_ref, f32[2,192,128]{2,1,0:T(8,128)S(1)} %get-tuple-element.38.zero_ref, f32[2,128,128]{2,1,0:T(8,128)S(1)} %get-tuple-element.39.one_ref, ...), custom_call_target="tpu_custom_call" | custom-call | tf_op jit(solution)/shard_map/last/pallas_call | solution.py:244
  (2 shorter events, 0.0 us)
Async XLA Ops:
  0.0 0.9 %copy-start = (f32[4,16,128]{2,1,0:T(8,128)S(1)}, f32[4,16,128]{2,1,0:T(8,128)}, u32[]{:S(2)}) copy-start(f32[4,16,128]{2,1,0:T(8,128)} %param.7) | copy-start | bytes 98308
  0.0 0.9 %copy-start.1 = (f32[4,16,128]{2,1,0:T(8,128)S(1)}, f32[4,16,128]{2,1,0:T(8,128)}, u32[]{:S(2)}) copy-start(f32[4,16,128]{2,1,0:T(8,128)} %param.6) | copy-start | bytes 98308
  0.9 14.3 %collective-permute-start.1 = (f32[4,64,128]{2,1,0:T(8,128)S(1)}, f32[4,64,128]{2,1,0:T(8,128)S(1)}, u32[]{:S(2)}, u32[]{:S(2)}) collective-permute-start(f32[4,64,128]{2,1,0:T(8,128)S(1)} %get-tuple-element.26.refs_1_), channel_id=1, source_target_pairs={{0,12},{1,13},{2,14},{3,15},{4,8},{5,9},{6,10},{7,11},{8,20},{9,21... | collective-permute-start | bytes 393224 | tf_op jit(solution)/shard_map/ppermute | solution.py:30
  3.4 7.2 %collective-permute-start.3 = (f32[4,24,128]{2,1,0:T(8,128)S(1)}, f32[4,24,128]{2,1,0:T(8,128)S(1)}, u32[]{:S(2)}, u32[]{:S(2)}) collective-permute-start(f32[4,24,128]{2,1,0:T(8,128)S(1)} %get-tuple-element.27), channel_id=1, source_target_pairs={{0,13},{1,14},{2,15},{3,12},{4,9},{5,10},{6,11},{7,8},{8,21},{9,22... | collective-permute-start | bytes 147464 | tf_op jit(solution)/shard_map/ppermute | solution.py:30
  6.1 9.1 %collective-permute-start = (f32[2,64,128]{2,1,0:T(8,128)S(1)}, f32[2,64,128]{2,1,0:T(8,128)S(1)}, u32[]{:S(2)}, u32[]{:S(2)}) collective-permute-start(f32[2,64,128]{2,1,0:T(8,128)S(1)} %get-tuple-element.25), channel_id=1, source_target_pairs={{0,8},{1,9},{2,10},{3,11},{4,12},{5,13},{6,14},{7,15},{8,16},{9,17... | collective-permute-start | bytes 196616 | tf_op jit(solution)/shard_map/ppermute | solution.py:30
  6.1 7.0 %collective-permute-start.2 = (f32[4,24,128]{2,1,0:T(8,128)S(1)}, f32[4,24,128]{2,1,0:T(8,128)S(1)}, u32[]{:S(2)}, u32[]{:S(2)}) collective-permute-start(f32[4,24,128]{2,1,0:T(8,128)S(1)} %get-tuple-element.27), channel_id=1, source_target_pairs={{0,9},{1,10},{2,11},{3,8},{4,13},{5,14},{6,15},{7,12},{8,17},{9,18... | collective-permute-start | bytes 147464 | tf_op jit(solution)/shard_map/ppermute | solution.py:30
  8.0 6.8 %collective-permute-start.5 = (f32[4,24,128]{2,1,0:T(8,128)S(1)}, f32[4,24,128]{2,1,0:T(8,128)S(1)}, u32[]{:S(2)}, u32[]{:S(2)}) collective-permute-start(f32[4,24,128]{2,1,0:T(8,128)S(1)} %get-tuple-element.28), channel_id=1, source_target_pairs={{0,15},{1,12},{2,13},{3,14},{4,11},{5,8},{6,9},{7,10},{8,23},{9,20... | collective-permute-start | bytes 147464 | tf_op jit(solution)/shard_map/ppermute | solution.py:30
  10.6 4.6 %collective-permute-start.4 = (f32[4,24,128]{2,1,0:T(8,128)S(1)}, f32[4,24,128]{2,1,0:T(8,128)S(1)}, u32[]{:S(2)}, u32[]{:S(2)}) collective-permute-start(f32[4,24,128]{2,1,0:T(8,128)S(1)} %get-tuple-element.28), channel_id=1, source_target_pairs={{0,11},{1,8},{2,9},{3,10},{4,15},{5,12},{6,13},{7,14},{8,19},{9,16... | collective-permute-start | bytes 147464 | tf_op jit(solution)/shard_map/ppermute | solution.py:30
  16.4 11.0 %collective-permute-start.6 = (f32[2,128,128]{2,1,0:T(8,128)S(1)}, f32[2,128,128]{2,1,0:T(8,128)S(1)}, u32[]{:S(2)}, u32[]{:S(2)}) collective-permute-start(f32[2,128,128]{2,1,0:T(8,128)S(1)} %get-tuple-element.33.two_ref), channel_id=1, source_target_pairs={{0,8},{1,9},{2,10},{3,11},{4,12},{5,13},{6,14},{7,15},{8,16},{9,17... | collective-permute-start | bytes 393224 | tf_op jit(solution)/shard_map/ppermute | solution.py:30
  17.0 10.4 %collective-permute-start.9 = (f32[4,40,128]{2,1,0:T(8,128)S(1)}, f32[4,40,128]{2,1,0:T(8,128)S(1)}, u32[]{:S(2)}, u32[]{:S(2)}) collective-permute-start(f32[4,40,128]{2,1,0:T(8,128)S(1)} %get-tuple-element.36), channel_id=1, source_target_pairs={{0,1},{1,2},{2,3},{3,0},{4,5},{5,6},{6,7},{7,4},{8,9},{9,10},{10,1... | collective-permute-start | bytes 245768 | tf_op jit(solution)/shard_map/ppermute | solution.py:30
  17.8 9.6 %collective-permute-start.10 = (f32[4,40,128]{2,1,0:T(8,128)S(1)}, f32[4,40,128]{2,1,0:T(8,128)S(1)}, u32[]{:S(2)}, u32[]{:S(2)}) collective-permute-start(f32[4,40,128]{2,1,0:T(8,128)S(1)} %get-tuple-element.37), channel_id=1, source_target_pairs={{0,3},{1,0},{2,1},{3,2},{4,7},{5,4},{6,5},{7,6},{8,11},{9,8},{10,9... | collective-permute-start | bytes 245768 | tf_op jit(solution)/shard_map/ppermute | solution.py:30
  20.9 6.6 %collective-permute-start.7 = (f32[2,40,128]{2,1,0:T(8,128)S(1)}, f32[2,40,128]{2,1,0:T(8,128)S(1)}, u32[]{:S(2)}, u32[]{:S(2)}) collective-permute-start(f32[2,40,128]{2,1,0:T(8,128)S(1)} %get-tuple-element.34), channel_id=1, source_target_pairs={{0,9},{1,10},{2,11},{3,8},{4,13},{5,14},{6,15},{7,12},{8,17},{9,18... | collective-permute-start | bytes 122888 | tf_op jit(solution)/shard_map/ppermute | solution.py:30
  20.9 6.6 %collective-permute-start.8 = (f32[2,40,128]{2,1,0:T(8,128)S(1)}, f32[2,40,128]{2,1,0:T(8,128)S(1)}, u32[]{:S(2)}, u32[]{:S(2)}) collective-permute-start(f32[2,40,128]{2,1,0:T(8,128)S(1)} %get-tuple-element.35), channel_id=1, source_target_pairs={{0,11},{1,8},{2,9},{3,10},{4,15},{5,12},{6,13},{7,14},{8,19},{9,16... | collective-permute-start | bytes 122888 | tf_op jit(solution)/shard_map/ppermute | solution.py:30
  29.4 10.6 %collective-permute-start.11 = (f32[2,128,128]{2,1,0:T(8,128)S(1)}, f32[2,128,128]{2,1,0:T(8,128)S(1)}, u32[]{:S(2)}, u32[]{:S(2)}) collective-permute-start(f32[2,128,128]{2,1,0:T(8,128)S(1)} %get-tuple-element.40.two_ref), channel_id=1, source_target_pairs={{0,8},{1,9},{2,10},{3,11},{4,12},{5,13},{6,14},{7,15},{8,16},{9,17... | collective-permute-start | bytes 393224 | tf_op jit(solution)/shard_map/ppermute | solution.py:30
  29.7 10.3 %collective-permute-start.14 = (f32[4,40,128]{2,1,0:T(8,128)S(1)}, f32[4,40,128]{2,1,0:T(8,128)S(1)}, u32[]{:S(2)}, u32[]{:S(2)}) collective-permute-start(f32[4,40,128]{2,1,0:T(8,128)S(1)} %get-tuple-element.43), channel_id=1, source_target_pairs={{0,1},{1,2},{2,3},{3,0},{4,5},{5,6},{6,7},{7,4},{8,9},{9,10},{10,1... | collective-permute-start | bytes 245768 | tf_op jit(solution)/shard_map/ppermute | solution.py:30
  30.4 9.6 %collective-permute-start.15 = (f32[4,40,128]{2,1,0:T(8,128)S(1)}, f32[4,40,128]{2,1,0:T(8,128)S(1)}, u32[]{:S(2)}, u32[]{:S(2)}) collective-permute-start(f32[4,40,128]{2,1,0:T(8,128)S(1)} %get-tuple-element.44), channel_id=1, source_target_pairs={{0,3},{1,0},{2,1},{3,2},{4,7},{5,4},{6,5},{7,6},{8,11},{9,8},{10,9... | collective-permute-start | bytes 245768 | tf_op jit(solution)/shard_map/ppermute | solution.py:30
  33.8 6.2 %collective-permute-start.12 = (f32[2,40,128]{2,1,0:T(8,128)S(1)}, f32[2,40,128]{2,1,0:T(8,128)S(1)}, u32[]{:S(2)}, u32[]{:S(2)}) collective-permute-start(f32[2,40,128]{2,1,0:T(8,128)S(1)} %get-tuple-element.41), channel_id=1, source_target_pairs={{0,9},{1,10},{2,11},{3,8},{4,13},{5,14},{6,15},{7,12},{8,17},{9,18... | collective-permute-start | bytes 122888 | tf_op jit(solution)/shard_map/ppermute | solution.py:30
  33.8 6.2 %collective-permute-start.13 = (f32[2,40,128]{2,1,0:T(8,128)S(1)}, f32[2,40,128]{2,1,0:T(8,128)S(1)}, u32[]{:S(2)}, u32[]{:S(2)}) collective-permute-start(f32[2,40,128]{2,1,0:T(8,128)S(1)} %get-tuple-element.42), channel_id=1, source_target_pairs={{0,11},{1,8},{2,9},{3,10},{4,15},{5,12},{6,13},{7,14},{8,19},{9,16... | collective-permute-start | bytes 122888 | tf_op jit(solution)/shard_map/ppermute | solution.py:30

commit v3 on v2

--- a/solution.py
+++ b/solution.py
@@ -16,7 +16,9 @@
 AXES = ("tm", "gy", "gx")
 HALO = 5
 RATE_HALO = 4
-PACK = 6
+DRIFT = 6
+TAKE = HALO + DRIFT
+BELOW, ABOVE = TAKE + 1, HALO + 1
 
 
 def shifted(value, by_tm, by_gy, by_gx):
@@ -150,8 +152,8 @@
     for field in range(n_fields):
         for x in range(n_x):
             all_ref[field, pl.ds(x, n_y, stride=n_x), :] = tiles_ref[field, x]
-        low_ref[field] = all_ref[field, pl.ds(0, PACK * n_x), :]
-        high_ref[field] = all_ref[field, pl.ds((n_y - PACK) * n_x, PACK * n_x), :]
+        low_ref[field] = all_ref[field, pl.ds(0, ABOVE * n_x), :]
+        high_ref[field] = all_ref[field, pl.ds((n_y - BELOW) * n_x, BELOW * n_x), :]
     for field in range(2):
         state_ref[field] = all_ref[field]
 
@@ -159,75 +161,89 @@
 def first_kernel(n_gy, n_x, n_y, *refs):
     state_ref, local_ref = refs[:2]
     others, lows, highs = refs[2 : 1 + n_gy], refs[1 + n_gy : 1 + 2 * n_gy], refs[1 + 2 * n_gy : 1 + 3 * n_gy]
-    start_ref, params_ref, zero_ref, one_ref, two_ref, two_low, two_high, low_ref, high_ref = refs[1 + 3 * n_gy :]
+    start_ref, params_ref, *outs = refs[1 + 3 * n_gy :]
     width = n_gy * n_x
 
     def collect(out_ref, field, source_field, middles):
         for gy in range(n_gy):
-            pieces = [(-PACK, lows[gy], PACK), (0, middles[gy], n_y), (n_y, highs[gy], PACK)]
+            pieces = [(-BELOW, lows[gy], BELOW), (0, middles[gy], n_y), (n_y, highs[gy], ABOVE)]
             for first, ref, count in pieces:
                 for k in range(count):
-                    if -HALO <= first + k < n_y + HALO:
-                        place = pl.ds((first + k + HALO) * width + gy * n_x, n_x)
+                    if -TAKE <= first + k < n_y + HALO:
+                        place = pl.ds((first + k + TAKE) * width + gy * n_x, n_x)
                         out_ref[field, place, :] = ref[source_field, pl.ds(k * n_x, n_x), :]
 
     for field in range(2):
         collect(start_ref, field, field, [state_ref, *others])
         collect(params_ref, field, 2 + field, [local_ref, *others])
-    start = rows_of(start_ref, width, -HALO)
-    params = rows_of(params_ref, width, -HALO)
+    start = rows_of(start_ref, width, -TAKE)
+    params = rows_of(params_ref, width, -TAKE)
     results = iteration(start, lambda r: params(r)[0], lambda r: params(r)[1], None)
-    write_nodes(results, width, n_y, zero_ref, one_ref, two_ref, two_low, two_high, low_ref, high_ref)
-
-
-def write_nodes(results, width, n_y, zero_ref, one_ref, two_ref, two_low, two_high, low_ref, high_ref):
+    write_nodes(results, width, n_y, -1, -RATE_HALO - DRIFT, *outs)
+
+
+def write_nodes(results, width, n_y, toward, zero_first, zero_ref, one_ref, two_ref, two_edge, edge_ref):
     rate_zero, node_one, node_two = results
-    for r in range(-RATE_HALO, n_y + RATE_HALO):
+    edge = 0 if toward > 0 else n_y - TAKE
+    zero_edge = RATE_HALO if toward > 0 else n_y - RATE_HALO - DRIFT
+    for r in range(zero_first, n_y + RATE_HALO):
         if 0 <= r < n_y:
             place = pl.ds(r * width, width)
             for field, (one, two) in enumerate(zip(node_one(r), node_two(r))):
                 one_ref[field, place, :] = one
                 two_ref[field, place, :] = two
-                for edge, pair_ref, edge_ref in ((0, two_low, low_ref), (n_y - HALO, two_high, high_ref)):
-                    if edge <= r < edge + HALO:
-                        beside = pl.ds((r - edge) * width, width)
-                        pair_ref[field, beside, :] = two
-                        edge_ref[field, beside, :] = one
-                        edge_ref[2 + field, beside, :] = two
+                if edge <= r < edge + TAKE:
+                    two_edge[field, pl.ds((r - edge) * width, width), :] = two
+                    edge_ref[pl.ds((field * TAKE + r - edge) * width, width), :] = one
+                    edge_ref[pl.ds(((2 + field) * TAKE + r - edge) * width, width), :] = two
         for field, zero in enumerate(rate_zero(r)):
-            zero_ref[field, pl.ds((r + RATE_HALO) * width, width), :] = zero
-
-
-def later_kernel(
-    width, n_y, out_x, first_ref, start_ref, params_ref, zero_ref, one_ref, two_ref, got_ref, got_low, got_high, low_ref, high_ref, *outs
-):
+            zero_ref[field, pl.ds((r - zero_first) * width, width), :] = zero
+            if zero_first == -RATE_HALO and zero_edge <= r < zero_edge + DRIFT:
+                edge_ref[pl.ds((4 * TAKE + field * DRIFT + r - zero_edge) * width, width), :] = zero
+
+
+def later_kernel(width, n_y, out_x, toward, offset, zero_first, *refs):
+    first_ref, start_ref, params_ref, zero_ref, one_ref, two_ref, got_ref, got_edge, edge_ref, *outs = refs
     is_first = first_ref[0] == 1
-    params = rows_of(params_ref, width, -HALO)
-    feed, kill = (lambda r: params(r)[0]), (lambda r: params(r)[1])
-    kept = rows_of(start_ref, width, -HALO)
-    sources = [rows_of(got_low, width, -HALO), rows_of(got_ref, width, 0), rows_of(got_high, width, n_y)]
-
-    def pick(r):
-        return 0 if r < 0 else 1 if r < n_y else 2
+    params = rows_of(params_ref, width, -TAKE)
+    feed, kill = (lambda r: params(r + offset)[0]), (lambda r: params(r + offset)[1])
+    kept = rows_of(start_ref, width, -TAKE)
+    beside = -TAKE if toward < 0 else n_y
+
+    def edge_rows(place, first, count):
+        @functools.cache
+        def at(r):
+            assert 0 <= r - first < count
+            return tuple(edge_ref[pl.ds((place + f * count + r - first) * width, width), :] for f in range(2))
+
+        return at
+
+    def moved(inside, outside, low, high):
+        return lambda r: (inside if low <= r + toward * DRIFT < high else outside)(r + toward * DRIFT)
+
+    got = moved(rows_of(got_ref, width, 0), rows_of(got_edge, width, beside), 0, n_y)
 
     @functools.cache
     def start(r):
-        return tuple(jnp.where(is_first, a, b) for a, b in zip(kept(r), sources[pick(r)](r)))
-
-    def own(tile_ref, offset):
-        pieces = [
-            rows_of(low_ref.at[pl.ds(offset, 2)], width, -HALO),
-            rows_of(tile_ref, width, 0),
-            rows_of(high_ref.at[pl.ds(offset, 2)], width, n_y),
-        ]
-        return lambda r: pieces[pick(r)](r)
-
-    old_zero = rows_of(zero_ref, width, -RATE_HALO)
+        return tuple(jnp.where(is_first, a, b) for a, b in zip(kept(r + offset), got(r)))
+
+    zero_beside = -RATE_HALO - DRIFT if toward < 0 else n_y + RATE_HALO
+    old_zero = moved(
+        rows_of(zero_ref, width, zero_first),
+        edge_rows(4 * TAKE, zero_beside, DRIFT),
+        zero_first,
+        n_y + RATE_HALO,
+    )
     feed_kill = functools.cache(lambda r: feed(r) + kill(r))
-    old_one, old_two = (rates_of(own(ref, offset), feed, feed_kill, 1.0) for ref, offset in ((one_ref, 0), (two_ref, 2)))
+    old_one, old_two = (
+        rates_of(
+            moved(rows_of(ref, width, 0), edge_rows(field * TAKE, beside, TAKE), 0, n_y), feed, feed_kill, 1.0
+        )
+        for field, ref in ((0, one_ref), (2, two_ref))
+    )
     results = iteration(start, feed, kill, (old_zero, old_one, old_two))
     if out_x is None:
-        write_nodes(results, width, n_y, *outs)
+        write_nodes(results, width, n_y, -toward, -RATE_HALO, *outs)
     else:
         out_ref, scratch = outs
         for r in range(n_y):
@@ -265,32 +281,41 @@
         "pack",
         0,
         (jnp.concatenate([sent, feed_rate[None], kill_rate[None]]),),
-        [(2, n_y * n_x, n_z), (4, n_y * n_x, n_z), (4, PACK * n_x, n_z), (4, PACK * n_x, n_z)],
+        [(2, n_y * n_x, n_z), (4, n_y * n_x, n_z), (4, ABOVE * n_x, n_z), (4, BELOW * n_x, n_z)],
     )
     got = [shifted(state, 1, 0, 0), local]
     got += [shifted(local, 1, -gy, 0) for gy in range(1, n_gy)]
     got += [shifted(high, 1, -gy, 1) for gy in range(n_gy)]
     got += [shifted(low, 1, -gy, -1) for gy in range(n_gy)]
 
-    tile, edge = (2, n_y * width, n_z), (2, HALO * width, n_z)
-    node_shapes = [(2, (n_y + 2 * RATE_HALO) * width, n_z), tile, tile, edge, edge, (4, *edge[1:]), (4, *edge[1:])]
-    window = (2, (n_y + 2 * HALO) * width, n_z)
+    def node_shapes(zero_rows, edge_rows):
+        tile = (2, n_y * width, n_z)
+        return [(2, zero_rows * width, n_z), tile, tile, (2, TAKE * width, n_z), (edge_rows * width, n_z)]
+
+    window = (2, (TAKE + n_y + HALO) * width, n_z)
     start, params, *nodes = call(
-        functools.partial(first_kernel, n_gy, n_x, n_y), "first", 0, got, [window, window, *node_shapes]
-    )
+        functools.partial(first_kernel, n_gy, n_x, n_y),
+        "first",
+        0,
+        got,
+        [window, window, *node_shapes(n_y + 2 * RATE_HALO + DRIFT, 4 * TAKE)],
+    )
+    zero_first = -RATE_HALO - DRIFT
     for sweep_index in range(1, ITERS):
-        zero, one, two, two_low, two_high, low, high = nodes
-        got = [shifted(two, 1, 0, 0), shifted(two_high, 1, 0, 1), shifted(two_low, 1, 0, -1)]
-        got += [shifted(high, 0, 0, 1), shifted(low, 0, 0, -1)]
+        toward = -1 if sweep_index % 2 else 1
+        zero, one, two, two_edge, edge = nodes
+        got = [shifted(two, 1, 0, 0), shifted(two_edge, 1, 0, -toward), shifted(edge, 0, 0, -toward)]
         done = sweep_index + 1 == ITERS
+        offset = -DRIFT if toward < 0 else 0
         nodes = call(
-            functools.partial(later_kernel, width, n_y, n_x if done else None),
+            functools.partial(later_kernel, width, n_y, n_x if done else None, toward, offset, zero_first),
             "last" if done else "later",
             1,
             (is_first, start, params, zero, one, two, *got),
-            [initial_state.shape] if done else node_shapes,
-            [pltpu.VMEM(tile, jnp.float32)] if done else (),
+            [initial_state.shape] if done else node_shapes(n_y + 2 * RATE_HALO, 4 * TAKE + 2 * DRIFT),
+            [pltpu.VMEM((2, n_y * width, n_z), jnp.float32)] if done else (),
         )
+        zero_first = -RATE_HALO
     return nodes[0][None]
 
 

time: 42.6 us -> 43.4 us (1.019); the launches traced: 42.5 us -> 42.7 us
  waiting for transfers between devices: 6.63 us -> 17.8 us
  starting transfers between devices: 29.3 us -> 18.2 us
    ppermute x16 -> x12, waiting for transfers between devices: 6.63 us -> 17.8 us  [shifted(): return lax.ppermute(value, AXES, pairs)]
    ppermute x16 -> x12, starting transfers between devices: 29.3 us -> 18.2 us  [shifted(): return lax.ppermute(value, AXES, pairs)]
  transfers between devices with their start and end apart: 16 -> 12, of which waited for: 4 -> 5; matrix products, arithmetic and copies ran while one was open for 0% -> 0% of each run, Pallas kernels for 0% -> 0%
where the time goes in v3:
time: 43.4 us; the launch traced here: 42.7 us
  starting transfers between devices  18.2 us (42%)
  waiting for transfers between devices  17.8 us (41%)
  Pallas kernels  5.72 us (13%)
  other arithmetic  0.87 us (2%)
    ppermute x12, starting transfers between devices, shifted(): return lax.ppermute(value, AXES, pairs)  18.2 us
    ppermute x12, waiting for transfers between devices, shifted(): return lax.ppermute(value, AXES, pairs)  17.8 us
    pallas_call x4, Pallas kernels, call(): pl.pallas_call(kernel, name=name, out_shape=[jax.ShapeDtypeStruct(shape,...  5.72 us
  transfers between devices with their start and end apart: 12, of which 5 were waited for; matrix products, arithmetic and copies ran while one was open for 0% of the time, Pallas kernels for 0%

profile of v3, /device:TPU:0, one launch (start us, length us, event | category | flops | bytes accessed | tf_op | source)
XLA Modules:
  0.0 42.7 jit_solution(5998678390710323384)
XLA Ops:
  0.0 0.0 copy-start
  0.0 0.0 copy-start.1
  0.0 0.9 %bitcast_select_fusion = f32[2,4,16,128]{3,2,1,0:T(8,128)S(1)} fusion(f32[2,4,16,128]{3,2,1,0:T(8,128)} %param.4, f32[1,2,4,16,128]{4,3,2,1,0:T(8,128)} %param.5, pred[]{:T(512)S(6)} %eq.7), kind=kLoop, calls=%fused_computation.1 | loop fusion | flops 16384 | bytes 196609 | tf_op jit(solution)/shard_map/jit(_where)/select_n | solution.py:278
  0.9 0.0 copy-done
  0.9 0.0 copy-done.1
  0.9 2.5 %collective-permute-start.1 = (f32[4,64,128]{2,1,0:T(8,128)S(1)}, f32[4,64,128]{2,1,0:T(8,128)S(1)}, u32[]{:S(2)}, u32[]{:S(2)}) collective-permute-start(f32[4,64,128]{2,1,0:T(8,128)S(1)} %get-tuple-element.22.refs_1_), channel_id=1, source_target_pairs={{0,12},{1,13},{2,14},{3,15},{4,8},{5,9},{6,10},{7,11},{8,20},{9,21... | collective-permute-start | bytes 393224 | tf_op jit(solution)/shard_map/ppermute | solution.py:32
  3.4 4.8 %collective-permute-start.5 = (f32[4,24,128]{2,1,0:T(8,128)S(1)}, f32[4,24,128]{2,1,0:T(8,128)S(1)}, u32[]{:S(2)}, u32[]{:S(2)}) collective-permute-start(f32[4,24,128]{2,1,0:T(8,128)S(1)} %get-tuple-element.24), channel_id=1, source_target_pairs={{0,15},{1,12},{2,13},{3,14},{4,11},{5,8},{6,9},{7,10},{8,23},{9,20... | collective-permute-start | bytes 147464 | tf_op jit(solution)/shard_map/ppermute | solution.py:32
  8.2 0.0 collective-permute-start.3
  8.2 0.6 %collective-permute-start.2 = (f32[4,48,128]{2,1,0:T(8,128)S(1)}, f32[4,48,128]{2,1,0:T(8,128)S(1)}, u32[]{:S(2)}, u32[]{:S(2)}) collective-permute-start(f32[4,48,128]{2,1,0:T(8,128)S(1)} %get-tuple-element.23), channel_id=1, source_target_pairs={{0,9},{1,10},{2,11},{3,8},{4,13},{5,14},{6,15},{7,12},{8,17},{9,18... | collective-permute-start | bytes 294920 | tf_op jit(solution)/shard_map/ppermute | solution.py:32
  8.8 0.0 collective-permute-start
  8.8 1.4 %collective-permute-done.5.refs_6_ = f32[4,24,128]{2,1,0:T(8,128)S(1)} collective-permute-done((f32[4,24,128]{2,1,0:T(8,128)S(1)}, f32[4,24,128]{2,1,0:T(8,128)S(1)}, u32[]{:S(2)}, u32[]{:S(2)}) %collective-permute-start.5) | collective-permute-done | bytes 49184 | tf_op jit(solution)/shard_map/ppermute | solution.py:32
  10.3 4.9 %collective-permute-start.4 = (f32[4,24,128]{2,1,0:T(8,128)S(1)}, f32[4,24,128]{2,1,0:T(8,128)S(1)}, u32[]{:S(2)}, u32[]{:S(2)}) collective-permute-start(f32[4,24,128]{2,1,0:T(8,128)S(1)} %get-tuple-element.24), channel_id=1, source_target_pairs={{0,11},{1,8},{2,9},{3,10},{4,15},{5,12},{6,13},{7,14},{8,19},{9,16... | collective-permute-start | bytes 147464 | tf_op jit(solution)/shard_map/ppermute | solution.py:32
  15.2 3.6 %collective-permute-done.4.refs_5_ = f32[4,24,128]{2,1,0:T(8,128)S(1)} collective-permute-done((f32[4,24,128]{2,1,0:T(8,128)S(1)}, f32[4,24,128]{2,1,0:T(8,128)S(1)}, u32[]{:S(2)}, u32[]{:S(2)}) %collective-permute-start.4) | collective-permute-done | bytes 49184 | tf_op jit(solution)/shard_map/ppermute | solution.py:32
  18.8 0.0 collective-permute-done.refs_0_
  18.8 0.0 collective-permute-done.3.refs_4_
  18.8 0.0 collective-permute-done.2.refs_3_
  18.8 0.0 collective-permute-done.1.refs_2_
  18.8 1.3 %first.1 = (f32[2,256,128]{2,1,0:T(8,128)S(1)}, f32[2,256,128]{2,1,0:T(8,128)S(1)}, f32[2,240,128]{2,1,0:T(8,128)S(1)}, f32[2,128,128]{2,1,0:T(8,128)S(1)}, f32[...) custom-call(f32[2,64,128]{2,1,0:T(8,128)S(1)} %collective-permute-done.refs_0_, ...), custom_call_target="tpu_custom_call" | custom-call | tf_op jit(solution)/shard_map/first/pallas_call | solution.py:260
  20.2 1.0 %collective-permute-start.8 = (f32[352,128]{1,0:T(8,128)S(1)}, f32[352,128]{1,0:T(8,128)S(1)}, u32[]{:S(2)}, u32[]{:S(2)}) collective-permute-start(f32[352,128]{1,0:T(8,128)S(1)} %get-tuple-element.31), channel_id=1, source_target_pairs={{0,1},{1,2},{2,3},{3,0},{4,5},{5,6},{6,7},{7,4},{8,9},{9,10},{10,1... | collective-permute-start | bytes 540680 | tf_op jit(solution)/shard_map/ppermute | solution.py:32
  21.2 0.0 collective-permute-start.6
  21.2 1.7 %collective-permute-start.7 = (f32[2,88,128]{2,1,0:T(8,128)S(1)}, f32[2,88,128]{2,1,0:T(8,128)S(1)}, u32[]{:S(2)}, u32[]{:S(2)}) collective-permute-start(f32[2,88,128]{2,1,0:T(8,128)S(1)} %get-tuple-element.30), channel_id=1, source_target_pairs={{0,9},{1,10},{2,11},{3,8},{4,13},{5,14},{6,15},{7,12},{8,17},{9,18... | collective-permute-start | bytes 270344 | tf_op jit(solution)/shard_map/ppermute | solution.py:32
  22.8 6.0 %collective-permute-done.7.refs_7_ = f32[2,88,128]{2,1,0:T(8,128)S(1)} collective-permute-done((f32[2,88,128]{2,1,0:T(8,128)S(1)}, f32[2,88,128]{2,1,0:T(8,128)S(1)}, u32[]{:S(2)}, u32[]{:S(2)}) %collective-permute-start.7) | collective-permute-done | bytes 90144 | tf_op jit(solution)/shard_map/ppermute | solution.py:32
  28.8 0.0 collective-permute-done.6.refs_6_
  28.8 0.4 %collective-permute-done.8.refs_8_ = f32[352,128]{1,0:T(8,128)S(1)} collective-permute-done((f32[352,128]{1,0:T(8,128)S(1)}, f32[352,128]{1,0:T(8,128)S(1)}, u32[]{:S(2)}, u32[]{:S(2)}) %collective-permute-start.8) | collective-permute-done | bytes 180256 | tf_op jit(solution)/shard_map/ppermute | solution.py:32
  29.2 1.9 %later.1 = (f32[2,192,128]{2,1,0:T(8,128)S(1)}, f32[2,128,128]{2,1,0:T(8,128)S(1)}, f32[2,128,128]{2,1,0:T(8,128)S(1)}, f32[2,88,128]{2,1,0:T(8,128)S(1)}, f32[448,128]{1,0:T(8,128)S(1)}) custom-call(s32[1]{0:T(128)} %bitcast.refs_0_, f32[2,256,128]{2,1,0:T(8,128)S(1)} %get-tuple-element.25.refs_1_, f32[2,256,128]{2,1,0:T(8,128)S(1)} %get-tuple-element.26.refs_2_, ...), custom_call_target="tpu_custom_call" | custom-call | tf_op jit(solution)/shard_map/later/pallas_call | solution.py:260
  31.1 0.7 %collective-permute-start.11 = (f32[448,128]{1,0:T(8,128)S(1)}, f32[448,128]{1,0:T(8,128)S(1)}, u32[]{:S(2)}, u32[]{:S(2)}) collective-permute-start(f32[448,128]{1,0:T(8,128)S(1)} %get-tuple-element.36), channel_id=1, source_target_pairs={{0,3},{1,0},{2,1},{3,2},{4,7},{5,4},{6,5},{7,6},{8,11},{9,8},{10,9... | collective-permute-start | bytes 688136 | tf_op jit(solution)/shard_map/ppermute | solution.py:32
  31.8 0.7 %collective-permute-start.9 = (f32[2,128,128]{2,1,0:T(8,128)S(1)}, f32[2,128,128]{2,1,0:T(8,128)S(1)}, u32[]{:S(2)}, u32[]{:S(2)}) collective-permute-start(f32[2,128,128]{2,1,0:T(8,128)S(1)} %get-tuple-element.34.refs_5_), channel_id=1, source_target_pairs={{0,8},{1,9},{2,10},{3,11},{4,12},{5,13},{6,14},{7,15},{8,16},{9,17... | collective-permute-start | bytes 393224 | tf_op jit(solution)/shard_map/ppermute | solution.py:32
  32.5 1.4 %collective-permute-start.10 = (f32[2,88,128]{2,1,0:T(8,128)S(1)}, f32[2,88,128]{2,1,0:T(8,128)S(1)}, u32[]{:S(2)}, u32[]{:S(2)}) collective-permute-start(f32[2,88,128]{2,1,0:T(8,128)S(1)} %get-tuple-element.35), channel_id=1, source_target_pairs={{0,11},{1,8},{2,9},{3,10},{4,15},{5,12},{6,13},{7,14},{8,19},{9,16... | collective-permute-start | bytes 270344 | tf_op jit(solution)/shard_map/ppermute | solution.py:32
  33.9 6.4 %collective-permute-done.10.refs_7_ = f32[2,88,128]{2,1,0:T(8,128)S(1)} collective-permute-done((f32[2,88,128]{2,1,0:T(8,128)S(1)}, f32[2,88,128]{2,1,0:T(8,128)S(1)}, u32[]{:S(2)}, u32[]{:S(2)}) %collective-permute-start.10) | collective-permute-done | bytes 90144 | tf_op jit(solution)/shard_map/ppermute | solution.py:32
  40.3 0.0 collective-permute-done.9.refs_6_
  40.3 0.0 collective-permute-done.11.refs_8_
  40.3 2.5 %last.1 = f32[2,4,16,128]{3,2,1,0:T(8,128)} custom-call(s32[1]{0:T(128)} %bitcast.refs_0_, f32[2,256,128]{2,1,0:T(8,128)S(1)} %get-tuple-element.25.refs_1_, f32[2,256,128]{2,1,0:T(8,128)S(1)} %get-tuple-element.26.refs_2_, f32[2,192,128]{2,1,0:T(8,128)S(1)} %get-tuple-element.32.refs_3_, f32[2,128,128]{2,1,0:T(8,128)S(1)} %get-tuple-element.33.refs_4_, ...), custom_call_target="tpu_custom_call" | custom-call | tf_op jit(solution)/shard_map/last/pallas_call | solution.py:260
  (2 shorter events, 0.0 us)
Async XLA Ops:
  0.0 0.9 %copy-start = (f32[4,16,128]{2,1,0:T(8,128)S(1)}, f32[4,16,128]{2,1,0:T(8,128)}, u32[]{:S(2)}) copy-start(f32[4,16,128]{2,1,0:T(8,128)} %param.7) | copy-start | bytes 98308
  0.0 0.9 %copy-start.1 = (f32[4,16,128]{2,1,0:T(8,128)S(1)}, f32[4,16,128]{2,1,0:T(8,128)}, u32[]{:S(2)}) copy-start(f32[4,16,128]{2,1,0:T(8,128)} %param.6) | copy-start | bytes 98308
  0.9 17.9 %collective-permute-start.1 = (f32[4,64,128]{2,1,0:T(8,128)S(1)}, f32[4,64,128]{2,1,0:T(8,128)S(1)}, u32[]{:S(2)}, u32[]{:S(2)}) collective-permute-start(f32[4,64,128]{2,1,0:T(8,128)S(1)} %get-tuple-element.22.refs_1_), channel_id=1, source_target_pairs={{0,12},{1,13},{2,14},{3,15},{4,8},{5,9},{6,10},{7,11},{8,20},{9,21... | collective-permute-start | bytes 393224 | tf_op jit(solution)/shard_map/ppermute | solution.py:32
  3.4 6.9 %collective-permute-start.5 = (f32[4,24,128]{2,1,0:T(8,128)S(1)}, f32[4,24,128]{2,1,0:T(8,128)S(1)}, u32[]{:S(2)}, u32[]{:S(2)}) collective-permute-start(f32[4,24,128]{2,1,0:T(8,128)S(1)} %get-tuple-element.24), channel_id=1, source_target_pairs={{0,15},{1,12},{2,13},{3,14},{4,11},{5,8},{6,9},{7,10},{8,23},{9,20... | collective-permute-start | bytes 147464 | tf_op jit(solution)/shard_map/ppermute | solution.py:32
  8.2 10.7 %collective-permute-start.3 = (f32[4,48,128]{2,1,0:T(8,128)S(1)}, f32[4,48,128]{2,1,0:T(8,128)S(1)}, u32[]{:S(2)}, u32[]{:S(2)}) collective-permute-start(f32[4,48,128]{2,1,0:T(8,128)S(1)} %get-tuple-element.23), channel_id=1, source_target_pairs={{0,13},{1,14},{2,15},{3,12},{4,9},{5,10},{6,11},{7,8},{8,21},{9,22... | collective-permute-start | bytes 294920 | tf_op jit(solution)/shard_map/ppermute | solution.py:32
  8.2 10.7 %collective-permute-start.2 = (f32[4,48,128]{2,1,0:T(8,128)S(1)}, f32[4,48,128]{2,1,0:T(8,128)S(1)}, u32[]{:S(2)}, u32[]{:S(2)}) collective-permute-start(f32[4,48,128]{2,1,0:T(8,128)S(1)} %get-tuple-element.23), channel_id=1, source_target_pairs={{0,9},{1,10},{2,11},{3,8},{4,13},{5,14},{6,15},{7,12},{8,17},{9,18... | collective-permute-start | bytes 294920 | tf_op jit(solution)/shard_map/ppermute | solution.py:32
  8.8 10.0 %collective-permute-start = (f32[2,64,128]{2,1,0:T(8,128)S(1)}, f32[2,64,128]{2,1,0:T(8,128)S(1)}, u32[]{:S(2)}, u32[]{:S(2)}) collective-permute-start(f32[2,64,128]{2,1,0:T(8,128)S(1)} %get-tuple-element.21), channel_id=1, source_target_pairs={{0,8},{1,9},{2,10},{3,11},{4,12},{5,13},{6,14},{7,15},{8,16},{9,17... | collective-permute-start | bytes 196616 | tf_op jit(solution)/shard_map/ppermute | solution.py:32
  10.3 8.6 %collective-permute-start.4 = (f32[4,24,128]{2,1,0:T(8,128)S(1)}, f32[4,24,128]{2,1,0:T(8,128)S(1)}, u32[]{:S(2)}, u32[]{:S(2)}) collective-permute-start(f32[4,24,128]{2,1,0:T(8,128)S(1)} %get-tuple-element.24), channel_id=1, source_target_pairs={{0,11},{1,8},{2,9},{3,10},{4,15},{5,12},{6,13},{7,14},{8,19},{9,16... | collective-permute-start | bytes 147464 | tf_op jit(solution)/shard_map/ppermute | solution.py:32
  20.2 9.0 %collective-permute-start.8 = (f32[352,128]{1,0:T(8,128)S(1)}, f32[352,128]{1,0:T(8,128)S(1)}, u32[]{:S(2)}, u32[]{:S(2)}) collective-permute-start(f32[352,128]{1,0:T(8,128)S(1)} %get-tuple-element.31), channel_id=1, source_target_pairs={{0,1},{1,2},{2,3},{3,0},{4,5},{5,6},{6,7},{7,4},{8,9},{9,10},{10,1... | collective-permute-start | bytes 540680 | tf_op jit(solution)/shard_map/ppermute | solution.py:32
  21.2 7.6 %collective-permute-start.6 = (f32[2,128,128]{2,1,0:T(8,128)S(1)}, f32[2,128,128]{2,1,0:T(8,128)S(1)}, u32[]{:S(2)}, u32[]{:S(2)}) collective-permute-start(f32[2,128,128]{2,1,0:T(8,128)S(1)} %get-tuple-element.29.refs_5_), channel_id=1, source_target_pairs={{0,8},{1,9},{2,10},{3,11},{4,12},{5,13},{6,14},{7,15},{8,16},{9,17... | collective-permute-start | bytes 393224 | tf_op jit(solution)/shard_map/ppermute | solution.py:32
  21.2 7.6 %collective-permute-start.7 = (f32[2,88,128]{2,1,0:T(8,128)S(1)}, f32[2,88,128]{2,1,0:T(8,128)S(1)}, u32[]{:S(2)}, u32[]{:S(2)}) collective-permute-start(f32[2,88,128]{2,1,0:T(8,128)S(1)} %get-tuple-element.30), channel_id=1, source_target_pairs={{0,9},{1,10},{2,11},{3,8},{4,13},{5,14},{6,15},{7,12},{8,17},{9,18... | collective-permute-start | bytes 270344 | tf_op jit(solution)/shard_map/ppermute | solution.py:32
  31.1 9.1 %collective-permute-start.11 = (f32[448,128]{1,0:T(8,128)S(1)}, f32[448,128]{1,0:T(8,128)S(1)}, u32[]{:S(2)}, u32[]{:S(2)}) collective-permute-start(f32[448,128]{1,0:T(8,128)S(1)} %get-tuple-element.36), channel_id=1, source_target_pairs={{0,3},{1,0},{2,1},{3,2},{4,7},{5,4},{6,5},{7,6},{8,11},{9,8},{10,9... | collective-permute-start | bytes 688136 | tf_op jit(solution)/shard_map/ppermute | solution.py:32
  31.8 8.4 %collective-permute-start.9 = (f32[2,128,128]{2,1,0:T(8,128)S(1)}, f32[2,128,128]{2,1,0:T(8,128)S(1)}, u32[]{:S(2)}, u32[]{:S(2)}) collective-permute-start(f32[2,128,128]{2,1,0:T(8,128)S(1)} %get-tuple-element.34.refs_5_), channel_id=1, source_target_pairs={{0,8},{1,9},{2,10},{3,11},{4,12},{5,13},{6,14},{7,15},{8,16},{9,17... | collective-permute-start | bytes 393224 | tf_op jit(solution)/shard_map/ppermute | solution.py:32
  32.5 7.8 %collective-permute-start.10 = (f32[2,88,128]{2,1,0:T(8,128)S(1)}, f32[2,88,128]{2,1,0:T(8,128)S(1)}, u32[]{:S(2)}, u32[]{:S(2)}) collective-permute-start(f32[2,88,128]{2,1,0:T(8,128)S(1)} %get-tuple-element.35), channel_id=1, source_target_pairs={{0,11},{1,8},{2,9},{3,10},{4,15},{5,12},{6,13},{7,14},{8,19},{9,16... | collective-permute-start | bytes 270344 | tf_op jit(solution)/shard_map/ppermute | solution.py:32

commit v4 on v2

--- a/solution.py
+++ b/solution.py
@@ -16,7 +16,9 @@
 AXES = ("tm", "gy", "gx")
 HALO = 5
 RATE_HALO = 4
-PACK = 6
+DRIFT = 6
+TAKE = HALO + DRIFT
+BELOW, ABOVE = TAKE + 1, HALO + 1
 
 
 def shifted(value, by_tm, by_gy, by_gx):
@@ -150,37 +152,37 @@
     for field in range(n_fields):
         for x in range(n_x):
             all_ref[field, pl.ds(x, n_y, stride=n_x), :] = tiles_ref[field, x]
-        low_ref[field] = all_ref[field, pl.ds(0, PACK * n_x), :]
-        high_ref[field] = all_ref[field, pl.ds((n_y - PACK) * n_x, PACK * n_x), :]
+        low_ref[field] = all_ref[field, pl.ds(0, ABOVE * n_x), :]
+        high_ref[field] = all_ref[field, pl.ds((n_y - BELOW) * n_x, BELOW * n_x), :]
     for field in range(2):
         state_ref[field] = all_ref[field]
 
 
+def collect(out_ref, field, source_field, n_x, lowest, pieces):
+    width = n_x * len(pieces[0][1])
+    for first, refs, count in pieces:
+        for gy, ref in enumerate(refs):
+            for k in range(count):
+                if first + k >= lowest:
+                    place = pl.ds((first + k - lowest) * width + gy * n_x, n_x)
+                    out_ref[field, place, :] = ref[source_field, pl.ds(k * n_x, n_x), :]
+
+
 def first_kernel(n_gy, n_x, n_y, *refs):
     state_ref, local_ref = refs[:2]
-    others, lows, highs = refs[2 : 1 + n_gy], refs[1 + n_gy : 1 + 2 * n_gy], refs[1 + 2 * n_gy : 1 + 3 * n_gy]
-    start_ref, params_ref, zero_ref, one_ref, two_ref, two_low, two_high, low_ref, high_ref = refs[1 + 3 * n_gy :]
+    others, lows = refs[2 : 1 + n_gy], refs[1 + n_gy : 1 + 2 * n_gy]
+    start_ref, params_ref, *outs = refs[1 + 2 * n_gy :]
     width = n_gy * n_x
-
-    def collect(out_ref, field, source_field, middles):
-        for gy in range(n_gy):
-            pieces = [(-PACK, lows[gy], PACK), (0, middles[gy], n_y), (n_y, highs[gy], PACK)]
-            for first, ref, count in pieces:
-                for k in range(count):
-                    if -HALO <= first + k < n_y + HALO:
-                        place = pl.ds((first + k + HALO) * width + gy * n_x, n_x)
-                        out_ref[field, place, :] = ref[source_field, pl.ds(k * n_x, n_x), :]
-
     for field in range(2):
-        collect(start_ref, field, field, [state_ref, *others])
-        collect(params_ref, field, 2 + field, [local_ref, *others])
+        collect(start_ref, field, field, n_x, -TAKE, [(-BELOW, lows, BELOW), (0, [state_ref, *others], n_y)])
+        collect(params_ref, field, 2 + field, n_x, -TAKE, [(-BELOW, lows, BELOW), (0, [local_ref, *others], n_y)])
     start = rows_of(start_ref, width, -HALO)
     params = rows_of(params_ref, width, -HALO)
     results = iteration(start, lambda r: params(r)[0], lambda r: params(r)[1], None)
-    write_nodes(results, width, n_y, zero_ref, one_ref, two_ref, two_low, two_high, low_ref, high_ref)
-
-
-def write_nodes(results, width, n_y, zero_ref, one_ref, two_ref, two_low, two_high, low_ref, high_ref):
+    write_nodes(results, width, n_y, [(0, TAKE)], *outs)
+
+
+def write_nodes(results, width, n_y, edges, zero_ref, one_ref, two_ref, *edge_refs):
     rate_zero, node_one, node_two = results
     for r in range(-RATE_HALO, n_y + RATE_HALO):
         if 0 <= r < n_y:
@@ -188,46 +190,85 @@
             for field, (one, two) in enumerate(zip(node_one(r), node_two(r))):
                 one_ref[field, place, :] = one
                 two_ref[field, place, :] = two
-                for edge, pair_ref, edge_ref in ((0, two_low, low_ref), (n_y - HALO, two_high, high_ref)):
-                    if edge <= r < edge + HALO:
-                        beside = pl.ds((r - edge) * width, width)
-                        pair_ref[field, beside, :] = two
-                        edge_ref[field, beside, :] = one
-                        edge_ref[2 + field, beside, :] = two
+                for i, (first, count) in enumerate(edges):
+                    if first <= r < first + count:
+                        beside = pl.ds((r - first) * width, width)
+                        edge_refs[2 * i][field, beside, :] = two
+                        edge_refs[2 * i + 1][field, beside, :] = one
+                        edge_refs[2 * i + 1][2 + field, beside, :] = two
         for field, zero in enumerate(rate_zero(r)):
             zero_ref[field, pl.ds((r + RATE_HALO) * width, width), :] = zero
 
 
-def later_kernel(
-    width, n_y, out_x, first_ref, start_ref, params_ref, zero_ref, one_ref, two_ref, got_ref, got_low, got_high, low_ref, high_ref, *outs
-):
-    is_first = first_ref[0] == 1
-    params = rows_of(params_ref, width, -HALO)
+def joined(*parts):
+    def at(r):
+        return [rows for first, rows in parts if first <= r][-1](r)
+
+    return at
+
+
+def pair_of(ref, field):
+    return ref.at[pl.ds(field, 2)]
+
+
+def later_iteration(width, n_y, is_first, kept, params, got, old_zero, ones, twos):
     feed, kill = (lambda r: params(r)[0]), (lambda r: params(r)[1])
-    kept = rows_of(start_ref, width, -HALO)
-    sources = [rows_of(got_low, width, -HALO), rows_of(got_ref, width, 0), rows_of(got_high, width, n_y)]
-
-    def pick(r):
-        return 0 if r < 0 else 1 if r < n_y else 2
+    feed_kill = functools.cache(lambda r: feed(r) + kill(r))
 
     @functools.cache
     def start(r):
-        return tuple(jnp.where(is_first, a, b) for a, b in zip(kept(r), sources[pick(r)](r)))
-
-    def own(tile_ref, offset):
-        pieces = [
-            rows_of(low_ref.at[pl.ds(offset, 2)], width, -HALO),
-            rows_of(tile_ref, width, 0),
-            rows_of(high_ref.at[pl.ds(offset, 2)], width, n_y),
-        ]
-        return lambda r: pieces[pick(r)](r)
-
+        return tuple(jnp.where(is_first, a, b) for a, b in zip(kept(r), got(r)))
+
+    old_rates = (
+        old_zero(feed, feed_kill),
+        rates_of(ones, feed, feed_kill, 1.0),
+        rates_of(twos, feed, feed_kill, 1.0),
+    )
+    return iteration(start, feed, kill, old_rates)
+
+
+def second_kernel(n_gy, n_x, n_y, first_ref, start_ref, params_ref, *refs):
+    highs, refs = refs[:n_gy], refs[n_gy:]
+    zero_ref, one_ref, two_ref, got_ref, got_edge, pair_edge, top_ref, *outs = refs
+    width = n_gy * n_x
+    for field in range(4):
+        collect(top_ref, field, field, n_x, n_y, [(n_y, highs, ABOVE)])
+    kept = joined((-TAKE, rows_of(start_ref, width, -TAKE)), (n_y, rows_of(pair_of(top_ref, 0), width, n_y)))
+    params = joined((-TAKE, rows_of(params_ref, width, -TAKE)), (n_y, rows_of(pair_of(top_ref, 2), width, n_y)))
+    end = n_y - DRIFT
+
+    def moved(tile_ref, edge_ref):
+        return joined((-DRIFT, rows_of(tile_ref, width, -DRIFT)), (end, rows_of(edge_ref, width, end)))
+
+    def old_zero(feed, feed_kill):
+        inside = rows_of(zero_ref, width, -RATE_HALO - DRIFT)
+        return joined((-RATE_HALO - DRIFT, inside), (end + RATE_HALO, rates_of(kept, feed, feed_kill, 1.0)))
+
+    ones, twos = moved(one_ref, pair_of(pair_edge, 0)), moved(two_ref, pair_of(pair_edge, 2))
+    results = later_iteration(
+        width, n_y, first_ref[0] == 1, kept, params, moved(got_ref, got_edge), old_zero, ones, twos
+    )
+    write_nodes(results, width, n_y, [(0, HALO), (n_y - HALO, HALO)], *outs)
+
+
+def later_kernel(width, n_y, out_x, first_ref, start_ref, params_ref, top_ref, *refs):
+    zero_ref, one_ref, two_ref, got_ref, got_low, got_high, pair_low, pair_high, *outs = refs
+    kept = joined((-TAKE, rows_of(start_ref, width, -TAKE)), (n_y, rows_of(pair_of(top_ref, 0), width, n_y)))
+    params = joined((-TAKE, rows_of(params_ref, width, -TAKE)), (n_y, rows_of(pair_of(top_ref, 2), width, n_y)))
+
+    def window(low_ref, tile_ref, high_ref):
+        refs = ((-HALO, low_ref), (0, tile_ref), (n_y, high_ref))
+        return joined(*((first, rows_of(ref, width, first)) for first, ref in refs))
+
+    ones = window(pair_of(pair_low, 0), one_ref, pair_of(pair_high, 0))
+    twos = window(pair_of(pair_low, 2), two_ref, pair_of(pair_high, 2))
     old_zero = rows_of(zero_ref, width, -RATE_HALO)
-    feed_kill = functools.cache(lambda r: feed(r) + kill(r))
-    old_one, old_two = (rates_of(own(ref, offset), feed, feed_kill, 1.0) for ref, offset in ((one_ref, 0), (two_ref, 2)))
-    results = iteration(start, feed, kill, (old_zero, old_one, old_two))
+    got = window(got_low, got_ref, got_high)
+    results = later_iteration(
+        width, n_y, first_ref[0] == 1, kept, params, got, lambda feed, feed_kill: old_zero, ones, twos
+    )
     if out_x is None:
-        write_nodes(results, width, n_y, *outs)
+        write_nodes(results, width, n_y, [(0, HALO), (n_y - HALO, HALO)], *outs)
     else:
         out_ref, scratch = outs
         for r in range(n_y):
@@ -265,30 +306,43 @@
         "pack",
         0,
         (jnp.concatenate([sent, feed_rate[None], kill_rate[None]]),),
-        [(2, n_y * n_x, n_z), (4, n_y * n_x, n_z), (4, PACK * n_x, n_z), (4, PACK * n_x, n_z)],
+        [(2, n_y * n_x, n_z), (4, n_y * n_x, n_z), (4, ABOVE * n_x, n_z), (4, BELOW * n_x, n_z)],
     )
     got = [shifted(state, 1, 0, 0), local]
     got += [shifted(local, 1, -gy, 0) for gy in range(1, n_gy)]
     got += [shifted(high, 1, -gy, 1) for gy in range(n_gy)]
-    got += [shifted(low, 1, -gy, -1) for gy in range(n_gy)]
-
-    tile, edge = (2, n_y * width, n_z), (2, HALO * width, n_z)
-    node_shapes = [(2, (n_y + 2 * RATE_HALO) * width, n_z), tile, tile, edge, edge, (4, *edge[1:]), (4, *edge[1:])]
-    window = (2, (n_y + 2 * HALO) * width, n_z)
+    above = [shifted(low, 1, -gy, -1) for gy in range(n_gy)]
+
+    tile, window = (2, n_y * width, n_z), (2, (TAKE + n_y) * width, n_z)
+    nodes_only = [(2, (n_y + 2 * RATE_HALO) * width, n_z), tile, tile]
+    edge = lambda rows: [(2, rows * width, n_z), (4, rows * width, n_z)]
     start, params, *nodes = call(
-        functools.partial(first_kernel, n_gy, n_x, n_y), "first", 0, got, [window, window, *node_shapes]
-    )
-    for sweep_index in range(1, ITERS):
-        zero, one, two, two_low, two_high, low, high = nodes
+        functools.partial(first_kernel, n_gy, n_x, n_y),
+        "first",
+        0,
+        got,
+        [window, window, *nodes_only, *edge(TAKE)],
+    )
+    zero, one, two, two_edge, pair_edge = nodes
+    got = [shifted(two, 1, 0, 0), shifted(two_edge, 1, 0, -1), shifted(pair_edge, 0, 0, -1)]
+    top, *nodes = call(
+        functools.partial(second_kernel, n_gy, n_x, n_y),
+        "second",
+        1,
+        (is_first, start, params, *above, zero, one, two, *got),
+        [(4, ABOVE * width, n_z), *nodes_only, *edge(HALO), *edge(HALO)],
+    )
+    for sweep_index in range(2, ITERS):
+        zero, one, two, two_low, pair_low, two_high, pair_high = nodes
         got = [shifted(two, 1, 0, 0), shifted(two_high, 1, 0, 1), shifted(two_low, 1, 0, -1)]
-        got += [shifted(high, 0, 0, 1), shifted(low, 0, 0, -1)]
+        got += [shifted(pair_high, 0, 0, 1), shifted(pair_low, 0, 0, -1)]
         done = sweep_index + 1 == ITERS
         nodes = call(
             functools.partial(later_kernel, width, n_y, n_x if done else None),
             "last" if done else "later",
             1,
-            (is_first, start, params, zero, one, two, *got),
-            [initial_state.shape] if done else node_shapes,
+            (is_first, start, params, top, zero, one, two, *got),
+            [initial_state.shape] if done else [*nodes_only, *edge(HALO), *edge(HALO)],
             [pltpu.VMEM(tile, jnp.float32)] if done else (),
         )
     return nodes[0][None]

time: 42.6 us -> 40.5 us (0.951)
  starting transfers between devices: 29.3 us -> 21.7 us
  waiting for transfers between devices: 6.63 us -> 11.9 us
    ppermute x16 -> x14, starting transfers between devices: 29.3 us -> 21.7 us  [shifted(): return lax.ppermute(value, AXES, pairs)]
    ppermute x16 -> x14, waiting for transfers between devices: 6.63 us -> 11.9 us  [shifted(): return lax.ppermute(value, AXES, pairs)]
  transfers between devices with their start and end apart: 16 -> 14, of which waited for: 4 -> 5; matrix products, arithmetic and copies ran while one was open for 0% -> 0% of each run, Pallas kernels for 0% -> 0%
where the time goes in v4:
time: 40.5 us; the launch traced here: 40.3 us
  starting transfers between devices  21.7 us (54%)
  waiting for transfers between devices  11.9 us (29%)
  Pallas kernels  5.78 us (14%)
  other arithmetic  0.87 us (2%)
    ppermute x14, starting transfers between devices, shifted(): return lax.ppermute(value, AXES, pairs)  21.7 us
    ppermute x14, waiting for transfers between devices, shifted(): return lax.ppermute(value, AXES, pairs)  11.9 us
    pallas_call x4, Pallas kernels, call(): pl.pallas_call(kernel, name=name, out_shape=[jax.ShapeDtypeStruct(shape,...  5.78 us
    select_n x1, other arithmetic, shards(): sent = jnp.where(place == n_tm - 1, initial_state, slice_guess[0])  0.86 us
  transfers between devices with their start and end apart: 14, of which 5 were waited for; matrix products, arithmetic and copies ran while one was open for 0% of the time, Pallas kernels for 0%

profile of v4, /device:TPU:0, one launch (start us, length us, event | category | flops | bytes accessed | tf_op | source)
XLA Modules:
  0.0 40.3 jit_solution(11849813956403663801)
XLA Ops:
  0.0 0.0 copy-start
  0.0 0.0 copy-start.1
  0.0 0.9 %bitcast_select_fusion = f32[2,4,16,128]{3,2,1,0:T(8,128)S(1)} fusion(f32[2,4,16,128]{3,2,1,0:T(8,128)} %param.4, f32[1,2,4,16,128]{4,3,2,1,0:T(8,128)} %param.5, pred[]{:T(512)S(6)} %eq.7), kind=kLoop, calls=%fused_computation.1 | loop fusion | flops 16384 | bytes 196609 | tf_op jit(solution)/shard_map/jit(_where)/select_n | solution.py:303
  0.9 0.0 copy-done
  0.9 0.0 copy-done.1
  0.9 2.5 %collective-permute-start.1 = (f32[4,64,128]{2,1,0:T(8,128)S(1)}, f32[4,64,128]{2,1,0:T(8,128)S(1)}, u32[]{:S(2)}, u32[]{:S(2)}) collective-permute-start(f32[4,64,128]{2,1,0:T(8,128)S(1)} %get-tuple-element.25.refs_1_), channel_id=1, source_target_pairs={{0,12},{1,13},{2,14},{3,15},{4,8},{5,9},{6,10},{7,11},{8,20},{9,21... | collective-permute-start | bytes 393224 | tf_op jit(solution)/shard_map/ppermute | solution.py:32
  3.4 2.7 %collective-permute-start.3 = (f32[4,48,128]{2,1,0:T(8,128)S(1)}, f32[4,48,128]{2,1,0:T(8,128)S(1)}, u32[]{:S(2)}, u32[]{:S(2)}) collective-permute-start(f32[4,48,128]{2,1,0:T(8,128)S(1)} %get-tuple-element.26), channel_id=1, source_target_pairs={{0,13},{1,14},{2,15},{3,12},{4,9},{5,10},{6,11},{7,8},{8,21},{9,22... | collective-permute-start | bytes 294920 | tf_op jit(solution)/shard_map/ppermute | solution.py:32
  6.1 1.1 %collective-permute-start.2 = (f32[4,48,128]{2,1,0:T(8,128)S(1)}, f32[4,48,128]{2,1,0:T(8,128)S(1)}, u32[]{:S(2)}, u32[]{:S(2)}) collective-permute-start(f32[4,48,128]{2,1,0:T(8,128)S(1)} %get-tuple-element.26), channel_id=1, source_target_pairs={{0,9},{1,10},{2,11},{3,8},{4,13},{5,14},{6,15},{7,12},{8,17},{9,18... | collective-permute-start | bytes 294920 | tf_op jit(solution)/shard_map/ppermute | solution.py:32
  7.3 0.5 %collective-permute-start = (f32[2,64,128]{2,1,0:T(8,128)S(1)}, f32[2,64,128]{2,1,0:T(8,128)S(1)}, u32[]{:S(2)}, u32[]{:S(2)}) collective-permute-start(f32[2,64,128]{2,1,0:T(8,128)S(1)} %get-tuple-element.24), channel_id=1, source_target_pairs={{0,8},{1,9},{2,10},{3,11},{4,12},{5,13},{6,14},{7,15},{8,16},{9,17... | collective-permute-start | bytes 196616 | tf_op jit(solution)/shard_map/ppermute | solution.py:32
  7.8 3.8 %collective-permute-done.refs_0_ = f32[2,64,128]{2,1,0:T(8,128)S(1)} collective-permute-done((f32[2,64,128]{2,1,0:T(8,128)S(1)}, f32[2,64,128]{2,1,0:T(8,128)S(1)}, u32[]{:S(2)}, u32[]{:S(2)}) %collective-permute-start) | collective-permute-done | bytes 65568 | tf_op jit(solution)/shard_map/ppermute | solution.py:32
  11.6 0.0 collective-permute-done.3.refs_4_
  11.6 2.1 %collective-permute-done.2.refs_3_ = f32[4,48,128]{2,1,0:T(8,128)S(1)} collective-permute-done((f32[4,48,128]{2,1,0:T(8,128)S(1)}, f32[4,48,128]{2,1,0:T(8,128)S(1)}, u32[]{:S(2)}, u32[]{:S(2)}) %collective-permute-start.2) | collective-permute-done | bytes 98336 | tf_op jit(solution)/shard_map/ppermute | solution.py:32
  13.6 0.0 collective-permute-done.1.refs_2_
  13.6 1.2 %first.1 = (f32[2,216,128]{2,1,0:T(8,128)S(1)}, f32[2,216,128]{2,1,0:T(8,128)S(1)}, f32[2,192,128]{2,1,0:T(8,128)S(1)}, f32[2,128,128]{2,1,0:T(8,128)S(1)}, f32[...) custom-call(f32[2,64,128]{2,1,0:T(8,128)S(1)} %collective-permute-done.refs_0_, ...), custom_call_target="tpu_custom_call" | custom-call | tf_op jit(solution)/shard_map/first/pallas_call | solution.py:285
  14.9 0.9 %collective-permute-start.8 = (f32[4,88,128]{2,1,0:T(8,128)S(1)}, f32[4,88,128]{2,1,0:T(8,128)S(1)}, u32[]{:S(2)}, u32[]{:S(2)}) collective-permute-start(f32[4,88,128]{2,1,0:T(8,128)S(1)} %get-tuple-element.34), channel_id=1, source_target_pairs={{0,3},{1,0},{2,1},{3,2},{4,7},{5,4},{6,5},{7,6},{8,11},{9,8},{10,9... | collective-permute-start | bytes 540680 | tf_op jit(solution)/shard_map/ppermute | solution.py:32
  15.7 0.3 collective-permute-start.6
  16.0 1.7 %collective-permute-start.7 = (f32[2,88,128]{2,1,0:T(8,128)S(1)}, f32[2,88,128]{2,1,0:T(8,128)S(1)}, u32[]{:S(2)}, u32[]{:S(2)}) collective-permute-start(f32[2,88,128]{2,1,0:T(8,128)S(1)} %get-tuple-element.33), channel_id=1, source_target_pairs={{0,11},{1,8},{2,9},{3,10},{4,15},{5,12},{6,13},{7,14},{8,19},{9,16... | collective-permute-start | bytes 270344 | tf_op jit(solution)/shard_map/ppermute | solution.py:32
  17.7 1.0 %collective-permute-start.5 = (f32[4,24,128]{2,1,0:T(8,128)S(1)}, f32[4,24,128]{2,1,0:T(8,128)S(1)}, u32[]{:S(2)}, u32[]{:S(2)}) collective-permute-start(f32[4,24,128]{2,1,0:T(8,128)S(1)} %get-tuple-element.29), channel_id=1, source_target_pairs={{0,15},{1,12},{2,13},{3,14},{4,11},{5,8},{6,9},{7,10},{8,23},{9,20... | collective-permute-start | bytes 147464 | tf_op jit(solution)/shard_map/ppermute | solution.py:32
  18.7 2.7 %collective-permute-start.4 = (f32[4,24,128]{2,1,0:T(8,128)S(1)}, f32[4,24,128]{2,1,0:T(8,128)S(1)}, u32[]{:S(2)}, u32[]{:S(2)}) collective-permute-start(f32[4,24,128]{2,1,0:T(8,128)S(1)} %get-tuple-element.29), channel_id=1, source_target_pairs={{0,11},{1,8},{2,9},{3,10},{4,15},{5,12},{6,13},{7,14},{8,19},{9,16... | collective-permute-start | bytes 147464 | tf_op jit(solution)/shard_map/ppermute | solution.py:32
  21.3 2.4 %collective-permute-done.5.refs_1_ = f32[4,24,128]{2,1,0:T(8,128)S(1)} collective-permute-done((f32[4,24,128]{2,1,0:T(8,128)S(1)}, f32[4,24,128]{2,1,0:T(8,128)S(1)}, u32[]{:S(2)}, u32[]{:S(2)}) %collective-permute-start.5) | collective-permute-done | bytes 49184 | tf_op jit(solution)/shard_map/ppermute | solution.py:32
  23.8 1.0 %collective-permute-done.4.refs_0_ = f32[4,24,128]{2,1,0:T(8,128)S(1)} collective-permute-done((f32[4,24,128]{2,1,0:T(8,128)S(1)}, f32[4,24,128]{2,1,0:T(8,128)S(1)}, u32[]{:S(2)}, u32[]{:S(2)}) %collective-permute-start.4) | collective-permute-done | bytes 49184 | tf_op jit(solution)/shard_map/ppermute | solution.py:32
  24.7 0.0 collective-permute-done.7.refs_6_
  24.7 0.0 collective-permute-done.6.refs_5_
  24.7 0.0 collective-permute-done.8.refs_7_
  24.7 2.1 %second.1 = (f32[4,48,128]{2,1,0:T(8,128)S(1)}, f32[2,192,128]{2,1,0:T(8,128)S(1)}, f32[2,128,128]{2,1,0:T(8,128)S(1)}, f32[2,128,128]{2,1,0:T(8,128)S(1)}, f32[...) custom-call(s32[1]{0:T(128)} %bitcast.first_ref, ...), custom_call_target="tpu_custom_call" | custom-call | tf_op jit(solution)/shard_map/second/pallas_call | solution.py:285
  26.8 0.7 %collective-permute-start.9 = (f32[2,128,128]{2,1,0:T(8,128)S(1)}, f32[2,128,128]{2,1,0:T(8,128)S(1)}, u32[]{:S(2)}, u32[]{:S(2)}) collective-permute-start(f32[2,128,128]{2,1,0:T(8,128)S(1)} %get-tuple-element.38.refs_2_), channel_id=1, source_target_pairs={{0,8},{1,9},{2,10},{3,11},{4,12},{5,13},{6,14},{7,15},{8,16},{9,17... | collective-permute-start | bytes 393224 | tf_op jit(solution)/shard_map/ppermute | solution.py:32
  27.5 0.0 collective-permute-start.12
  27.5 3.8 %collective-permute-start.13 = (f32[4,40,128]{2,1,0:T(8,128)S(1)}, f32[4,40,128]{2,1,0:T(8,128)S(1)}, u32[]{:S(2)}, u32[]{:S(2)}) collective-permute-start(f32[4,40,128]{2,1,0:T(8,128)S(1)} %get-tuple-element.42), channel_id=1, source_target_pairs={{0,3},{1,0},{2,1},{3,2},{4,7},{5,4},{6,5},{7,6},{8,11},{9,8},{10,9... | collective-permute-start | bytes 245768 | tf_op jit(solution)/shard_map/ppermute | solution.py:32
  31.3 0.0 collective-permute-start.10
  31.4 3.8 %collective-permute-start.11 = (f32[2,40,128]{2,1,0:T(8,128)S(1)}, f32[2,40,128]{2,1,0:T(8,128)S(1)}, u32[]{:S(2)}, u32[]{:S(2)}) collective-permute-start(f32[2,40,128]{2,1,0:T(8,128)S(1)} %get-tuple-element.40), channel_id=1, source_target_pairs={{0,11},{1,8},{2,9},{3,10},{4,15},{5,12},{6,13},{7,14},{8,19},{9,16... | collective-permute-start | bytes 122888 | tf_op jit(solution)/shard_map/ppermute | solution.py:32
  35.2 2.7 %collective-permute-done.10.refs_4_ = f32[2,40,128]{2,1,0:T(8,128)S(1)} collective-permute-done((f32[2,40,128]{2,1,0:T(8,128)S(1)}, f32[2,40,128]{2,1,0:T(8,128)S(1)}, u32[]{:S(2)}, u32[]{:S(2)}) %collective-permute-start.10) | collective-permute-done | bytes 40992 | tf_op jit(solution)/shard_map/ppermute | solution.py:32
  37.8 0.0 collective-permute-done.11.refs_5_
  37.8 0.0 collective-permute-done.12.refs_6_
  37.8 0.0 collective-permute-done.13.refs_7_
  37.8 0.0 collective-permute-done.9.refs_3_
  37.8 2.5 %last.1 = f32[2,4,16,128]{3,2,1,0:T(8,128)} custom-call(s32[1]{0:T(128)} %bitcast.first_ref, f32[2,216,128]{2,1,0:T(8,128)S(1)} %get-tuple-element.27.start_ref, f32[2,216,128]{2,1,0:T(8,128)S(1)} %get-tuple-element.28.params_ref, f32[4,48,128]{2,1,0:T(8,128)S(1)} %get-tuple-element.35.top_ref, f32[2,192,128]{2,1,0:T(8,128)S(1)} %get-tuple-element.36.refs_0_, ...), custom_call_target="tpu_custom_call" | custom-call | tf_op jit(solution)/shard_map/last/pallas_call | solution.py:285
  (2 shorter events, 0.0 us)
Async XLA Ops:
  0.0 0.9 %copy-start = (f32[4,16,128]{2,1,0:T(8,128)S(1)}, f32[4,16,128]{2,1,0:T(8,128)}, u32[]{:S(2)}) copy-start(f32[4,16,128]{2,1,0:T(8,128)} %param.7) | copy-start | bytes 98308
  0.0 0.9 %copy-start.1 = (f32[4,16,128]{2,1,0:T(8,128)S(1)}, f32[4,16,128]{2,1,0:T(8,128)}, u32[]{:S(2)}) copy-start(f32[4,16,128]{2,1,0:T(8,128)} %param.6) | copy-start | bytes 98308
  0.9 12.7 %collective-permute-start.1 = (f32[4,64,128]{2,1,0:T(8,128)S(1)}, f32[4,64,128]{2,1,0:T(8,128)S(1)}, u32[]{:S(2)}, u32[]{:S(2)}) collective-permute-start(f32[4,64,128]{2,1,0:T(8,128)S(1)} %get-tuple-element.25.refs_1_), channel_id=1, source_target_pairs={{0,12},{1,13},{2,14},{3,15},{4,8},{5,9},{6,10},{7,11},{8,20},{9,21... | collective-permute-start | bytes 393224 | tf_op jit(solution)/shard_map/ppermute | solution.py:32
  3.4 8.2 %collective-permute-start.3 = (f32[4,48,128]{2,1,0:T(8,128)S(1)}, f32[4,48,128]{2,1,0:T(8,128)S(1)}, u32[]{:S(2)}, u32[]{:S(2)}) collective-permute-start(f32[4,48,128]{2,1,0:T(8,128)S(1)} %get-tuple-element.26), channel_id=1, source_target_pairs={{0,13},{1,14},{2,15},{3,12},{4,9},{5,10},{6,11},{7,8},{8,21},{9,22... | collective-permute-start | bytes 294920 | tf_op jit(solution)/shard_map/ppermute | solution.py:32
  6.1 7.5 %collective-permute-start.2 = (f32[4,48,128]{2,1,0:T(8,128)S(1)}, f32[4,48,128]{2,1,0:T(8,128)S(1)}, u32[]{:S(2)}, u32[]{:S(2)}) collective-permute-start(f32[4,48,128]{2,1,0:T(8,128)S(1)} %get-tuple-element.26), channel_id=1, source_target_pairs={{0,9},{1,10},{2,11},{3,8},{4,13},{5,14},{6,15},{7,12},{8,17},{9,18... | collective-permute-start | bytes 294920 | tf_op jit(solution)/shard_map/ppermute | solution.py:32
  7.3 4.3 %collective-permute-start = (f32[2,64,128]{2,1,0:T(8,128)S(1)}, f32[2,64,128]{2,1,0:T(8,128)S(1)}, u32[]{:S(2)}, u32[]{:S(2)}) collective-permute-start(f32[2,64,128]{2,1,0:T(8,128)S(1)} %get-tuple-element.24), channel_id=1, source_target_pairs={{0,8},{1,9},{2,10},{3,11},{4,12},{5,13},{6,14},{7,15},{8,16},{9,17... | collective-permute-start | bytes 196616 | tf_op jit(solution)/shard_map/ppermute | solution.py:32
  14.9 9.9 %collective-permute-start.8 = (f32[4,88,128]{2,1,0:T(8,128)S(1)}, f32[4,88,128]{2,1,0:T(8,128)S(1)}, u32[]{:S(2)}, u32[]{:S(2)}) collective-permute-start(f32[4,88,128]{2,1,0:T(8,128)S(1)} %get-tuple-element.34), channel_id=1, source_target_pairs={{0,3},{1,0},{2,1},{3,2},{4,7},{5,4},{6,5},{7,6},{8,11},{9,8},{10,9... | collective-permute-start | bytes 540680 | tf_op jit(solution)/shard_map/ppermute | solution.py:32
  15.7 9.0 %collective-permute-start.6 = (f32[2,128,128]{2,1,0:T(8,128)S(1)}, f32[2,128,128]{2,1,0:T(8,128)S(1)}, u32[]{:S(2)}, u32[]{:S(2)}) collective-permute-start(f32[2,128,128]{2,1,0:T(8,128)S(1)} %get-tuple-element.32.refs_4_), channel_id=1, source_target_pairs={{0,8},{1,9},{2,10},{3,11},{4,12},{5,13},{6,14},{7,15},{8,16},{9,17... | collective-permute-start | bytes 393224 | tf_op jit(solution)/shard_map/ppermute | solution.py:32
  16.0 8.7 %collective-permute-start.7 = (f32[2,88,128]{2,1,0:T(8,128)S(1)}, f32[2,88,128]{2,1,0:T(8,128)S(1)}, u32[]{:S(2)}, u32[]{:S(2)}) collective-permute-start(f32[2,88,128]{2,1,0:T(8,128)S(1)} %get-tuple-element.33), channel_id=1, source_target_pairs={{0,11},{1,8},{2,9},{3,10},{4,15},{5,12},{6,13},{7,14},{8,19},{9,16... | collective-permute-start | bytes 270344 | tf_op jit(solution)/shard_map/ppermute | solution.py:32
  17.7 6.1 %collective-permute-start.5 = (f32[4,24,128]{2,1,0:T(8,128)S(1)}, f32[4,24,128]{2,1,0:T(8,128)S(1)}, u32[]{:S(2)}, u32[]{:S(2)}) collective-permute-start(f32[4,24,128]{2,1,0:T(8,128)S(1)} %get-tuple-element.29), channel_id=1, source_target_pairs={{0,15},{1,12},{2,13},{3,14},{4,11},{5,8},{6,9},{7,10},{8,23},{9,20... | collective-permute-start | bytes 147464 | tf_op jit(solution)/shard_map/ppermute | solution.py:32
  18.7 6.1 %collective-permute-start.4 = (f32[4,24,128]{2,1,0:T(8,128)S(1)}, f32[4,24,128]{2,1,0:T(8,128)S(1)}, u32[]{:S(2)}, u32[]{:S(2)}) collective-permute-start(f32[4,24,128]{2,1,0:T(8,128)S(1)} %get-tuple-element.29), channel_id=1, source_target_pairs={{0,11},{1,8},{2,9},{3,10},{4,15},{5,12},{6,13},{7,14},{8,19},{9,16... | collective-permute-start | bytes 147464 | tf_op jit(solution)/shard_map/ppermute | solution.py:32
  26.8 11.0 %collective-permute-start.9 = (f32[2,128,128]{2,1,0:T(8,128)S(1)}, f32[2,128,128]{2,1,0:T(8,128)S(1)}, u32[]{:S(2)}, u32[]{:S(2)}) collective-permute-start(f32[2,128,128]{2,1,0:T(8,128)S(1)} %get-tuple-element.38.refs_2_), channel_id=1, source_target_pairs={{0,8},{1,9},{2,10},{3,11},{4,12},{5,13},{6,14},{7,15},{8,16},{9,17... | collective-permute-start | bytes 393224 | tf_op jit(solution)/shard_map/ppermute | solution.py:32
  27.5 10.3 %collective-permute-start.12 = (f32[4,40,128]{2,1,0:T(8,128)S(1)}, f32[4,40,128]{2,1,0:T(8,128)S(1)}, u32[]{:S(2)}, u32[]{:S(2)}) collective-permute-start(f32[4,40,128]{2,1,0:T(8,128)S(1)} %get-tuple-element.41), channel_id=1, source_target_pairs={{0,1},{1,2},{2,3},{3,0},{4,5},{5,6},{6,7},{7,4},{8,9},{9,10},{10,1... | collective-permute-start | bytes 245768 | tf_op jit(solution)/shard_map/ppermute | solution.py:32
  27.5 10.3 %collective-permute-start.13 = (f32[4,40,128]{2,1,0:T(8,128)S(1)}, f32[4,40,128]{2,1,0:T(8,128)S(1)}, u32[]{:S(2)}, u32[]{:S(2)}) collective-permute-start(f32[4,40,128]{2,1,0:T(8,128)S(1)} %get-tuple-element.42), channel_id=1, source_target_pairs={{0,3},{1,0},{2,1},{3,2},{4,7},{5,4},{6,5},{7,6},{8,11},{9,8},{10,9... | collective-permute-start | bytes 245768 | tf_op jit(solution)/shard_map/ppermute | solution.py:32
  31.3 6.5 %collective-permute-start.10 = (f32[2,40,128]{2,1,0:T(8,128)S(1)}, f32[2,40,128]{2,1,0:T(8,128)S(1)}, u32[]{:S(2)}, u32[]{:S(2)}) collective-permute-start(f32[2,40,128]{2,1,0:T(8,128)S(1)} %get-tuple-element.39), channel_id=1, source_target_pairs={{0,9},{1,10},{2,11},{3,8},{4,13},{5,14},{6,15},{7,12},{8,17},{9,18... | collective-permute-start | bytes 122888 | tf_op jit(solution)/shard_map/ppermute | solution.py:32
  31.4 6.5 %collective-permute-start.11 = (f32[2,40,128]{2,1,0:T(8,128)S(1)}, f32[2,40,128]{2,1,0:T(8,128)S(1)}, u32[]{:S(2)}, u32[]{:S(2)}) collective-permute-start(f32[2,40,128]{2,1,0:T(8,128)S(1)} %get-tuple-element.40), channel_id=1, source_target_pairs={{0,11},{1,8},{2,9},{3,10},{4,15},{5,12},{6,13},{7,14},{8,19},{9,16... | collective-permute-start | bytes 122888 | tf_op jit(solution)/shard_map/ppermute | solution.py:32

commit v5 on v4

--- a/solution.py
+++ b/solution.py
@@ -18,7 +18,7 @@
 RATE_HALO = 4
 DRIFT = 6
 TAKE = HALO + DRIFT
-BELOW, ABOVE = TAKE + 1, HALO + 1
+BELOW = TAKE + 1
 
 
 def shifted(value, by_tm, by_gy, by_gx):
@@ -147,12 +147,11 @@
     return at
 
 
-def pack_kernel(tiles_ref, state_ref, all_ref, low_ref, high_ref):
+def pack_kernel(tiles_ref, state_ref, all_ref, high_ref):
     n_fields, n_x, n_y, _ = tiles_ref.shape
     for field in range(n_fields):
         for x in range(n_x):
             all_ref[field, pl.ds(x, n_y, stride=n_x), :] = tiles_ref[field, x]
-        low_ref[field] = all_ref[field, pl.ds(0, ABOVE * n_x), :]
         high_ref[field] = all_ref[field, pl.ds((n_y - BELOW) * n_x, BELOW * n_x), :]
     for field in range(2):
         state_ref[field] = all_ref[field]
@@ -180,6 +179,9 @@
     params = rows_of(params_ref, width, -HALO)
     results = iteration(start, lambda r: params(r)[0], lambda r: params(r)[1], None)
     write_nodes(results, width, n_y, [(0, TAKE)], *outs)
+    for r in range(HALO):
+        for field, value in enumerate((*start(r + DRIFT), *params(r + DRIFT))):
+            outs[-1][pl.ds((4 * TAKE + field * HALO + r) * width, width), :] = value
 
 
 def write_nodes(results, width, n_y, edges, zero_ref, one_ref, two_ref, *edge_refs):
@@ -194,8 +196,8 @@
                     if first <= r < first + count:
                         beside = pl.ds((r - first) * width, width)
                         edge_refs[2 * i][field, beside, :] = two
-                        edge_refs[2 * i + 1][field, beside, :] = one
-                        edge_refs[2 * i + 1][2 + field, beside, :] = two
+                        for at, value in ((field, one), (2 + field, two)):
+                            edge_refs[2 * i + 1][pl.ds((at * count + r - first) * width, width), :] = value
         for field, zero in enumerate(rate_zero(r)):
             zero_ref[field, pl.ds((r + RATE_HALO) * width, width), :] = zero
 
@@ -207,8 +209,22 @@
     return at
 
 
-def pair_of(ref, field):
-    return ref.at[pl.ds(field, 2)]
+def flat_rows(ref, width, place, first, count):
+    @functools.cache
+    def at(r):
+        assert 0 <= r - first < count
+        return tuple(ref[pl.ds((place + field * count + r - first) * width, width), :] for field in range(2))
+
+    return at
+
+
+def known(width, n_y, start_ref, params_ref, edge_ref):
+    return (
+        joined(
+            (-TAKE, rows_of(ref, width, -TAKE)), (n_y, flat_rows(edge_ref, width, 4 * TAKE + place * HALO, n_y, HALO))
+        )
+        for ref, place in ((start_ref, 0), (params_ref, 2))
+    )
 
 
 def later_iteration(width, n_y, is_first, kept, params, got, old_zero, ones, twos):
@@ -227,43 +243,43 @@
     return iteration(start, feed, kill, old_rates)
 
 
-def second_kernel(n_gy, n_x, n_y, first_ref, start_ref, params_ref, *refs):
-    highs, refs = refs[:n_gy], refs[n_gy:]
-    zero_ref, one_ref, two_ref, got_ref, got_edge, pair_edge, top_ref, *outs = refs
-    width = n_gy * n_x
-    for field in range(4):
-        collect(top_ref, field, field, n_x, n_y, [(n_y, highs, ABOVE)])
-    kept = joined((-TAKE, rows_of(start_ref, width, -TAKE)), (n_y, rows_of(pair_of(top_ref, 0), width, n_y)))
-    params = joined((-TAKE, rows_of(params_ref, width, -TAKE)), (n_y, rows_of(pair_of(top_ref, 2), width, n_y)))
+def second_kernel(width, n_y, first_ref, start_ref, params_ref, *refs):
+    zero_ref, one_ref, two_ref, got_ref, got_edge, pair_edge, *outs = refs
+    kept, params = known(width, n_y, start_ref, params_ref, pair_edge)
     end = n_y - DRIFT
 
-    def moved(tile_ref, edge_ref):
-        return joined((-DRIFT, rows_of(tile_ref, width, -DRIFT)), (end, rows_of(edge_ref, width, end)))
+    def moved(tile_ref, beside):
+        return joined((-DRIFT, rows_of(tile_ref, width, -DRIFT)), (end, beside))
+
+    def pair(place):
+        return flat_rows(pair_edge, width, place * TAKE, end, TAKE)
 
     def old_zero(feed, feed_kill):
         inside = rows_of(zero_ref, width, -RATE_HALO - DRIFT)
         return joined((-RATE_HALO - DRIFT, inside), (end + RATE_HALO, rates_of(kept, feed, feed_kill, 1.0)))
 
-    ones, twos = moved(one_ref, pair_of(pair_edge, 0)), moved(two_ref, pair_of(pair_edge, 2))
-    results = later_iteration(
-        width, n_y, first_ref[0] == 1, kept, params, moved(got_ref, got_edge), old_zero, ones, twos
-    )
+    ones, twos = moved(one_ref, pair(0)), moved(two_ref, pair(2))
+    got = moved(got_ref, rows_of(got_edge, width, end))
+    results = later_iteration(width, n_y, first_ref[0] == 1, kept, params, got, old_zero, ones, twos)
     write_nodes(results, width, n_y, [(0, HALO), (n_y - HALO, HALO)], *outs)
 
 
-def later_kernel(width, n_y, out_x, first_ref, start_ref, params_ref, top_ref, *refs):
+def later_kernel(width, n_y, out_x, first_ref, start_ref, params_ref, known_ref, *refs):
     zero_ref, one_ref, two_ref, got_ref, got_low, got_high, pair_low, pair_high, *outs = refs
-    kept = joined((-TAKE, rows_of(start_ref, width, -TAKE)), (n_y, rows_of(pair_of(top_ref, 0), width, n_y)))
-    params = joined((-TAKE, rows_of(params_ref, width, -TAKE)), (n_y, rows_of(pair_of(top_ref, 2), width, n_y)))
-
-    def window(low_ref, tile_ref, high_ref):
-        refs = ((-HALO, low_ref), (0, tile_ref), (n_y, high_ref))
-        return joined(*((first, rows_of(ref, width, first)) for first, ref in refs))
-
-    ones = window(pair_of(pair_low, 0), one_ref, pair_of(pair_high, 0))
-    twos = window(pair_of(pair_low, 2), two_ref, pair_of(pair_high, 2))
+    kept, params = known(width, n_y, start_ref, params_ref, known_ref)
+
+    def window(low, tile_ref, high):
+        return joined((-HALO, low), (0, rows_of(tile_ref, width, 0)), (n_y, high))
+
+    def pair(tile_ref, place):
+        low, high = (
+            flat_rows(ref, width, place * HALO, first, HALO) for ref, first in ((pair_low, -HALO), (pair_high, n_y))
+        )
+        return window(low, tile_ref, high)
+
+    ones, twos = pair(one_ref, 0), pair(two_ref, 2)
     old_zero = rows_of(zero_ref, width, -RATE_HALO)
-    got = window(got_low, got_ref, got_high)
+    got = window(rows_of(got_low, width, -HALO), got_ref, rows_of(got_high, width, n_y))
     results = later_iteration(
         width, n_y, first_ref[0] == 1, kept, params, got, lambda feed, feed_kill: old_zero, ones, twos
     )
@@ -301,36 +317,36 @@
     is_first = (place == 0).astype(jnp.int32)[None]
 
     sent = jnp.where(place == n_tm - 1, initial_state, slice_guess[0])
-    state, local, low, high = call(
+    state, local, high = call(
         pack_kernel,
         "pack",
         0,
         (jnp.concatenate([sent, feed_rate[None], kill_rate[None]]),),
-        [(2, n_y * n_x, n_z), (4, n_y * n_x, n_z), (4, ABOVE * n_x, n_z), (4, BELOW * n_x, n_z)],
+        [(2, n_y * n_x, n_z), (4, n_y * n_x, n_z), (4, BELOW * n_x, n_z)],
     )
     got = [shifted(state, 1, 0, 0), local]
     got += [shifted(local, 1, -gy, 0) for gy in range(1, n_gy)]
     got += [shifted(high, 1, -gy, 1) for gy in range(n_gy)]
-    above = [shifted(low, 1, -gy, -1) for gy in range(n_gy)]
 
     tile, window = (2, n_y * width, n_z), (2, (TAKE + n_y) * width, n_z)
     nodes_only = [(2, (n_y + 2 * RATE_HALO) * width, n_z), tile, tile]
-    edge = lambda rows: [(2, rows * width, n_z), (4, rows * width, n_z)]
+    edge = lambda rows, more=0: [(2, rows * width, n_z), ((4 * rows + more) * width, n_z)]
     start, params, *nodes = call(
         functools.partial(first_kernel, n_gy, n_x, n_y),
         "first",
         0,
         got,
-        [window, window, *nodes_only, *edge(TAKE)],
+        [window, window, *nodes_only, *edge(TAKE, 4 * HALO)],
     )
     zero, one, two, two_edge, pair_edge = nodes
     got = [shifted(two, 1, 0, 0), shifted(two_edge, 1, 0, -1), shifted(pair_edge, 0, 0, -1)]
-    top, *nodes = call(
-        functools.partial(second_kernel, n_gy, n_x, n_y),
+    known_edge = got[-1]
+    nodes = call(
+        functools.partial(second_kernel, width, n_y),
         "second",
         1,
-        (is_first, start, params, *above, zero, one, two, *got),
-        [(4, ABOVE * width, n_z), *nodes_only, *edge(HALO), *edge(HALO)],
+        (is_first, start, params, zero, one, two, *got),
+        [*nodes_only, *edge(HALO), *edge(HALO)],
     )
     for sweep_index in range(2, ITERS):
         zero, one, two, two_low, pair_low, two_high, pair_high = nodes
@@ -341,7 +357,7 @@
             functools.partial(later_kernel, width, n_y, n_x if done else None),
             "last" if done else "later",
             1,
-            (is_first, start, params, top, zero, one, two, *got),
+            (is_first, start, params, known_edge, zero, one, two, *got),
             [initial_state.shape] if done else [*nodes_only, *edge(HALO), *edge(HALO)],
             [pltpu.VMEM(tile, jnp.float32)] if done else (),
         )

time: 40.5 us -> 40 us (0.988)
  starting transfers between devices: 21.7 us -> 18.3 us
  waiting for transfers between devices: 11.9 us -> 14.7 us
    ppermute x14 -> x12, starting transfers between devices: 21.7 us -> 18.3 us  [shifted(): return lax.ppermute(value, AXES, pairs)]
    ppermute x14 -> x12, waiting for transfers between devices: 11.9 us -> 14.7 us  [shifted(): return lax.ppermute(value, AXES, pairs)]
  transfers between devices with their start and end apart: 14 -> 12, of which waited for: 5 -> 5; matrix products, arithmetic and copies ran while one was open for 0% -> 0% of each run, Pallas kernels for 0% -> 0%
where the time goes in v5:
time: 40 us; the launch traced here: 39.8 us
  starting transfers between devices  18.3 us (46%)
  waiting for transfers between devices  14.7 us (37%)
  Pallas kernels  5.76 us (14%)
  other arithmetic  0.87 us (2%)
    ppermute x12, starting transfers between devices, shifted(): return lax.ppermute(value, AXES, pairs)  18.3 us
    ppermute x12, waiting for transfers between devices, shifted(): return lax.ppermute(value, AXES, pairs)  14.7 us
    pallas_call x4, Pallas kernels, call(): pl.pallas_call(kernel, name=name, out_shape=[jax.ShapeDtypeStruct(shape,...  5.76 us
    select_n x1, other arithmetic, shards(): sent = jnp.where(place == n_tm - 1, initial_state, slice_guess[0])  0.86 us
  transfers between devices with their start and end apart: 12, of which 5 were waited for; matrix products, arithmetic and copies ran while one was open for 0% of the time, Pallas kernels for 0%

profile of v5, /device:TPU:0, one launch (start us, length us, event | category | flops | bytes accessed | tf_op | source)
XLA Modules:
  0.0 39.8 jit_solution(1699264762286376387)
XLA Ops:
  0.0 0.0 copy-start
  0.0 0.0 copy-start.1
  0.0 0.9 %bitcast_select_fusion = f32[2,4,16,128]{3,2,1,0:T(8,128)S(1)} fusion(f32[2,4,16,128]{3,2,1,0:T(8,128)} %param.4, f32[1,2,4,16,128]{4,3,2,1,0:T(8,128)} %param.5, pred[]{:T(512)S(6)} %eq.7), kind=kLoop, calls=%fused_computation.1 | loop fusion | flops 16384 | bytes 196609 | tf_op jit(solution)/shard_map/jit(_where)/select_n | solution.py:319
  0.9 0.0 copy-done
  0.9 0.0 copy-done.1
  0.9 2.5 %collective-permute-start.1 = (f32[4,64,128]{2,1,0:T(8,128)S(1)}, f32[4,64,128]{2,1,0:T(8,128)S(1)}, u32[]{:S(2)}, u32[]{:S(2)}) collective-permute-start(f32[4,64,128]{2,1,0:T(8,128)S(1)} %get-tuple-element.23.refs_1_), channel_id=1, source_target_pairs={{0,12},{1,13},{2,14},{3,15},{4,8},{5,9},{6,10},{7,11},{8,20},{9,21... | collective-permute-start | bytes 393224 | tf_op jit(solution)/shard_map/ppermute | solution.py:32
  3.4 2.7 %collective-permute-start.3 = (f32[4,48,128]{2,1,0:T(8,128)S(1)}, f32[4,48,128]{2,1,0:T(8,128)S(1)}, u32[]{:S(2)}, u32[]{:S(2)}) collective-permute-start(f32[4,48,128]{2,1,0:T(8,128)S(1)} %get-tuple-element.24), channel_id=1, source_target_pairs={{0,13},{1,14},{2,15},{3,12},{4,9},{5,10},{6,11},{7,8},{8,21},{9,22... | collective-permute-start | bytes 294920 | tf_op jit(solution)/shard_map/ppermute | solution.py:32
  6.1 1.1 %collective-permute-start.2 = (f32[4,48,128]{2,1,0:T(8,128)S(1)}, f32[4,48,128]{2,1,0:T(8,128)S(1)}, u32[]{:S(2)}, u32[]{:S(2)}) collective-permute-start(f32[4,48,128]{2,1,0:T(8,128)S(1)} %get-tuple-element.24), channel_id=1, source_target_pairs={{0,9},{1,10},{2,11},{3,8},{4,13},{5,14},{6,15},{7,12},{8,17},{9,18... | collective-permute-start | bytes 294920 | tf_op jit(solution)/shard_map/ppermute | solution.py:32
  7.3 0.5 %collective-permute-start = (f32[2,64,128]{2,1,0:T(8,128)S(1)}, f32[2,64,128]{2,1,0:T(8,128)S(1)}, u32[]{:S(2)}, u32[]{:S(2)}) collective-permute-start(f32[2,64,128]{2,1,0:T(8,128)S(1)} %get-tuple-element.22), channel_id=1, source_target_pairs={{0,8},{1,9},{2,10},{3,11},{4,12},{5,13},{6,14},{7,15},{8,16},{9,17... | collective-permute-start | bytes 196616 | tf_op jit(solution)/shard_map/ppermute | solution.py:32
  7.8 3.8 %collective-permute-done.refs_0_ = f32[2,64,128]{2,1,0:T(8,128)S(1)} collective-permute-done((f32[2,64,128]{2,1,0:T(8,128)S(1)}, f32[2,64,128]{2,1,0:T(8,128)S(1)}, u32[]{:S(2)}, u32[]{:S(2)}) %collective-permute-start) | collective-permute-done | bytes 65568 | tf_op jit(solution)/shard_map/ppermute | solution.py:32
  11.6 0.0 collective-permute-done.3.refs_4_
  11.6 2.1 %collective-permute-done.2.refs_3_ = f32[4,48,128]{2,1,0:T(8,128)S(1)} collective-permute-done((f32[4,48,128]{2,1,0:T(8,128)S(1)}, f32[4,48,128]{2,1,0:T(8,128)S(1)}, u32[]{:S(2)}, u32[]{:S(2)}) %collective-permute-start.2) | collective-permute-done | bytes 98336 | tf_op jit(solution)/shard_map/ppermute | solution.py:32
  13.6 0.0 collective-permute-done.1.refs_2_
  13.6 1.2 %first.1 = (f32[2,216,128]{2,1,0:T(8,128)S(1)}, f32[2,216,128]{2,1,0:T(8,128)S(1)}, f32[2,192,128]{2,1,0:T(8,128)S(1)}, f32[2,128,128]{2,1,0:T(8,128)S(1)}, f32[...) custom-call(f32[2,64,128]{2,1,0:T(8,128)S(1)} %collective-permute-done.refs_0_, ...), custom_call_target="tpu_custom_call" | custom-call | tf_op jit(solution)/shard_map/first/pallas_call | solution.py:301
  14.9 0.9 %collective-permute-start.4 = (f32[512,128]{1,0:T(8,128)S(1)}, f32[512,128]{1,0:T(8,128)S(1)}, u32[]{:S(2)}, u32[]{:S(2)}) collective-permute-start(f32[512,128]{1,0:T(8,128)S(1)} %get-tuple-element.27), channel_id=1, source_target_pairs={{0,3},{1,0},{2,1},{3,2},{4,7},{5,4},{6,5},{7,6},{8,11},{9,8},{10,9... | collective-permute-start | bytes 786440 | tf_op jit(solution)/shard_map/ppermute | solution.py:32
  15.7 0.3 collective-permute-start.5
  16.0 1.7 %collective-permute-start.6 = (f32[2,88,128]{2,1,0:T(8,128)S(1)}, f32[2,88,128]{2,1,0:T(8,128)S(1)}, u32[]{:S(2)}, u32[]{:S(2)}) collective-permute-start(f32[2,88,128]{2,1,0:T(8,128)S(1)} %get-tuple-element.31), channel_id=1, source_target_pairs={{0,11},{1,8},{2,9},{3,10},{4,15},{5,12},{6,13},{7,14},{8,19},{9,16... | collective-permute-start | bytes 270344 | tf_op jit(solution)/shard_map/ppermute | solution.py:32
  17.7 6.3 %collective-permute-done.6.refs_4_ = f32[2,88,128]{2,1,0:T(8,128)S(1)} collective-permute-done((f32[2,88,128]{2,1,0:T(8,128)S(1)}, f32[2,88,128]{2,1,0:T(8,128)S(1)}, u32[]{:S(2)}, u32[]{:S(2)}) %collective-permute-start.6) | collective-permute-done | bytes 90144 | tf_op jit(solution)/shard_map/ppermute | solution.py:32
  24.0 0.0 collective-permute-done.5.refs_3_
  24.0 0.1 collective-permute-done.4.refs_5_.known_ref
  24.1 2.0 %second.1 = (f32[2,192,128]{2,1,0:T(8,128)S(1)}, f32[2,128,128]{2,1,0:T(8,128)S(1)}, f32[2,128,128]{2,1,0:T(8,128)S(1)}, f32[2,40,128]{2,1,0:T(8,128)S(1)}, f32[...) custom-call(s32[1]{0:T(128)} %bitcast.first_ref, ...), custom_call_target="tpu_custom_call" | custom-call | tf_op jit(solution)/shard_map/second/pallas_call | solution.py:301
  26.1 1.0 %collective-permute-start.7 = (f32[2,128,128]{2,1,0:T(8,128)S(1)}, f32[2,128,128]{2,1,0:T(8,128)S(1)}, u32[]{:S(2)}, u32[]{:S(2)}) collective-permute-start(f32[2,128,128]{2,1,0:T(8,128)S(1)} %get-tuple-element.34.refs_2_), channel_id=1, source_target_pairs={{0,8},{1,9},{2,10},{3,11},{4,12},{5,13},{6,14},{7,15},{8,16},{9,17... | collective-permute-start | bytes 393224 | tf_op jit(solution)/shard_map/ppermute | solution.py:32
  27.1 0.0 collective-permute-start.10
  27.1 3.8 %collective-permute-start.11 = (f32[160,128]{1,0:T(8,128)S(1)}, f32[160,128]{1,0:T(8,128)S(1)}, u32[]{:S(2)}, u32[]{:S(2)}) collective-permute-start(f32[160,128]{1,0:T(8,128)S(1)} %get-tuple-element.38), channel_id=1, source_target_pairs={{0,3},{1,0},{2,1},{3,2},{4,7},{5,4},{6,5},{7,6},{8,11},{9,8},{10,9... | collective-permute-start | bytes 245768 | tf_op jit(solution)/shard_map/ppermute | solution.py:32
  30.9 0.0 collective-permute-start.8
  30.9 3.9 %collective-permute-start.9 = (f32[2,40,128]{2,1,0:T(8,128)S(1)}, f32[2,40,128]{2,1,0:T(8,128)S(1)}, u32[]{:S(2)}, u32[]{:S(2)}) collective-permute-start(f32[2,40,128]{2,1,0:T(8,128)S(1)} %get-tuple-element.36), channel_id=1, source_target_pairs={{0,11},{1,8},{2,9},{3,10},{4,15},{5,12},{6,13},{7,14},{8,19},{9,16... | collective-permute-start | bytes 122888 | tf_op jit(solution)/shard_map/ppermute | solution.py:32
  34.8 2.5 %collective-permute-done.8.refs_4_ = f32[2,40,128]{2,1,0:T(8,128)S(1)} collective-permute-done((f32[2,40,128]{2,1,0:T(8,128)S(1)}, f32[2,40,128]{2,1,0:T(8,128)S(1)}, u32[]{:S(2)}, u32[]{:S(2)}) %collective-permute-start.8) | collective-permute-done | bytes 40992 | tf_op jit(solution)/shard_map/ppermute | solution.py:32
  37.3 0.0 collective-permute-done.9.refs_5_
  37.3 0.0 collective-permute-done.10.refs_6_
  37.3 0.0 collective-permute-done.11.refs_7_
  37.3 0.0 collective-permute-done.7.refs_3_
  37.3 2.5 %last.1 = f32[2,4,16,128]{3,2,1,0:T(8,128)} custom-call(s32[1]{0:T(128)} %bitcast.first_ref, f32[2,216,128]{2,1,0:T(8,128)S(1)} %get-tuple-element.25.start_ref, f32[2,216,128]{2,1,0:T(8,128)S(1)} %get-tuple-element.26.params_ref, f32[512,128]{1,0:T(8,128)S(1)} %collective-permute-done.4.refs_5_.known_ref, f32[2,192,128]{2,1,0:T(8,128)S(1)} %get-tuple-element.32.refs_0_, ...), custom_call_target="tpu_custom_call" | custom-call | tf_op jit(solution)/shard_map/last/pallas_call | solution.py:301
  (2 shorter events, 0.0 us)
Async XLA Ops:
  0.0 0.9 %copy-start = (f32[4,16,128]{2,1,0:T(8,128)S(1)}, f32[4,16,128]{2,1,0:T(8,128)}, u32[]{:S(2)}) copy-start(f32[4,16,128]{2,1,0:T(8,128)} %param.7) | copy-start | bytes 98308
  0.0 0.9 %copy-start.1 = (f32[4,16,128]{2,1,0:T(8,128)S(1)}, f32[4,16,128]{2,1,0:T(8,128)}, u32[]{:S(2)}) copy-start(f32[4,16,128]{2,1,0:T(8,128)} %param.6) | copy-start | bytes 98308
  0.9 12.7 %collective-permute-start.1 = (f32[4,64,128]{2,1,0:T(8,128)S(1)}, f32[4,64,128]{2,1,0:T(8,128)S(1)}, u32[]{:S(2)}, u32[]{:S(2)}) collective-permute-start(f32[4,64,128]{2,1,0:T(8,128)S(1)} %get-tuple-element.23.refs_1_), channel_id=1, source_target_pairs={{0,12},{1,13},{2,14},{3,15},{4,8},{5,9},{6,10},{7,11},{8,20},{9,21... | collective-permute-start | bytes 393224 | tf_op jit(solution)/shard_map/ppermute | solution.py:32
  3.4 8.2 %collective-permute-start.3 = (f32[4,48,128]{2,1,0:T(8,128)S(1)}, f32[4,48,128]{2,1,0:T(8,128)S(1)}, u32[]{:S(2)}, u32[]{:S(2)}) collective-permute-start(f32[4,48,128]{2,1,0:T(8,128)S(1)} %get-tuple-element.24), channel_id=1, source_target_pairs={{0,13},{1,14},{2,15},{3,12},{4,9},{5,10},{6,11},{7,8},{8,21},{9,22... | collective-permute-start | bytes 294920 | tf_op jit(solution)/shard_map/ppermute | solution.py:32
  6.1 7.5 %collective-permute-start.2 = (f32[4,48,128]{2,1,0:T(8,128)S(1)}, f32[4,48,128]{2,1,0:T(8,128)S(1)}, u32[]{:S(2)}, u32[]{:S(2)}) collective-permute-start(f32[4,48,128]{2,1,0:T(8,128)S(1)} %get-tuple-element.24), channel_id=1, source_target_pairs={{0,9},{1,10},{2,11},{3,8},{4,13},{5,14},{6,15},{7,12},{8,17},{9,18... | collective-permute-start | bytes 294920 | tf_op jit(solution)/shard_map/ppermute | solution.py:32
  7.3 4.3 %collective-permute-start = (f32[2,64,128]{2,1,0:T(8,128)S(1)}, f32[2,64,128]{2,1,0:T(8,128)S(1)}, u32[]{:S(2)}, u32[]{:S(2)}) collective-permute-start(f32[2,64,128]{2,1,0:T(8,128)S(1)} %get-tuple-element.22), channel_id=1, source_target_pairs={{0,8},{1,9},{2,10},{3,11},{4,12},{5,13},{6,14},{7,15},{8,16},{9,17... | collective-permute-start | bytes 196616 | tf_op jit(solution)/shard_map/ppermute | solution.py:32
  14.9 9.2 %collective-permute-start.4 = (f32[512,128]{1,0:T(8,128)S(1)}, f32[512,128]{1,0:T(8,128)S(1)}, u32[]{:S(2)}, u32[]{:S(2)}) collective-permute-start(f32[512,128]{1,0:T(8,128)S(1)} %get-tuple-element.27), channel_id=1, source_target_pairs={{0,3},{1,0},{2,1},{3,2},{4,7},{5,4},{6,5},{7,6},{8,11},{9,8},{10,9... | collective-permute-start | bytes 786440 | tf_op jit(solution)/shard_map/ppermute | solution.py:32
  15.7 8.2 %collective-permute-start.5 = (f32[2,128,128]{2,1,0:T(8,128)S(1)}, f32[2,128,128]{2,1,0:T(8,128)S(1)}, u32[]{:S(2)}, u32[]{:S(2)}) collective-permute-start(f32[2,128,128]{2,1,0:T(8,128)S(1)} %get-tuple-element.30.refs_2_), channel_id=1, source_target_pairs={{0,8},{1,9},{2,10},{3,11},{4,12},{5,13},{6,14},{7,15},{8,16},{9,17... | collective-permute-start | bytes 393224 | tf_op jit(solution)/shard_map/ppermute | solution.py:32
  16.0 7.9 %collective-permute-start.6 = (f32[2,88,128]{2,1,0:T(8,128)S(1)}, f32[2,88,128]{2,1,0:T(8,128)S(1)}, u32[]{:S(2)}, u32[]{:S(2)}) collective-permute-start(f32[2,88,128]{2,1,0:T(8,128)S(1)} %get-tuple-element.31), channel_id=1, source_target_pairs={{0,11},{1,8},{2,9},{3,10},{4,15},{5,12},{6,13},{7,14},{8,19},{9,16... | collective-permute-start | bytes 270344 | tf_op jit(solution)/shard_map/ppermute | solution.py:32
  26.1 11.2 %collective-permute-start.7 = (f32[2,128,128]{2,1,0:T(8,128)S(1)}, f32[2,128,128]{2,1,0:T(8,128)S(1)}, u32[]{:S(2)}, u32[]{:S(2)}) collective-permute-start(f32[2,128,128]{2,1,0:T(8,128)S(1)} %get-tuple-element.34.refs_2_), channel_id=1, source_target_pairs={{0,8},{1,9},{2,10},{3,11},{4,12},{5,13},{6,14},{7,15},{8,16},{9,17... | collective-permute-start | bytes 393224 | tf_op jit(solution)/shard_map/ppermute | solution.py:32
  27.1 10.2 %collective-permute-start.10 = (f32[160,128]{1,0:T(8,128)S(1)}, f32[160,128]{1,0:T(8,128)S(1)}, u32[]{:S(2)}, u32[]{:S(2)}) collective-permute-start(f32[160,128]{1,0:T(8,128)S(1)} %get-tuple-element.37), channel_id=1, source_target_pairs={{0,1},{1,2},{2,3},{3,0},{4,5},{5,6},{6,7},{7,4},{8,9},{9,10},{10,1... | collective-permute-start | bytes 245768 | tf_op jit(solution)/shard_map/ppermute | solution.py:32
  27.1 10.2 %collective-permute-start.11 = (f32[160,128]{1,0:T(8,128)S(1)}, f32[160,128]{1,0:T(8,128)S(1)}, u32[]{:S(2)}, u32[]{:S(2)}) collective-permute-start(f32[160,128]{1,0:T(8,128)S(1)} %get-tuple-element.38), channel_id=1, source_target_pairs={{0,3},{1,0},{2,1},{3,2},{4,7},{5,4},{6,5},{7,6},{8,11},{9,8},{10,9... | collective-permute-start | bytes 245768 | tf_op jit(solution)/shard_map/ppermute | solution.py:32
  30.9 6.4 %collective-permute-start.8 = (f32[2,40,128]{2,1,0:T(8,128)S(1)}, f32[2,40,128]{2,1,0:T(8,128)S(1)}, u32[]{:S(2)}, u32[]{:S(2)}) collective-permute-start(f32[2,40,128]{2,1,0:T(8,128)S(1)} %get-tuple-element.35), channel_id=1, source_target_pairs={{0,9},{1,10},{2,11},{3,8},{4,13},{5,14},{6,15},{7,12},{8,17},{9,18... | collective-permute-start | bytes 122888 | tf_op jit(solution)/shard_map/ppermute | solution.py:32
  30.9 6.4 %collective-permute-start.9 = (f32[2,40,128]{2,1,0:T(8,128)S(1)}, f32[2,40,128]{2,1,0:T(8,128)S(1)}, u32[]{:S(2)}, u32[]{:S(2)}) collective-permute-start(f32[2,40,128]{2,1,0:T(8,128)S(1)} %get-tuple-element.36), channel_id=1, source_target_pairs={{0,11},{1,8},{2,9},{3,10},{4,15},{5,12},{6,13},{7,14},{8,19},{9,16... | collective-permute-start | bytes 122888 | tf_op jit(solution)/shard_map/ppermute | solution.py:32

commit v6 on v5

--- a/solution.py
+++ b/solution.py
@@ -7,7 +7,6 @@
 from jax.experimental.pallas import tpu as pltpu
 from jax.sharding import PartitionSpec as P
 
-ITERS = 3
 DIFF_U = 0.2
 DIFF_V = 0.1
 HALF_STEP = 0.5
@@ -16,9 +15,8 @@
 AXES = ("tm", "gy", "gx")
 HALO = 5
 RATE_HALO = 4
-DRIFT = 6
-TAKE = HALO + DRIFT
-BELOW = TAKE + 1
+LOW, DROP, SHIFT = 9, 6, 4
+BELOW = 16
 
 
 def shifted(value, by_tm, by_gy, by_gx):
@@ -167,39 +165,43 @@
                     out_ref[field, place, :] = ref[source_field, pl.ds(k * n_x, n_x), :]
 
 
+def emit(width, sinks):
+    for r in range(min(sink[0] for sink in sinks), max(sink[1] for sink in sinks)):
+        for low, high, values, ref, place in sinks:
+            if low <= r < high:
+                for field, value in enumerate(values(r)):
+                    if place is None:
+                        ref[field, pl.ds((r - low) * width, width), :] = value
+                    else:
+                        ref[pl.ds((place + field * (high - low) + r - low) * width, width), :] = value
+
+
 def first_kernel(n_gy, n_x, n_y, *refs):
     state_ref, local_ref = refs[:2]
     others, lows = refs[2 : 1 + n_gy], refs[1 + n_gy : 1 + 2 * n_gy]
-    start_ref, params_ref, *outs = refs[1 + 2 * n_gy :]
+    start_ref, params_ref, zero_ref, one_ref, two_ref, two_edge, pair_edge = refs[1 + 2 * n_gy :]
     width = n_gy * n_x
     for field in range(2):
-        collect(start_ref, field, field, n_x, -TAKE, [(-BELOW, lows, BELOW), (0, [state_ref, *others], n_y)])
-        collect(params_ref, field, 2 + field, n_x, -TAKE, [(-BELOW, lows, BELOW), (0, [local_ref, *others], n_y)])
-    start = rows_of(start_ref, width, -HALO)
-    params = rows_of(params_ref, width, -HALO)
-    results = iteration(start, lambda r: params(r)[0], lambda r: params(r)[1], None)
-    write_nodes(results, width, n_y, [(0, TAKE)], *outs)
-    for r in range(HALO):
-        for field, value in enumerate((*start(r + DRIFT), *params(r + DRIFT))):
-            outs[-1][pl.ds((4 * TAKE + field * HALO + r) * width, width), :] = value
-
-
-def write_nodes(results, width, n_y, edges, zero_ref, one_ref, two_ref, *edge_refs):
-    rate_zero, node_one, node_two = results
-    for r in range(-RATE_HALO, n_y + RATE_HALO):
-        if 0 <= r < n_y:
-            place = pl.ds(r * width, width)
-            for field, (one, two) in enumerate(zip(node_one(r), node_two(r))):
-                one_ref[field, place, :] = one
-                two_ref[field, place, :] = two
-                for i, (first, count) in enumerate(edges):
-                    if first <= r < first + count:
-                        beside = pl.ds((r - first) * width, width)
-                        edge_refs[2 * i][field, beside, :] = two
-                        for at, value in ((field, one), (2 + field, two)):
-                            edge_refs[2 * i + 1][pl.ds((at * count + r - first) * width, width), :] = value
-        for field, zero in enumerate(rate_zero(r)):
-            zero_ref[field, pl.ds((r + RATE_HALO) * width, width), :] = zero
+        collect(start_ref, field, field, n_x, -BELOW, [(-BELOW, lows, BELOW), (0, [state_ref, *others], n_y)])
+        collect(params_ref, field, 2 + field, n_x, -BELOW, [(-BELOW, lows, BELOW), (0, [local_ref, *others], n_y)])
+    start = rows_of(start_ref, width, -BELOW)
+    params = rows_of(params_ref, width, -BELOW)
+    zero, one, two = iteration(start, lambda r: params(r)[0], lambda r: params(r)[1], None)
+    high = n_y - DROP
+    edge = (-DROP, HALO - SHIFT)
+    count = edge[1] - edge[0]
+    emit(
+        width,
+        [
+            (-SHIFT - RATE_HALO, n_y - 1, zero, zero_ref, None),
+            (-LOW, high, one, one_ref, None),
+            (-LOW, high, two, two_ref, None),
+            (*edge, two, two_edge, None),
+            (*edge, one, pair_edge, 0),
+            (*edge, two, pair_edge, 2 * count),
+            (0, edge[1], start, pair_edge, 4 * count),
+        ],
+    )
 
 
 def joined(*parts):
@@ -218,16 +220,7 @@
     return at
 
 
-def known(width, n_y, start_ref, params_ref, edge_ref):
-    return (
-        joined(
-            (-TAKE, rows_of(ref, width, -TAKE)), (n_y, flat_rows(edge_ref, width, 4 * TAKE + place * HALO, n_y, HALO))
-        )
-        for ref, place in ((start_ref, 0), (params_ref, 2))
-    )
-
-
-def later_iteration(width, n_y, is_first, kept, params, got, old_zero, ones, twos):
+def later_iteration(is_first, kept, params, got, old_zero, ones, twos):
     feed, kill = (lambda r: params(r)[0]), (lambda r: params(r)[1])
     feed_kill = functools.cache(lambda r: feed(r) + kill(r))
 
@@ -240,59 +233,80 @@
         rates_of(ones, feed, feed_kill, 1.0),
         rates_of(twos, feed, feed_kill, 1.0),
     )
-    return iteration(start, feed, kill, old_rates)
+    return start, iteration(start, feed, kill, old_rates)
 
 
 def second_kernel(width, n_y, first_ref, start_ref, params_ref, *refs):
     zero_ref, one_ref, two_ref, got_ref, got_edge, pair_edge, *outs = refs
-    kept, params = known(width, n_y, start_ref, params_ref, pair_edge)
-    end = n_y - DRIFT
+    high = n_y - DROP
+    top = n_y - SHIFT + HALO
+    count = top - high
+    kept = joined(
+        (-BELOW, rows_of(start_ref, width, -BELOW)), (n_y, flat_rows(pair_edge, width, 4 * count, n_y, top - n_y))
+    )
+    params = rows_of(params_ref, width, -BELOW)
 
     def moved(tile_ref, beside):
-        return joined((-DRIFT, rows_of(tile_ref, width, -DRIFT)), (end, beside))
-
-    def pair(place):
-        return flat_rows(pair_edge, width, place * TAKE, end, TAKE)
+        return joined((-LOW, rows_of(tile_ref, width, -LOW)), (high, beside))
 
     def old_zero(feed, feed_kill):
-        inside = rows_of(zero_ref, width, -RATE_HALO - DRIFT)
-        return joined((-RATE_HALO - DRIFT, inside), (end + RATE_HALO, rates_of(kept, feed, feed_kill, 1.0)))
-
-    ones, twos = moved(one_ref, pair(0)), moved(two_ref, pair(2))
-    got = moved(got_ref, rows_of(got_edge, width, end))
-    results = later_iteration(width, n_y, first_ref[0] == 1, kept, params, got, old_zero, ones, twos)
-    write_nodes(results, width, n_y, [(0, HALO), (n_y - HALO, HALO)], *outs)
-
-
-def later_kernel(width, n_y, out_x, first_ref, start_ref, params_ref, known_ref, *refs):
-    zero_ref, one_ref, two_ref, got_ref, got_low, got_high, pair_low, pair_high, *outs = refs
-    kept, params = known(width, n_y, start_ref, params_ref, known_ref)
-
-    def window(low, tile_ref, high):
-        return joined((-HALO, low), (0, rows_of(tile_ref, width, 0)), (n_y, high))
+        inside = rows_of(zero_ref, width, -SHIFT - RATE_HALO)
+        return joined((-SHIFT - RATE_HALO, inside), (n_y - 1, rates_of(kept, feed, feed_kill, 1.0)))
+
+    ones = moved(one_ref, flat_rows(pair_edge, width, 0, high, count))
+    twos = moved(two_ref, flat_rows(pair_edge, width, 2 * count, high, count))
+    got = moved(got_ref, rows_of(got_edge, width, high))
+    start, (zero, one, two) = later_iteration(first_ref[0] == 1, kept, params, got, old_zero, ones, twos)
+    zero_ref, one_ref, two_ref, two_up, pair_up, two_down, pair_down = outs
+    up, down = (-SHIFT, HALO), (n_y - HALO, n_y - SHIFT)
+    count = up[1] - up[0]
+    emit(
+        width,
+        [
+            (-RATE_HALO, n_y, zero, zero_ref, None),
+            (-SHIFT, n_y - SHIFT, one, one_ref, None),
+            (-SHIFT, n_y - SHIFT, two, two_ref, None),
+            (*up, two, two_up, None),
+            (*up, one, pair_up, 0),
+            (*up, two, pair_up, 2 * count),
+            (-1, HALO, start, pair_up, 4 * count),
+            (-1, HALO, params, pair_up, 4 * count + 2 * (HALO + 1)),
+            (*down, two, two_down, None),
+            (*down, one, pair_down, 0),
+            (*down, two, pair_down, 2 * (down[1] - down[0])),
+        ],
+    )
+
+
+def third_kernel(width, n_y, out_x, first_ref, start_ref, params_ref, *refs):
+    zero_ref, one_ref, two_ref, got_ref, got_high, got_low, pair_high, pair_low, out_ref, scratch = refs
+    high = n_y - SHIFT
+    count, under = n_y + HALO - high, HALO - SHIFT
+    last_start, last_params = (
+        flat_rows(pair_high, width, 4 * count + place * (HALO + 1), n_y - 1, HALO + 1) for place in (0, 2)
+    )
+    kept = joined((-BELOW, rows_of(start_ref, width, -BELOW)), (n_y, last_start))
+    params = joined((-BELOW, rows_of(params_ref, width, -BELOW)), (n_y, last_params))
+
+    def window(low, tile_ref, beside):
+        return joined((-HALO, low), (-SHIFT, rows_of(tile_ref, width, -SHIFT)), (high, beside))
 
     def pair(tile_ref, place):
-        low, high = (
-            flat_rows(ref, width, place * HALO, first, HALO) for ref, first in ((pair_low, -HALO), (pair_high, n_y))
-        )
-        return window(low, tile_ref, high)
-
-    ones, twos = pair(one_ref, 0), pair(two_ref, 2)
-    old_zero = rows_of(zero_ref, width, -RATE_HALO)
-    got = window(rows_of(got_low, width, -HALO), got_ref, rows_of(got_high, width, n_y))
-    results = later_iteration(
-        width, n_y, first_ref[0] == 1, kept, params, got, lambda feed, feed_kill: old_zero, ones, twos
-    )
-    if out_x is None:
-        write_nodes(results, width, n_y, [(0, HALO), (n_y - HALO, HALO)], *outs)
-    else:
-        out_ref, scratch = outs
-        for r in range(n_y):
-            for field, value in enumerate(results[2](r)):
-                scratch[field, pl.ds(r * width, width), :] = value
-        for x in range(out_x):
-            for field in range(2):
-                out_ref[field, x] = scratch[field, pl.ds(x, n_y, stride=width), :]
+        low = flat_rows(pair_low, width, place * under, -HALO, under)
+        return window(low, tile_ref, flat_rows(pair_high, width, place * count, high, count))
+
+    def old_zero(feed, feed_kill):
+        inside = rows_of(zero_ref, width, -RATE_HALO)
+        return joined((-RATE_HALO, inside), (n_y, rates_of(last_start, feed, feed_kill, 1.0)))
+
+    got = window(rows_of(got_low, width, -HALO), got_ref, rows_of(got_high, width, high))
+    _, (_, _, two) = later_iteration(
+        first_ref[0] == 1, kept, params, got, old_zero, pair(one_ref, 0), pair(two_ref, 2)
+    )
+    emit(width, [(0, n_y, two, scratch, None)])
+    for x in range(out_x):
+        for field in range(2):
+            out_ref[field, x] = scratch[field, pl.ds(x, n_y, stride=width), :]
 
 
 def call(kernel, name, n_scalars, operands, shapes, scratch=()):
@@ -328,40 +342,43 @@
     got += [shifted(local, 1, -gy, 0) for gy in range(1, n_gy)]
     got += [shifted(high, 1, -gy, 1) for gy in range(n_gy)]
 
-    tile, window = (2, n_y * width, n_z), (2, (TAKE + n_y) * width, n_z)
-    nodes_only = [(2, (n_y + 2 * RATE_HALO) * width, n_z), tile, tile]
-    edge = lambda rows, more=0: [(2, rows * width, n_z), ((4 * rows + more) * width, n_z)]
-    start, params, *nodes = call(
+    rows = lambda count: (2, count * width, n_z)
+    flat = lambda count: (count * width, n_z)
+    window, nodes = rows(BELOW + n_y), rows(LOW + n_y - DROP)
+    count = DROP + HALO - SHIFT
+    start, params, *nodes, two_edge, pair_edge = call(
         functools.partial(first_kernel, n_gy, n_x, n_y),
         "first",
         0,
         got,
-        [window, window, *nodes_only, *edge(TAKE, 4 * HALO)],
-    )
-    zero, one, two, two_edge, pair_edge = nodes
-    got = [shifted(two, 1, 0, 0), shifted(two_edge, 1, 0, -1), shifted(pair_edge, 0, 0, -1)]
-    known_edge = got[-1]
-    nodes = call(
+        [
+            *(window, window, rows(SHIFT + RATE_HALO + n_y - 1), nodes, nodes),
+            *(rows(count), flat(4 * count + 2 * (HALO - SHIFT))),
+        ],
+    )
+    got = [shifted(nodes[2], 1, 0, 0), shifted(two_edge, 1, 0, -1), shifted(pair_edge, 0, 0, -1)]
+    count, under = SHIFT + HALO, HALO - SHIFT
+    *nodes, two_up, pair_up, two_down, pair_down = call(
         functools.partial(second_kernel, width, n_y),
         "second",
         1,
-        (is_first, start, params, zero, one, two, *got),
-        [*nodes_only, *edge(HALO), *edge(HALO)],
-    )
-    for sweep_index in range(2, ITERS):
-        zero, one, two, two_low, pair_low, two_high, pair_high = nodes
-        got = [shifted(two, 1, 0, 0), shifted(two_high, 1, 0, 1), shifted(two_low, 1, 0, -1)]
-        got += [shifted(pair_high, 0, 0, 1), shifted(pair_low, 0, 0, -1)]
-        done = sweep_index + 1 == ITERS
-        nodes = call(
-            functools.partial(later_kernel, width, n_y, n_x if done else None),
-            "last" if done else "later",
-            1,
-            (is_first, start, params, known_edge, zero, one, two, *got),
-            [initial_state.shape] if done else [*nodes_only, *edge(HALO), *edge(HALO)],
-            [pltpu.VMEM(tile, jnp.float32)] if done else (),
-        )
-    return nodes[0][None]
+        (is_first, start, params, *nodes, *got),
+        [
+            *(rows(RATE_HALO + n_y), rows(n_y), rows(n_y)),
+            *(rows(count), flat(4 * count + 4 * (HALO + 1)), rows(under), flat(4 * under)),
+        ],
+    )
+    got = [shifted(nodes[2], 1, 0, 0), shifted(two_up, 1, 0, -1), shifted(two_down, 1, 0, 1)]
+    got += [shifted(pair_up, 0, 0, -1), shifted(pair_down, 0, 0, 1)]
+    (final,) = call(
+        functools.partial(third_kernel, width, n_y, n_x),
+        "third",
+        1,
+        (is_first, start, params, *nodes, *got),
+        [initial_state.shape],
+        [pltpu.VMEM(rows(n_y), jnp.float32)],
+    )
+    return final[None]
 
 
 def solution(mesh):

time: 40 us -> 41 us (1.025)
  waiting for transfers between devices: 14.7 us -> 18.6 us
  starting transfers between devices: 18.3 us -> 15.2 us
    ppermute x12, waiting for transfers between devices: 14.7 us -> 18.6 us  [shifted(): return lax.ppermute(value, AXES, pairs)]
    ppermute x12, starting transfers between devices: 18.3 us -> 15.2 us  [shifted(): return lax.ppermute(value, AXES, pairs)]
where the time goes in v6:
time: 41 us; the launch traced here: 40.9 us
  waiting for transfers between devices  18.6 us (45%)
  starting transfers between devices  15.2 us (37%)
  Pallas kernels  6.1 us (15%)
  other arithmetic  0.87 us (2%)
    ppermute x12, waiting for transfers between devices, shifted(): return lax.ppermute(value, AXES, pairs)  18.6 us
    ppermute x12, starting transfers between devices, shifted(): return lax.ppermute(value, AXES, pairs)  15.2 us
    pallas_call x4, Pallas kernels, call(): pl.pallas_call(kernel, name=name, out_shape=[jax.ShapeDtypeStruct(shape,...  6.1 us
    select_n x1, other arithmetic, shards(): sent = jnp.where(place == n_tm - 1, initial_state, slice_guess[0])  0.86 us
  transfers between devices with their start and end apart: 12, of which 5 were waited for; matrix products, arithmetic and copies ran while one was open for 0% of the time, Pallas kernels for 0%

profile of v6, /device:TPU:0, one launch (start us, length us, event | category | flops | bytes accessed | tf_op | source)
XLA Modules:
  0.0 40.9 jit_solution(14247539713765078965)
XLA Ops:
  0.0 0.0 copy-start
  0.0 0.0 copy-start.1
  0.0 0.9 %bitcast_select_fusion = f32[2,4,16,128]{3,2,1,0:T(8,128)S(1)} fusion(f32[2,4,16,128]{3,2,1,0:T(8,128)} %param.4, f32[1,2,4,16,128]{4,3,2,1,0:T(8,128)} %param.5, pred[]{:T(512)S(6)} %eq.7), kind=kLoop, calls=%fused_computation.1 | loop fusion | flops 16384 | bytes 196609 | tf_op jit(solution)/shard_map/jit(_where)/select_n | solution.py:333
  0.9 0.0 copy-done
  0.9 0.0 copy-done.1
  0.9 2.5 %collective-permute-start.1 = (f32[4,64,128]{2,1,0:T(8,128)S(1)}, f32[4,64,128]{2,1,0:T(8,128)S(1)}, u32[]{:S(2)}, u32[]{:S(2)}) collective-permute-start(f32[4,64,128]{2,1,0:T(8,128)S(1)} %get-tuple-element.23.refs_1_), channel_id=1, source_target_pairs={{0,12},{1,13},{2,14},{3,15},{4,8},{5,9},{6,10},{7,11},{8,20},{9,21... | collective-permute-start | bytes 393224 | tf_op jit(solution)/shard_map/ppermute | solution.py:30
  3.4 2.7 %collective-permute-start.3 = (f32[4,64,128]{2,1,0:T(8,128)S(1)}, f32[4,64,128]{2,1,0:T(8,128)S(1)}, u32[]{:S(2)}, u32[]{:S(2)}) collective-permute-start(f32[4,64,128]{2,1,0:T(8,128)S(1)} %get-tuple-element.24), channel_id=1, source_target_pairs={{0,13},{1,14},{2,15},{3,12},{4,9},{5,10},{6,11},{7,8},{8,21},{9,22... | collective-permute-start | bytes 393224 | tf_op jit(solution)/shard_map/ppermute | solution.py:30
  6.1 1.1 %collective-permute-start.2 = (f32[4,64,128]{2,1,0:T(8,128)S(1)}, f32[4,64,128]{2,1,0:T(8,128)S(1)}, u32[]{:S(2)}, u32[]{:S(2)}) collective-permute-start(f32[4,64,128]{2,1,0:T(8,128)S(1)} %get-tuple-element.24), channel_id=1, source_target_pairs={{0,9},{1,10},{2,11},{3,8},{4,13},{5,14},{6,15},{7,12},{8,17},{9,18... | collective-permute-start | bytes 393224 | tf_op jit(solution)/shard_map/ppermute | solution.py:30
  7.3 0.5 %collective-permute-start = (f32[2,64,128]{2,1,0:T(8,128)S(1)}, f32[2,64,128]{2,1,0:T(8,128)S(1)}, u32[]{:S(2)}, u32[]{:S(2)}) collective-permute-start(f32[2,64,128]{2,1,0:T(8,128)S(1)} %get-tuple-element.22), channel_id=1, source_target_pairs={{0,8},{1,9},{2,10},{3,11},{4,12},{5,13},{6,14},{7,15},{8,16},{9,17... | collective-permute-start | bytes 196616 | tf_op jit(solution)/shard_map/ppermute | solution.py:30
  7.8 3.9 %collective-permute-done.refs_0_ = f32[2,64,128]{2,1,0:T(8,128)S(1)} collective-permute-done((f32[2,64,128]{2,1,0:T(8,128)S(1)}, f32[2,64,128]{2,1,0:T(8,128)S(1)}, u32[]{:S(2)}, u32[]{:S(2)}) %collective-permute-start) | collective-permute-done | bytes 65568 | tf_op jit(solution)/shard_map/ppermute | solution.py:30
  11.7 0.0 collective-permute-done.1.refs_2_
  11.7 0.3 collective-permute-done.3.refs_4_
  12.0 3.0 %collective-permute-done.2.refs_3_ = f32[4,64,128]{2,1,0:T(8,128)S(1)} collective-permute-done((f32[4,64,128]{2,1,0:T(8,128)S(1)}, f32[4,64,128]{2,1,0:T(8,128)S(1)}, u32[]{:S(2)}, u32[]{:S(2)}) %collective-permute-start.2) | collective-permute-done | bytes 131104 | tf_op jit(solution)/shard_map/ppermute | solution.py:30
  15.0 1.7 %first.1 = (f32[2,256,128]{2,1,0:T(8,128)S(1)}, f32[2,256,128]{2,1,0:T(8,128)S(1)}, f32[2,184,128]{2,1,0:T(8,128)S(1)}, f32[2,152,128]{2,1,0:T(8,128)S(1)}, f32[...) custom-call(f32[2,64,128]{2,1,0:T(8,128)S(1)} %collective-permute-done.refs_0_, ...), custom_call_target="tpu_custom_call" | custom-call | tf_op jit(solution)/shard_map/first/pallas_call | solution.py:315
  16.7 0.2 collective-permute-start.4
  16.9 1.3 %collective-permute-start.6 = (f32[240,128]{1,0:T(8,128)S(1)}, f32[240,128]{1,0:T(8,128)S(1)}, u32[]{:S(2)}, u32[]{:S(2)}) collective-permute-start(f32[240,128]{1,0:T(8,128)S(1)} %get-tuple-element.31), channel_id=1, source_target_pairs={{0,3},{1,0},{2,1},{3,2},{4,7},{5,4},{6,5},{7,6},{8,11},{9,8},{10,9... | collective-permute-start | bytes 368648 | tf_op jit(solution)/shard_map/ppermute | solution.py:30
  18.2 0.8 %collective-permute-start.5 = (f32[2,56,128]{2,1,0:T(8,128)S(1)}, f32[2,56,128]{2,1,0:T(8,128)S(1)}, u32[]{:S(2)}, u32[]{:S(2)}) collective-permute-start(f32[2,56,128]{2,1,0:T(8,128)S(1)} %get-tuple-element.30), channel_id=1, source_target_pairs={{0,11},{1,8},{2,9},{3,10},{4,15},{5,12},{6,13},{7,14},{8,19},{9,16... | collective-permute-start | bytes 172040 | tf_op jit(solution)/shard_map/ppermute | solution.py:30
  19.0 5.7 %collective-permute-done.5.refs_4_ = f32[2,56,128]{2,1,0:T(8,128)S(1)} collective-permute-done((f32[2,56,128]{2,1,0:T(8,128)S(1)}, f32[2,56,128]{2,1,0:T(8,128)S(1)}, u32[]{:S(2)}, u32[]{:S(2)}) %collective-permute-start.5) | collective-permute-done | bytes 57376 | tf_op jit(solution)/shard_map/ppermute | solution.py:30
  24.7 0.0 collective-permute-done.6.refs_5_
  24.7 0.0 collective-permute-done.4.refs_3_
  24.7 1.9 %second.1 = (f32[2,160,128]{2,1,0:T(8,128)S(1)}, f32[2,128,128]{2,1,0:T(8,128)S(1)}, f32[2,128,128]{2,1,0:T(8,128)S(1)}, f32[2,72,128]{2,1,0:T(8,128)S(1)}, f32[...) custom-call(s32[1]{0:T(128)} %bitcast.first_ref, ...), custom_call_target="tpu_custom_call" | custom-call | tf_op jit(solution)/shard_map/second/pallas_call | solution.py:315
  26.6 2.5 %collective-permute-start.10 = (f32[480,128]{1,0:T(8,128)S(1)}, f32[480,128]{1,0:T(8,128)S(1)}, u32[]{:S(2)}, u32[]{:S(2)}) collective-permute-start(f32[480,128]{1,0:T(8,128)S(1)} %get-tuple-element.37), channel_id=1, source_target_pairs={{0,3},{1,0},{2,1},{3,2},{4,7},{5,4},{6,5},{7,6},{8,11},{9,8},{10,9... | collective-permute-start | bytes 737288 | tf_op jit(solution)/shard_map/ppermute | solution.py:30
  29.1 0.0 collective-permute-start.7
  29.1 1.5 %collective-permute-start.8 = (f32[2,72,128]{2,1,0:T(8,128)S(1)}, f32[2,72,128]{2,1,0:T(8,128)S(1)}, u32[]{:S(2)}, u32[]{:S(2)}) collective-permute-start(f32[2,72,128]{2,1,0:T(8,128)S(1)} %get-tuple-element.35), channel_id=1, source_target_pairs={{0,11},{1,8},{2,9},{3,10},{4,15},{5,12},{6,13},{7,14},{8,19},{9,16... | collective-permute-start | bytes 221192 | tf_op jit(solution)/shard_map/ppermute | solution.py:30
  30.6 2.0 %collective-permute-start.11 = (f32[32,128]{1,0:T(8,128)S(1)}, f32[32,128]{1,0:T(8,128)S(1)}, u32[]{:S(2)}, u32[]{:S(2)}) collective-permute-start(f32[32,128]{1,0:T(8,128)S(1)} %get-tuple-element.38), channel_id=1, source_target_pairs={{0,1},{1,2},{2,3},{3,0},{4,5},{5,6},{6,7},{7,4},{8,9},{9,10},{10,1... | collective-permute-start | bytes 49160 | tf_op jit(solution)/shard_map/ppermute | solution.py:30
  32.6 0.0 collective-permute-start.9
  32.6 5.8 %collective-permute-done.9.refs_5_ = f32[2,8,128]{2,1,0:T(8,128)S(1)} collective-permute-done((f32[2,8,128]{2,1,0:T(8,128)S(1)}, f32[2,8,128]{2,1,0:T(8,128)S(1)}, u32[]{:S(2)}, u32[]{:S(2)}) %collective-permute-start.9) | collective-permute-done | bytes 8224 | tf_op jit(solution)/shard_map/ppermute | solution.py:30
  38.3 0.0 collective-permute-done.11.refs_7_
  38.4 0.0 collective-permute-done.8.refs_4_
  38.4 0.0 collective-permute-done.7.refs_3_
  38.4 0.0 collective-permute-done.10.refs_6_
  38.4 2.5 %third.1 = f32[2,4,16,128]{3,2,1,0:T(8,128)} custom-call(s32[1]{0:T(128)} %bitcast.first_ref, f32[2,256,128]{2,1,0:T(8,128)S(1)} %get-tuple-element.25.start_ref, f32[2,256,128]{2,1,0:T(8,128)S(1)} %get-tuple-element.26.params_ref, f32[2,160,128]{2,1,0:T(8,128)S(1)} %get-tuple-element.32.refs_0_, f32[2,128,128]{2,1,0:T(8,128)S(1)} %get-tuple-element.33.refs_1_, ...), custom_call_target="tpu_custom_call" | custom-call | tf_op jit(solution)/shard_map/third/pallas_call | solution.py:315
  (2 shorter events, 0.0 us)
Async XLA Ops:
  0.0 0.9 %copy-start = (f32[4,16,128]{2,1,0:T(8,128)S(1)}, f32[4,16,128]{2,1,0:T(8,128)}, u32[]{:S(2)}) copy-start(f32[4,16,128]{2,1,0:T(8,128)} %param.7) | copy-start | bytes 98308
  0.0 0.9 %copy-start.1 = (f32[4,16,128]{2,1,0:T(8,128)S(1)}, f32[4,16,128]{2,1,0:T(8,128)}, u32[]{:S(2)}) copy-start(f32[4,16,128]{2,1,0:T(8,128)} %param.6) | copy-start | bytes 98308
  0.9 10.7 %collective-permute-start.1 = (f32[4,64,128]{2,1,0:T(8,128)S(1)}, f32[4,64,128]{2,1,0:T(8,128)S(1)}, u32[]{:S(2)}, u32[]{:S(2)}) collective-permute-start(f32[4,64,128]{2,1,0:T(8,128)S(1)} %get-tuple-element.23.refs_1_), channel_id=1, source_target_pairs={{0,12},{1,13},{2,14},{3,15},{4,8},{5,9},{6,10},{7,11},{8,20},{9,21... | collective-permute-start | bytes 393224 | tf_op jit(solution)/shard_map/ppermute | solution.py:30
  3.4 8.6 %collective-permute-start.3 = (f32[4,64,128]{2,1,0:T(8,128)S(1)}, f32[4,64,128]{2,1,0:T(8,128)S(1)}, u32[]{:S(2)}, u32[]{:S(2)}) collective-permute-start(f32[4,64,128]{2,1,0:T(8,128)S(1)} %get-tuple-element.24), channel_id=1, source_target_pairs={{0,13},{1,14},{2,15},{3,12},{4,9},{5,10},{6,11},{7,8},{8,21},{9,22... | collective-permute-start | bytes 393224 | tf_op jit(solution)/shard_map/ppermute | solution.py:30
  6.1 8.8 %collective-permute-start.2 = (f32[4,64,128]{2,1,0:T(8,128)S(1)}, f32[4,64,128]{2,1,0:T(8,128)S(1)}, u32[]{:S(2)}, u32[]{:S(2)}) collective-permute-start(f32[4,64,128]{2,1,0:T(8,128)S(1)} %get-tuple-element.24), channel_id=1, source_target_pairs={{0,9},{1,10},{2,11},{3,8},{4,13},{5,14},{6,15},{7,12},{8,17},{9,18... | collective-permute-start | bytes 393224 | tf_op jit(solution)/shard_map/ppermute | solution.py:30
  7.3 4.4 %collective-permute-start = (f32[2,64,128]{2,1,0:T(8,128)S(1)}, f32[2,64,128]{2,1,0:T(8,128)S(1)}, u32[]{:S(2)}, u32[]{:S(2)}) collective-permute-start(f32[2,64,128]{2,1,0:T(8,128)S(1)} %get-tuple-element.22), channel_id=1, source_target_pairs={{0,8},{1,9},{2,10},{3,11},{4,12},{5,13},{6,14},{7,15},{8,16},{9,17... | collective-permute-start | bytes 196616 | tf_op jit(solution)/shard_map/ppermute | solution.py:30
  16.7 8.0 %collective-permute-start.4 = (f32[2,152,128]{2,1,0:T(8,128)S(1)}, f32[2,152,128]{2,1,0:T(8,128)S(1)}, u32[]{:S(2)}, u32[]{:S(2)}) collective-permute-start(f32[2,152,128]{2,1,0:T(8,128)S(1)} %get-tuple-element.29.refs_2_), channel_id=1, source_target_pairs={{0,8},{1,9},{2,10},{3,11},{4,12},{5,13},{6,14},{7,15},{8,16},{9,17... | collective-permute-start | bytes 466952 | tf_op jit(solution)/shard_map/ppermute | solution.py:30
  16.9 7.8 %collective-permute-start.6 = (f32[240,128]{1,0:T(8,128)S(1)}, f32[240,128]{1,0:T(8,128)S(1)}, u32[]{:S(2)}, u32[]{:S(2)}) collective-permute-start(f32[240,128]{1,0:T(8,128)S(1)} %get-tuple-element.31), channel_id=1, source_target_pairs={{0,3},{1,0},{2,1},{3,2},{4,7},{5,4},{6,5},{7,6},{8,11},{9,8},{10,9... | collective-permute-start | bytes 368648 | tf_op jit(solution)/shard_map/ppermute | solution.py:30
  18.2 6.5 %collective-permute-start.5 = (f32[2,56,128]{2,1,0:T(8,128)S(1)}, f32[2,56,128]{2,1,0:T(8,128)S(1)}, u32[]{:S(2)}, u32[]{:S(2)}) collective-permute-start(f32[2,56,128]{2,1,0:T(8,128)S(1)} %get-tuple-element.30), channel_id=1, source_target_pairs={{0,11},{1,8},{2,9},{3,10},{4,15},{5,12},{6,13},{7,14},{8,19},{9,16... | collective-permute-start | bytes 172040 | tf_op jit(solution)/shard_map/ppermute | solution.py:30
  26.6 11.8 %collective-permute-start.10 = (f32[480,128]{1,0:T(8,128)S(1)}, f32[480,128]{1,0:T(8,128)S(1)}, u32[]{:S(2)}, u32[]{:S(2)}) collective-permute-start(f32[480,128]{1,0:T(8,128)S(1)} %get-tuple-element.37), channel_id=1, source_target_pairs={{0,3},{1,0},{2,1},{3,2},{4,7},{5,4},{6,5},{7,6},{8,11},{9,8},{10,9... | collective-permute-start | bytes 737288 | tf_op jit(solution)/shard_map/ppermute | solution.py:30
  29.1 9.2 %collective-permute-start.7 = (f32[2,128,128]{2,1,0:T(8,128)S(1)}, f32[2,128,128]{2,1,0:T(8,128)S(1)}, u32[]{:S(2)}, u32[]{:S(2)}) collective-permute-start(f32[2,128,128]{2,1,0:T(8,128)S(1)} %get-tuple-element.34.refs_2_), channel_id=1, source_target_pairs={{0,8},{1,9},{2,10},{3,11},{4,12},{5,13},{6,14},{7,15},{8,16},{9,17... | collective-permute-start | bytes 393224 | tf_op jit(solution)/shard_map/ppermute | solution.py:30
  29.1 9.2 %collective-permute-start.8 = (f32[2,72,128]{2,1,0:T(8,128)S(1)}, f32[2,72,128]{2,1,0:T(8,128)S(1)}, u32[]{:S(2)}, u32[]{:S(2)}) collective-permute-start(f32[2,72,128]{2,1,0:T(8,128)S(1)} %get-tuple-element.35), channel_id=1, source_target_pairs={{0,11},{1,8},{2,9},{3,10},{4,15},{5,12},{6,13},{7,14},{8,19},{9,16... | collective-permute-start | bytes 221192 | tf_op jit(solution)/shard_map/ppermute | solution.py:30
  30.6 7.7 %collective-permute-start.11 = (f32[32,128]{1,0:T(8,128)S(1)}, f32[32,128]{1,0:T(8,128)S(1)}, u32[]{:S(2)}, u32[]{:S(2)}) collective-permute-start(f32[32,128]{1,0:T(8,128)S(1)} %get-tuple-element.38), channel_id=1, source_target_pairs={{0,1},{1,2},{2,3},{3,0},{4,5},{5,6},{6,7},{7,4},{8,9},{9,10},{10,1... | collective-permute-start | bytes 49160 | tf_op jit(solution)/shard_map/ppermute | solution.py:30
  32.6 5.8 %collective-permute-start.9 = (f32[2,8,128]{2,1,0:T(8,128)S(1)}, f32[2,8,128]{2,1,0:T(8,128)S(1)}, u32[]{:S(2)}, u32[]{:S(2)}) collective-permute-start(f32[2,8,128]{2,1,0:T(8,128)S(1)} %get-tuple-element.36), channel_id=1, source_target_pairs={{0,9},{1,10},{2,11},{3,8},{4,13},{5,14},{6,15},{7,12},{8,17},{9,18... | collective-permute-start | bytes 24584 | tf_op jit(solution)/shard_map/ppermute | solution.py:30

commit v7 on v5

--- a/solution.py
+++ b/solution.py
@@ -85,7 +85,18 @@
     return at
 
 
-def iteration(start, feed, kill, old_rates):
+def inner_rows(n_y, tile_first):
+    low, high = max(tile_first + 1, -RATE_HALO), tile_first + n_y - 1
+    return [(low + k, high - k) for k in (0, 0, 1, 1, 2)]
+
+
+def iteration(start, feed, kill, old_rates, inner=()):
+    inner = iter(inner)
+
+    def known_or(values):
+        low, high, known = next(inner, (0, 0, None))
+        return lambda r: (known if low <= r < high else values)(r)
+
     feed_kill = functools.cache(lambda r: feed(r) + kill(r))
     coarse_feed = functools.cache(lambda c: half_sum(feed(2 * c), feed(2 * c + 1)))
     coarse_sum = functools.cache(lambda c: half_sum(feed_kill(2 * c), feed_kill(2 * c + 1)))
@@ -104,11 +115,11 @@
 
     fine = lambda state: rates_of(state, feed, feed_kill, 1.0)
     coarse = lambda state: rates_of(state, coarse_feed, coarse_sum, 2.0)
-    rate_zero = fine(start)
-    node_one = stepped(start, rate_zero, 0)
-    rate_one = fine(node_one)
-    node_two = stepped(node_one, rate_one, 1)
-    rate_two = fine(node_two)
+    rate_zero = known_or(fine(start))
+    node_one = known_or(stepped(start, rate_zero, 0))
+    rate_one = known_or(fine(node_one))
+    node_two = known_or(stepped(node_one, rate_one, 1))
+    rate_two = known_or(fine(node_two))
     fresh = (rate_zero, rate_one, rate_two)
     rest_zero, rest_one, rest_two = restricted(start), restricted(node_one), restricted(node_two)
     rest_integral = [restricted(quadrature(fresh, interval)) for interval in (0, 1)]
@@ -135,7 +146,8 @@
 
         return at
 
-    return rate_zero, corrected(node_one, coarse_one, rest_one), corrected(node_two, coarse_two, rest_two)
+    nodes = corrected(node_one, coarse_one, rest_one), corrected(node_two, coarse_two, rest_two)
+    return (rate_zero, *nodes), (rate_zero, node_one, rate_one, node_two, rate_two)
 
 
 def rows_of(ref, width, first):
@@ -177,7 +189,7 @@
         collect(params_ref, field, 2 + field, n_x, -TAKE, [(-BELOW, lows, BELOW), (0, [local_ref, *others], n_y)])
     start = rows_of(start_ref, width, -HALO)
     params = rows_of(params_ref, width, -HALO)
-    results = iteration(start, lambda r: params(r)[0], lambda r: params(r)[1], None)
+    results, _ = iteration(start, lambda r: params(r)[0], lambda r: params(r)[1], None)
     write_nodes(results, width, n_y, [(0, TAKE)], *outs)
     for r in range(HALO):
         for field, value in enumerate((*start(r + DRIFT), *params(r + DRIFT))):
@@ -227,7 +239,7 @@
     )
 
 
-def later_iteration(width, n_y, is_first, kept, params, got, old_zero, ones, twos):
+def later_iteration(is_first, kept, params, got, old_zero, ones, twos, inner=()):
     feed, kill = (lambda r: params(r)[0]), (lambda r: params(r)[1])
     feed_kill = functools.cache(lambda r: feed(r) + kill(r))
 
@@ -240,11 +252,29 @@
         rates_of(ones, feed, feed_kill, 1.0),
         rates_of(twos, feed, feed_kill, 1.0),
     )
-    return iteration(start, feed, kill, old_rates)
+    return iteration(start, feed, kill, old_rates, inner)
+
+
+def inner_kernel(width, n_y, tile_first, first_ref, start_ref, params_ref, zero_ref, one_ref, two_ref, got_ref, *outs):
+    kept, params = rows_of(start_ref, width, -TAKE), rows_of(params_ref, width, -TAKE)
+    old_zero = rows_of(zero_ref, width, tile_first - RATE_HALO)
+    ones, twos, got = (rows_of(ref, width, tile_first) for ref in (one_ref, two_ref, got_ref))
+    _, values = later_iteration(first_ref[0] == 1, kept, params, got, lambda feed, feed_kill: old_zero, ones, twos)
+    ranges = inner_rows(n_y, tile_first)
+    for r in range(ranges[0][0], ranges[0][1] + 2):
+        for k, (low, high), rows, ref in zip((0, 0, 1, 1, 2), ranges, values, outs):
+            if low <= r - k < high:
+                for field, value in enumerate(rows(r - k)):
+                    ref[field, pl.ds((r - k - low) * width, width), :] = value
+
+
+def inner_of(refs, width, n_y, tile_first):
+    return [(low, high, rows_of(ref, width, low)) for (low, high), ref in zip(inner_rows(n_y, tile_first), refs)]
 
 
 def second_kernel(width, n_y, first_ref, start_ref, params_ref, *refs):
-    zero_ref, one_ref, two_ref, got_ref, got_edge, pair_edge, *outs = refs
+    zero_ref, one_ref, two_ref, got_ref, got_edge, pair_edge, *outs = refs[5:]
+    inner = inner_of(refs, width, n_y, -DRIFT)
     kept, params = known(width, n_y, start_ref, params_ref, pair_edge)
     end = n_y - DRIFT
 
@@ -260,12 +290,13 @@
 
     ones, twos = moved(one_ref, pair(0)), moved(two_ref, pair(2))
     got = moved(got_ref, rows_of(got_edge, width, end))
-    results = later_iteration(width, n_y, first_ref[0] == 1, kept, params, got, old_zero, ones, twos)
+    results, _ = later_iteration(first_ref[0] == 1, kept, params, got, old_zero, ones, twos, inner)
     write_nodes(results, width, n_y, [(0, HALO), (n_y - HALO, HALO)], *outs)
 
 
 def later_kernel(width, n_y, out_x, first_ref, start_ref, params_ref, known_ref, *refs):
-    zero_ref, one_ref, two_ref, got_ref, got_low, got_high, pair_low, pair_high, *outs = refs
+    zero_ref, one_ref, two_ref, got_ref, got_low, got_high, pair_low, pair_high, *outs = refs[5:]
+    inner = inner_of(refs, width, n_y, 0)
     kept, params = known(width, n_y, start_ref, params_ref, known_ref)
 
     def window(low, tile_ref, high):
@@ -280,8 +311,8 @@
     ones, twos = pair(one_ref, 0), pair(two_ref, 2)
     old_zero = rows_of(zero_ref, width, -RATE_HALO)
     got = window(rows_of(got_low, width, -HALO), got_ref, rows_of(got_high, width, n_y))
-    results = later_iteration(
-        width, n_y, first_ref[0] == 1, kept, params, got, lambda feed, feed_kill: old_zero, ones, twos
+    results, _ = later_iteration(
+        first_ref[0] == 1, kept, params, got, lambda feed, feed_kill: old_zero, ones, twos, inner
     )
     if out_x is None:
         write_nodes(results, width, n_y, [(0, HALO), (n_y - HALO, HALO)], *outs)
@@ -341,11 +372,21 @@
     zero, one, two, two_edge, pair_edge = nodes
     got = [shifted(two, 1, 0, 0), shifted(two_edge, 1, 0, -1), shifted(pair_edge, 0, 0, -1)]
     known_edge = got[-1]
+
+    def inner(tile_first):
+        return call(
+            functools.partial(inner_kernel, width, n_y, tile_first),
+            "inner",
+            1,
+            (is_first, start, params, *nodes[:3], got[0]),
+            [(2, (high - low) * width, n_z) for low, high in inner_rows(n_y, tile_first)],
+        )
+
     nodes = call(
         functools.partial(second_kernel, width, n_y),
         "second",
         1,
-        (is_first, start, params, zero, one, two, *got),
+        (is_first, start, params, *inner(-DRIFT), zero, one, two, *got),
         [*nodes_only, *edge(HALO), *edge(HALO)],
     )
     for sweep_index in range(2, ITERS):
@@ -357,7 +398,7 @@
             functools.partial(later_kernel, width, n_y, n_x if done else None),
             "last" if done else "later",
             1,
-            (is_first, start, params, known_edge, zero, one, two, *got),
+            (is_first, start, params, known_edge, *inner(0), zero, one, two, *got),
             [initial_state.shape] if done else [*nodes_only, *edge(HALO), *edge(HALO)],
             [pltpu.VMEM(tile, jnp.float32)] if done else (),
         )

time: 40 us -> 38.3 us (0.957)
  waiting for transfers between devices: 14.7 us -> 13.7 us
  Pallas kernels: 5.76 us -> 5.22 us
    ppermute x12, waiting for transfers between devices: 14.7 us -> 13.7 us  [shifted(): return lax.ppermute(value, AXES, pairs)]
    pallas_call x4 -> x6, Pallas kernels: 5.76 us -> 5.22 us  [call(): pl.pallas_call(kernel, name=name, out_shape=[jax.ShapeDtypeStruct(shape,...]
  transfers between devices with their start and end apart: 12 -> 12, of which waited for: 5 -> 6; matrix products, arithmetic and copies ran while one was open for 0% -> 0% of each run, Pallas kernels for 0% -> 3%
where the time goes in v7:
time: 38.3 us; the launch traced here: 38.2 us
  starting transfers between devices  18.3 us (48%)
  waiting for transfers between devices  13.7 us (36%)
  Pallas kernels  5.22 us (14%)
  other arithmetic  0.87 us (2%)
    ppermute x12, starting transfers between devices, shifted(): return lax.ppermute(value, AXES, pairs)  18.3 us
    ppermute x12, waiting for transfers between devices, shifted(): return lax.ppermute(value, AXES, pairs)  13.7 us
    pallas_call x6, Pallas kernels, call(): pl.pallas_call(kernel, name=name, out_shape=[jax.ShapeDtypeStruct(shape,...  5.22 us
    select_n x1, other arithmetic, shards(): sent = jnp.where(place == n_tm - 1, initial_state, slice_guess[0])  0.86 us
  transfers between devices with their start and end apart: 12, of which 6 were waited for; matrix products, arithmetic and copies ran while one was open for 0% of the time, Pallas kernels for 3%

profile of v7, /device:TPU:0, one launch (start us, length us, event | category | flops | bytes accessed | tf_op | source)
XLA Modules:
  0.0 38.2 jit_solution(7947682927896048229)
XLA Ops:
  0.0 0.0 copy-start
  0.0 0.0 copy-start.1
  0.0 0.9 %bitcast_select_fusion = f32[2,4,16,128]{3,2,1,0:T(8,128)S(1)} fusion(f32[2,4,16,128]{3,2,1,0:T(8,128)} %param.4, f32[1,2,4,16,128]{4,3,2,1,0:T(8,128)} %param.5, pred[]{:T(512)S(6)} %eq.7), kind=kLoop, calls=%fused_computation.1 | loop fusion | flops 16384 | bytes 196609 | tf_op jit(solution)/shard_map/jit(_where)/select_n | solution.py:350
  0.9 0.0 copy-done
  0.9 0.0 copy-done.1
  0.9 2.5 %collective-permute-start.1 = (f32[4,64,128]{2,1,0:T(8,128)S(1)}, f32[4,64,128]{2,1,0:T(8,128)S(1)}, u32[]{:S(2)}, u32[]{:S(2)}) collective-permute-start(f32[4,64,128]{2,1,0:T(8,128)S(1)} %get-tuple-element.33.refs_1_), channel_id=1, source_target_pairs={{0,12},{1,13},{2,14},{3,15},{4,8},{5,9},{6,10},{7,11},{8,20},{9,21... | collective-permute-start | bytes 393224 | tf_op jit(solution)/shard_map/ppermute | solution.py:32
  3.4 2.7 %collective-permute-start.3 = (f32[4,48,128]{2,1,0:T(8,128)S(1)}, f32[4,48,128]{2,1,0:T(8,128)S(1)}, u32[]{:S(2)}, u32[]{:S(2)}) collective-permute-start(f32[4,48,128]{2,1,0:T(8,128)S(1)} %get-tuple-element.34), channel_id=1, source_target_pairs={{0,13},{1,14},{2,15},{3,12},{4,9},{5,10},{6,11},{7,8},{8,21},{9,22... | collective-permute-start | bytes 294920 | tf_op jit(solution)/shard_map/ppermute | solution.py:32
  6.1 1.1 %collective-permute-start.2 = (f32[4,48,128]{2,1,0:T(8,128)S(1)}, f32[4,48,128]{2,1,0:T(8,128)S(1)}, u32[]{:S(2)}, u32[]{:S(2)}) collective-permute-start(f32[4,48,128]{2,1,0:T(8,128)S(1)} %get-tuple-element.34), channel_id=1, source_target_pairs={{0,9},{1,10},{2,11},{3,8},{4,13},{5,14},{6,15},{7,12},{8,17},{9,18... | collective-permute-start | bytes 294920 | tf_op jit(solution)/shard_map/ppermute | solution.py:32
  7.3 0.5 %collective-permute-start = (f32[2,64,128]{2,1,0:T(8,128)S(1)}, f32[2,64,128]{2,1,0:T(8,128)S(1)}, u32[]{:S(2)}, u32[]{:S(2)}) collective-permute-start(f32[2,64,128]{2,1,0:T(8,128)S(1)} %get-tuple-element.32), channel_id=1, source_target_pairs={{0,8},{1,9},{2,10},{3,11},{4,12},{5,13},{6,14},{7,15},{8,16},{9,17... | collective-permute-start | bytes 196616 | tf_op jit(solution)/shard_map/ppermute | solution.py:32
  7.8 3.8 %collective-permute-done.refs_0_ = f32[2,64,128]{2,1,0:T(8,128)S(1)} collective-permute-done((f32[2,64,128]{2,1,0:T(8,128)S(1)}, f32[2,64,128]{2,1,0:T(8,128)S(1)}, u32[]{:S(2)}, u32[]{:S(2)}) %collective-permute-start) | collective-permute-done | bytes 65568 | tf_op jit(solution)/shard_map/ppermute | solution.py:32
  11.6 0.0 collective-permute-done.3.refs_4_
  11.6 2.1 %collective-permute-done.2.refs_3_ = f32[4,48,128]{2,1,0:T(8,128)S(1)} collective-permute-done((f32[4,48,128]{2,1,0:T(8,128)S(1)}, f32[4,48,128]{2,1,0:T(8,128)S(1)}, u32[]{:S(2)}, u32[]{:S(2)}) %collective-permute-start.2) | collective-permute-done | bytes 98336 | tf_op jit(solution)/shard_map/ppermute | solution.py:32
  13.6 0.0 collective-permute-done.1.refs_2_
  13.6 1.2 %first.1 = (f32[2,216,128]{2,1,0:T(8,128)S(1)}, f32[2,216,128]{2,1,0:T(8,128)S(1)}, f32[2,192,128]{2,1,0:T(8,128)S(1)}, f32[2,128,128]{2,1,0:T(8,128)S(1)}, f32[...) custom-call(f32[2,64,128]{2,1,0:T(8,128)S(1)} %collective-permute-done.refs_0_, ...), custom_call_target="tpu_custom_call" | custom-call | tf_op jit(solution)/shard_map/first/pallas_call | solution.py:332
  14.9 0.9 %collective-permute-start.4 = (f32[512,128]{1,0:T(8,128)S(1)}, f32[512,128]{1,0:T(8,128)S(1)}, u32[]{:S(2)}, u32[]{:S(2)}) collective-permute-start(f32[512,128]{1,0:T(8,128)S(1)} %get-tuple-element.37), channel_id=1, source_target_pairs={{0,3},{1,0},{2,1},{3,2},{4,7},{5,4},{6,5},{7,6},{8,11},{9,8},{10,9... | collective-permute-start | bytes 786440 | tf_op jit(solution)/shard_map/ppermute | solution.py:32
  15.7 0.3 collective-permute-start.5
  16.0 1.7 %collective-permute-start.6 = (f32[2,88,128]{2,1,0:T(8,128)S(1)}, f32[2,88,128]{2,1,0:T(8,128)S(1)}, u32[]{:S(2)}, u32[]{:S(2)}) collective-permute-start(f32[2,88,128]{2,1,0:T(8,128)S(1)} %get-tuple-element.46), channel_id=1, source_target_pairs={{0,11},{1,8},{2,9},{3,10},{4,15},{5,12},{6,13},{7,14},{8,19},{9,16... | collective-permute-start | bytes 270344 | tf_op jit(solution)/shard_map/ppermute | solution.py:32
  17.7 2.4 %collective-permute-done.5.got_ref.refs_8_ = f32[2,128,128]{2,1,0:T(8,128)S(1)} collective-permute-done((f32[2,128,128]{2,1,0:T(8,128)S(1)}, f32[2,128,128]{2,1,0:T(8,128)S(1)}, u32[]{:S(2)}, u32[]{:S(2)}) %collective-permute-start.5) | collective-permute-done | bytes 131104 | tf_op jit(solution)/shard_map/ppermute | solution.py:32
  20.1 0.5 %inner.2 = (f32[2,104,128]{2,1,0:T(8,128)S(1)}, f32[2,104,128]{2,1,0:T(8,128)S(1)}, f32[2,88,128]{2,1,0:T(8,128)S(1)}, f32[2,88,128]{2,1,0:T(8,128)S(1)}, f32[2,72,128]{2,1,0:T(8,128)S(1)}) custom-call(s32[1]{0:T(128)} %bitcast.first_ref, f32[2,216,128]{2,1,0:T(8,128)S(1)} %get-tuple-element.35.start_ref, f32[2,216,128]{2,1,0:T(8,128)S(1)} %get-tuple-element.36.params_ref, ...), custom_call_target="tpu_custom_call" | custom-call | tf_op jit(solution)/shard_map/inner/pallas_call | solution.py:332
  20.7 3.3 %collective-permute-done.6.refs_9_ = f32[2,88,128]{2,1,0:T(8,128)S(1)} collective-permute-done((f32[2,88,128]{2,1,0:T(8,128)S(1)}, f32[2,88,128]{2,1,0:T(8,128)S(1)}, u32[]{:S(2)}, u32[]{:S(2)}) %collective-permute-start.6) | collective-permute-done | bytes 90144 | tf_op jit(solution)/shard_map/ppermute | solution.py:32
  24.0 0.1 collective-permute-done.4.refs_10_.known_ref
  24.1 1.2 %second.1 = (f32[2,192,128]{2,1,0:T(8,128)S(1)}, f32[2,128,128]{2,1,0:T(8,128)S(1)}, f32[2,128,128]{2,1,0:T(8,128)S(1)}, f32[2,40,128]{2,1,0:T(8,128)S(1)}, f32[...) custom-call(s32[1]{0:T(128)} %bitcast.first_ref, ...), custom_call_target="tpu_custom_call" | custom-call | tf_op jit(solution)/shard_map/second/pallas_call | solution.py:332
  25.2 1.0 %collective-permute-start.7 = (f32[2,128,128]{2,1,0:T(8,128)S(1)}, f32[2,128,128]{2,1,0:T(8,128)S(1)}, u32[]{:S(2)}, u32[]{:S(2)}) collective-permute-start(f32[2,128,128]{2,1,0:T(8,128)S(1)} %get-tuple-element.49.two_ref.refs_7_), channel_id=1, source_target_pairs={{0,8},{1,9},{2,10},{3,11},{4,12},{5,13},{6,14},{7,15},{8,16},{9,17... | collective-permute-start | bytes 393224 | tf_op jit(solution)/shard_map/ppermute | solution.py:32
  26.2 0.0 collective-permute-start.10
  26.2 3.8 %collective-permute-start.11 = (f32[160,128]{1,0:T(8,128)S(1)}, f32[160,128]{1,0:T(8,128)S(1)}, u32[]{:S(2)}, u32[]{:S(2)}) collective-permute-start(f32[160,128]{1,0:T(8,128)S(1)} %get-tuple-element.58), channel_id=1, source_target_pairs={{0,3},{1,0},{2,1},{3,2},{4,7},{5,4},{6,5},{7,6},{8,11},{9,8},{10,9... | collective-permute-start | bytes 245768 | tf_op jit(solution)/shard_map/ppermute | solution.py:32
  30.0 0.0 collective-permute-start.8
  30.1 3.9 %collective-permute-start.9 = (f32[2,40,128]{2,1,0:T(8,128)S(1)}, f32[2,40,128]{2,1,0:T(8,128)S(1)}, u32[]{:S(2)}, u32[]{:S(2)}) collective-permute-start(f32[2,40,128]{2,1,0:T(8,128)S(1)} %get-tuple-element.56), channel_id=1, source_target_pairs={{0,11},{1,8},{2,9},{3,10},{4,15},{5,12},{6,13},{7,14},{8,19},{9,16... | collective-permute-start | bytes 122888 | tf_op jit(solution)/shard_map/ppermute | solution.py:32
  33.9 0.0 collective-permute-done.7.got_ref.refs_8_
  33.9 0.6 %inner.3 = (f32[2,112,128]{2,1,0:T(8,128)S(1)}, f32[2,112,128]{2,1,0:T(8,128)S(1)}, f32[2,96,128]{2,1,0:T(8,128)S(1)}, f32[2,96,128]{2,1,0:T(8,128)S(1)}, f32[2,80,128]{2,1,0:T(8,128)S(1)}) custom-call(s32[1]{0:T(128)} %bitcast.first_ref, f32[2,216,128]{2,1,0:T(8,128)S(1)} %get-tuple-element.35.start_ref, f32[2,216,128]{2,1,0:T(8,128)S(1)} %get-tuple-element.36.params_ref, ...), custom_call_target="tpu_custom_call" | custom-call | tf_op jit(solution)/shard_map/inner/pallas_call | solution.py:332
  34.5 2.0 %collective-permute-done.8.refs_9_ = f32[2,40,128]{2,1,0:T(8,128)S(1)} collective-permute-done((f32[2,40,128]{2,1,0:T(8,128)S(1)}, f32[2,40,128]{2,1,0:T(8,128)S(1)}, u32[]{:S(2)}, u32[]{:S(2)}) %collective-permute-start.8) | collective-permute-done | bytes 40992 | tf_op jit(solution)/shard_map/ppermute | solution.py:32
  36.4 0.0 collective-permute-done.9.refs_10_
  36.4 0.0 collective-permute-done.10.refs_11_
  36.4 0.0 collective-permute-done.11.refs_12_
  36.4 1.8 %last.1 = f32[2,4,16,128]{3,2,1,0:T(8,128)} custom-call(s32[1]{0:T(128)} %bitcast.first_ref, f32[2,216,128]{2,1,0:T(8,128)S(1)} %get-tuple-element.35.start_ref, f32[2,216,128]{2,1,0:T(8,128)S(1)} %get-tuple-element.36.params_ref, f32[512,128]{1,0:T(8,128)S(1)} %collective-permute-done.4.refs_10_.known_ref, f32[2,112,128]{2,1,0:T(8,128)S(1)} %get-tuple-element.50.refs_0_, ...), custom_call_target="tpu_custom_call" | custom-call | tf_op jit(solution)/shard_map/last/pallas_call | solution.py:332
  (2 shorter events, 0.0 us)
Async XLA Ops:
  0.0 0.9 %copy-start = (f32[4,16,128]{2,1,0:T(8,128)S(1)}, f32[4,16,128]{2,1,0:T(8,128)}, u32[]{:S(2)}) copy-start(f32[4,16,128]{2,1,0:T(8,128)} %param.7) | copy-start | bytes 98308
  0.0 0.9 %copy-start.1 = (f32[4,16,128]{2,1,0:T(8,128)S(1)}, f32[4,16,128]{2,1,0:T(8,128)}, u32[]{:S(2)}) copy-start(f32[4,16,128]{2,1,0:T(8,128)} %param.6) | copy-start | bytes 98308
  0.9 12.7 %collective-permute-start.1 = (f32[4,64,128]{2,1,0:T(8,128)S(1)}, f32[4,64,128]{2,1,0:T(8,128)S(1)}, u32[]{:S(2)}, u32[]{:S(2)}) collective-permute-start(f32[4,64,128]{2,1,0:T(8,128)S(1)} %get-tuple-element.33.refs_1_), channel_id=1, source_target_pairs={{0,12},{1,13},{2,14},{3,15},{4,8},{5,9},{6,10},{7,11},{8,20},{9,21... | collective-permute-start | bytes 393224 | tf_op jit(solution)/shard_map/ppermute | solution.py:32
  3.4 8.2 %collective-permute-start.3 = (f32[4,48,128]{2,1,0:T(8,128)S(1)}, f32[4,48,128]{2,1,0:T(8,128)S(1)}, u32[]{:S(2)}, u32[]{:S(2)}) collective-permute-start(f32[4,48,128]{2,1,0:T(8,128)S(1)} %get-tuple-element.34), channel_id=1, source_target_pairs={{0,13},{1,14},{2,15},{3,12},{4,9},{5,10},{6,11},{7,8},{8,21},{9,22... | collective-permute-start | bytes 294920 | tf_op jit(solution)/shard_map/ppermute | solution.py:32
  6.1 7.5 %collective-permute-start.2 = (f32[4,48,128]{2,1,0:T(8,128)S(1)}, f32[4,48,128]{2,1,0:T(8,128)S(1)}, u32[]{:S(2)}, u32[]{:S(2)}) collective-permute-start(f32[4,48,128]{2,1,0:T(8,128)S(1)} %get-tuple-element.34), channel_id=1, source_target_pairs={{0,9},{1,10},{2,11},{3,8},{4,13},{5,14},{6,15},{7,12},{8,17},{9,18... | collective-permute-start | bytes 294920 | tf_op jit(solution)/shard_map/ppermute | solution.py:32
  7.3 4.3 %collective-permute-start = (f32[2,64,128]{2,1,0:T(8,128)S(1)}, f32[2,64,128]{2,1,0:T(8,128)S(1)}, u32[]{:S(2)}, u32[]{:S(2)}) collective-permute-start(f32[2,64,128]{2,1,0:T(8,128)S(1)} %get-tuple-element.32), channel_id=1, source_target_pairs={{0,8},{1,9},{2,10},{3,11},{4,12},{5,13},{6,14},{7,15},{8,16},{9,17... | collective-permute-start | bytes 196616 | tf_op jit(solution)/shard_map/ppermute | solution.py:32
  14.9 9.2 %collective-permute-start.4 = (f32[512,128]{1,0:T(8,128)S(1)}, f32[512,128]{1,0:T(8,128)S(1)}, u32[]{:S(2)}, u32[]{:S(2)}) collective-permute-start(f32[512,128]{1,0:T(8,128)S(1)} %get-tuple-element.37), channel_id=1, source_target_pairs={{0,3},{1,0},{2,1},{3,2},{4,7},{5,4},{6,5},{7,6},{8,11},{9,8},{10,9... | collective-permute-start | bytes 786440 | tf_op jit(solution)/shard_map/ppermute | solution.py:32
  15.7 4.4 %collective-permute-start.5 = (f32[2,128,128]{2,1,0:T(8,128)S(1)}, f32[2,128,128]{2,1,0:T(8,128)S(1)}, u32[]{:S(2)}, u32[]{:S(2)}) collective-permute-start(f32[2,128,128]{2,1,0:T(8,128)S(1)} %get-tuple-element.40.two_ref.refs_7_), channel_id=1, source_target_pairs={{0,8},{1,9},{2,10},{3,11},{4,12},{5,13},{6,14},{7,15},{8,16},{9,17... | collective-permute-start | bytes 393224 | tf_op jit(solution)/shard_map/ppermute | solution.py:32
  16.0 7.9 %collective-permute-start.6 = (f32[2,88,128]{2,1,0:T(8,128)S(1)}, f32[2,88,128]{2,1,0:T(8,128)S(1)}, u32[]{:S(2)}, u32[]{:S(2)}) collective-permute-start(f32[2,88,128]{2,1,0:T(8,128)S(1)} %get-tuple-element.46), channel_id=1, source_target_pairs={{0,11},{1,8},{2,9},{3,10},{4,15},{5,12},{6,13},{7,14},{8,19},{9,16... | collective-permute-start | bytes 270344 | tf_op jit(solution)/shard_map/ppermute | solution.py:32
  25.2 8.7 %collective-permute-start.7 = (f32[2,128,128]{2,1,0:T(8,128)S(1)}, f32[2,128,128]{2,1,0:T(8,128)S(1)}, u32[]{:S(2)}, u32[]{:S(2)}) collective-permute-start(f32[2,128,128]{2,1,0:T(8,128)S(1)} %get-tuple-element.49.two_ref.refs_7_), channel_id=1, source_target_pairs={{0,8},{1,9},{2,10},{3,11},{4,12},{5,13},{6,14},{7,15},{8,16},{9,17... | collective-permute-start | bytes 393224 | tf_op jit(solution)/shard_map/ppermute | solution.py:32
  26.2 10.2 %collective-permute-start.10 = (f32[160,128]{1,0:T(8,128)S(1)}, f32[160,128]{1,0:T(8,128)S(1)}, u32[]{:S(2)}, u32[]{:S(2)}) collective-permute-start(f32[160,128]{1,0:T(8,128)S(1)} %get-tuple-element.57), channel_id=1, source_target_pairs={{0,1},{1,2},{2,3},{3,0},{4,5},{5,6},{6,7},{7,4},{8,9},{9,10},{10,1... | collective-permute-start | bytes 245768 | tf_op jit(solution)/shard_map/ppermute | solution.py:32
  26.2 10.2 %collective-permute-start.11 = (f32[160,128]{1,0:T(8,128)S(1)}, f32[160,128]{1,0:T(8,128)S(1)}, u32[]{:S(2)}, u32[]{:S(2)}) collective-permute-start(f32[160,128]{1,0:T(8,128)S(1)} %get-tuple-element.58), channel_id=1, source_target_pairs={{0,3},{1,0},{2,1},{3,2},{4,7},{5,4},{6,5},{7,6},{8,11},{9,8},{10,9... | collective-permute-start | bytes 245768 | tf_op jit(solution)/shard_map/ppermute | solution.py:32
  30.0 6.4 %collective-permute-start.8 = (f32[2,40,128]{2,1,0:T(8,128)S(1)}, f32[2,40,128]{2,1,0:T(8,128)S(1)}, u32[]{:S(2)}, u32[]{:S(2)}) collective-permute-start(f32[2,40,128]{2,1,0:T(8,128)S(1)} %get-tuple-element.55), channel_id=1, source_target_pairs={{0,9},{1,10},{2,11},{3,8},{4,13},{5,14},{6,15},{7,12},{8,17},{9,18... | collective-permute-start | bytes 122888 | tf_op jit(solution)/shard_map/ppermute | solution.py:32
  30.1 6.4 %collective-permute-start.9 = (f32[2,40,128]{2,1,0:T(8,128)S(1)}, f32[2,40,128]{2,1,0:T(8,128)S(1)}, u32[]{:S(2)}, u32[]{:S(2)}) collective-permute-start(f32[2,40,128]{2,1,0:T(8,128)S(1)} %get-tuple-element.56), channel_id=1, source_target_pairs={{0,11},{1,8},{2,9},{3,10},{4,15},{5,12},{6,13},{7,14},{8,19},{9,16... | collective-permute-start | bytes 122888 | tf_op jit(solution)/shard_map/ppermute | solution.py:32

commit v8 on v7

--- a/solution.py
+++ b/solution.py
@@ -86,8 +86,25 @@
 
 
 def inner_rows(n_y, tile_first):
-    low, high = max(tile_first + 1, -RATE_HALO), tile_first + n_y - 1
+    low, high = max(tile_first + 1, -RATE_HALO), min(tile_first + n_y - 1, n_y + RATE_HALO)
     return [(low + k, high - k) for k in (0, 0, 1, 1, 2)]
+
+
+def inner_shapes(width, n_y, n_z, tile_first):
+    return [(2, (high - low) * width, n_z) for low, high in inner_rows(n_y, tile_first)]
+
+
+def inner_of(refs, width, n_y, tile_first):
+    return [(low, high, rows_of(ref, width, low)) for (low, high), ref in zip(inner_rows(n_y, tile_first), refs)]
+
+
+def write_inner(values, width, n_y, tile_first, refs):
+    ranges = inner_rows(n_y, tile_first)
+    for r in range(ranges[0][0], ranges[0][1] + 2):
+        for k, (low, high), rows, ref in zip((0, 0, 1, 1, 2), ranges, values, refs):
+            if low <= r - k < high:
+                for field, value in enumerate(rows(r - k)):
+                    ref[field, pl.ds((r - k - low) * width, width), :] = value
 
 
 def iteration(start, feed, kill, old_rates, inner=()):
@@ -179,17 +196,31 @@
                     out_ref[field, place, :] = ref[source_field, pl.ds(k * n_x, n_x), :]
 
 
-def first_kernel(n_gy, n_x, n_y, *refs):
+def first_inner_kernel(n_gy, n_x, n_y, *refs):
     state_ref, local_ref = refs[:2]
-    others, lows = refs[2 : 1 + n_gy], refs[1 + n_gy : 1 + 2 * n_gy]
-    start_ref, params_ref, *outs = refs[1 + 2 * n_gy :]
+    others = refs[2 : 1 + n_gy]
+    start_ref, params_ref, *outs = refs[1 + n_gy :]
     width = n_gy * n_x
     for field in range(2):
-        collect(start_ref, field, field, n_x, -TAKE, [(-BELOW, lows, BELOW), (0, [state_ref, *others], n_y)])
-        collect(params_ref, field, 2 + field, n_x, -TAKE, [(-BELOW, lows, BELOW), (0, [local_ref, *others], n_y)])
+        collect(start_ref, field, field, n_x, 0, [(0, [state_ref, *others], n_y)])
+        collect(params_ref, field, 2 + field, n_x, 0, [(0, [local_ref, *others], n_y)])
+    start, params = rows_of(start_ref, width, DRIFT), rows_of(params_ref, width, DRIFT)
+    _, values = iteration(start, lambda r: params(r)[0], lambda r: params(r)[1], None)
+    write_inner(values, width, n_y, DRIFT, outs)
+
+
+def first_kernel(n_gy, n_x, n_y, *refs):
+    tiles, inner_refs, lows = refs[:2], refs[2:7], refs[7 : 7 + n_gy]
+    start_ref, params_ref, *outs = refs[7 + n_gy :]
+    width = n_gy * n_x
+    for field in range(2):
+        for out_ref, tile_ref, place in zip((start_ref, params_ref), tiles, (0, 2)):
+            collect(out_ref, field, place + field, n_x, -TAKE, [(-BELOW, lows, BELOW)])
+            out_ref[field, pl.ds(TAKE * width, n_y * width), :] = tile_ref[field]
     start = rows_of(start_ref, width, -HALO)
     params = rows_of(params_ref, width, -HALO)
-    results, _ = iteration(start, lambda r: params(r)[0], lambda r: params(r)[1], None)
+    inner = inner_of(inner_refs, width, n_y, DRIFT)
+    results, _ = iteration(start, lambda r: params(r)[0], lambda r: params(r)[1], None, inner)
     write_nodes(results, width, n_y, [(0, TAKE)], *outs)
     for r in range(HALO):
         for field, value in enumerate((*start(r + DRIFT), *params(r + DRIFT))):
@@ -260,16 +291,7 @@
     old_zero = rows_of(zero_ref, width, tile_first - RATE_HALO)
     ones, twos, got = (rows_of(ref, width, tile_first) for ref in (one_ref, two_ref, got_ref))
     _, values = later_iteration(first_ref[0] == 1, kept, params, got, lambda feed, feed_kill: old_zero, ones, twos)
-    ranges = inner_rows(n_y, tile_first)
-    for r in range(ranges[0][0], ranges[0][1] + 2):
-        for k, (low, high), rows, ref in zip((0, 0, 1, 1, 2), ranges, values, outs):
-            if low <= r - k < high:
-                for field, value in enumerate(rows(r - k)):
-                    ref[field, pl.ds((r - k - low) * width, width), :] = value
-
-
-def inner_of(refs, width, n_y, tile_first):
-    return [(low, high, rows_of(ref, width, low)) for (low, high), ref in zip(inner_rows(n_y, tile_first), refs)]
+    write_inner(values, width, n_y, tile_first, outs)
 
 
 def second_kernel(width, n_y, first_ref, start_ref, params_ref, *refs):
@@ -357,16 +379,23 @@
     )
     got = [shifted(state, 1, 0, 0), local]
     got += [shifted(local, 1, -gy, 0) for gy in range(1, n_gy)]
-    got += [shifted(high, 1, -gy, 1) for gy in range(n_gy)]
+    below = [shifted(high, 1, -gy, 1) for gy in range(n_gy)]
 
     tile, window = (2, n_y * width, n_z), (2, (TAKE + n_y) * width, n_z)
     nodes_only = [(2, (n_y + 2 * RATE_HALO) * width, n_z), tile, tile]
     edge = lambda rows, more=0: [(2, rows * width, n_z), ((4 * rows + more) * width, n_z)]
+    inner_first = call(
+        functools.partial(first_inner_kernel, n_gy, n_x, n_y),
+        "inner_first",
+        0,
+        got,
+        [tile, tile, *inner_shapes(width, n_y, n_z, DRIFT)],
+    )
     start, params, *nodes = call(
         functools.partial(first_kernel, n_gy, n_x, n_y),
         "first",
         0,
-        got,
+        [*inner_first, *below],
         [window, window, *nodes_only, *edge(TAKE, 4 * HALO)],
     )
     zero, one, two, two_edge, pair_edge = nodes
@@ -379,7 +408,7 @@
             "inner",
             1,
             (is_first, start, params, *nodes[:3], got[0]),
-            [(2, (high - low) * width, n_z) for low, high in inner_rows(n_y, tile_first)],
+            inner_shapes(width, n_y, n_z, tile_first),
         )
 
     nodes = call(

time: 38.3 us -> 38 us (level)
  waiting for transfers between devices: 13.7 us -> 13.3 us
    pallas_call x6 -> x7, Pallas kernels: 5.22 us -> 5.18 us  [call(): pl.pallas_call(kernel, name=name, out_shape=[jax.ShapeDtypeStruct(shape,...]
  transfers between devices with their start and end apart: 12 -> 12, of which waited for: 6 -> 6; matrix products, arithmetic and copies ran while one was open for 0% -> 0% of each run, Pallas kernels for 3% -> 4%
where the time goes in v8:
time: 38 us; the launch traced here: 37.8 us
  starting transfers between devices  18.3 us (48%)
  waiting for transfers between devices  13.3 us (35%)
  Pallas kernels  5.18 us (14%)
  other arithmetic  0.87 us (2%)
    ppermute x12, starting transfers between devices, shifted(): return lax.ppermute(value, AXES, pairs)  18.3 us
    ppermute x12, waiting for transfers between devices, shifted(): return lax.ppermute(value, AXES, pairs)  13.3 us
    pallas_call x7, Pallas kernels, call(): pl.pallas_call(kernel, name=name, out_shape=[jax.ShapeDtypeStruct(shape,...  5.18 us
    select_n x1, other arithmetic, shards(): sent = jnp.where(place == n_tm - 1, initial_state, slice_guess[0])  0.86 us
  transfers between devices with their start and end apart: 12, of which 6 were waited for; matrix products, arithmetic and copies ran while one was open for 0% of the time, Pallas kernels for 4%

profile of v8, /device:TPU:0, one launch (start us, length us, event | category | flops | bytes accessed | tf_op | source)
XLA Modules:
  0.0 37.8 jit_solution(15301552765443344218)
XLA Ops:
  0.0 0.0 copy-start
  0.0 0.0 copy-start.1
  0.0 0.9 %bitcast_select_fusion = f32[2,4,16,128]{3,2,1,0:T(8,128)S(1)} fusion(f32[2,4,16,128]{3,2,1,0:T(8,128)} %param.4, f32[1,2,4,16,128]{4,3,2,1,0:T(8,128)} %param.5, pred[]{:T(512)S(6)} %eq.7), kind=kLoop, calls=%fused_computation.1 | loop fusion | flops 16384 | bytes 196609 | tf_op jit(solution)/shard_map/jit(_where)/select_n | solution.py:372
  0.9 0.0 copy-done
  0.9 0.0 copy-done.1
  0.9 2.5 %collective-permute-start.1 = (f32[4,64,128]{2,1,0:T(8,128)S(1)}, f32[4,64,128]{2,1,0:T(8,128)S(1)}, u32[]{:S(2)}, u32[]{:S(2)}) collective-permute-start(f32[4,64,128]{2,1,0:T(8,128)S(1)} %get-tuple-element.40.refs_1_), channel_id=1, source_target_pairs={{0,12},{1,13},{2,14},{3,15},{4,8},{5,9},{6,10},{7,11},{8,20},{9,21... | collective-permute-start | bytes 393224 | tf_op jit(solution)/shard_map/ppermute | solution.py:32
  3.4 2.7 %collective-permute-start.3 = (f32[4,48,128]{2,1,0:T(8,128)S(1)}, f32[4,48,128]{2,1,0:T(8,128)S(1)}, u32[]{:S(2)}, u32[]{:S(2)}) collective-permute-start(f32[4,48,128]{2,1,0:T(8,128)S(1)} %get-tuple-element.48), channel_id=1, source_target_pairs={{0,13},{1,14},{2,15},{3,12},{4,9},{5,10},{6,11},{7,8},{8,21},{9,22... | collective-permute-start | bytes 294920 | tf_op jit(solution)/shard_map/ppermute | solution.py:32
  6.1 1.1 %collective-permute-start.2 = (f32[4,48,128]{2,1,0:T(8,128)S(1)}, f32[4,48,128]{2,1,0:T(8,128)S(1)}, u32[]{:S(2)}, u32[]{:S(2)}) collective-permute-start(f32[4,48,128]{2,1,0:T(8,128)S(1)} %get-tuple-element.48), channel_id=1, source_target_pairs={{0,9},{1,10},{2,11},{3,8},{4,13},{5,14},{6,15},{7,12},{8,17},{9,18... | collective-permute-start | bytes 294920 | tf_op jit(solution)/shard_map/ppermute | solution.py:32
  7.3 0.5 %collective-permute-start = (f32[2,64,128]{2,1,0:T(8,128)S(1)}, f32[2,64,128]{2,1,0:T(8,128)S(1)}, u32[]{:S(2)}, u32[]{:S(2)}) collective-permute-start(f32[2,64,128]{2,1,0:T(8,128)S(1)} %get-tuple-element.39), channel_id=1, source_target_pairs={{0,8},{1,9},{2,10},{3,11},{4,12},{5,13},{6,14},{7,15},{8,16},{9,17... | collective-permute-start | bytes 196616 | tf_op jit(solution)/shard_map/ppermute | solution.py:32
  7.8 3.8 %collective-permute-done.refs_0_ = f32[2,64,128]{2,1,0:T(8,128)S(1)} collective-permute-done((f32[2,64,128]{2,1,0:T(8,128)S(1)}, f32[2,64,128]{2,1,0:T(8,128)S(1)}, u32[]{:S(2)}, u32[]{:S(2)}) %collective-permute-start) | collective-permute-done | bytes 65568 | tf_op jit(solution)/shard_map/ppermute | solution.py:32
  11.6 0.0 collective-permute-done.1.refs_2_
  11.6 0.3 inner_first.1
  11.9 0.0 collective-permute-done.3.refs_8_
  11.9 1.7 %collective-permute-done.2.refs_7_ = f32[4,48,128]{2,1,0:T(8,128)S(1)} collective-permute-done((f32[4,48,128]{2,1,0:T(8,128)S(1)}, f32[4,48,128]{2,1,0:T(8,128)S(1)}, u32[]{:S(2)}, u32[]{:S(2)}) %collective-permute-start.2) | collective-permute-done | bytes 98336 | tf_op jit(solution)/shard_map/ppermute | solution.py:32
  13.6 0.9 %first.1 = (f32[2,216,128]{2,1,0:T(8,128)S(1)}, f32[2,216,128]{2,1,0:T(8,128)S(1)}, f32[2,192,128]{2,1,0:T(8,128)S(1)}, f32[2,128,128]{2,1,0:T(8,128)S(1)}, f32[...) custom-call(f32[2,128,128]{2,1,0:T(8,128)S(1)} %get-tuple-element.41.refs_0_, ...), custom_call_target="tpu_custom_call" | custom-call | tf_op jit(solution)/shard_map/first/pallas_call | solution.py:354
  14.5 0.9 %collective-permute-start.4 = (f32[512,128]{1,0:T(8,128)S(1)}, f32[512,128]{1,0:T(8,128)S(1)}, u32[]{:S(2)}, u32[]{:S(2)}) collective-permute-start(f32[512,128]{1,0:T(8,128)S(1)} %get-tuple-element.51), channel_id=1, source_target_pairs={{0,3},{1,0},{2,1},{3,2},{4,7},{5,4},{6,5},{7,6},{8,11},{9,8},{10,9... | collective-permute-start | bytes 786440 | tf_op jit(solution)/shard_map/ppermute | solution.py:32
  15.4 0.3 collective-permute-start.5
  15.7 1.7 %collective-permute-start.6 = (f32[2,88,128]{2,1,0:T(8,128)S(1)}, f32[2,88,128]{2,1,0:T(8,128)S(1)}, u32[]{:S(2)}, u32[]{:S(2)}) collective-permute-start(f32[2,88,128]{2,1,0:T(8,128)S(1)} %get-tuple-element.60), channel_id=1, source_target_pairs={{0,11},{1,8},{2,9},{3,10},{4,15},{5,12},{6,13},{7,14},{8,19},{9,16... | collective-permute-start | bytes 270344 | tf_op jit(solution)/shard_map/ppermute | solution.py:32
  17.3 2.4 %collective-permute-done.5.got_ref.refs_8_ = f32[2,128,128]{2,1,0:T(8,128)S(1)} collective-permute-done((f32[2,128,128]{2,1,0:T(8,128)S(1)}, f32[2,128,128]{2,1,0:T(8,128)S(1)}, u32[]{:S(2)}, u32[]{:S(2)}) %collective-permute-start.5) | collective-permute-done | bytes 131104 | tf_op jit(solution)/shard_map/ppermute | solution.py:32
  19.8 0.5 %inner.2 = (f32[2,104,128]{2,1,0:T(8,128)S(1)}, f32[2,104,128]{2,1,0:T(8,128)S(1)}, f32[2,88,128]{2,1,0:T(8,128)S(1)}, f32[2,88,128]{2,1,0:T(8,128)S(1)}, f32[2,72,128]{2,1,0:T(8,128)S(1)}) custom-call(s32[1]{0:T(128)} %bitcast.first_ref, f32[2,216,128]{2,1,0:T(8,128)S(1)} %get-tuple-element.49.start_ref, f32[2,216,128]{2,1,0:T(8,128)S(1)} %get-tuple-element.50.params_ref, ...), custom_call_target="tpu_custom_call" | custom-call | tf_op jit(solution)/shard_map/inner/pallas_call | solution.py:354
  20.3 3.3 %collective-permute-done.6.refs_9_ = f32[2,88,128]{2,1,0:T(8,128)S(1)} collective-permute-done((f32[2,88,128]{2,1,0:T(8,128)S(1)}, f32[2,88,128]{2,1,0:T(8,128)S(1)}, u32[]{:S(2)}, u32[]{:S(2)}) %collective-permute-start.6) | collective-permute-done | bytes 90144 | tf_op jit(solution)/shard_map/ppermute | solution.py:32
  23.6 0.1 collective-permute-done.4.refs_10_.known_ref
  23.7 1.2 %second.1 = (f32[2,192,128]{2,1,0:T(8,128)S(1)}, f32[2,128,128]{2,1,0:T(8,128)S(1)}, f32[2,128,128]{2,1,0:T(8,128)S(1)}, f32[2,40,128]{2,1,0:T(8,128)S(1)}, f32[...) custom-call(s32[1]{0:T(128)} %bitcast.first_ref, ...), custom_call_target="tpu_custom_call" | custom-call | tf_op jit(solution)/shard_map/second/pallas_call | solution.py:354
  24.9 1.0 %collective-permute-start.7 = (f32[2,128,128]{2,1,0:T(8,128)S(1)}, f32[2,128,128]{2,1,0:T(8,128)S(1)}, u32[]{:S(2)}, u32[]{:S(2)}) collective-permute-start(f32[2,128,128]{2,1,0:T(8,128)S(1)} %get-tuple-element.63.two_ref.refs_7_), channel_id=1, source_target_pairs={{0,8},{1,9},{2,10},{3,11},{4,12},{5,13},{6,14},{7,15},{8,16},{9,17... | collective-permute-start | bytes 393224 | tf_op jit(solution)/shard_map/ppermute | solution.py:32
  25.9 0.0 collective-permute-start.10
  25.9 3.8 %collective-permute-start.11 = (f32[160,128]{1,0:T(8,128)S(1)}, f32[160,128]{1,0:T(8,128)S(1)}, u32[]{:S(2)}, u32[]{:S(2)}) collective-permute-start(f32[160,128]{1,0:T(8,128)S(1)} %get-tuple-element.72), channel_id=1, source_target_pairs={{0,3},{1,0},{2,1},{3,2},{4,7},{5,4},{6,5},{7,6},{8,11},{9,8},{10,9... | collective-permute-start | bytes 245768 | tf_op jit(solution)/shard_map/ppermute | solution.py:32
  29.7 0.0 collective-permute-start.8
  29.7 3.9 %collective-permute-start.9 = (f32[2,40,128]{2,1,0:T(8,128)S(1)}, f32[2,40,128]{2,1,0:T(8,128)S(1)}, u32[]{:S(2)}, u32[]{:S(2)}) collective-permute-start(f32[2,40,128]{2,1,0:T(8,128)S(1)} %get-tuple-element.70), channel_id=1, source_target_pairs={{0,11},{1,8},{2,9},{3,10},{4,15},{5,12},{6,13},{7,14},{8,19},{9,16... | collective-permute-start | bytes 122888 | tf_op jit(solution)/shard_map/ppermute | solution.py:32
  33.5 0.0 collective-permute-done.7.got_ref.refs_8_
  33.5 0.6 %inner.3 = (f32[2,112,128]{2,1,0:T(8,128)S(1)}, f32[2,112,128]{2,1,0:T(8,128)S(1)}, f32[2,96,128]{2,1,0:T(8,128)S(1)}, f32[2,96,128]{2,1,0:T(8,128)S(1)}, f32[2,80,128]{2,1,0:T(8,128)S(1)}) custom-call(s32[1]{0:T(128)} %bitcast.first_ref, f32[2,216,128]{2,1,0:T(8,128)S(1)} %get-tuple-element.49.start_ref, f32[2,216,128]{2,1,0:T(8,128)S(1)} %get-tuple-element.50.params_ref, ...), custom_call_target="tpu_custom_call" | custom-call | tf_op jit(solution)/shard_map/inner/pallas_call | solution.py:354
  34.1 2.0 %collective-permute-done.8.refs_9_ = f32[2,40,128]{2,1,0:T(8,128)S(1)} collective-permute-done((f32[2,40,128]{2,1,0:T(8,128)S(1)}, f32[2,40,128]{2,1,0:T(8,128)S(1)}, u32[]{:S(2)}, u32[]{:S(2)}) %collective-permute-start.8) | collective-permute-done | bytes 40992 | tf_op jit(solution)/shard_map/ppermute | solution.py:32
  36.1 0.0 collective-permute-done.9.refs_10_
  36.1 0.0 collective-permute-done.10.refs_11_
  36.1 0.0 collective-permute-done.11.refs_12_
  36.1 1.8 %last.1 = f32[2,4,16,128]{3,2,1,0:T(8,128)} custom-call(s32[1]{0:T(128)} %bitcast.first_ref, f32[2,216,128]{2,1,0:T(8,128)S(1)} %get-tuple-element.49.start_ref, f32[2,216,128]{2,1,0:T(8,128)S(1)} %get-tuple-element.50.params_ref, f32[512,128]{1,0:T(8,128)S(1)} %collective-permute-done.4.refs_10_.known_ref, f32[2,112,128]{2,1,0:T(8,128)S(1)} %get-tuple-element.64.refs_0_, ...), custom_call_target="tpu_custom_call" | custom-call | tf_op jit(solution)/shard_map/last/pallas_call | solution.py:354
  (2 shorter events, 0.0 us)
Async XLA Ops:
  0.0 0.9 %copy-start = (f32[4,16,128]{2,1,0:T(8,128)S(1)}, f32[4,16,128]{2,1,0:T(8,128)}, u32[]{:S(2)}) copy-start(f32[4,16,128]{2,1,0:T(8,128)} %param.7) | copy-start | bytes 98308
  0.0 0.9 %copy-start.1 = (f32[4,16,128]{2,1,0:T(8,128)S(1)}, f32[4,16,128]{2,1,0:T(8,128)}, u32[]{:S(2)}) copy-start(f32[4,16,128]{2,1,0:T(8,128)} %param.6) | copy-start | bytes 98308
  0.9 10.6 %collective-permute-start.1 = (f32[4,64,128]{2,1,0:T(8,128)S(1)}, f32[4,64,128]{2,1,0:T(8,128)S(1)}, u32[]{:S(2)}, u32[]{:S(2)}) collective-permute-start(f32[4,64,128]{2,1,0:T(8,128)S(1)} %get-tuple-element.40.refs_1_), channel_id=1, source_target_pairs={{0,12},{1,13},{2,14},{3,15},{4,8},{5,9},{6,10},{7,11},{8,20},{9,21... | collective-permute-start | bytes 393224 | tf_op jit(solution)/shard_map/ppermute | solution.py:32
  3.4 8.5 %collective-permute-start.3 = (f32[4,48,128]{2,1,0:T(8,128)S(1)}, f32[4,48,128]{2,1,0:T(8,128)S(1)}, u32[]{:S(2)}, u32[]{:S(2)}) collective-permute-start(f32[4,48,128]{2,1,0:T(8,128)S(1)} %get-tuple-element.48), channel_id=1, source_target_pairs={{0,13},{1,14},{2,15},{3,12},{4,9},{5,10},{6,11},{7,8},{8,21},{9,22... | collective-permute-start | bytes 294920 | tf_op jit(solution)/shard_map/ppermute | solution.py:32
  6.1 7.5 %collective-permute-start.2 = (f32[4,48,128]{2,1,0:T(8,128)S(1)}, f32[4,48,128]{2,1,0:T(8,128)S(1)}, u32[]{:S(2)}, u32[]{:S(2)}) collective-permute-start(f32[4,48,128]{2,1,0:T(8,128)S(1)} %get-tuple-element.48), channel_id=1, source_target_pairs={{0,9},{1,10},{2,11},{3,8},{4,13},{5,14},{6,15},{7,12},{8,17},{9,18... | collective-permute-start | bytes 294920 | tf_op jit(solution)/shard_map/ppermute | solution.py:32
  7.3 4.3 %collective-permute-start = (f32[2,64,128]{2,1,0:T(8,128)S(1)}, f32[2,64,128]{2,1,0:T(8,128)S(1)}, u32[]{:S(2)}, u32[]{:S(2)}) collective-permute-start(f32[2,64,128]{2,1,0:T(8,128)S(1)} %get-tuple-element.39), channel_id=1, source_target_pairs={{0,8},{1,9},{2,10},{3,11},{4,12},{5,13},{6,14},{7,15},{8,16},{9,17... | collective-permute-start | bytes 196616 | tf_op jit(solution)/shard_map/ppermute | solution.py:32
  14.5 9.2 %collective-permute-start.4 = (f32[512,128]{1,0:T(8,128)S(1)}, f32[512,128]{1,0:T(8,128)S(1)}, u32[]{:S(2)}, u32[]{:S(2)}) collective-permute-start(f32[512,128]{1,0:T(8,128)S(1)} %get-tuple-element.51), channel_id=1, source_target_pairs={{0,3},{1,0},{2,1},{3,2},{4,7},{5,4},{6,5},{7,6},{8,11},{9,8},{10,9... | collective-permute-start | bytes 786440 | tf_op jit(solution)/shard_map/ppermute | solution.py:32
  15.4 4.4 %collective-permute-start.5 = (f32[2,128,128]{2,1,0:T(8,128)S(1)}, f32[2,128,128]{2,1,0:T(8,128)S(1)}, u32[]{:S(2)}, u32[]{:S(2)}) collective-permute-start(f32[2,128,128]{2,1,0:T(8,128)S(1)} %get-tuple-element.54.two_ref.refs_7_), channel_id=1, source_target_pairs={{0,8},{1,9},{2,10},{3,11},{4,12},{5,13},{6,14},{7,15},{8,16},{9,17... | collective-permute-start | bytes 393224 | tf_op jit(solution)/shard_map/ppermute | solution.py:32
  15.7 7.9 %collective-permute-start.6 = (f32[2,88,128]{2,1,0:T(8,128)S(1)}, f32[2,88,128]{2,1,0:T(8,128)S(1)}, u32[]{:S(2)}, u32[]{:S(2)}) collective-permute-start(f32[2,88,128]{2,1,0:T(8,128)S(1)} %get-tuple-element.60), channel_id=1, source_target_pairs={{0,11},{1,8},{2,9},{3,10},{4,15},{5,12},{6,13},{7,14},{8,19},{9,16... | collective-permute-start | bytes 270344 | tf_op jit(solution)/shard_map/ppermute | solution.py:32
  24.9 8.7 %collective-permute-start.7 = (f32[2,128,128]{2,1,0:T(8,128)S(1)}, f32[2,128,128]{2,1,0:T(8,128)S(1)}, u32[]{:S(2)}, u32[]{:S(2)}) collective-permute-start(f32[2,128,128]{2,1,0:T(8,128)S(1)} %get-tuple-element.63.two_ref.refs_7_), channel_id=1, source_target_pairs={{0,8},{1,9},{2,10},{3,11},{4,12},{5,13},{6,14},{7,15},{8,16},{9,17... | collective-permute-start | bytes 393224 | tf_op jit(solution)/shard_map/ppermute | solution.py:32
  25.9 10.2 %collective-permute-start.10 = (f32[160,128]{1,0:T(8,128)S(1)}, f32[160,128]{1,0:T(8,128)S(1)}, u32[]{:S(2)}, u32[]{:S(2)}) collective-permute-start(f32[160,128]{1,0:T(8,128)S(1)} %get-tuple-element.71), channel_id=1, source_target_pairs={{0,1},{1,2},{2,3},{3,0},{4,5},{5,6},{6,7},{7,4},{8,9},{9,10},{10,1... | collective-permute-start | bytes 245768 | tf_op jit(solution)/shard_map/ppermute | solution.py:32
  25.9 10.2 %collective-permute-start.11 = (f32[160,128]{1,0:T(8,128)S(1)}, f32[160,128]{1,0:T(8,128)S(1)}, u32[]{:S(2)}, u32[]{:S(2)}) collective-permute-start(f32[160,128]{1,0:T(8,128)S(1)} %get-tuple-element.72), channel_id=1, source_target_pairs={{0,3},{1,0},{2,1},{3,2},{4,7},{5,4},{6,5},{7,6},{8,11},{9,8},{10,9... | collective-permute-start | bytes 245768 | tf_op jit(solution)/shard_map/ppermute | solution.py:32
  29.7 6.4 %collective-permute-start.8 = (f32[2,40,128]{2,1,0:T(8,128)S(1)}, f32[2,40,128]{2,1,0:T(8,128)S(1)}, u32[]{:S(2)}, u32[]{:S(2)}) collective-permute-start(f32[2,40,128]{2,1,0:T(8,128)S(1)} %get-tuple-element.69), channel_id=1, source_target_pairs={{0,9},{1,10},{2,11},{3,8},{4,13},{5,14},{6,15},{7,12},{8,17},{9,18... | collective-permute-start | bytes 122888 | tf_op jit(solution)/shard_map/ppermute | solution.py:32
  29.7 6.4 %collective-permute-start.9 = (f32[2,40,128]{2,1,0:T(8,128)S(1)}, f32[2,40,128]{2,1,0:T(8,128)S(1)}, u32[]{:S(2)}, u32[]{:S(2)}) collective-permute-start(f32[2,40,128]{2,1,0:T(8,128)S(1)} %get-tuple-element.70), channel_id=1, source_target_pairs={{0,11},{1,8},{2,9},{3,10},{4,15},{5,12},{6,13},{7,14},{8,19},{9,16... | collective-permute-start | bytes 122888 | tf_op jit(solution)/shard_map/ppermute | solution.py:32

commit v9 on v8

--- a/solution.py
+++ b/solution.py
@@ -85,9 +85,18 @@
     return at
 
 
+INNER_COUNT = 11
+
+
 def inner_rows(n_y, tile_first):
-    low, high = max(tile_first + 1, -RATE_HALO), min(tile_first + n_y - 1, n_y + RATE_HALO)
-    return [(low + k, high - k) for k in (0, 0, 1, 1, 2)]
+    low, high = max(tile_first, -HALO), min(tile_first + n_y, n_y + HALO)
+    halves = lambda first, last: (-(-first // 2), last // 2)
+    clip = lambda rows, by: (max(rows[0], -by), min(rows[1], n_y // 2 + by))
+    inside = lambda rows: (rows[0] + 1, rows[1] - 1)
+    fine = [(low + k, high - k) for k in (1, 1, 2, 2, 3)]
+    start, one, integral = halves(low, high), halves(*fine[1]), halves(*fine[4])
+    coarse = [clip(start, 2), clip(one, 1), clip(integral, 1), clip(integral, 0)]
+    return [*fine, *coarse, clip(inside(start), 1), clip(inside(one), 0)]
 
 
 def inner_shapes(width, n_y, n_z, tile_first):
@@ -99,12 +108,14 @@
 
 
 def write_inner(values, width, n_y, tile_first, refs):
-    ranges = inner_rows(n_y, tile_first)
-    for r in range(ranges[0][0], ranges[0][1] + 2):
-        for k, (low, high), rows, ref in zip((0, 0, 1, 1, 2), ranges, values, refs):
-            if low <= r - k < high:
-                for field, value in enumerate(rows(r - k)):
-                    ref[field, pl.ds((r - k - low) * width, width), :] = value
+    items = []
+    for i, ((low, high), rows, ref) in enumerate(zip(inner_rows(n_y, tile_first), values, refs)):
+        for r in range(low, high):
+            ready = r + (0, 0, 1, 1, 2)[i] if i < 5 else 2 * r + (1, 1, 3, 3, 3, 3)[i - 5]
+            items.append((ready, i, r, rows, ref, low))
+    for _, _, r, rows, ref, low in sorted(items, key=lambda item: item[:3]):
+        for field, value in enumerate(rows(r)):
+            ref[field, pl.ds((r - low) * width, width), :] = value
 
 
 def iteration(start, feed, kill, old_rates, inner=()):
@@ -138,9 +149,10 @@
     node_two = known_or(stepped(node_one, rate_one, 1))
     rate_two = known_or(fine(node_two))
     fresh = (rate_zero, rate_one, rate_two)
-    rest_zero, rest_one, rest_two = restricted(start), restricted(node_one), restricted(node_two)
-    rest_integral = [restricted(quadrature(fresh, interval)) for interval in (0, 1)]
-    coarse_start = rest_zero
+    rest_zero, rest_one, rest_two = known_or(restricted(start)), known_or(restricted(node_one)), restricted(node_two)
+    rest_integral = [known_or(restricted(quadrature(fresh, interval))) for interval in (0, 1)]
+    rate_rest_zero, rate_rest_one = known_or(coarse(rest_zero)), known_or(coarse(rest_one))
+    coarse_start, rate_coarse_start = rest_zero, rate_rest_zero
 
     def coarse_stepped(state, rate, rest_rate, integral):
         @functools.cache
@@ -151,8 +163,8 @@
 
         return at
 
-    coarse_one = coarse_stepped(coarse_start, coarse(coarse_start), coarse(rest_zero), rest_integral[0])
-    coarse_two = coarse_stepped(coarse_one, coarse(coarse_one), coarse(rest_one), rest_integral[1])
+    coarse_one = coarse_stepped(coarse_start, rate_coarse_start, rate_rest_zero, rest_integral[0])
+    coarse_two = coarse_stepped(coarse_one, coarse(coarse_one), rate_rest_one, rest_integral[1])
 
     def corrected(node, coarse_node, rest):
         change = functools.cache(lambda c: tuple(spread(w - m) for w, m in zip(coarse_node(c), rest(c))))
@@ -164,7 +176,8 @@
         return at
 
     nodes = corrected(node_one, coarse_one, rest_one), corrected(node_two, coarse_two, rest_two)
-    return (rate_zero, *nodes), (rate_zero, node_one, rate_one, node_two, rate_two)
+    fine_rows = (rate_zero, node_one, rate_one, node_two, rate_two)
+    return (rate_zero, *nodes), (*fine_rows, rest_zero, rest_one, *rest_integral, rate_rest_zero, rate_rest_one)
 
 
 def rows_of(ref, width, first):
@@ -210,8 +223,8 @@
 
 
 def first_kernel(n_gy, n_x, n_y, *refs):
-    tiles, inner_refs, lows = refs[:2], refs[2:7], refs[7 : 7 + n_gy]
-    start_ref, params_ref, *outs = refs[7 + n_gy :]
+    tiles, inner_refs, refs = refs[:2], refs[2 : 2 + INNER_COUNT], refs[2 + INNER_COUNT :]
+    lows, (start_ref, params_ref, *outs) = refs[:n_gy], refs[n_gy:]
     width = n_gy * n_x
     for field in range(2):
         for out_ref, tile_ref, place in zip((start_ref, params_ref), tiles, (0, 2)):
@@ -295,7 +308,7 @@
 
 
 def second_kernel(width, n_y, first_ref, start_ref, params_ref, *refs):
-    zero_ref, one_ref, two_ref, got_ref, got_edge, pair_edge, *outs = refs[5:]
+    zero_ref, one_ref, two_ref, got_ref, got_edge, pair_edge, *outs = refs[INNER_COUNT:]
     inner = inner_of(refs, width, n_y, -DRIFT)
     kept, params = known(width, n_y, start_ref, params_ref, pair_edge)
     end = n_y - DRIFT
@@ -317,7 +330,7 @@
 
 
 def later_kernel(width, n_y, out_x, first_ref, start_ref, params_ref, known_ref, *refs):
-    zero_ref, one_ref, two_ref, got_ref, got_low, got_high, pair_low, pair_high, *outs = refs[5:]
+    zero_ref, one_ref, two_ref, got_ref, got_low, got_high, pair_low, pair_high, *outs = refs[INNER_COUNT:]
     inner = inner_of(refs, width, n_y, 0)
     kept, params = known(width, n_y, start_ref, params_ref, known_ref)
 

time: 38 us -> 37.3 us (0.982)
  waiting for transfers between devices: 13.3 us -> 12.8 us
    ppermute x12, waiting for transfers between devices: 13.3 us -> 12.8 us  [shifted(): return lax.ppermute(value, AXES, pairs)]
  transfers between devices with their start and end apart: 12 -> 12, of which waited for: 6 -> 6; matrix products, arithmetic and copies ran while one was open for 0% -> 0% of each run, Pallas kernels for 4% -> 5%
where the time goes in v9:
time: 37.3 us; the launch traced here: 37.1 us
  starting transfers between devices  18.4 us (49%)
  waiting for transfers between devices  12.8 us (34%)
  Pallas kernels  5.01 us (13%)
  other arithmetic  0.87 us (2%)
    ppermute x12, starting transfers between devices, shifted(): return lax.ppermute(value, AXES, pairs)  18.4 us
    ppermute x12, waiting for transfers between devices, shifted(): return lax.ppermute(value, AXES, pairs)  12.8 us
    pallas_call x7, Pallas kernels, call(): pl.pallas_call(kernel, name=name, out_shape=[jax.ShapeDtypeStruct(shape,...  5.01 us
    select_n x1, other arithmetic, shards(): sent = jnp.where(place == n_tm - 1, initial_state, slice_guess[0])  0.86 us
  transfers between devices with their start and end apart: 12, of which 6 were waited for; matrix products, arithmetic and copies ran while one was open for 0% of the time, Pallas kernels for 5%

profile of v9, /device:TPU:0, one launch (start us, length us, event | category | flops | bytes accessed | tf_op | source)
XLA Modules:
  0.0 37.1 jit_solution(4377796974968785541)
XLA Ops:
  0.0 0.0 copy-start
  0.0 0.0 copy-start.1
  0.0 0.9 %bitcast_select_fusion = f32[2,4,16,128]{3,2,1,0:T(8,128)S(1)} fusion(f32[2,4,16,128]{3,2,1,0:T(8,128)} %param.4, f32[1,2,4,16,128]{4,3,2,1,0:T(8,128)} %param.5, pred[]{:T(512)S(6)} %eq.7), kind=kLoop, calls=%fused_computation.1 | loop fusion | flops 16384 | bytes 196609 | tf_op jit(solution)/shard_map/jit(_where)/select_n | solution.py:385
  0.9 0.0 copy-done
  0.9 0.0 copy-done.1
  0.9 2.5 %collective-permute-start.1 = (f32[4,64,128]{2,1,0:T(8,128)S(1)}, f32[4,64,128]{2,1,0:T(8,128)S(1)}, u32[]{:S(2)}, u32[]{:S(2)}) collective-permute-start(f32[4,64,128]{2,1,0:T(8,128)S(1)} %get-tuple-element.58.refs_1_), channel_id=1, source_target_pairs={{0,12},{1,13},{2,14},{3,15},{4,8},{5,9},{6,10},{7,11},{8,20},{9,21... | collective-permute-start | bytes 393224 | tf_op jit(solution)/shard_map/ppermute | solution.py:32
  3.4 2.7 %collective-permute-start.3 = (f32[4,48,128]{2,1,0:T(8,128)S(1)}, f32[4,48,128]{2,1,0:T(8,128)S(1)}, u32[]{:S(2)}, u32[]{:S(2)}) collective-permute-start(f32[4,48,128]{2,1,0:T(8,128)S(1)} %get-tuple-element.72), channel_id=1, source_target_pairs={{0,13},{1,14},{2,15},{3,12},{4,9},{5,10},{6,11},{7,8},{8,21},{9,22... | collective-permute-start | bytes 294920 | tf_op jit(solution)/shard_map/ppermute | solution.py:32
  6.1 1.1 %collective-permute-start.2 = (f32[4,48,128]{2,1,0:T(8,128)S(1)}, f32[4,48,128]{2,1,0:T(8,128)S(1)}, u32[]{:S(2)}, u32[]{:S(2)}) collective-permute-start(f32[4,48,128]{2,1,0:T(8,128)S(1)} %get-tuple-element.72), channel_id=1, source_target_pairs={{0,9},{1,10},{2,11},{3,8},{4,13},{5,14},{6,15},{7,12},{8,17},{9,18... | collective-permute-start | bytes 294920 | tf_op jit(solution)/shard_map/ppermute | solution.py:32
  7.3 0.5 %collective-permute-start = (f32[2,64,128]{2,1,0:T(8,128)S(1)}, f32[2,64,128]{2,1,0:T(8,128)S(1)}, u32[]{:S(2)}, u32[]{:S(2)}) collective-permute-start(f32[2,64,128]{2,1,0:T(8,128)S(1)} %get-tuple-element.57), channel_id=1, source_target_pairs={{0,8},{1,9},{2,10},{3,11},{4,12},{5,13},{6,14},{7,15},{8,16},{9,17... | collective-permute-start | bytes 196616 | tf_op jit(solution)/shard_map/ppermute | solution.py:32
  7.8 3.8 %collective-permute-done.refs_0_ = f32[2,64,128]{2,1,0:T(8,128)S(1)} collective-permute-done((f32[2,64,128]{2,1,0:T(8,128)S(1)}, f32[2,64,128]{2,1,0:T(8,128)S(1)}, u32[]{:S(2)}, u32[]{:S(2)}) %collective-permute-start) | collective-permute-done | bytes 65568 | tf_op jit(solution)/shard_map/ppermute | solution.py:32
  11.6 0.0 collective-permute-done.1.refs_2_
  11.6 0.4 %inner_first.1 = (f32[2,128,128]{2,1,0:T(8,128)S(1)}, f32[2,128,128]{2,1,0:T(8,128)S(1)}, f32[2,104,128]{2,1,0:T(8,128)S(1)}, f32[2,104,128]{2,1,0:T(8,128)S(1)}...) custom-call(f32[2,64,128]{2,1,0:T(8,128)S(1)} %collective-permute-do, ...), custom_call_target="tpu_custom_call" | custom-call | tf_op jit(solution)/shard_map/inner_first/pallas_call | solution.py:367
  12.0 0.0 collective-permute-done.3.refs_14_
  12.0 1.6 %collective-permute-done.2.refs_13_ = f32[4,48,128]{2,1,0:T(8,128)S(1)} collective-permute-done((f32[4,48,128]{2,1,0:T(8,128)S(1)}, f32[4,48,128]{2,1,0:T(8,128)S(1)}, u32[]{:S(2)}, u32[]{:S(2)}) %collective-permute-start.2) | collective-permute-done | bytes 98336 | tf_op jit(solution)/shard_map/ppermute | solution.py:32
  13.6 0.7 %first.1 = (f32[2,216,128]{2,1,0:T(8,128)S(1)}, f32[2,216,128]{2,1,0:T(8,128)S(1)}, f32[2,192,128]{2,1,0:T(8,128)S(1)}, f32[2,128,128]{2,1,0:T(8,128)S(1)}, f32[...) custom-call(f32[2,128,128]{2,1,0:T(8,128)S(1)} %get-tuple-element.59.refs_0_, ...), custom_call_target="tpu_custom_call" | custom-call | tf_op jit(solution)/shard_map/first/pallas_call | solution.py:367
  14.4 0.9 %collective-permute-start.4 = (f32[512,128]{1,0:T(8,128)S(1)}, f32[512,128]{1,0:T(8,128)S(1)}, u32[]{:S(2)}, u32[]{:S(2)}) collective-permute-start(f32[512,128]{1,0:T(8,128)S(1)} %get-tuple-element.75), channel_id=1, source_target_pairs={{0,3},{1,0},{2,1},{3,2},{4,7},{5,4},{6,5},{7,6},{8,11},{9,8},{10,9... | collective-permute-start | bytes 786440 | tf_op jit(solution)/shard_map/ppermute | solution.py:32
  15.3 0.2 collective-permute-start.5
  15.5 1.7 %collective-permute-start.6 = (f32[2,88,128]{2,1,0:T(8,128)S(1)}, f32[2,88,128]{2,1,0:T(8,128)S(1)}, u32[]{:S(2)}, u32[]{:S(2)}) collective-permute-start(f32[2,88,128]{2,1,0:T(8,128)S(1)} %get-tuple-element.90), channel_id=1, source_target_pairs={{0,11},{1,8},{2,9},{3,10},{4,15},{5,12},{6,13},{7,14},{8,19},{9,16... | collective-permute-start | bytes 270344 | tf_op jit(solution)/shard_map/ppermute | solution.py:32
  17.2 2.4 %collective-permute-done.5.got_ref.refs_14_ = f32[2,128,128]{2,1,0:T(8,128)S(1)} collective-permute-done((f32[2,128,128]{2,1,0:T(8,128)S(1)}, f32[2,128,128]{2,1,0:T(8,128)S(1)}, u32[]{:S(2)}, u32[]{:S(2)}) %collective-permute-start.5) | collective-permute-done | bytes 131104 | tf_op jit(solution)/shard_map/ppermute | solution.py:32
  19.6 0.7 %inner.2 = (f32[2,104,128]{2,1,0:T(8,128)S(1)}, f32[2,104,128]{2,1,0:T(8,128)S(1)}, f32[2,88,128]{2,1,0:T(8,128)S(1)}, f32[2,88,128]{2,1,0:T(8,128)S(1)}, f32[2,...) custom-call(s32[1]{0:T(128)} %bitcast.first_ref, ...), custom_call_target="tpu_custom_call" | custom-call | tf_op jit(solution)/shard_map/inner/pallas_call | solution.py:367
  20.4 3.1 %collective-permute-done.6.refs_15_ = f32[2,88,128]{2,1,0:T(8,128)S(1)} collective-permute-done((f32[2,88,128]{2,1,0:T(8,128)S(1)}, f32[2,88,128]{2,1,0:T(8,128)S(1)}, u32[]{:S(2)}, u32[]{:S(2)}) %collective-permute-start.6) | collective-permute-done | bytes 90144 | tf_op jit(solution)/shard_map/ppermute | solution.py:32
  23.4 0.1 collective-permute-done.4.refs_16_.known_ref
  23.6 0.8 %second.1 = (f32[2,192,128]{2,1,0:T(8,128)S(1)}, f32[2,128,128]{2,1,0:T(8,128)S(1)}, f32[2,128,128]{2,1,0:T(8,128)S(1)}, f32[2,40,128]{2,1,0:T(8,128)S(1)}, f32[...) custom-call(s32[1]{0:T(128)} %bitcast.first_ref, ...), custom_call_target="tpu_custom_call" | custom-call | tf_op jit(solution)/shard_map/second/pallas_call | solution.py:367
  24.4 1.0 %collective-permute-start.7 = (f32[2,128,128]{2,1,0:T(8,128)S(1)}, f32[2,128,128]{2,1,0:T(8,128)S(1)}, u32[]{:S(2)}, u32[]{:S(2)}) collective-permute-start(f32[2,128,128]{2,1,0:T(8,128)S(1)} %get-tuple-element.93.two_ref.refs_13_), channel_id=1, source_target_pairs={{0,8},{1,9},{2,10},{3,11},{4,12},{5,13},{6,14},{7,15},{8,16},{9,17... | collective-permute-start | bytes 393224 | tf_op jit(solution)/shard_map/ppermute | solution.py:32
  25.4 0.0 collective-permute-start.10
  25.4 3.8 %collective-permute-start.11 = (f32[160,128]{1,0:T(8,128)S(1)}, f32[160,128]{1,0:T(8,128)S(1)}, u32[]{:S(2)}, u32[]{:S(2)}) collective-permute-start(f32[160,128]{1,0:T(8,128)S(1)} %get-tuple-element.108), channel_id=1, source_target_pairs={{0,3},{1,0},{2,1},{3,2},{4,7},{5,4},{6,5},{7,6},{8,11},{9,8},{10,9... | collective-permute-start | bytes 245768 | tf_op jit(solution)/shard_map/ppermute | solution.py:32
  29.2 0.0 collective-permute-start.8
  29.2 3.9 %collective-permute-start.9 = (f32[2,40,128]{2,1,0:T(8,128)S(1)}, f32[2,40,128]{2,1,0:T(8,128)S(1)}, u32[]{:S(2)}, u32[]{:S(2)}) collective-permute-start(f32[2,40,128]{2,1,0:T(8,128)S(1)} %get-tuple-element.106), channel_id=1, source_target_pairs={{0,11},{1,8},{2,9},{3,10},{4,15},{5,12},{6,13},{7,14},{8,19},{9,16... | collective-permute-start | bytes 122888 | tf_op jit(solution)/shard_map/ppermute | solution.py:32
  33.1 0.0 collective-permute-done.7.got_ref.refs_14_
  33.1 0.8 %inner.3 = (f32[2,112,128]{2,1,0:T(8,128)S(1)}, f32[2,112,128]{2,1,0:T(8,128)S(1)}, f32[2,96,128]{2,1,0:T(8,128)S(1)}, f32[2,96,128]{2,1,0:T(8,128)S(1)}, f32[2,...) custom-call(s32[1]{0:T(128)} %bitcast.first_ref, ...), custom_call_target="tpu_custom_call" | custom-call | tf_op jit(solution)/shard_map/inner/pallas_call | solution.py:367
  33.9 1.7 %collective-permute-done.8.refs_15_ = f32[2,40,128]{2,1,0:T(8,128)S(1)} collective-permute-done((f32[2,40,128]{2,1,0:T(8,128)S(1)}, f32[2,40,128]{2,1,0:T(8,128)S(1)}, u32[]{:S(2)}, u32[]{:S(2)}) %collective-permute-start.8) | collective-permute-done | bytes 40992 | tf_op jit(solution)/shard_map/ppermute | solution.py:32
  35.6 0.0 collective-permute-done.9.refs_16_
  35.6 0.0 collective-permute-done.10.refs_17_
  35.6 0.0 collective-permute-done.11.refs_18_
  35.6 1.5 %last.1 = f32[2,4,16,128]{3,2,1,0:T(8,128)} custom-call(s32[1]{0:T(128)} %bitcast.first_ref, f32[2,216,128]{2,1,0:T(8,128)S(1)} %get-tuple-element.73.start_ref, f32[2,216,128]{2,1,0:T(8,128)S(1)} %get-tuple-element.74.params_ref, f32[512,128]{1,0:T(8,128)S(1)} %collective-permute-done.4.refs_16_.known_ref, f32[2,112,128]{2,1,0:T(8,128)S(1)} %get-tuple-element.94.refs_0_, ...), custom_call_target="tpu_custom_call" | custom-call | tf_op jit(solution)/shard_map/last/pallas_call | solution.py:367
  (2 shorter events, 0.0 us)
Async XLA Ops:
  0.0 0.9 %copy-start = (f32[4,16,128]{2,1,0:T(8,128)S(1)}, f32[4,16,128]{2,1,0:T(8,128)}, u32[]{:S(2)}) copy-start(f32[4,16,128]{2,1,0:T(8,128)} %param.7) | copy-start | bytes 98308
  0.0 0.9 %copy-start.1 = (f32[4,16,128]{2,1,0:T(8,128)S(1)}, f32[4,16,128]{2,1,0:T(8,128)}, u32[]{:S(2)}) copy-start(f32[4,16,128]{2,1,0:T(8,128)} %param.6) | copy-start | bytes 98308
  0.9 10.6 %collective-permute-start.1 = (f32[4,64,128]{2,1,0:T(8,128)S(1)}, f32[4,64,128]{2,1,0:T(8,128)S(1)}, u32[]{:S(2)}, u32[]{:S(2)}) collective-permute-start(f32[4,64,128]{2,1,0:T(8,128)S(1)} %get-tuple-element.58.refs_1_), channel_id=1, source_target_pairs={{0,12},{1,13},{2,14},{3,15},{4,8},{5,9},{6,10},{7,11},{8,20},{9,21... | collective-permute-start | bytes 393224 | tf_op jit(solution)/shard_map/ppermute | solution.py:32
  3.4 8.6 %collective-permute-start.3 = (f32[4,48,128]{2,1,0:T(8,128)S(1)}, f32[4,48,128]{2,1,0:T(8,128)S(1)}, u32[]{:S(2)}, u32[]{:S(2)}) collective-permute-start(f32[4,48,128]{2,1,0:T(8,128)S(1)} %get-tuple-element.72), channel_id=1, source_target_pairs={{0,13},{1,14},{2,15},{3,12},{4,9},{5,10},{6,11},{7,8},{8,21},{9,22... | collective-permute-start | bytes 294920 | tf_op jit(solution)/shard_map/ppermute | solution.py:32
  6.1 7.5 %collective-permute-start.2 = (f32[4,48,128]{2,1,0:T(8,128)S(1)}, f32[4,48,128]{2,1,0:T(8,128)S(1)}, u32[]{:S(2)}, u32[]{:S(2)}) collective-permute-start(f32[4,48,128]{2,1,0:T(8,128)S(1)} %get-tuple-element.72), channel_id=1, source_target_pairs={{0,9},{1,10},{2,11},{3,8},{4,13},{5,14},{6,15},{7,12},{8,17},{9,18... | collective-permute-start | bytes 294920 | tf_op jit(solution)/shard_map/ppermute | solution.py:32
  7.3 4.3 %collective-permute-start = (f32[2,64,128]{2,1,0:T(8,128)S(1)}, f32[2,64,128]{2,1,0:T(8,128)S(1)}, u32[]{:S(2)}, u32[]{:S(2)}) collective-permute-start(f32[2,64,128]{2,1,0:T(8,128)S(1)} %get-tuple-element.57), channel_id=1, source_target_pairs={{0,8},{1,9},{2,10},{3,11},{4,12},{5,13},{6,14},{7,15},{8,16},{9,17... | collective-permute-start | bytes 196616 | tf_op jit(solution)/shard_map/ppermute | solution.py:32
  14.4 9.2 %collective-permute-start.4 = (f32[512,128]{1,0:T(8,128)S(1)}, f32[512,128]{1,0:T(8,128)S(1)}, u32[]{:S(2)}, u32[]{:S(2)}) collective-permute-start(f32[512,128]{1,0:T(8,128)S(1)} %get-tuple-element.75), channel_id=1, source_target_pairs={{0,3},{1,0},{2,1},{3,2},{4,7},{5,4},{6,5},{7,6},{8,11},{9,8},{10,9... | collective-permute-start | bytes 786440 | tf_op jit(solution)/shard_map/ppermute | solution.py:32
  15.3 4.4 %collective-permute-start.5 = (f32[2,128,128]{2,1,0:T(8,128)S(1)}, f32[2,128,128]{2,1,0:T(8,128)S(1)}, u32[]{:S(2)}, u32[]{:S(2)}) collective-permute-start(f32[2,128,128]{2,1,0:T(8,128)S(1)} %get-tuple-element.78.two_ref.refs_13_), channel_id=1, source_target_pairs={{0,8},{1,9},{2,10},{3,11},{4,12},{5,13},{6,14},{7,15},{8,16},{9,17... | collective-permute-start | bytes 393224 | tf_op jit(solution)/shard_map/ppermute | solution.py:32
  15.5 7.9 %collective-permute-start.6 = (f32[2,88,128]{2,1,0:T(8,128)S(1)}, f32[2,88,128]{2,1,0:T(8,128)S(1)}, u32[]{:S(2)}, u32[]{:S(2)}) collective-permute-start(f32[2,88,128]{2,1,0:T(8,128)S(1)} %get-tuple-element.90), channel_id=1, source_target_pairs={{0,11},{1,8},{2,9},{3,10},{4,15},{5,12},{6,13},{7,14},{8,19},{9,16... | collective-permute-start | bytes 270344 | tf_op jit(solution)/shard_map/ppermute | solution.py:32
  24.4 8.7 %collective-permute-start.7 = (f32[2,128,128]{2,1,0:T(8,128)S(1)}, f32[2,128,128]{2,1,0:T(8,128)S(1)}, u32[]{:S(2)}, u32[]{:S(2)}) collective-permute-start(f32[2,128,128]{2,1,0:T(8,128)S(1)} %get-tuple-element.93.two_ref.refs_13_), channel_id=1, source_target_pairs={{0,8},{1,9},{2,10},{3,11},{4,12},{5,13},{6,14},{7,15},{8,16},{9,17... | collective-permute-start | bytes 393224 | tf_op jit(solution)/shard_map/ppermute | solution.py:32
  25.4 10.2 %collective-permute-start.10 = (f32[160,128]{1,0:T(8,128)S(1)}, f32[160,128]{1,0:T(8,128)S(1)}, u32[]{:S(2)}, u32[]{:S(2)}) collective-permute-start(f32[160,128]{1,0:T(8,128)S(1)} %get-tuple-element.107), channel_id=1, source_target_pairs={{0,1},{1,2},{2,3},{3,0},{4,5},{5,6},{6,7},{7,4},{8,9},{9,10},{10,1... | collective-permute-start | bytes 245768 | tf_op jit(solution)/shard_map/ppermute | solution.py:32
  25.4 10.2 %collective-permute-start.11 = (f32[160,128]{1,0:T(8,128)S(1)}, f32[160,128]{1,0:T(8,128)S(1)}, u32[]{:S(2)}, u32[]{:S(2)}) collective-permute-start(f32[160,128]{1,0:T(8,128)S(1)} %get-tuple-element.108), channel_id=1, source_target_pairs={{0,3},{1,0},{2,1},{3,2},{4,7},{5,4},{6,5},{7,6},{8,11},{9,8},{10,9... | collective-permute-start | bytes 245768 | tf_op jit(solution)/shard_map/ppermute | solution.py:32
  29.2 6.4 %collective-permute-start.8 = (f32[2,40,128]{2,1,0:T(8,128)S(1)}, f32[2,40,128]{2,1,0:T(8,128)S(1)}, u32[]{:S(2)}, u32[]{:S(2)}) collective-permute-start(f32[2,40,128]{2,1,0:T(8,128)S(1)} %get-tuple-element.105), channel_id=1, source_target_pairs={{0,9},{1,10},{2,11},{3,8},{4,13},{5,14},{6,15},{7,12},{8,17},{9,18... | collective-permute-start | bytes 122888 | tf_op jit(solution)/shard_map/ppermute | solution.py:32
  29.2 6.4 %collective-permute-start.9 = (f32[2,40,128]{2,1,0:T(8,128)S(1)}, f32[2,40,128]{2,1,0:T(8,128)S(1)}, u32[]{:S(2)}, u32[]{:S(2)}) collective-permute-start(f32[2,40,128]{2,1,0:T(8,128)S(1)} %get-tuple-element.106), channel_id=1, source_target_pairs={{0,11},{1,8},{2,9},{3,10},{4,15},{5,12},{6,13},{7,14},{8,19},{9,16... | collective-permute-start | bytes 122888 | tf_op jit(solution)/shard_map/ppermute | solution.py:32

commit v10 on v9

--- a/solution.py
+++ b/solution.py
@@ -118,7 +118,38 @@
             ref[field, pl.ds((r - low) * width, width), :] = value
 
 
-def iteration(start, feed, kill, old_rates, inner=()):
+def old_terms(rates):
+    def term(interval):
+        @functools.cache
+        def at(r):
+            return tuple(q - HALF_STEP * f for q, f in zip(quadrature(rates, interval)(r), rates[interval](r)))
+
+        return at
+
+    return term(0), term(1)
+
+
+def rim_rows(n_y, tile_first):
+    needed = ((-RATE_HALO, n_y + RATE_HALO), (1 - RATE_HALO, n_y + RATE_HALO - 1))
+    inner = (inner_rows(n_y, tile_first)[place] for place in (1, 3))
+    return [[r for r in range(*every) if not low <= r < high] for every, (low, high) in zip(needed, inner)]
+
+
+def write_rim(terms, width, n_y, tile_first, refs):
+    places = [(r, i, k) for i, rows in enumerate(rim_rows(n_y, tile_first)) for k, r in enumerate(rows)]
+    for r, i, k in sorted(places):
+        for field, value in enumerate(terms[i](r)):
+            refs[i][field, pl.ds(k * width, width), :] = value
+
+
+def rim_of(refs, width, n_y, tile_first):
+    def one(ref, rows):
+        return lambda r: rows_of(ref, width, 0)(rows.index(r))
+
+    return [one(ref, rows) for ref, rows in zip(refs, rim_rows(n_y, tile_first))]
+
+
+def iteration(start, feed, kill, terms, inner=()):
     inner = iter(inner)
 
     def known_or(values):
@@ -133,10 +164,8 @@
         @functools.cache
         def at(r):
             out = [s + HALF_STEP * f for s, f in zip(state(r), rate(r))]
-            if old_rates is not None:
-                integral = quadrature(old_rates, interval)(r)
-                old = old_rates[interval](r)
-                out = [o + (q - HALF_STEP * f) for o, q, f in zip(out, integral, old)]
+            if terms is not None:
+                out = [o + term for o, term in zip(out, terms[interval](r))]
             return tuple(out)
 
         return at
@@ -283,72 +312,85 @@
     )
 
 
-def later_iteration(is_first, kept, params, got, old_zero, ones, twos, inner=()):
-    feed, kill = (lambda r: params(r)[0]), (lambda r: params(r)[1])
-    feed_kill = functools.cache(lambda r: feed(r) + kill(r))
-
+def later_iteration(is_first, kept, params, got, terms, inner=()):
     @functools.cache
     def start(r):
         return tuple(jnp.where(is_first, a, b) for a, b in zip(kept(r), got(r)))
 
-    old_rates = (
-        old_zero(feed, feed_kill),
-        rates_of(ones, feed, feed_kill, 1.0),
-        rates_of(twos, feed, feed_kill, 1.0),
-    )
-    return iteration(start, feed, kill, old_rates, inner)
+    return iteration(start, lambda r: params(r)[0], lambda r: params(r)[1], terms, inner)
+
+
+def terms_of(params, old_zero, ones, twos):
+    feed = lambda r: params(r)[0]
+    feed_kill = functools.cache(lambda r: params(r)[0] + params(r)[1])
+    return old_terms((old_zero(feed, feed_kill), *(rates_of(rows, feed, feed_kill, 1.0) for rows in (ones, twos))))
 
 
 def inner_kernel(width, n_y, tile_first, first_ref, start_ref, params_ref, zero_ref, one_ref, two_ref, got_ref, *outs):
     kept, params = rows_of(start_ref, width, -TAKE), rows_of(params_ref, width, -TAKE)
     old_zero = rows_of(zero_ref, width, tile_first - RATE_HALO)
     ones, twos, got = (rows_of(ref, width, tile_first) for ref in (one_ref, two_ref, got_ref))
-    _, values = later_iteration(first_ref[0] == 1, kept, params, got, lambda feed, feed_kill: old_zero, ones, twos)
+    terms = terms_of(params, lambda feed, feed_kill: old_zero, ones, twos)
+    _, values = later_iteration(first_ref[0] == 1, kept, params, got, terms)
     write_inner(values, width, n_y, tile_first, outs)
 
 
-def second_kernel(width, n_y, first_ref, start_ref, params_ref, *refs):
-    zero_ref, one_ref, two_ref, got_ref, got_edge, pair_edge, *outs = refs[INNER_COUNT:]
-    inner = inner_of(refs, width, n_y, -DRIFT)
+def moved(width, n_y, tile_ref, beside):
+    return joined((-DRIFT, rows_of(tile_ref, width, -DRIFT)), (n_y - DRIFT, beside))
+
+
+def second_rim_kernel(width, n_y, start_ref, params_ref, zero_ref, one_ref, two_ref, pair_edge, *outs):
     kept, params = known(width, n_y, start_ref, params_ref, pair_edge)
     end = n_y - DRIFT
-
-    def moved(tile_ref, beside):
-        return joined((-DRIFT, rows_of(tile_ref, width, -DRIFT)), (end, beside))
-
-    def pair(place):
-        return flat_rows(pair_edge, width, place * TAKE, end, TAKE)
+    ones, twos = (
+        moved(width, n_y, ref, flat_rows(pair_edge, width, place * TAKE, end, TAKE))
+        for ref, place in ((one_ref, 0), (two_ref, 2))
+    )
 
     def old_zero(feed, feed_kill):
         inside = rows_of(zero_ref, width, -RATE_HALO - DRIFT)
         return joined((-RATE_HALO - DRIFT, inside), (end + RATE_HALO, rates_of(kept, feed, feed_kill, 1.0)))
 
-    ones, twos = moved(one_ref, pair(0)), moved(two_ref, pair(2))
-    got = moved(got_ref, rows_of(got_edge, width, end))
-    results, _ = later_iteration(first_ref[0] == 1, kept, params, got, old_zero, ones, twos, inner)
+    write_rim(terms_of(params, old_zero, ones, twos), width, n_y, -DRIFT, outs)
+
+
+def second_kernel(width, n_y, first_ref, start_ref, params_ref, *refs):
+    inner = inner_of(refs, width, n_y, -DRIFT)
+    terms = rim_of(refs[INNER_COUNT:], width, n_y, -DRIFT)
+    got_ref, got_edge, pair_edge, *outs = refs[INNER_COUNT + 2 :]
+    kept, params = known(width, n_y, start_ref, params_ref, pair_edge)
+    got = moved(width, n_y, got_ref, rows_of(got_edge, width, n_y - DRIFT))
+    results, _ = later_iteration(first_ref[0] == 1, kept, params, got, terms, inner)
     write_nodes(results, width, n_y, [(0, HALO), (n_y - HALO, HALO)], *outs)
 
 
-def later_kernel(width, n_y, out_x, first_ref, start_ref, params_ref, known_ref, *refs):
-    zero_ref, one_ref, two_ref, got_ref, got_low, got_high, pair_low, pair_high, *outs = refs[INNER_COUNT:]
-    inner = inner_of(refs, width, n_y, 0)
-    kept, params = known(width, n_y, start_ref, params_ref, known_ref)
-
-    def window(low, tile_ref, high):
-        return joined((-HALO, low), (0, rows_of(tile_ref, width, 0)), (n_y, high))
+def window(width, n_y, low, tile_ref, high):
+    return joined((-HALO, low), (0, rows_of(tile_ref, width, 0)), (n_y, high))
+
+
+def later_rim_kernel(
+    width, n_y, start_ref, params_ref, known_ref, zero_ref, one_ref, two_ref, pair_low, pair_high, *outs
+):
+    _, params = known(width, n_y, start_ref, params_ref, known_ref)
 
     def pair(tile_ref, place):
         low, high = (
             flat_rows(ref, width, place * HALO, first, HALO) for ref, first in ((pair_low, -HALO), (pair_high, n_y))
         )
-        return window(low, tile_ref, high)
-
-    ones, twos = pair(one_ref, 0), pair(two_ref, 2)
+        return window(width, n_y, low, tile_ref, high)
+
     old_zero = rows_of(zero_ref, width, -RATE_HALO)
-    got = window(rows_of(got_low, width, -HALO), got_ref, rows_of(got_high, width, n_y))
-    results, _ = later_iteration(
-        first_ref[0] == 1, kept, params, got, lambda feed, feed_kill: old_zero, ones, twos, inner
-    )
+    terms = terms_of(params, lambda feed, feed_kill: old_zero, pair(one_ref, 0), pair(two_ref, 2))
+    write_rim(terms, width, n_y, 0, outs)
+
+
+def later_kernel(width, n_y, out_x, first_ref, start_ref, params_ref, known_ref, *refs):
+    inner = inner_of(refs, width, n_y, 0)
+    terms = rim_of(refs[INNER_COUNT:], width, n_y, 0)
+    got_ref, got_low, got_high, *outs = refs[INNER_COUNT + 2 :]
+    kept, params = known(width, n_y, start_ref, params_ref, known_ref)
+    got = window(width, n_y, rows_of(got_low, width, -HALO), got_ref, rows_of(got_high, width, n_y))
+    results, _ = later_iteration(first_ref[0] == 1, kept, params, got, terms, inner)
     if out_x is None:
         write_nodes(results, width, n_y, [(0, HALO), (n_y - HALO, HALO)], *outs)
     else:
@@ -424,11 +466,17 @@
             inner_shapes(width, n_y, n_z, tile_first),
         )
 
+    def rim(kernel, name, tile_first, operands):
+        shapes = [(2, len(rows) * width, n_z) for rows in rim_rows(n_y, tile_first)]
+        return call(functools.partial(kernel, width, n_y), name, 0, operands, shapes)
+
+    zero, one, two = nodes[:3]
+    second_rim = rim(second_rim_kernel, "second_rim", -DRIFT, (start, params, zero, one, two, known_edge))
     nodes = call(
         functools.partial(second_kernel, width, n_y),
         "second",
         1,
-        (is_first, start, params, *inner(-DRIFT), zero, one, two, *got),
+        (is_first, start, params, *inner(-DRIFT), *second_rim, *got),
         [*nodes_only, *edge(HALO), *edge(HALO)],
     )
     for sweep_index in range(2, ITERS):
@@ -436,11 +484,12 @@
         got = [shifted(two, 1, 0, 0), shifted(two_high, 1, 0, 1), shifted(two_low, 1, 0, -1)]
         got += [shifted(pair_high, 0, 0, 1), shifted(pair_low, 0, 0, -1)]
         done = sweep_index + 1 == ITERS
+        later_rim = rim(later_rim_kernel, "later_rim", 0, (start, params, known_edge, zero, one, two, *got[3:]))
         nodes = call(
             functools.partial(later_kernel, width, n_y, n_x if done else None),
             "last" if done else "later",
             1,
-            (is_first, start, params, known_edge, *inner(0), zero, one, two, *got),
+            (is_first, start, params, known_edge, *inner(0), *later_rim, *got[:3]),
             [initial_state.shape] if done else [*nodes_only, *edge(HALO), *edge(HALO)],
             [pltpu.VMEM(tile, jnp.float32)] if done else (),
         )

time: 37.3 us -> 36.9 us (0.989)
    pallas_call x7 -> x9, Pallas kernels: 5.01 us -> 4.91 us  [call(): pl.pallas_call(kernel, name=name, out_shape=[jax.ShapeDtypeStruct(shape,...]
  transfers between devices with their start and end apart: 12 -> 12, of which waited for: 6 -> 5; matrix products, arithmetic and copies ran while one was open for 0% -> 0% of each run, Pallas kernels for 5% -> 6%
where the time goes in v10:
time: 36.9 us; the launch traced here: 36.7 us
  starting transfers between devices  18.2 us (49%)
  waiting for transfers between devices  12.7 us (34%)
  Pallas kernels  4.91 us (13%)
  other arithmetic  0.87 us (2%)
    ppermute x12, starting transfers between devices, shifted(): return lax.ppermute(value, AXES, pairs)  18.2 us
    ppermute x12, waiting for transfers between devices, shifted(): return lax.ppermute(value, AXES, pairs)  12.7 us
    pallas_call x9, Pallas kernels, call(): pl.pallas_call(kernel, name=name, out_shape=[jax.ShapeDtypeStruct(shape,...  4.91 us
    select_n x1, other arithmetic, shards(): sent = jnp.where(place == n_tm - 1, initial_state, slice_guess[0])  0.86 us
  transfers between devices with their start and end apart: 12, of which 5 were waited for; matrix products, arithmetic and copies ran while one was open for 0% of the time, Pallas kernels for 6%

profile of v10, /device:TPU:0, one launch (start us, length us, event | category | flops | bytes accessed | tf_op | source)
XLA Modules:
  0.0 36.7 jit_solution(16407729062176192566)
XLA Ops:
  0.0 0.0 copy-start
  0.0 0.0 copy-start.1
  0.0 0.9 %bitcast_select_fusion = f32[2,4,16,128]{3,2,1,0:T(8,128)S(1)} fusion(f32[2,4,16,128]{3,2,1,0:T(8,128)} %param.4, f32[1,2,4,16,128]{4,3,2,1,0:T(8,128)} %param.5, pred[]{:T(512)S(6)} %eq.7), kind=kLoop, calls=%fused_computation.1 | loop fusion | flops 16384 | bytes 196609 | tf_op jit(solution)/shard_map/jit(_where)/select_n | solution.py:427
  0.9 0.0 copy-done
  0.9 0.0 copy-done.1
  0.9 2.5 %collective-permute-start.1 = (f32[4,64,128]{2,1,0:T(8,128)S(1)}, f32[4,64,128]{2,1,0:T(8,128)S(1)}, u32[]{:S(2)}, u32[]{:S(2)}) collective-permute-start(f32[4,64,128]{2,1,0:T(8,128)S(1)} %get-tuple-element.62.refs_1_), channel_id=1, source_target_pairs={{0,12},{1,13},{2,14},{3,15},{4,8},{5,9},{6,10},{7,11},{8,20},{9,21... | collective-permute-start | bytes 393224 | tf_op jit(solution)/shard_map/ppermute | solution.py:32
  3.4 2.7 %collective-permute-start.3 = (f32[4,48,128]{2,1,0:T(8,128)S(1)}, f32[4,48,128]{2,1,0:T(8,128)S(1)}, u32[]{:S(2)}, u32[]{:S(2)}) collective-permute-start(f32[4,48,128]{2,1,0:T(8,128)S(1)} %get-tuple-element.76), channel_id=1, source_target_pairs={{0,13},{1,14},{2,15},{3,12},{4,9},{5,10},{6,11},{7,8},{8,21},{9,22... | collective-permute-start | bytes 294920 | tf_op jit(solution)/shard_map/ppermute | solution.py:32
  6.1 1.1 %collective-permute-start.2 = (f32[4,48,128]{2,1,0:T(8,128)S(1)}, f32[4,48,128]{2,1,0:T(8,128)S(1)}, u32[]{:S(2)}, u32[]{:S(2)}) collective-permute-start(f32[4,48,128]{2,1,0:T(8,128)S(1)} %get-tuple-element.76), channel_id=1, source_target_pairs={{0,9},{1,10},{2,11},{3,8},{4,13},{5,14},{6,15},{7,12},{8,17},{9,18... | collective-permute-start | bytes 294920 | tf_op jit(solution)/shard_map/ppermute | solution.py:32
  7.3 0.5 %collective-permute-start = (f32[2,64,128]{2,1,0:T(8,128)S(1)}, f32[2,64,128]{2,1,0:T(8,128)S(1)}, u32[]{:S(2)}, u32[]{:S(2)}) collective-permute-start(f32[2,64,128]{2,1,0:T(8,128)S(1)} %get-tuple-element.61), channel_id=1, source_target_pairs={{0,8},{1,9},{2,10},{3,11},{4,12},{5,13},{6,14},{7,15},{8,16},{9,17... | collective-permute-start | bytes 196616 | tf_op jit(solution)/shard_map/ppermute | solution.py:32
  7.8 3.8 %collective-permute-done.refs_0_ = f32[2,64,128]{2,1,0:T(8,128)S(1)} collective-permute-done((f32[2,64,128]{2,1,0:T(8,128)S(1)}, f32[2,64,128]{2,1,0:T(8,128)S(1)}, u32[]{:S(2)}, u32[]{:S(2)}) %collective-permute-start) | collective-permute-done | bytes 65568 | tf_op jit(solution)/shard_map/ppermute | solution.py:32
  11.6 0.0 collective-permute-done.1.refs_2_
  11.6 0.4 %inner_first.1 = (f32[2,128,128]{2,1,0:T(8,128)S(1)}, f32[2,128,128]{2,1,0:T(8,128)S(1)}, f32[2,104,128]{2,1,0:T(8,128)S(1)}, f32[2,104,128]{2,1,0:T(8,128)S(1)}...) custom-call(f32[2,64,128]{2,1,0:T(8,128)S(1)} %collective-permute-do, ...), custom_call_target="tpu_custom_call" | custom-call | tf_op jit(solution)/shard_map/inner_first/pallas_call | solution.py:409
  12.0 0.0 collective-permute-done.3.refs_14_
  12.0 1.6 %collective-permute-done.2.refs_13_ = f32[4,48,128]{2,1,0:T(8,128)S(1)} collective-permute-done((f32[4,48,128]{2,1,0:T(8,128)S(1)}, f32[4,48,128]{2,1,0:T(8,128)S(1)}, u32[]{:S(2)}, u32[]{:S(2)}) %collective-permute-start.2) | collective-permute-done | bytes 98336 | tf_op jit(solution)/shard_map/ppermute | solution.py:32
  13.6 0.7 %first.1 = (f32[2,216,128]{2,1,0:T(8,128)S(1)}, f32[2,216,128]{2,1,0:T(8,128)S(1)}, f32[2,192,128]{2,1,0:T(8,128)S(1)}, f32[2,128,128]{2,1,0:T(8,128)S(1)}, f32[...) custom-call(f32[2,128,128]{2,1,0:T(8,128)S(1)} %get-tuple-element.63.refs_0_, ...), custom_call_target="tpu_custom_call" | custom-call | tf_op jit(solution)/shard_map/first/pallas_call | solution.py:409
  14.4 0.9 %collective-permute-start.4 = (f32[512,128]{1,0:T(8,128)S(1)}, f32[512,128]{1,0:T(8,128)S(1)}, u32[]{:S(2)}, u32[]{:S(2)}) collective-permute-start(f32[512,128]{1,0:T(8,128)S(1)} %get-tuple-element.79), channel_id=1, source_target_pairs={{0,3},{1,0},{2,1},{3,2},{4,7},{5,4},{6,5},{7,6},{8,11},{9,8},{10,9... | collective-permute-start | bytes 786440 | tf_op jit(solution)/shard_map/ppermute | solution.py:32
  15.3 0.2 collective-permute-start.5
  15.5 1.7 %collective-permute-start.6 = (f32[2,88,128]{2,1,0:T(8,128)S(1)}, f32[2,88,128]{2,1,0:T(8,128)S(1)}, u32[]{:S(2)}, u32[]{:S(2)}) collective-permute-start(f32[2,88,128]{2,1,0:T(8,128)S(1)} %get-tuple-element.96), channel_id=1, source_target_pairs={{0,11},{1,8},{2,9},{3,10},{4,15},{5,12},{6,13},{7,14},{8,19},{9,16... | collective-permute-start | bytes 270344 | tf_op jit(solution)/shard_map/ppermute | solution.py:32
  17.2 2.4 %collective-permute-done.5.got_ref.refs_13_ = f32[2,128,128]{2,1,0:T(8,128)S(1)} collective-permute-done((f32[2,128,128]{2,1,0:T(8,128)S(1)}, f32[2,128,128]{2,1,0:T(8,128)S(1)}, u32[]{:S(2)}, u32[]{:S(2)}) %collective-permute-start.5) | collective-permute-done | bytes 131104 | tf_op jit(solution)/shard_map/ppermute | solution.py:32
  19.6 0.7 %inner.2 = (f32[2,104,128]{2,1,0:T(8,128)S(1)}, f32[2,104,128]{2,1,0:T(8,128)S(1)}, f32[2,88,128]{2,1,0:T(8,128)S(1)}, f32[2,88,128]{2,1,0:T(8,128)S(1)}, f32[2,...) custom-call(s32[1]{0:T(128)} %bitcast.first_ref, ...), custom_call_target="tpu_custom_call" | custom-call | tf_op jit(solution)/shard_map/inner/pallas_call | solution.py:409
  20.4 3.2 %collective-permute-done.4.pair_edge.refs_15_.known_ref = f32[512,128]{1,0:T(8,128)S(1)} collective-permute-done((f32[512,128]{1,0:T(8,128)S(1)}, f32[512,128]{1,0:T(8,128)S(1)}, u32[]{:S(2)}, u32[]{:S(2)}) %collective-permute-start.4) | collective-permute-done | bytes 262176 | tf_op jit(solution)/shard_map/ppermute | solution.py:32
  23.6 0.2 second_rim.1
  23.8 0.0 collective-permute-done.6.refs_14_
  23.8 0.6 %second.1 = (f32[2,192,128]{2,1,0:T(8,128)S(1)}, f32[2,128,128]{2,1,0:T(8,128)S(1)}, f32[2,128,128]{2,1,0:T(8,128)S(1)}, f32[2,40,128]{2,1,0:T(8,128)S(1)}, f32[...) custom-call(s32[1]{0:T(128)} %bitcast.first_ref, ...), custom_call_target="tpu_custom_call" | custom-call | tf_op jit(solution)/shard_map/second/pallas_call | solution.py:409
  24.4 0.7 %collective-permute-start.7 = (f32[2,128,128]{2,1,0:T(8,128)S(1)}, f32[2,128,128]{2,1,0:T(8,128)S(1)}, u32[]{:S(2)}, u32[]{:S(2)}) collective-permute-start(f32[2,128,128]{2,1,0:T(8,128)S(1)} %get-tuple-element.99.two_ref), channel_id=1, source_target_pairs={{0,8},{1,9},{2,10},{3,11},{4,12},{5,13},{6,14},{7,15},{8,16},{9,17... | collective-permute-start | bytes 393224 | tf_op jit(solution)/shard_map/ppermute | solution.py:32
  25.2 0.0 collective-permute-start.8
  25.2 3.8 %collective-permute-start.9 = (f32[160,128]{1,0:T(8,128)S(1)}, f32[160,128]{1,0:T(8,128)S(1)}, u32[]{:S(2)}, u32[]{:S(2)}) collective-permute-start(f32[160,128]{1,0:T(8,128)S(1)} %get-tuple-element.112), channel_id=1, source_target_pairs={{0,3},{1,0},{2,1},{3,2},{4,7},{5,4},{6,5},{7,6},{8,11},{9,8},{10,9... | collective-permute-start | bytes 245768 | tf_op jit(solution)/shard_map/ppermute | solution.py:32
  29.0 0.0 collective-permute-start.10
  29.0 3.9 %collective-permute-start.11 = (f32[2,40,128]{2,1,0:T(8,128)S(1)}, f32[2,40,128]{2,1,0:T(8,128)S(1)}, u32[]{:S(2)}, u32[]{:S(2)}) collective-permute-start(f32[2,40,128]{2,1,0:T(8,128)S(1)} %get-tuple-element.116), channel_id=1, source_target_pairs={{0,11},{1,8},{2,9},{3,10},{4,15},{5,12},{6,13},{7,14},{8,19},{9,16... | collective-permute-start | bytes 122888 | tf_op jit(solution)/shard_map/ppermute | solution.py:32
  32.9 0.0 collective-permute-done.8.pair_low
  32.9 0.0 collective-permute-done.9.pair_high
  32.9 0.2 later_rim.1
  33.0 0.0 collective-permute-done.7.got_ref.refs_13_
  33.1 0.8 %inner.3 = (f32[2,112,128]{2,1,0:T(8,128)S(1)}, f32[2,112,128]{2,1,0:T(8,128)S(1)}, f32[2,96,128]{2,1,0:T(8,128)S(1)}, f32[2,96,128]{2,1,0:T(8,128)S(1)}, f32[2,...) custom-call(s32[1]{0:T(128)} %bitcast.first_ref, ...), custom_call_target="tpu_custom_call" | custom-call | tf_op jit(solution)/shard_map/inner/pallas_call | solution.py:409
  33.8 1.6 %collective-permute-done.10.refs_14_ = f32[2,40,128]{2,1,0:T(8,128)S(1)} collective-permute-done((f32[2,40,128]{2,1,0:T(8,128)S(1)}, f32[2,40,128]{2,1,0:T(8,128)S(1)}, u32[]{:S(2)}, u32[]{:S(2)}) %collective-permute-start.10) | collective-permute-done | bytes 40992 | tf_op jit(solution)/shard_map/ppermute | solution.py:32
  35.5 0.0 collective-permute-done.11.refs_15_
  35.5 1.3 %last.1 = f32[2,4,16,128]{3,2,1,0:T(8,128)} custom-call(s32[1]{0:T(128)} %bitcast.first_ref, f32[2,216,128]{2,1,0:T(8,128)S(1)} %get-tuple-element.77.start_ref, f32[2,216,128]{2,1,0:T(8,128)S(1)} %get-tuple-element.78.params_ref, f32[512,128]{1,0:T(8,128)S(1)} %collective-permute-done.4.pair_edge.refs_15_.known_ref, ...), custom_call_target="tpu_custom_call" | custom-call | tf_op jit(solution)/shard_map/last/pallas_call | solution.py:409
  (2 shorter events, 0.0 us)
Async XLA Ops:
  0.0 0.9 %copy-start = (f32[4,16,128]{2,1,0:T(8,128)S(1)}, f32[4,16,128]{2,1,0:T(8,128)}, u32[]{:S(2)}) copy-start(f32[4,16,128]{2,1,0:T(8,128)} %param.7) | copy-start | bytes 98308
  0.0 0.9 %copy-start.1 = (f32[4,16,128]{2,1,0:T(8,128)S(1)}, f32[4,16,128]{2,1,0:T(8,128)}, u32[]{:S(2)}) copy-start(f32[4,16,128]{2,1,0:T(8,128)} %param.6) | copy-start | bytes 98308
  0.9 10.6 %collective-permute-start.1 = (f32[4,64,128]{2,1,0:T(8,128)S(1)}, f32[4,64,128]{2,1,0:T(8,128)S(1)}, u32[]{:S(2)}, u32[]{:S(2)}) collective-permute-start(f32[4,64,128]{2,1,0:T(8,128)S(1)} %get-tuple-element.62.refs_1_), channel_id=1, source_target_pairs={{0,12},{1,13},{2,14},{3,15},{4,8},{5,9},{6,10},{7,11},{8,20},{9,21... | collective-permute-start | bytes 393224 | tf_op jit(solution)/shard_map/ppermute | solution.py:32
  3.4 8.6 %collective-permute-start.3 = (f32[4,48,128]{2,1,0:T(8,128)S(1)}, f32[4,48,128]{2,1,0:T(8,128)S(1)}, u32[]{:S(2)}, u32[]{:S(2)}) collective-permute-start(f32[4,48,128]{2,1,0:T(8,128)S(1)} %get-tuple-element.76), channel_id=1, source_target_pairs={{0,13},{1,14},{2,15},{3,12},{4,9},{5,10},{6,11},{7,8},{8,21},{9,22... | collective-permute-start | bytes 294920 | tf_op jit(solution)/shard_map/ppermute | solution.py:32
  6.1 7.5 %collective-permute-start.2 = (f32[4,48,128]{2,1,0:T(8,128)S(1)}, f32[4,48,128]{2,1,0:T(8,128)S(1)}, u32[]{:S(2)}, u32[]{:S(2)}) collective-permute-start(f32[4,48,128]{2,1,0:T(8,128)S(1)} %get-tuple-element.76), channel_id=1, source_target_pairs={{0,9},{1,10},{2,11},{3,8},{4,13},{5,14},{6,15},{7,12},{8,17},{9,18... | collective-permute-start | bytes 294920 | tf_op jit(solution)/shard_map/ppermute | solution.py:32
  7.3 4.3 %collective-permute-start = (f32[2,64,128]{2,1,0:T(8,128)S(1)}, f32[2,64,128]{2,1,0:T(8,128)S(1)}, u32[]{:S(2)}, u32[]{:S(2)}) collective-permute-start(f32[2,64,128]{2,1,0:T(8,128)S(1)} %get-tuple-element.61), channel_id=1, source_target_pairs={{0,8},{1,9},{2,10},{3,11},{4,12},{5,13},{6,14},{7,15},{8,16},{9,17... | collective-permute-start | bytes 196616 | tf_op jit(solution)/shard_map/ppermute | solution.py:32
  14.4 9.2 %collective-permute-start.4 = (f32[512,128]{1,0:T(8,128)S(1)}, f32[512,128]{1,0:T(8,128)S(1)}, u32[]{:S(2)}, u32[]{:S(2)}) collective-permute-start(f32[512,128]{1,0:T(8,128)S(1)} %get-tuple-element.79), channel_id=1, source_target_pairs={{0,3},{1,0},{2,1},{3,2},{4,7},{5,4},{6,5},{7,6},{8,11},{9,8},{10,9... | collective-permute-start | bytes 786440 | tf_op jit(solution)/shard_map/ppermute | solution.py:32
  15.3 4.4 %collective-permute-start.5 = (f32[2,128,128]{2,1,0:T(8,128)S(1)}, f32[2,128,128]{2,1,0:T(8,128)S(1)}, u32[]{:S(2)}, u32[]{:S(2)}) collective-permute-start(f32[2,128,128]{2,1,0:T(8,128)S(1)} %get-tuple-element.82.two_ref), channel_id=1, source_target_pairs={{0,8},{1,9},{2,10},{3,11},{4,12},{5,13},{6,14},{7,15},{8,16},{9,17... | collective-permute-start | bytes 393224 | tf_op jit(solution)/shard_map/ppermute | solution.py:32
  15.5 8.3 %collective-permute-start.6 = (f32[2,88,128]{2,1,0:T(8,128)S(1)}, f32[2,88,128]{2,1,0:T(8,128)S(1)}, u32[]{:S(2)}, u32[]{:S(2)}) collective-permute-start(f32[2,88,128]{2,1,0:T(8,128)S(1)} %get-tuple-element.96), channel_id=1, source_target_pairs={{0,11},{1,8},{2,9},{3,10},{4,15},{5,12},{6,13},{7,14},{8,19},{9,16... | collective-permute-start | bytes 270344 | tf_op jit(solution)/shard_map/ppermute | solution.py:32
  24.4 8.6 %collective-permute-start.7 = (f32[2,128,128]{2,1,0:T(8,128)S(1)}, f32[2,128,128]{2,1,0:T(8,128)S(1)}, u32[]{:S(2)}, u32[]{:S(2)}) collective-permute-start(f32[2,128,128]{2,1,0:T(8,128)S(1)} %get-tuple-element.99.two_ref), channel_id=1, source_target_pairs={{0,8},{1,9},{2,10},{3,11},{4,12},{5,13},{6,14},{7,15},{8,16},{9,17... | collective-permute-start | bytes 393224 | tf_op jit(solution)/shard_map/ppermute | solution.py:32
  25.2 7.7 %collective-permute-start.8 = (f32[160,128]{1,0:T(8,128)S(1)}, f32[160,128]{1,0:T(8,128)S(1)}, u32[]{:S(2)}, u32[]{:S(2)}) collective-permute-start(f32[160,128]{1,0:T(8,128)S(1)} %get-tuple-element.111), channel_id=1, source_target_pairs={{0,1},{1,2},{2,3},{3,0},{4,5},{5,6},{6,7},{7,4},{8,9},{9,10},{10,1... | collective-permute-start | bytes 245768 | tf_op jit(solution)/shard_map/ppermute | solution.py:32
  25.2 7.7 %collective-permute-start.9 = (f32[160,128]{1,0:T(8,128)S(1)}, f32[160,128]{1,0:T(8,128)S(1)}, u32[]{:S(2)}, u32[]{:S(2)}) collective-permute-start(f32[160,128]{1,0:T(8,128)S(1)} %get-tuple-element.112), channel_id=1, source_target_pairs={{0,3},{1,0},{2,1},{3,2},{4,7},{5,4},{6,5},{7,6},{8,11},{9,8},{10,9... | collective-permute-start | bytes 245768 | tf_op jit(solution)/shard_map/ppermute | solution.py:32
  29.0 6.5 %collective-permute-start.10 = (f32[2,40,128]{2,1,0:T(8,128)S(1)}, f32[2,40,128]{2,1,0:T(8,128)S(1)}, u32[]{:S(2)}, u32[]{:S(2)}) collective-permute-start(f32[2,40,128]{2,1,0:T(8,128)S(1)} %get-tuple-element.115), channel_id=1, source_target_pairs={{0,9},{1,10},{2,11},{3,8},{4,13},{5,14},{6,15},{7,12},{8,17},{9,18... | collective-permute-start | bytes 122888 | tf_op jit(solution)/shard_map/ppermute | solution.py:32
  29.0 6.5 %collective-permute-start.11 = (f32[2,40,128]{2,1,0:T(8,128)S(1)}, f32[2,40,128]{2,1,0:T(8,128)S(1)}, u32[]{:S(2)}, u32[]{:S(2)}) collective-permute-start(f32[2,40,128]{2,1,0:T(8,128)S(1)} %get-tuple-element.116), channel_id=1, source_target_pairs={{0,11},{1,8},{2,9},{3,10},{4,15},{5,12},{6,13},{7,14},{8,19},{9,16... | collective-permute-start | bytes 122888 | tf_op jit(solution)/shard_map/ppermute | solution.py:32

commit v11 on v10

--- a/solution.py
+++ b/solution.py
@@ -18,7 +18,7 @@
 RATE_HALO = 4
 DRIFT = 6
 TAKE = HALO + DRIFT
-BELOW = TAKE + 1
+BELOW = (TAKE, TAKE, TAKE - 1, TAKE - 1)
 
 
 def shifted(value, by_tm, by_gy, by_gx):
@@ -223,7 +223,9 @@
     for field in range(n_fields):
         for x in range(n_x):
             all_ref[field, pl.ds(x, n_y, stride=n_x), :] = tiles_ref[field, x]
-        high_ref[field] = all_ref[field, pl.ds((n_y - BELOW) * n_x, BELOW * n_x), :]
+        count = BELOW[field]
+        rows = all_ref[field, pl.ds((n_y - count) * n_x, count * n_x), :]
+        high_ref[pl.ds(sum(BELOW[:field]) * n_x, count * n_x), :] = rows
     for field in range(2):
         state_ref[field] = all_ref[field]
 
@@ -257,16 +259,21 @@
     width = n_gy * n_x
     for field in range(2):
         for out_ref, tile_ref, place in zip((start_ref, params_ref), tiles, (0, 2)):
-            collect(out_ref, field, place + field, n_x, -TAKE, [(-BELOW, lows, BELOW)])
+            count, begin = BELOW[place + field], sum(BELOW[: place + field])
+            for gy, low_ref in enumerate(lows):
+                for k in range(count):
+                    row = pl.ds((TAKE - count + k) * width + gy * n_x, n_x)
+                    out_ref[field, row, :] = low_ref[pl.ds((begin + k) * n_x, n_x), :]
             out_ref[field, pl.ds(TAKE * width, n_y * width), :] = tile_ref[field]
     start = rows_of(start_ref, width, -HALO)
     params = rows_of(params_ref, width, -HALO)
     inner = inner_of(inner_refs, width, n_y, DRIFT)
     results, _ = iteration(start, lambda r: params(r)[0], lambda r: params(r)[1], None, inner)
     write_nodes(results, width, n_y, [(0, TAKE)], *outs)
-    for r in range(HALO):
-        for field, value in enumerate((*start(r + DRIFT), *params(r + DRIFT))):
-            outs[-1][pl.ds((4 * TAKE + field * HALO + r) * width, width), :] = value
+    for rows, place, count in ((start, 4 * TAKE, HALO), (params, 4 * TAKE + 2 * HALO, RATE_HALO)):
+        for r in range(count):
+            for field, value in enumerate(rows(r + DRIFT)):
+                outs[-1][pl.ds((place + field * count + r) * width, width), :] = value
 
 
 def write_nodes(results, width, n_y, edges, zero_ref, one_ref, two_ref, *edge_refs):
@@ -305,10 +312,8 @@
 
 def known(width, n_y, start_ref, params_ref, edge_ref):
     return (
-        joined(
-            (-TAKE, rows_of(ref, width, -TAKE)), (n_y, flat_rows(edge_ref, width, 4 * TAKE + place * HALO, n_y, HALO))
-        )
-        for ref, place in ((start_ref, 0), (params_ref, 2))
+        joined((-TAKE, rows_of(ref, width, -TAKE)), (n_y, flat_rows(edge_ref, width, place, n_y, count)))
+        for ref, place, count in ((start_ref, 4 * TAKE, HALO), (params_ref, 4 * TAKE + 2 * HALO, RATE_HALO))
     )
 
 
@@ -430,7 +435,7 @@
         "pack",
         0,
         (jnp.concatenate([sent, feed_rate[None], kill_rate[None]]),),
-        [(2, n_y * n_x, n_z), (4, n_y * n_x, n_z), (4, BELOW * n_x, n_z)],
+        [(2, n_y * n_x, n_z), (4, n_y * n_x, n_z), (sum(BELOW) * n_x, n_z)],
     )
     got = [shifted(state, 1, 0, 0), local]
     got += [shifted(local, 1, -gy, 0) for gy in range(1, n_gy)]
@@ -451,7 +456,7 @@
         "first",
         0,
         [*inner_first, *below],
-        [window, window, *nodes_only, *edge(TAKE, 4 * HALO)],
+        [window, window, *nodes_only, *edge(TAKE, 2 * HALO + 2 * RATE_HALO)],
     )
     zero, one, two, two_edge, pair_edge = nodes
     got = [shifted(two, 1, 0, 0), shifted(two_edge, 1, 0, -1), shifted(pair_edge, 0, 0, -1)]

time: 36.9 us -> 36.2 us (0.981)
  waiting for transfers between devices: 12.7 us -> 11.6 us
    ppermute x12, waiting for transfers between devices: 12.7 us -> 11.6 us  [shifted(): return lax.ppermute(value, AXES, pairs)]
where the time goes in v11:
time: 36.2 us; the launch traced here: 36 us
  starting transfers between devices  18.5 us (51%)
  waiting for transfers between devices  11.6 us (32%)
  Pallas kernels  4.92 us (14%)
  other arithmetic  0.87 us (2%)
    ppermute x12, starting transfers between devices, shifted(): return lax.ppermute(value, AXES, pairs)  18.5 us
    ppermute x12, waiting for transfers between devices, shifted(): return lax.ppermute(value, AXES, pairs)  11.6 us
    pallas_call x9, Pallas kernels, call(): pl.pallas_call(kernel, name=name, out_shape=[jax.ShapeDtypeStruct(shape,...  4.92 us
    select_n x1, other arithmetic, shards(): sent = jnp.where(place == n_tm - 1, initial_state, slice_guess[0])  0.86 us
  transfers between devices with their start and end apart: 12, of which 5 were waited for; matrix products, arithmetic and copies ran while one was open for 0% of the time, Pallas kernels for 6%

profile of v11, /device:TPU:0, one launch (start us, length us, event | category | flops | bytes accessed | tf_op | source)
XLA Modules:
  0.0 36.0 jit_solution(13191466472242613498)
XLA Ops:
  0.0 0.0 copy-start
  0.0 0.0 copy-start.1
  0.0 0.9 %bitcast_select_fusion = f32[2,4,16,128]{3,2,1,0:T(8,128)S(1)} fusion(f32[2,4,16,128]{3,2,1,0:T(8,128)} %param.4, f32[1,2,4,16,128]{4,3,2,1,0:T(8,128)} %param.5, pred[]{:T(512)S(6)} %eq.7), kind=kLoop, calls=%fused_computation.1 | loop fusion | flops 16384 | bytes 196609 | tf_op jit(solution)/shard_map/jit(_where)/select_n | solution.py:432
  0.9 0.0 copy-done
  0.9 0.0 copy-done.1
  0.9 2.5 %collective-permute-start.1 = (f32[4,64,128]{2,1,0:T(8,128)S(1)}, f32[4,64,128]{2,1,0:T(8,128)S(1)}, u32[]{:S(2)}, u32[]{:S(2)}) collective-permute-start(f32[4,64,128]{2,1,0:T(8,128)S(1)} %get-tuple-element.62.refs_1_), channel_id=1, source_target_pairs={{0,12},{1,13},{2,14},{3,15},{4,8},{5,9},{6,10},{7,11},{8,20},{9,21... | collective-permute-start | bytes 393224 | tf_op jit(solution)/shard_map/ppermute | solution.py:32
  3.4 2.7 %collective-permute-start.3 = (f32[168,128]{1,0:T(8,128)S(1)}, f32[168,128]{1,0:T(8,128)S(1)}, u32[]{:S(2)}, u32[]{:S(2)}) collective-permute-start(f32[168,128]{1,0:T(8,128)S(1)} %get-tuple-element.76), channel_id=1, source_target_pairs={{0,13},{1,14},{2,15},{3,12},{4,9},{5,10},{6,11},{7,8},{8,21},{9,22... | collective-permute-start | bytes 258056 | tf_op jit(solution)/shard_map/ppermute | solution.py:32
  6.1 1.1 %collective-permute-start.2 = (f32[168,128]{1,0:T(8,128)S(1)}, f32[168,128]{1,0:T(8,128)S(1)}, u32[]{:S(2)}, u32[]{:S(2)}) collective-permute-start(f32[168,128]{1,0:T(8,128)S(1)} %get-tuple-element.76), channel_id=1, source_target_pairs={{0,9},{1,10},{2,11},{3,8},{4,13},{5,14},{6,15},{7,12},{8,17},{9,18... | collective-permute-start | bytes 258056 | tf_op jit(solution)/shard_map/ppermute | solution.py:32
  7.3 0.5 %collective-permute-start = (f32[2,64,128]{2,1,0:T(8,128)S(1)}, f32[2,64,128]{2,1,0:T(8,128)S(1)}, u32[]{:S(2)}, u32[]{:S(2)}) collective-permute-start(f32[2,64,128]{2,1,0:T(8,128)S(1)} %get-tuple-element.61), channel_id=1, source_target_pairs={{0,8},{1,9},{2,10},{3,11},{4,12},{5,13},{6,14},{7,15},{8,16},{9,17... | collective-permute-start | bytes 196616 | tf_op jit(solution)/shard_map/ppermute | solution.py:32
  7.8 3.6 %collective-permute-done.refs_0_ = f32[2,64,128]{2,1,0:T(8,128)S(1)} collective-permute-done((f32[2,64,128]{2,1,0:T(8,128)S(1)}, f32[2,64,128]{2,1,0:T(8,128)S(1)}, u32[]{:S(2)}, u32[]{:S(2)}) %collective-permute-start) | collective-permute-done | bytes 65568 | tf_op jit(solution)/shard_map/ppermute | solution.py:32
  11.4 0.0 collective-permute-done.1.refs_2_
  11.4 0.4 %inner_first.1 = (f32[2,128,128]{2,1,0:T(8,128)S(1)}, f32[2,128,128]{2,1,0:T(8,128)S(1)}, f32[2,104,128]{2,1,0:T(8,128)S(1)}, f32[2,104,128]{2,1,0:T(8,128)S(1)}...) custom-call(f32[2,64,128]{2,1,0:T(8,128)S(1)} %collective-permute-do, ...), custom_call_target="tpu_custom_call" | custom-call | tf_op jit(solution)/shard_map/inner_first/pallas_call | solution.py:414
  11.9 0.0 collective-permute-done.3.refs_14_
  11.9 1.2 %collective-permute-done.2.refs_13_ = f32[168,128]{1,0:T(8,128)S(1)} collective-permute-done((f32[168,128]{1,0:T(8,128)S(1)}, f32[168,128]{1,0:T(8,128)S(1)}, u32[]{:S(2)}, u32[]{:S(2)}) %collective-permute-start.2) | collective-permute-done | bytes 86048 | tf_op jit(solution)/shard_map/ppermute | solution.py:32
  13.1 0.7 %first.1 = (f32[2,216,128]{2,1,0:T(8,128)S(1)}, f32[2,216,128]{2,1,0:T(8,128)S(1)}, f32[2,192,128]{2,1,0:T(8,128)S(1)}, f32[2,128,128]{2,1,0:T(8,128)S(1)}, f32[...) custom-call(f32[2,128,128]{2,1,0:T(8,128)S(1)} %get-tuple-element.63.refs_0_, ...), custom_call_target="tpu_custom_call" | custom-call | tf_op jit(solution)/shard_map/first/pallas_call | solution.py:414
  13.8 1.3 %collective-permute-start.4 = (f32[496,128]{1,0:T(8,128)S(1)}, f32[496,128]{1,0:T(8,128)S(1)}, u32[]{:S(2)}, u32[]{:S(2)}) collective-permute-start(f32[496,128]{1,0:T(8,128)S(1)} %get-tuple-element.79), channel_id=1, source_target_pairs={{0,3},{1,0},{2,1},{3,2},{4,7},{5,4},{6,5},{7,6},{8,11},{9,8},{10,9... | collective-permute-start | bytes 761864 | tf_op jit(solution)/shard_map/ppermute | solution.py:32
  15.2 0.0 collective-permute-start.5
  15.2 1.9 %collective-permute-start.6 = (f32[2,88,128]{2,1,0:T(8,128)S(1)}, f32[2,88,128]{2,1,0:T(8,128)S(1)}, u32[]{:S(2)}, u32[]{:S(2)}) collective-permute-start(f32[2,88,128]{2,1,0:T(8,128)S(1)} %get-tuple-element.96), channel_id=1, source_target_pairs={{0,11},{1,8},{2,9},{3,10},{4,15},{5,12},{6,13},{7,14},{8,19},{9,16... | collective-permute-start | bytes 270344 | tf_op jit(solution)/shard_map/ppermute | solution.py:32
  17.1 2.7 %collective-permute-done.5.got_ref.refs_13_ = f32[2,128,128]{2,1,0:T(8,128)S(1)} collective-permute-done((f32[2,128,128]{2,1,0:T(8,128)S(1)}, f32[2,128,128]{2,1,0:T(8,128)S(1)}, u32[]{:S(2)}, u32[]{:S(2)}) %collective-permute-start.5) | collective-permute-done | bytes 131104 | tf_op jit(solution)/shard_map/ppermute | solution.py:32
  19.7 0.7 %inner.2 = (f32[2,104,128]{2,1,0:T(8,128)S(1)}, f32[2,104,128]{2,1,0:T(8,128)S(1)}, f32[2,88,128]{2,1,0:T(8,128)S(1)}, f32[2,88,128]{2,1,0:T(8,128)S(1)}, f32[2,...) custom-call(s32[1]{0:T(128)} %bitcast.first_ref, ...), custom_call_target="tpu_custom_call" | custom-call | tf_op jit(solution)/shard_map/inner/pallas_call | solution.py:414
  20.5 2.4 %collective-permute-done.4.pair_edge.refs_15_.known_ref = f32[496,128]{1,0:T(8,128)S(1)} collective-permute-done((f32[496,128]{1,0:T(8,128)S(1)}, f32[496,128]{1,0:T(8,128)S(1)}, u32[]{:S(2)}, u32[]{:S(2)}) %collective-permute-start.4) | collective-permute-done | bytes 253984 | tf_op jit(solution)/shard_map/ppermute | solution.py:32
  22.9 0.2 second_rim.1
  23.1 0.0 collective-permute-done.6.refs_14_
  23.1 0.6 %second.1 = (f32[2,192,128]{2,1,0:T(8,128)S(1)}, f32[2,128,128]{2,1,0:T(8,128)S(1)}, f32[2,128,128]{2,1,0:T(8,128)S(1)}, f32[2,40,128]{2,1,0:T(8,128)S(1)}, f32[...) custom-call(s32[1]{0:T(128)} %bitcast.first_ref, ...), custom_call_target="tpu_custom_call" | custom-call | tf_op jit(solution)/shard_map/second/pallas_call | solution.py:414
  23.7 0.7 %collective-permute-start.7 = (f32[2,128,128]{2,1,0:T(8,128)S(1)}, f32[2,128,128]{2,1,0:T(8,128)S(1)}, u32[]{:S(2)}, u32[]{:S(2)}) collective-permute-start(f32[2,128,128]{2,1,0:T(8,128)S(1)} %get-tuple-element.99.two_ref), channel_id=1, source_target_pairs={{0,8},{1,9},{2,10},{3,11},{4,12},{5,13},{6,14},{7,15},{8,16},{9,17... | collective-permute-start | bytes 393224 | tf_op jit(solution)/shard_map/ppermute | solution.py:32
  24.5 0.0 collective-permute-start.8
  24.5 3.8 %collective-permute-start.9 = (f32[160,128]{1,0:T(8,128)S(1)}, f32[160,128]{1,0:T(8,128)S(1)}, u32[]{:S(2)}, u32[]{:S(2)}) collective-permute-start(f32[160,128]{1,0:T(8,128)S(1)} %get-tuple-element.112), channel_id=1, source_target_pairs={{0,3},{1,0},{2,1},{3,2},{4,7},{5,4},{6,5},{7,6},{8,11},{9,8},{10,9... | collective-permute-start | bytes 245768 | tf_op jit(solution)/shard_map/ppermute | solution.py:32
  28.3 0.0 collective-permute-start.10
  28.3 3.9 %collective-permute-start.11 = (f32[2,40,128]{2,1,0:T(8,128)S(1)}, f32[2,40,128]{2,1,0:T(8,128)S(1)}, u32[]{:S(2)}, u32[]{:S(2)}) collective-permute-start(f32[2,40,128]{2,1,0:T(8,128)S(1)} %get-tuple-element.116), channel_id=1, source_target_pairs={{0,11},{1,8},{2,9},{3,10},{4,15},{5,12},{6,13},{7,14},{8,19},{9,16... | collective-permute-start | bytes 122888 | tf_op jit(solution)/shard_map/ppermute | solution.py:32
  32.1 0.0 collective-permute-done.8.pair_low
  32.2 0.0 collective-permute-done.9.pair_high
  32.2 0.2 later_rim.1
  32.3 0.0 collective-permute-done.7.got_ref.refs_13_
  32.3 0.8 %inner.3 = (f32[2,112,128]{2,1,0:T(8,128)S(1)}, f32[2,112,128]{2,1,0:T(8,128)S(1)}, f32[2,96,128]{2,1,0:T(8,128)S(1)}, f32[2,96,128]{2,1,0:T(8,128)S(1)}, f32[2,...) custom-call(s32[1]{0:T(128)} %bitcast.first_ref, ...), custom_call_target="tpu_custom_call" | custom-call | tf_op jit(solution)/shard_map/inner/pallas_call | solution.py:414
  33.1 1.6 %collective-permute-done.10.refs_14_ = f32[2,40,128]{2,1,0:T(8,128)S(1)} collective-permute-done((f32[2,40,128]{2,1,0:T(8,128)S(1)}, f32[2,40,128]{2,1,0:T(8,128)S(1)}, u32[]{:S(2)}, u32[]{:S(2)}) %collective-permute-start.10) | collective-permute-done | bytes 40992 | tf_op jit(solution)/shard_map/ppermute | solution.py:32
  34.8 0.0 collective-permute-done.11.refs_15_
  34.8 1.3 %last.1 = f32[2,4,16,128]{3,2,1,0:T(8,128)} custom-call(s32[1]{0:T(128)} %bitcast.first_ref, f32[2,216,128]{2,1,0:T(8,128)S(1)} %get-tuple-element.77.start_ref, f32[2,216,128]{2,1,0:T(8,128)S(1)} %get-tuple-element.78.params_ref, f32[496,128]{1,0:T(8,128)S(1)} %collective-permute-done.4.pair_edge.refs_15_.known_ref, ...), custom_call_target="tpu_custom_call" | custom-call | tf_op jit(solution)/shard_map/last/pallas_call | solution.py:414
  (2 shorter events, 0.0 us)
Async XLA Ops:
  0.0 0.9 %copy-start = (f32[4,16,128]{2,1,0:T(8,128)S(1)}, f32[4,16,128]{2,1,0:T(8,128)}, u32[]{:S(2)}) copy-start(f32[4,16,128]{2,1,0:T(8,128)} %param.7) | copy-start | bytes 98308
  0.0 0.9 %copy-start.1 = (f32[4,16,128]{2,1,0:T(8,128)S(1)}, f32[4,16,128]{2,1,0:T(8,128)}, u32[]{:S(2)}) copy-start(f32[4,16,128]{2,1,0:T(8,128)} %param.6) | copy-start | bytes 98308
  0.9 10.5 %collective-permute-start.1 = (f32[4,64,128]{2,1,0:T(8,128)S(1)}, f32[4,64,128]{2,1,0:T(8,128)S(1)}, u32[]{:S(2)}, u32[]{:S(2)}) collective-permute-start(f32[4,64,128]{2,1,0:T(8,128)S(1)} %get-tuple-element.62.refs_1_), channel_id=1, source_target_pairs={{0,12},{1,13},{2,14},{3,15},{4,8},{5,9},{6,10},{7,11},{8,20},{9,21... | collective-permute-start | bytes 393224 | tf_op jit(solution)/shard_map/ppermute | solution.py:32
  3.4 8.5 %collective-permute-start.3 = (f32[168,128]{1,0:T(8,128)S(1)}, f32[168,128]{1,0:T(8,128)S(1)}, u32[]{:S(2)}, u32[]{:S(2)}) collective-permute-start(f32[168,128]{1,0:T(8,128)S(1)} %get-tuple-element.76), channel_id=1, source_target_pairs={{0,13},{1,14},{2,15},{3,12},{4,9},{5,10},{6,11},{7,8},{8,21},{9,22... | collective-permute-start | bytes 258056 | tf_op jit(solution)/shard_map/ppermute | solution.py:32
  6.1 7.0 %collective-permute-start.2 = (f32[168,128]{1,0:T(8,128)S(1)}, f32[168,128]{1,0:T(8,128)S(1)}, u32[]{:S(2)}, u32[]{:S(2)}) collective-permute-start(f32[168,128]{1,0:T(8,128)S(1)} %get-tuple-element.76), channel_id=1, source_target_pairs={{0,9},{1,10},{2,11},{3,8},{4,13},{5,14},{6,15},{7,12},{8,17},{9,18... | collective-permute-start | bytes 258056 | tf_op jit(solution)/shard_map/ppermute | solution.py:32
  7.3 4.2 %collective-permute-start = (f32[2,64,128]{2,1,0:T(8,128)S(1)}, f32[2,64,128]{2,1,0:T(8,128)S(1)}, u32[]{:S(2)}, u32[]{:S(2)}) collective-permute-start(f32[2,64,128]{2,1,0:T(8,128)S(1)} %get-tuple-element.61), channel_id=1, source_target_pairs={{0,8},{1,9},{2,10},{3,11},{4,12},{5,13},{6,14},{7,15},{8,16},{9,17... | collective-permute-start | bytes 196616 | tf_op jit(solution)/shard_map/ppermute | solution.py:32
  13.8 9.0 %collective-permute-start.4 = (f32[496,128]{1,0:T(8,128)S(1)}, f32[496,128]{1,0:T(8,128)S(1)}, u32[]{:S(2)}, u32[]{:S(2)}) collective-permute-start(f32[496,128]{1,0:T(8,128)S(1)} %get-tuple-element.79), channel_id=1, source_target_pairs={{0,3},{1,0},{2,1},{3,2},{4,7},{5,4},{6,5},{7,6},{8,11},{9,8},{10,9... | collective-permute-start | bytes 761864 | tf_op jit(solution)/shard_map/ppermute | solution.py:32
  15.2 4.6 %collective-permute-start.5 = (f32[2,128,128]{2,1,0:T(8,128)S(1)}, f32[2,128,128]{2,1,0:T(8,128)S(1)}, u32[]{:S(2)}, u32[]{:S(2)}) collective-permute-start(f32[2,128,128]{2,1,0:T(8,128)S(1)} %get-tuple-element.82.two_ref), channel_id=1, source_target_pairs={{0,8},{1,9},{2,10},{3,11},{4,12},{5,13},{6,14},{7,15},{8,16},{9,17... | collective-permute-start | bytes 393224 | tf_op jit(solution)/shard_map/ppermute | solution.py:32
  15.2 7.9 %collective-permute-start.6 = (f32[2,88,128]{2,1,0:T(8,128)S(1)}, f32[2,88,128]{2,1,0:T(8,128)S(1)}, u32[]{:S(2)}, u32[]{:S(2)}) collective-permute-start(f32[2,88,128]{2,1,0:T(8,128)S(1)} %get-tuple-element.96), channel_id=1, source_target_pairs={{0,11},{1,8},{2,9},{3,10},{4,15},{5,12},{6,13},{7,14},{8,19},{9,16... | collective-permute-start | bytes 270344 | tf_op jit(solution)/shard_map/ppermute | solution.py:32
  23.7 8.6 %collective-permute-start.7 = (f32[2,128,128]{2,1,0:T(8,128)S(1)}, f32[2,128,128]{2,1,0:T(8,128)S(1)}, u32[]{:S(2)}, u32[]{:S(2)}) collective-permute-start(f32[2,128,128]{2,1,0:T(8,128)S(1)} %get-tuple-element.99.two_ref), channel_id=1, source_target_pairs={{0,8},{1,9},{2,10},{3,11},{4,12},{5,13},{6,14},{7,15},{8,16},{9,17... | collective-permute-start | bytes 393224 | tf_op jit(solution)/shard_map/ppermute | solution.py:32
  24.5 7.7 %collective-permute-start.8 = (f32[160,128]{1,0:T(8,128)S(1)}, f32[160,128]{1,0:T(8,128)S(1)}, u32[]{:S(2)}, u32[]{:S(2)}) collective-permute-start(f32[160,128]{1,0:T(8,128)S(1)} %get-tuple-element.111), channel_id=1, source_target_pairs={{0,1},{1,2},{2,3},{3,0},{4,5},{5,6},{6,7},{7,4},{8,9},{9,10},{10,1... | collective-permute-start | bytes 245768 | tf_op jit(solution)/shard_map/ppermute | solution.py:32
  24.5 7.7 %collective-permute-start.9 = (f32[160,128]{1,0:T(8,128)S(1)}, f32[160,128]{1,0:T(8,128)S(1)}, u32[]{:S(2)}, u32[]{:S(2)}) collective-permute-start(f32[160,128]{1,0:T(8,128)S(1)} %get-tuple-element.112), channel_id=1, source_target_pairs={{0,3},{1,0},{2,1},{3,2},{4,7},{5,4},{6,5},{7,6},{8,11},{9,8},{10,9... | collective-permute-start | bytes 245768 | tf_op jit(solution)/shard_map/ppermute | solution.py:32
  28.3 6.5 %collective-permute-start.10 = (f32[2,40,128]{2,1,0:T(8,128)S(1)}, f32[2,40,128]{2,1,0:T(8,128)S(1)}, u32[]{:S(2)}, u32[]{:S(2)}) collective-permute-start(f32[2,40,128]{2,1,0:T(8,128)S(1)} %get-tuple-element.115), channel_id=1, source_target_pairs={{0,9},{1,10},{2,11},{3,8},{4,13},{5,14},{6,15},{7,12},{8,17},{9,18... | collective-permute-start | bytes 122888 | tf_op jit(solution)/shard_map/ppermute | solution.py:32
  28.3 6.5 %collective-permute-start.11 = (f32[2,40,128]{2,1,0:T(8,128)S(1)}, f32[2,40,128]{2,1,0:T(8,128)S(1)}, u32[]{:S(2)}, u32[]{:S(2)}) collective-permute-start(f32[2,40,128]{2,1,0:T(8,128)S(1)} %get-tuple-element.116), channel_id=1, source_target_pairs={{0,11},{1,8},{2,9},{3,10},{4,15},{5,12},{6,13},{7,14},{8,19},{9,16... | collective-permute-start | bytes 122888 | tf_op jit(solution)/shard_map/ppermute | solution.py:32

commit v12 on v11

--- a/solution.py
+++ b/solution.py
@@ -30,6 +30,24 @@
                 target = ((t + by_tm) % n_tm * n_gy + (y + by_gy) % n_gy) * n_gx + (x + by_gx) % n_gx
                 pairs.append(((t * n_gy + y) * n_gx + x, target))
     return lax.ppermute(value, AXES, pairs)
+
+
+def from_beside(to_above, to_below, by_tm):
+    n_tm, n_gy, n_gx = (lax.axis_size(axis) for axis in AXES)
+    if n_gx % 2:
+        return shifted(to_above, by_tm, 0, 1), shifted(to_below, by_tm, 0, -1)
+    even = lax.axis_index("gx") % 2 == 0
+    got = []
+    for value, odd in ((jnp.where(even, to_above, to_below), 0), (jnp.where(even, to_below, to_above), 1)):
+        pairs = []
+        for t in range(n_tm):
+            for y in range(n_gy):
+                for x in range(n_gx):
+                    beside = (x + (1 if x % 2 == odd else -1)) % n_gx
+                    target = ((t + by_tm) % n_tm * n_gy + y) * n_gx + beside
+                    pairs.append(((t * n_gy + y) * n_gx + x, target))
+        got.append(lax.ppermute(value, AXES, pairs))
+    return jnp.where(even, got[1], got[0]), jnp.where(even, got[0], got[1])
 
 
 def near(row, distance, axis):
@@ -486,8 +504,7 @@
     )
     for sweep_index in range(2, ITERS):
         zero, one, two, two_low, pair_low, two_high, pair_high = nodes
-        got = [shifted(two, 1, 0, 0), shifted(two_high, 1, 0, 1), shifted(two_low, 1, 0, -1)]
-        got += [shifted(pair_high, 0, 0, 1), shifted(pair_low, 0, 0, -1)]
+        got = [shifted(two, 1, 0, 0), *from_beside(two_high, two_low, 1), *from_beside(pair_high, pair_low, 0)]
         done = sweep_index + 1 == ITERS
         later_rim = rim(later_rim_kernel, "later_rim", 0, (start, params, known_edge, zero, one, two, *got[3:]))
         nodes = call(

time: 36.2 us -> 37.7 us (1.041)
  waiting for transfers between devices: 11.6 us -> 15.7 us
  starting transfers between devices: 18.5 us -> 15.8 us
    ppermute x12 -> x8, starting transfers between devices: 18.5 us -> 10.1 us  [shifted(): return lax.ppermute(value, AXES, pairs)]
    ppermute x0 -> x4, waiting for transfers between devices: none -> 5.73 us  [from_beside(): got.append(lax.ppermute(value, AXES, pairs))]
    ppermute x0 -> x4, starting transfers between devices: none -> 5.72 us  [from_beside(): got.append(lax.ppermute(value, AXES, pairs))]
    ppermute x12 -> x8, waiting for transfers between devices: 11.6 us -> 9.98 us  [shifted(): return lax.ppermute(value, AXES, pairs)]
  transfers between devices with their start and end apart: 12 -> 12, of which waited for: 5 -> 7; matrix products, arithmetic and copies ran while one was open for 0% -> 0% of each run, Pallas kernels for 6% -> 4%
where the time goes in v12:
time: 37.7 us; the launch traced here: 37.5 us
  starting transfers between devices  15.8 us (42%)
  waiting for transfers between devices  15.7 us (42%)
  Pallas kernels  4.93 us (13%)
  other arithmetic  0.92 us (2%)
    ppermute x8, starting transfers between devices, shifted(): return lax.ppermute(value, AXES, pairs)  10.1 us
    ppermute x8, waiting for transfers between devices, shifted(): return lax.ppermute(value, AXES, pairs)  9.98 us
    ppermute x4, waiting for transfers between devices, from_beside(): got.append(lax.ppermute(value, AXES, pairs))  5.73 us
    ppermute x4, starting transfers between devices, from_beside(): got.append(lax.ppermute(value, AXES, pairs))  5.72 us
    pallas_call x9, Pallas kernels, call(): pl.pallas_call(kernel, name=name, out_shape=[jax.ShapeDtypeStruct(shape,...  4.93 us
    select_n x1, other arithmetic, shards(): sent = jnp.where(place == n_tm - 1, initial_state, slice_guess[0])  0.86 us
  transfers between devices with their start and end apart: 12, of which 7 were waited for; matrix products, arithmetic and copies ran while one was open for 0% of the time, Pallas kernels for 4%

profile of v12, /device:TPU:0, one launch (start us, length us, event | category | flops | bytes accessed | tf_op | source)
XLA Modules:
  0.0 37.5 jit_solution(2174637236364845177)
XLA Ops:
  0.0 0.0 copy-start
  0.0 0.0 copy-start.1
  0.0 0.9 %bitcast_select_fusion = f32[2,4,16,128]{3,2,1,0:T(8,128)S(1)} fusion(f32[2,4,16,128]{3,2,1,0:T(8,128)} %param.4, f32[1,2,4,16,128]{4,3,2,1,0:T(8,128)} %param.5, pred[]{:T(512)S(6)} %eq.14), kind=kLoop, calls=%fused_computation.1 | loop fusion | flops 16384 | bytes 196609 | tf_op jit(solution)/shard_map/jit(_where)/select_n | solution.py:450
  0.9 0.0 copy-done
  0.9 0.0 copy-done.1
  0.9 2.5 %collective-permute-start.1 = (f32[4,64,128]{2,1,0:T(8,128)S(1)}, f32[4,64,128]{2,1,0:T(8,128)S(1)}, u32[]{:S(2)}, u32[]{:S(2)}) collective-permute-start(f32[4,64,128]{2,1,0:T(8,128)S(1)} %get-tuple-element.62.refs_1_), channel_id=1, source_target_pairs={{0,12},{1,13},{2,14},{3,15},{4,8},{5,9},{6,10},{7,11},{8,20},{9,21... | collective-permute-start | bytes 393224 | tf_op jit(solution)/shard_map/ppermute | solution.py:32
  3.4 2.7 %collective-permute-start.3 = (f32[168,128]{1,0:T(8,128)S(1)}, f32[168,128]{1,0:T(8,128)S(1)}, u32[]{:S(2)}, u32[]{:S(2)}) collective-permute-start(f32[168,128]{1,0:T(8,128)S(1)} %get-tuple-element.76), channel_id=1, source_target_pairs={{0,13},{1,14},{2,15},{3,12},{4,9},{5,10},{6,11},{7,8},{8,21},{9,22... | collective-permute-start | bytes 258056 | tf_op jit(solution)/shard_map/ppermute | solution.py:32
  6.1 1.1 %collective-permute-start.2 = (f32[168,128]{1,0:T(8,128)S(1)}, f32[168,128]{1,0:T(8,128)S(1)}, u32[]{:S(2)}, u32[]{:S(2)}) collective-permute-start(f32[168,128]{1,0:T(8,128)S(1)} %get-tuple-element.76), channel_id=1, source_target_pairs={{0,9},{1,10},{2,11},{3,8},{4,13},{5,14},{6,15},{7,12},{8,17},{9,18... | collective-permute-start | bytes 258056 | tf_op jit(solution)/shard_map/ppermute | solution.py:32
  7.3 0.5 %collective-permute-start = (f32[2,64,128]{2,1,0:T(8,128)S(1)}, f32[2,64,128]{2,1,0:T(8,128)S(1)}, u32[]{:S(2)}, u32[]{:S(2)}) collective-permute-start(f32[2,64,128]{2,1,0:T(8,128)S(1)} %get-tuple-element.61), channel_id=1, source_target_pairs={{0,8},{1,9},{2,10},{3,11},{4,12},{5,13},{6,14},{7,15},{8,16},{9,17... | collective-permute-start | bytes 196616 | tf_op jit(solution)/shard_map/ppermute | solution.py:32
  7.8 3.6 %collective-permute-done.refs_0_ = f32[2,64,128]{2,1,0:T(8,128)S(1)} collective-permute-done((f32[2,64,128]{2,1,0:T(8,128)S(1)}, f32[2,64,128]{2,1,0:T(8,128)S(1)}, u32[]{:S(2)}, u32[]{:S(2)}) %collective-permute-start) | collective-permute-done | bytes 65568 | tf_op jit(solution)/shard_map/ppermute | solution.py:32
  11.4 0.0 collective-permute-done.1.refs_2_
  11.4 0.4 %inner_first.1 = (f32[2,128,128]{2,1,0:T(8,128)S(1)}, f32[2,128,128]{2,1,0:T(8,128)S(1)}, f32[2,104,128]{2,1,0:T(8,128)S(1)}, f32[2,104,128]{2,1,0:T(8,128)S(1)}...) custom-call(f32[2,64,128]{2,1,0:T(8,128)S(1)} %collective-permute-do, ...), custom_call_target="tpu_custom_call" | custom-call | tf_op jit(solution)/shard_map/inner_first/pallas_call | solution.py:432
  11.9 0.0 collective-permute-done.3.refs_14_
  11.9 1.2 %collective-permute-done.2.refs_13_ = f32[168,128]{1,0:T(8,128)S(1)} collective-permute-done((f32[168,128]{1,0:T(8,128)S(1)}, f32[168,128]{1,0:T(8,128)S(1)}, u32[]{:S(2)}, u32[]{:S(2)}) %collective-permute-start.2) | collective-permute-done | bytes 86048 | tf_op jit(solution)/shard_map/ppermute | solution.py:32
  13.1 0.7 %first.1 = (f32[2,216,128]{2,1,0:T(8,128)S(1)}, f32[2,216,128]{2,1,0:T(8,128)S(1)}, f32[2,192,128]{2,1,0:T(8,128)S(1)}, f32[2,128,128]{2,1,0:T(8,128)S(1)}, f32[...) custom-call(f32[2,128,128]{2,1,0:T(8,128)S(1)} %get-tuple-element.63.refs_0_, ...), custom_call_target="tpu_custom_call" | custom-call | tf_op jit(solution)/shard_map/first/pallas_call | solution.py:432
  13.8 1.3 %collective-permute-start.4 = (f32[496,128]{1,0:T(8,128)S(1)}, f32[496,128]{1,0:T(8,128)S(1)}, u32[]{:S(2)}, u32[]{:S(2)}) collective-permute-start(f32[496,128]{1,0:T(8,128)S(1)} %get-tuple-element.79), channel_id=1, source_target_pairs={{0,3},{1,0},{2,1},{3,2},{4,7},{5,4},{6,5},{7,6},{8,11},{9,8},{10,9... | collective-permute-start | bytes 761864 | tf_op jit(solution)/shard_map/ppermute | solution.py:32
  15.2 0.0 collective-permute-start.5
  15.2 1.9 %collective-permute-start.6 = (f32[2,88,128]{2,1,0:T(8,128)S(1)}, f32[2,88,128]{2,1,0:T(8,128)S(1)}, u32[]{:S(2)}, u32[]{:S(2)}) collective-permute-start(f32[2,88,128]{2,1,0:T(8,128)S(1)} %get-tuple-element.96), channel_id=1, source_target_pairs={{0,11},{1,8},{2,9},{3,10},{4,15},{5,12},{6,13},{7,14},{8,19},{9,16... | collective-permute-start | bytes 270344 | tf_op jit(solution)/shard_map/ppermute | solution.py:32
  17.1 2.7 %collective-permute-done.5.got_ref.refs_13_ = f32[2,128,128]{2,1,0:T(8,128)S(1)} collective-permute-done((f32[2,128,128]{2,1,0:T(8,128)S(1)}, f32[2,128,128]{2,1,0:T(8,128)S(1)}, u32[]{:S(2)}, u32[]{:S(2)}) %collective-permute-start.5) | collective-permute-done | bytes 131104 | tf_op jit(solution)/shard_map/ppermute | solution.py:32
  19.7 0.7 %inner.2 = (f32[2,104,128]{2,1,0:T(8,128)S(1)}, f32[2,104,128]{2,1,0:T(8,128)S(1)}, f32[2,88,128]{2,1,0:T(8,128)S(1)}, f32[2,88,128]{2,1,0:T(8,128)S(1)}, f32[2,...) custom-call(s32[1]{0:T(128)} %bitcast.first_ref, ...), custom_call_target="tpu_custom_call" | custom-call | tf_op jit(solution)/shard_map/inner/pallas_call | solution.py:432
  20.5 2.4 %collective-permute-done.4.pair_edge.refs_15_.known_ref = f32[496,128]{1,0:T(8,128)S(1)} collective-permute-done((f32[496,128]{1,0:T(8,128)S(1)}, f32[496,128]{1,0:T(8,128)S(1)}, u32[]{:S(2)}, u32[]{:S(2)}) %collective-permute-start.4) | collective-permute-done | bytes 253984 | tf_op jit(solution)/shard_map/ppermute | solution.py:32
  22.9 0.2 second_rim.1
  23.1 0.0 collective-permute-done.6.refs_14_
  23.1 0.6 %second.1 = (f32[2,192,128]{2,1,0:T(8,128)S(1)}, f32[2,128,128]{2,1,0:T(8,128)S(1)}, f32[2,128,128]{2,1,0:T(8,128)S(1)}, f32[2,40,128]{2,1,0:T(8,128)S(1)}, f32[...) custom-call(s32[1]{0:T(128)} %bitcast.first_ref, ...), custom_call_target="tpu_custom_call" | custom-call | tf_op jit(solution)/shard_map/second/pallas_call | solution.py:432
  23.7 0.1 collective-permute-start.11
  23.8 3.4 %collective-permute-start.10 = (f32[2,40,128]{2,1,0:T(8,128)S(1)}, f32[2,40,128]{2,1,0:T(8,128)S(1)}, u32[]{:S(2)}, u32[]{:S(2)}) collective-permute-start(f32[2,40,128]{2,1,0:T(8,128)S(1)} %get-tuple-element.124), channel_id=1, source_target_pairs={{0,11},{1,10},{2,9},{3,8},{4,15},{5,14},{6,13},{7,12},{8,19},{9,18... | collective-permute-start | bytes 122888 | tf_op jit(solution)/shard_map/ppermute | solution.py:49
  27.2 1.5 %collective-permute-start.9 = (f32[160,128]{1,0:T(8,128)S(1)}, f32[160,128]{1,0:T(8,128)S(1)}, u32[]{:S(2)}, u32[]{:S(2)}) collective-permute-start(f32[160,128]{1,0:T(8,128)S(1)} %get-tuple-element.119), channel_id=1, source_target_pairs={{0,1},{1,0},{2,3},{3,2},{4,5},{5,4},{6,7},{7,6},{8,9},{9,8},{10,11... | collective-permute-start | bytes 245768 | tf_op jit(solution)/shard_map/ppermute | solution.py:49
  28.7 0.8 %collective-permute-start.8 = (f32[160,128]{1,0:T(8,128)S(1)}, f32[160,128]{1,0:T(8,128)S(1)}, u32[]{:S(2)}, u32[]{:S(2)}) collective-permute-start(f32[160,128]{1,0:T(8,128)S(1)} %get-tuple-element.120), channel_id=1, source_target_pairs={{0,3},{1,2},{2,1},{3,0},{4,7},{5,6},{6,5},{7,4},{8,11},{9,10},{10,... | collective-permute-start | bytes 245768 | tf_op jit(solution)/shard_map/ppermute | solution.py:49
  29.5 0.0 collective-permute-start.7
  29.5 0.0 collective-permute-done.11
  29.5 1.4 %collective-permute-done.10 = f32[2,40,128]{2,1,0:T(8,128)S(1)} collective-permute-done((f32[2,40,128]{2,1,0:T(8,128)S(1)}, f32[2,40,128]{2,1,0:T(8,128)S(1)}, u32[]{:S(2)}, u32[]{:S(2)}) %collective-permute-start.10) | collective-permute-done | bytes 40992 | tf_op jit(solution)/shard_map/ppermute | solution.py:49
  30.9 1.5 %collective-permute-done.9 = f32[160,128]{1,0:T(8,128)S(1)} collective-permute-done((f32[160,128]{1,0:T(8,128)S(1)}, f32[160,128]{1,0:T(8,128)S(1)}, u32[]{:S(2)}, u32[]{:S(2)}) %collective-permute-start.9) | collective-permute-done | bytes 81952 | tf_op jit(solution)/shard_map/ppermute | solution.py:49
  32.4 2.8 %collective-permute-done.8 = f32[160,128]{1,0:T(8,128)S(1)} collective-permute-done((f32[160,128]{1,0:T(8,128)S(1)}, f32[160,128]{1,0:T(8,128)S(1)}, u32[]{:S(2)}, u32[]{:S(2)}) %collective-permute-start.8) | collective-permute-done | bytes 81952 | tf_op jit(solution)/shard_map/ppermute | solution.py:49
  35.2 0.2 later_rim.1
  35.4 0.0 collective-permute-done.7.got_ref.refs_13_
  35.4 0.8 %inner.3 = (f32[2,112,128]{2,1,0:T(8,128)S(1)}, f32[2,112,128]{2,1,0:T(8,128)S(1)}, f32[2,96,128]{2,1,0:T(8,128)S(1)}, f32[2,96,128]{2,1,0:T(8,128)S(1)}, f32[2,...) custom-call(s32[1]{0:T(128)} %bitcast.first_ref, ...), custom_call_target="tpu_custom_call" | custom-call | tf_op jit(solution)/shard_map/inner/pallas_call | solution.py:432
  36.2 1.3 %last.1 = f32[2,4,16,128]{3,2,1,0:T(8,128)} custom-call(s32[1]{0:T(128)} %bitcast.first_ref, f32[2,216,128]{2,1,0:T(8,128)S(1)} %get-tuple-element.77.start_ref, f32[2,216,128]{2,1,0:T(8,128)S(1)} %get-tuple-element.78.params_ref, f32[496,128]{1,0:T(8,128)S(1)} %collective-permute-done.4.pair_edge.refs_15_.known_ref, ...), custom_call_target="tpu_custom_call" | custom-call | tf_op jit(solution)/shard_map/last/pallas_call | solution.py:432
  (6 shorter events, 0.1 us)
Async XLA Ops:
  0.0 0.9 %copy-start = (f32[4,16,128]{2,1,0:T(8,128)S(1)}, f32[4,16,128]{2,1,0:T(8,128)}, u32[]{:S(2)}) copy-start(f32[4,16,128]{2,1,0:T(8,128)} %param.7) | copy-start | bytes 98308
  0.0 0.9 %copy-start.1 = (f32[4,16,128]{2,1,0:T(8,128)S(1)}, f32[4,16,128]{2,1,0:T(8,128)}, u32[]{:S(2)}) copy-start(f32[4,16,128]{2,1,0:T(8,128)} %param.6) | copy-start | bytes 98308
  0.9 10.5 %collective-permute-start.1 = (f32[4,64,128]{2,1,0:T(8,128)S(1)}, f32[4,64,128]{2,1,0:T(8,128)S(1)}, u32[]{:S(2)}, u32[]{:S(2)}) collective-permute-start(f32[4,64,128]{2,1,0:T(8,128)S(1)} %get-tuple-element.62.refs_1_), channel_id=1, source_target_pairs={{0,12},{1,13},{2,14},{3,15},{4,8},{5,9},{6,10},{7,11},{8,20},{9,21... | collective-permute-start | bytes 393224 | tf_op jit(solution)/shard_map/ppermute | solution.py:32
  3.4 8.5 %collective-permute-start.3 = (f32[168,128]{1,0:T(8,128)S(1)}, f32[168,128]{1,0:T(8,128)S(1)}, u32[]{:S(2)}, u32[]{:S(2)}) collective-permute-start(f32[168,128]{1,0:T(8,128)S(1)} %get-tuple-element.76), channel_id=1, source_target_pairs={{0,13},{1,14},{2,15},{3,12},{4,9},{5,10},{6,11},{7,8},{8,21},{9,22... | collective-permute-start | bytes 258056 | tf_op jit(solution)/shard_map/ppermute | solution.py:32
  6.1 7.0 %collective-permute-start.2 = (f32[168,128]{1,0:T(8,128)S(1)}, f32[168,128]{1,0:T(8,128)S(1)}, u32[]{:S(2)}, u32[]{:S(2)}) collective-permute-start(f32[168,128]{1,0:T(8,128)S(1)} %get-tuple-element.76), channel_id=1, source_target_pairs={{0,9},{1,10},{2,11},{3,8},{4,13},{5,14},{6,15},{7,12},{8,17},{9,18... | collective-permute-start | bytes 258056 | tf_op jit(solution)/shard_map/ppermute | solution.py:32
  7.3 4.2 %collective-permute-start = (f32[2,64,128]{2,1,0:T(8,128)S(1)}, f32[2,64,128]{2,1,0:T(8,128)S(1)}, u32[]{:S(2)}, u32[]{:S(2)}) collective-permute-start(f32[2,64,128]{2,1,0:T(8,128)S(1)} %get-tuple-element.61), channel_id=1, source_target_pairs={{0,8},{1,9},{2,10},{3,11},{4,12},{5,13},{6,14},{7,15},{8,16},{9,17... | collective-permute-start | bytes 196616 | tf_op jit(solution)/shard_map/ppermute | solution.py:32
  13.8 9.0 %collective-permute-start.4 = (f32[496,128]{1,0:T(8,128)S(1)}, f32[496,128]{1,0:T(8,128)S(1)}, u32[]{:S(2)}, u32[]{:S(2)}) collective-permute-start(f32[496,128]{1,0:T(8,128)S(1)} %get-tuple-element.79), channel_id=1, source_target_pairs={{0,3},{1,0},{2,1},{3,2},{4,7},{5,4},{6,5},{7,6},{8,11},{9,8},{10,9... | collective-permute-start | bytes 761864 | tf_op jit(solution)/shard_map/ppermute | solution.py:32
  15.2 4.6 %collective-permute-start.5 = (f32[2,128,128]{2,1,0:T(8,128)S(1)}, f32[2,128,128]{2,1,0:T(8,128)S(1)}, u32[]{:S(2)}, u32[]{:S(2)}) collective-permute-start(f32[2,128,128]{2,1,0:T(8,128)S(1)} %get-tuple-element.82.two_ref), channel_id=1, source_target_pairs={{0,8},{1,9},{2,10},{3,11},{4,12},{5,13},{6,14},{7,15},{8,16},{9,17... | collective-permute-start | bytes 393224 | tf_op jit(solution)/shard_map/ppermute | solution.py:32
  15.2 7.9 %collective-permute-start.6 = (f32[2,88,128]{2,1,0:T(8,128)S(1)}, f32[2,88,128]{2,1,0:T(8,128)S(1)}, u32[]{:S(2)}, u32[]{:S(2)}) collective-permute-start(f32[2,88,128]{2,1,0:T(8,128)S(1)} %get-tuple-element.96), channel_id=1, source_target_pairs={{0,11},{1,8},{2,9},{3,10},{4,15},{5,12},{6,13},{7,14},{8,19},{9,16... | collective-permute-start | bytes 270344 | tf_op jit(solution)/shard_map/ppermute | solution.py:32
  23.7 5.7 %collective-permute-start.11 = (f32[2,40,128]{2,1,0:T(8,128)S(1)}, f32[2,40,128]{2,1,0:T(8,128)S(1)}, u32[]{:S(2)}, u32[]{:S(2)}) collective-permute-start(f32[2,40,128]{2,1,0:T(8,128)S(1)} %get-tuple-element.123), channel_id=1, source_target_pairs={{0,9},{1,8},{2,11},{3,10},{4,13},{5,12},{6,15},{7,14},{8,17},{9,16... | collective-permute-start | bytes 122888 | tf_op jit(solution)/shard_map/ppermute | solution.py:49
  23.8 7.1 %collective-permute-start.10 = (f32[2,40,128]{2,1,0:T(8,128)S(1)}, f32[2,40,128]{2,1,0:T(8,128)S(1)}, u32[]{:S(2)}, u32[]{:S(2)}) collective-permute-start(f32[2,40,128]{2,1,0:T(8,128)S(1)} %get-tuple-element.124), channel_id=1, source_target_pairs={{0,11},{1,10},{2,9},{3,8},{4,15},{5,14},{6,13},{7,12},{8,19},{9,18... | collective-permute-start | bytes 122888 | tf_op jit(solution)/shard_map/ppermute | solution.py:49
  27.2 5.2 %collective-permute-start.9 = (f32[160,128]{1,0:T(8,128)S(1)}, f32[160,128]{1,0:T(8,128)S(1)}, u32[]{:S(2)}, u32[]{:S(2)}) collective-permute-start(f32[160,128]{1,0:T(8,128)S(1)} %get-tuple-element.119), channel_id=1, source_target_pairs={{0,1},{1,0},{2,3},{3,2},{4,5},{5,4},{6,7},{7,6},{8,9},{9,8},{10,11... | collective-permute-start | bytes 245768 | tf_op jit(solution)/shard_map/ppermute | solution.py:49
  28.7 6.5 %collective-permute-start.8 = (f32[160,128]{1,0:T(8,128)S(1)}, f32[160,128]{1,0:T(8,128)S(1)}, u32[]{:S(2)}, u32[]{:S(2)}) collective-permute-start(f32[160,128]{1,0:T(8,128)S(1)} %get-tuple-element.120), channel_id=1, source_target_pairs={{0,3},{1,2},{2,1},{3,0},{4,7},{5,6},{6,5},{7,4},{8,11},{9,10},{10,... | collective-permute-start | bytes 245768 | tf_op jit(solution)/shard_map/ppermute | solution.py:49
  29.5 5.9 %collective-permute-start.7 = (f32[2,128,128]{2,1,0:T(8,128)S(1)}, f32[2,128,128]{2,1,0:T(8,128)S(1)}, u32[]{:S(2)}, u32[]{:S(2)}) collective-permute-start(f32[2,128,128]{2,1,0:T(8,128)S(1)} %get-tuple-element.99.two_ref), channel_id=1, source_target_pairs={{0,8},{1,9},{2,10},{3,11},{4,12},{5,13},{6,14},{7,15},{8,16},{9,17... | collective-permute-start | bytes 393224 | tf_op jit(solution)/shard_map/ppermute | solution.py:32

commit v13 on v11

--- a/solution.py
+++ b/solution.py
@@ -218,16 +218,15 @@
     return at
 
 
-def pack_kernel(tiles_ref, state_ref, all_ref, high_ref):
+def pack_kernel(tiles_ref, state_ref, rates_ref, high_ref):
     n_fields, n_x, n_y, _ = tiles_ref.shape
     for field in range(n_fields):
+        out_ref = (state_ref, rates_ref)[field // 2].at[field % 2]
         for x in range(n_x):
-            all_ref[field, pl.ds(x, n_y, stride=n_x), :] = tiles_ref[field, x]
+            out_ref[pl.ds(x, n_y, stride=n_x), :] = tiles_ref[field, x]
         count = BELOW[field]
-        rows = all_ref[field, pl.ds((n_y - count) * n_x, count * n_x), :]
+        rows = out_ref[pl.ds((n_y - count) * n_x, count * n_x), :]
         high_ref[pl.ds(sum(BELOW[:field]) * n_x, count * n_x), :] = rows
-    for field in range(2):
-        state_ref[field] = all_ref[field]
 
 
 def collect(out_ref, field, source_field, n_x, lowest, pieces):
@@ -241,13 +240,11 @@
 
 
 def first_inner_kernel(n_gy, n_x, n_y, *refs):
-    state_ref, local_ref = refs[:2]
-    others = refs[2 : 1 + n_gy]
-    start_ref, params_ref, *outs = refs[1 + n_gy :]
+    states, rates, (start_ref, params_ref, *outs) = refs[:n_gy], refs[n_gy : 2 * n_gy], refs[2 * n_gy :]
     width = n_gy * n_x
     for field in range(2):
-        collect(start_ref, field, field, n_x, 0, [(0, [state_ref, *others], n_y)])
-        collect(params_ref, field, 2 + field, n_x, 0, [(0, [local_ref, *others], n_y)])
+        collect(start_ref, field, field, n_x, 0, [(0, states, n_y)])
+        collect(params_ref, field, field, n_x, 0, [(0, rates, n_y)])
     start, params = rows_of(start_ref, width, DRIFT), rows_of(params_ref, width, DRIFT)
     _, values = iteration(start, lambda r: params(r)[0], lambda r: params(r)[1], None)
     write_inner(values, width, n_y, DRIFT, outs)
@@ -430,15 +427,15 @@
     is_first = (place == 0).astype(jnp.int32)[None]
 
     sent = jnp.where(place == n_tm - 1, initial_state, slice_guess[0])
-    state, local, high = call(
+    state, rates, high = call(
         pack_kernel,
         "pack",
         0,
         (jnp.concatenate([sent, feed_rate[None], kill_rate[None]]),),
-        [(2, n_y * n_x, n_z), (4, n_y * n_x, n_z), (sum(BELOW) * n_x, n_z)],
-    )
-    got = [shifted(state, 1, 0, 0), local]
-    got += [shifted(local, 1, -gy, 0) for gy in range(1, n_gy)]
+        [(2, n_y * n_x, n_z), (2, n_y * n_x, n_z), (sum(BELOW) * n_x, n_z)],
+    )
+    got = [shifted(state, 1, -gy, 0) for gy in range(n_gy)]
+    got += [rates, *(shifted(rates, 0, -gy, 0) for gy in range(1, n_gy))]
     below = [shifted(high, 1, -gy, 1) for gy in range(n_gy)]
 
     tile, window = (2, n_y * width, n_z), (2, (TAKE + n_y) * width, n_z)

time: 36.2 us -> 36.3 us (level)
  starting transfers between devices: 18.5 us -> 20.5 us
  waiting for transfers between devices: 11.6 us -> 9.72 us
    ppermute x12 -> x13, starting transfers between devices: 18.5 us -> 20.5 us  [shifted(): return lax.ppermute(value, AXES, pairs)]
    ppermute x12 -> x13, waiting for transfers between devices: 11.6 us -> 9.72 us  [shifted(): return lax.ppermute(value, AXES, pairs)]
  transfers between devices with their start and end apart: 12 -> 13, of which waited for: 5 -> 7; matrix products, arithmetic and copies ran while one was open for 0% -> 0% of each run, Pallas kernels for 6% -> 6%
where the time goes in v13:
time: 36.3 us; the launch traced here: 36.1 us
  starting transfers between devices  20.5 us (56%)
  waiting for transfers between devices  9.72 us (27%)
  Pallas kernels  4.91 us (14%)
  other arithmetic  0.87 us (2%)
    ppermute x13, starting transfers between devices, shifted(): return lax.ppermute(value, AXES, pairs)  20.5 us
    ppermute x13, waiting for transfers between devices, shifted(): return lax.ppermute(value, AXES, pairs)  9.72 us
    pallas_call x9, Pallas kernels, call(): pl.pallas_call(kernel, name=name, out_shape=[jax.ShapeDtypeStruct(shape,...  4.91 us
    select_n x1, other arithmetic, shards(): sent = jnp.where(place == n_tm - 1, initial_state, slice_guess[0])  0.86 us
  transfers between devices with their start and end apart: 13, of which 7 were waited for; matrix products, arithmetic and copies ran while one was open for 0% of the time, Pallas kernels for 6%

profile of v13, /device:TPU:0, one launch (start us, length us, event | category | flops | bytes accessed | tf_op | source)
XLA Modules:
  0.0 36.1 jit_solution(12254683414796019748)
XLA Ops:
  0.0 0.0 copy-start
  0.0 0.0 copy-start.1
  0.0 0.9 %bitcast_select_fusion = f32[2,4,16,128]{3,2,1,0:T(8,128)S(1)} fusion(f32[2,4,16,128]{3,2,1,0:T(8,128)} %param.4, f32[1,2,4,16,128]{4,3,2,1,0:T(8,128)} %param.5, pred[]{:T(512)S(6)} %eq.7), kind=kLoop, calls=%fused_computation.1 | loop fusion | flops 16384 | bytes 196609 | tf_op jit(solution)/shard_map/jit(_where)/select_n | solution.py:429
  0.9 0.0 copy-done
  0.9 0.0 copy-done.1
  0.9 3.5 %collective-permute-start.4 = (f32[168,128]{1,0:T(8,128)S(1)}, f32[168,128]{1,0:T(8,128)S(1)}, u32[]{:S(2)}, u32[]{:S(2)}) collective-permute-start(f32[168,128]{1,0:T(8,128)S(1)} %get-tuple-element.76), channel_id=1, source_target_pairs={{0,13},{1,14},{2,15},{3,12},{4,9},{5,10},{6,11},{7,8},{8,21},{9,22... | collective-permute-start | bytes 258056 | tf_op jit(solution)/shard_map/ppermute | solution.py:32
  4.4 2.8 %collective-permute-start.3 = (f32[168,128]{1,0:T(8,128)S(1)}, f32[168,128]{1,0:T(8,128)S(1)}, u32[]{:S(2)}, u32[]{:S(2)}) collective-permute-start(f32[168,128]{1,0:T(8,128)S(1)} %get-tuple-element.76), channel_id=1, source_target_pairs={{0,9},{1,10},{2,11},{3,8},{4,13},{5,14},{6,15},{7,12},{8,17},{9,18... | collective-permute-start | bytes 258056 | tf_op jit(solution)/shard_map/ppermute | solution.py:32
  7.2 0.0 collective-permute-start.1
  7.2 0.6 %collective-permute-start = (f32[2,64,128]{2,1,0:T(8,128)S(1)}, f32[2,64,128]{2,1,0:T(8,128)S(1)}, u32[]{:S(2)}, u32[]{:S(2)}) collective-permute-start(f32[2,64,128]{2,1,0:T(8,128)S(1)} %get-tuple-element.61), channel_id=1, source_target_pairs={{0,8},{1,9},{2,10},{3,11},{4,12},{5,13},{6,14},{7,15},{8,16},{9,17... | collective-permute-start | bytes 196616 | tf_op jit(solution)/shard_map/ppermute | solution.py:32
  7.8 1.5 %collective-permute-start.2 = (f32[2,64,128]{2,1,0:T(8,128)S(1)}, f32[2,64,128]{2,1,0:T(8,128)S(1)}, u32[]{:S(2)}, u32[]{:S(2)}) collective-permute-start(f32[2,64,128]{2,1,0:T(8,128)S(1)} %get-tuple-element.62.refs_2_), channel_id=1, source_target_pairs={{0,4},{1,5},{2,6},{3,7},{4,0},{5,1},{6,2},{7,3},{8,12},{9,13},{10,... | collective-permute-start | bytes 196616 | tf_op jit(solution)/shard_map/ppermute | solution.py:32
  9.3 3.0 %collective-permute-done.1.refs_1_ = f32[2,64,128]{2,1,0:T(8,128)S(1)} collective-permute-done((f32[2,64,128]{2,1,0:T(8,128)S(1)}, f32[2,64,128]{2,1,0:T(8,128)S(1)}, u32[]{:S(2)}, u32[]{:S(2)}) %collective-permute-start.1) | collective-permute-done | bytes 65568 | tf_op jit(solution)/shard_map/ppermute | solution.py:32
  12.3 0.6 %collective-permute-done.refs_0_ = f32[2,64,128]{2,1,0:T(8,128)S(1)} collective-permute-done((f32[2,64,128]{2,1,0:T(8,128)S(1)}, f32[2,64,128]{2,1,0:T(8,128)S(1)}, u32[]{:S(2)}, u32[]{:S(2)}) %collective-permute-start) | collective-permute-done | bytes 65568 | tf_op jit(solution)/shard_map/ppermute | solution.py:32
  12.8 0.4 %collective-permute-done.2.refs_3_ = f32[2,64,128]{2,1,0:T(8,128)S(1)} collective-permute-done((f32[2,64,128]{2,1,0:T(8,128)S(1)}, f32[2,64,128]{2,1,0:T(8,128)S(1)}, u32[]{:S(2)}, u32[]{:S(2)}) %collective-permute-start.2) | collective-permute-done | bytes 65568 | tf_op jit(solution)/shard_map/ppermute | solution.py:32
  13.2 0.4 %inner_first.1 = (f32[2,128,128]{2,1,0:T(8,128)S(1)}, f32[2,128,128]{2,1,0:T(8,128)S(1)}, f32[2,104,128]{2,1,0:T(8,128)S(1)}, f32[2,104,128]{2,1,0:T(8,128)S(1)}...) custom-call(f32[2,64,128]{2,1,0:T(8,128)S(1)} %collective-permute-do, ...), custom_call_target="tpu_custom_call" | custom-call | tf_op jit(solution)/shard_map/inner_first/pallas_call | solution.py:411
  13.6 0.0 collective-permute-done.4.refs_14_
  13.6 0.0 collective-permute-done.3.refs_13_
  13.6 0.7 %first.1 = (f32[2,216,128]{2,1,0:T(8,128)S(1)}, f32[2,216,128]{2,1,0:T(8,128)S(1)}, f32[2,192,128]{2,1,0:T(8,128)S(1)}, f32[2,128,128]{2,1,0:T(8,128)S(1)}, f32[...) custom-call(f32[2,128,128]{2,1,0:T(8,128)S(1)} %get-tuple-element.63.refs_0_, ...), custom_call_target="tpu_custom_call" | custom-call | tf_op jit(solution)/shard_map/first/pallas_call | solution.py:411
  14.4 2.2 %collective-permute-start.5 = (f32[496,128]{1,0:T(8,128)S(1)}, f32[496,128]{1,0:T(8,128)S(1)}, u32[]{:S(2)}, u32[]{:S(2)}) collective-permute-start(f32[496,128]{1,0:T(8,128)S(1)} %get-tuple-element.79), channel_id=1, source_target_pairs={{0,3},{1,0},{2,1},{3,2},{4,7},{5,4},{6,5},{7,6},{8,11},{9,8},{10,9... | collective-permute-start | bytes 761864 | tf_op jit(solution)/shard_map/ppermute | solution.py:32
  16.6 0.0 collective-permute-start.6
  16.6 1.4 %collective-permute-start.7 = (f32[2,88,128]{2,1,0:T(8,128)S(1)}, f32[2,88,128]{2,1,0:T(8,128)S(1)}, u32[]{:S(2)}, u32[]{:S(2)}) collective-permute-start(f32[2,88,128]{2,1,0:T(8,128)S(1)} %get-tuple-element.96), channel_id=1, source_target_pairs={{0,11},{1,8},{2,9},{3,10},{4,15},{5,12},{6,13},{7,14},{8,19},{9,16... | collective-permute-start | bytes 270344 | tf_op jit(solution)/shard_map/ppermute | solution.py:32
  17.9 3.0 %collective-permute-done.6.got_ref.refs_13_ = f32[2,128,128]{2,1,0:T(8,128)S(1)} collective-permute-done((f32[2,128,128]{2,1,0:T(8,128)S(1)}, f32[2,128,128]{2,1,0:T(8,128)S(1)}, u32[]{:S(2)}, u32[]{:S(2)}) %collective-permute-start.6) | collective-permute-done | bytes 131104 | tf_op jit(solution)/shard_map/ppermute | solution.py:32
  21.0 0.7 %inner.2 = (f32[2,104,128]{2,1,0:T(8,128)S(1)}, f32[2,104,128]{2,1,0:T(8,128)S(1)}, f32[2,88,128]{2,1,0:T(8,128)S(1)}, f32[2,88,128]{2,1,0:T(8,128)S(1)}, f32[2,...) custom-call(s32[1]{0:T(128)} %bitcast.first_ref, ...), custom_call_target="tpu_custom_call" | custom-call | tf_op jit(solution)/shard_map/inner/pallas_call | solution.py:411
  21.7 1.2 %collective-permute-done.5.pair_edge.refs_15_.known_ref = f32[496,128]{1,0:T(8,128)S(1)} collective-permute-done((f32[496,128]{1,0:T(8,128)S(1)}, f32[496,128]{1,0:T(8,128)S(1)}, u32[]{:S(2)}, u32[]{:S(2)}) %collective-permute-start.5) | collective-permute-done | bytes 253984 | tf_op jit(solution)/shard_map/ppermute | solution.py:32
  22.9 0.2 second_rim.1
  23.1 0.5 %collective-permute-done.7.refs_14_ = f32[2,88,128]{2,1,0:T(8,128)S(1)} collective-permute-done((f32[2,88,128]{2,1,0:T(8,128)S(1)}, f32[2,88,128]{2,1,0:T(8,128)S(1)}, u32[]{:S(2)}, u32[]{:S(2)}) %collective-permute-start.7) | collective-permute-done | bytes 90144 | tf_op jit(solution)/shard_map/ppermute | solution.py:32
  23.6 0.6 %second.1 = (f32[2,192,128]{2,1,0:T(8,128)S(1)}, f32[2,128,128]{2,1,0:T(8,128)S(1)}, f32[2,128,128]{2,1,0:T(8,128)S(1)}, f32[2,40,128]{2,1,0:T(8,128)S(1)}, f32[...) custom-call(s32[1]{0:T(128)} %bitcast.first_ref, ...), custom_call_target="tpu_custom_call" | custom-call | tf_op jit(solution)/shard_map/second/pallas_call | solution.py:411
  24.3 0.1 collective-permute-start.8
  24.4 1.6 %collective-permute-start.9 = (f32[160,128]{1,0:T(8,128)S(1)}, f32[160,128]{1,0:T(8,128)S(1)}, u32[]{:S(2)}, u32[]{:S(2)}) collective-permute-start(f32[160,128]{1,0:T(8,128)S(1)} %get-tuple-element.111), channel_id=1, source_target_pairs={{0,1},{1,2},{2,3},{3,0},{4,5},{5,6},{6,7},{7,4},{8,9},{9,10},{10,1... | collective-permute-start | bytes 245768 | tf_op jit(solution)/shard_map/ppermute | solution.py:32
  26.0 2.5 %collective-permute-start.10 = (f32[160,128]{1,0:T(8,128)S(1)}, f32[160,128]{1,0:T(8,128)S(1)}, u32[]{:S(2)}, u32[]{:S(2)}) collective-permute-start(f32[160,128]{1,0:T(8,128)S(1)} %get-tuple-element.112), channel_id=1, source_target_pairs={{0,3},{1,0},{2,1},{3,2},{4,7},{5,4},{6,5},{7,6},{8,11},{9,8},{10,9... | collective-permute-start | bytes 245768 | tf_op jit(solution)/shard_map/ppermute | solution.py:32
  28.4 0.0 collective-permute-start.11
  28.4 4.4 %collective-permute-start.12 = (f32[2,40,128]{2,1,0:T(8,128)S(1)}, f32[2,40,128]{2,1,0:T(8,128)S(1)}, u32[]{:S(2)}, u32[]{:S(2)}) collective-permute-start(f32[2,40,128]{2,1,0:T(8,128)S(1)} %get-tuple-element.116), channel_id=1, source_target_pairs={{0,11},{1,8},{2,9},{3,10},{4,15},{5,12},{6,13},{7,14},{8,19},{9,16... | collective-permute-start | bytes 122888 | tf_op jit(solution)/shard_map/ppermute | solution.py:32
  32.8 0.0 collective-permute-done.9.pair_low
  32.8 0.0 collective-permute-done.10.pair_high
  32.8 0.2 later_rim.1
  33.0 0.0 collective-permute-done.8.got_ref.refs_13_
  33.0 0.8 %inner.3 = (f32[2,112,128]{2,1,0:T(8,128)S(1)}, f32[2,112,128]{2,1,0:T(8,128)S(1)}, f32[2,96,128]{2,1,0:T(8,128)S(1)}, f32[2,96,128]{2,1,0:T(8,128)S(1)}, f32[2,...) custom-call(s32[1]{0:T(128)} %bitcast.first_ref, ...), custom_call_target="tpu_custom_call" | custom-call | tf_op jit(solution)/shard_map/inner/pallas_call | solution.py:411
  33.8 1.1 %collective-permute-done.11.refs_14_ = f32[2,40,128]{2,1,0:T(8,128)S(1)} collective-permute-done((f32[2,40,128]{2,1,0:T(8,128)S(1)}, f32[2,40,128]{2,1,0:T(8,128)S(1)}, u32[]{:S(2)}, u32[]{:S(2)}) %collective-permute-start.11) | collective-permute-done | bytes 40992 | tf_op jit(solution)/shard_map/ppermute | solution.py:32
  34.9 0.0 collective-permute-done.12.refs_15_
  34.9 1.3 %last.1 = f32[2,4,16,128]{3,2,1,0:T(8,128)} custom-call(s32[1]{0:T(128)} %bitcast.first_ref, f32[2,216,128]{2,1,0:T(8,128)S(1)} %get-tuple-element.77.start_ref, f32[2,216,128]{2,1,0:T(8,128)S(1)} %get-tuple-element.78.params_ref, f32[496,128]{1,0:T(8,128)S(1)} %collective-permute-done.5.pair_edge.refs_15_.known_ref, ...), custom_call_target="tpu_custom_call" | custom-call | tf_op jit(solution)/shard_map/last/pallas_call | solution.py:411
  (2 shorter events, 0.0 us)
Async XLA Ops:
  0.0 0.9 %copy-start = (f32[4,16,128]{2,1,0:T(8,128)S(1)}, f32[4,16,128]{2,1,0:T(8,128)}, u32[]{:S(2)}) copy-start(f32[4,16,128]{2,1,0:T(8,128)} %param.7) | copy-start | bytes 98308
  0.0 0.9 %copy-start.1 = (f32[4,16,128]{2,1,0:T(8,128)S(1)}, f32[4,16,128]{2,1,0:T(8,128)}, u32[]{:S(2)}) copy-start(f32[4,16,128]{2,1,0:T(8,128)} %param.6) | copy-start | bytes 98308
  0.9 12.7 %collective-permute-start.4 = (f32[168,128]{1,0:T(8,128)S(1)}, f32[168,128]{1,0:T(8,128)S(1)}, u32[]{:S(2)}, u32[]{:S(2)}) collective-permute-start(f32[168,128]{1,0:T(8,128)S(1)} %get-tuple-element.76), channel_id=1, source_target_pairs={{0,13},{1,14},{2,15},{3,12},{4,9},{5,10},{6,11},{7,8},{8,21},{9,22... | collective-permute-start | bytes 258056 | tf_op jit(solution)/shard_map/ppermute | solution.py:32
  4.4 9.2 %collective-permute-start.3 = (f32[168,128]{1,0:T(8,128)S(1)}, f32[168,128]{1,0:T(8,128)S(1)}, u32[]{:S(2)}, u32[]{:S(2)}) collective-permute-start(f32[168,128]{1,0:T(8,128)S(1)} %get-tuple-element.76), channel_id=1, source_target_pairs={{0,9},{1,10},{2,11},{3,8},{4,13},{5,14},{6,15},{7,12},{8,17},{9,18... | collective-permute-start | bytes 258056 | tf_op jit(solution)/shard_map/ppermute | solution.py:32
  7.2 5.1 %collective-permute-start.1 = (f32[2,64,128]{2,1,0:T(8,128)S(1)}, f32[2,64,128]{2,1,0:T(8,128)S(1)}, u32[]{:S(2)}, u32[]{:S(2)}) collective-permute-start(f32[2,64,128]{2,1,0:T(8,128)S(1)} %get-tuple-element.61), channel_id=1, source_target_pairs={{0,12},{1,13},{2,14},{3,15},{4,8},{5,9},{6,10},{7,11},{8,20},{9,21... | collective-permute-start | bytes 196616 | tf_op jit(solution)/shard_map/ppermute | solution.py:32
  7.2 5.6 %collective-permute-start = (f32[2,64,128]{2,1,0:T(8,128)S(1)}, f32[2,64,128]{2,1,0:T(8,128)S(1)}, u32[]{:S(2)}, u32[]{:S(2)}) collective-permute-start(f32[2,64,128]{2,1,0:T(8,128)S(1)} %get-tuple-element.61), channel_id=1, source_target_pairs={{0,8},{1,9},{2,10},{3,11},{4,12},{5,13},{6,14},{7,15},{8,16},{9,17... | collective-permute-start | bytes 196616 | tf_op jit(solution)/shard_map/ppermute | solution.py:32
  7.8 5.4 %collective-permute-start.2 = (f32[2,64,128]{2,1,0:T(8,128)S(1)}, f32[2,64,128]{2,1,0:T(8,128)S(1)}, u32[]{:S(2)}, u32[]{:S(2)}) collective-permute-start(f32[2,64,128]{2,1,0:T(8,128)S(1)} %get-tuple-element.62.refs_2_), channel_id=1, source_target_pairs={{0,4},{1,5},{2,6},{3,7},{4,0},{5,1},{6,2},{7,3},{8,12},{9,13},{10,... | collective-permute-start | bytes 196616 | tf_op jit(solution)/shard_map/ppermute | solution.py:32
  14.4 8.5 %collective-permute-start.5 = (f32[496,128]{1,0:T(8,128)S(1)}, f32[496,128]{1,0:T(8,128)S(1)}, u32[]{:S(2)}, u32[]{:S(2)}) collective-permute-start(f32[496,128]{1,0:T(8,128)S(1)} %get-tuple-element.79), channel_id=1, source_target_pairs={{0,3},{1,0},{2,1},{3,2},{4,7},{5,4},{6,5},{7,6},{8,11},{9,8},{10,9... | collective-permute-start | bytes 761864 | tf_op jit(solution)/shard_map/ppermute | solution.py:32
  16.6 4.4 %collective-permute-start.6 = (f32[2,128,128]{2,1,0:T(8,128)S(1)}, f32[2,128,128]{2,1,0:T(8,128)S(1)}, u32[]{:S(2)}, u32[]{:S(2)}) collective-permute-start(f32[2,128,128]{2,1,0:T(8,128)S(1)} %get-tuple-element.82.two_ref), channel_id=1, source_target_pairs={{0,8},{1,9},{2,10},{3,11},{4,12},{5,13},{6,14},{7,15},{8,16},{9,17... | collective-permute-start | bytes 393224 | tf_op jit(solution)/shard_map/ppermute | solution.py:32
  16.6 7.0 %collective-permute-start.7 = (f32[2,88,128]{2,1,0:T(8,128)S(1)}, f32[2,88,128]{2,1,0:T(8,128)S(1)}, u32[]{:S(2)}, u32[]{:S(2)}) collective-permute-start(f32[2,88,128]{2,1,0:T(8,128)S(1)} %get-tuple-element.96), channel_id=1, source_target_pairs={{0,11},{1,8},{2,9},{3,10},{4,15},{5,12},{6,13},{7,14},{8,19},{9,16... | collective-permute-start | bytes 270344 | tf_op jit(solution)/shard_map/ppermute | solution.py:32
  24.3 8.7 %collective-permute-start.8 = (f32[2,128,128]{2,1,0:T(8,128)S(1)}, f32[2,128,128]{2,1,0:T(8,128)S(1)}, u32[]{:S(2)}, u32[]{:S(2)}) collective-permute-start(f32[2,128,128]{2,1,0:T(8,128)S(1)} %get-tuple-element.99.two_ref), channel_id=1, source_target_pairs={{0,8},{1,9},{2,10},{3,11},{4,12},{5,13},{6,14},{7,15},{8,16},{9,17... | collective-permute-start | bytes 393224 | tf_op jit(solution)/shard_map/ppermute | solution.py:32
  24.4 8.4 %collective-permute-start.9 = (f32[160,128]{1,0:T(8,128)S(1)}, f32[160,128]{1,0:T(8,128)S(1)}, u32[]{:S(2)}, u32[]{:S(2)}) collective-permute-start(f32[160,128]{1,0:T(8,128)S(1)} %get-tuple-element.111), channel_id=1, source_target_pairs={{0,1},{1,2},{2,3},{3,0},{4,5},{5,6},{6,7},{7,4},{8,9},{9,10},{10,1... | collective-permute-start | bytes 245768 | tf_op jit(solution)/shard_map/ppermute | solution.py:32
  26.0 6.9 %collective-permute-start.10 = (f32[160,128]{1,0:T(8,128)S(1)}, f32[160,128]{1,0:T(8,128)S(1)}, u32[]{:S(2)}, u32[]{:S(2)}) collective-permute-start(f32[160,128]{1,0:T(8,128)S(1)} %get-tuple-element.112), channel_id=1, source_target_pairs={{0,3},{1,0},{2,1},{3,2},{4,7},{5,4},{6,5},{7,6},{8,11},{9,8},{10,9... | collective-permute-start | bytes 245768 | tf_op jit(solution)/shard_map/ppermute | solution.py:32
  28.4 6.4 %collective-permute-start.11 = (f32[2,40,128]{2,1,0:T(8,128)S(1)}, f32[2,40,128]{2,1,0:T(8,128)S(1)}, u32[]{:S(2)}, u32[]{:S(2)}) collective-permute-start(f32[2,40,128]{2,1,0:T(8,128)S(1)} %get-tuple-element.115), channel_id=1, source_target_pairs={{0,9},{1,10},{2,11},{3,8},{4,13},{5,14},{6,15},{7,12},{8,17},{9,18... | collective-permute-start | bytes 122888 | tf_op jit(solution)/shard_map/ppermute | solution.py:32
  28.4 6.4 %collective-permute-start.12 = (f32[2,40,128]{2,1,0:T(8,128)S(1)}, f32[2,40,128]{2,1,0:T(8,128)S(1)}, u32[]{:S(2)}, u32[]{:S(2)}) collective-permute-start(f32[2,40,128]{2,1,0:T(8,128)S(1)} %get-tuple-element.116), channel_id=1, source_target_pairs={{0,11},{1,8},{2,9},{3,10},{4,15},{5,12},{6,13},{7,14},{8,19},{9,16... | collective-permute-start | bytes 122888 | tf_op jit(solution)/shard_map/ppermute | solution.py:32

commit v14 on v11

--- a/solution.py
+++ b/solution.py
@@ -85,7 +85,7 @@
     return at
 
 
-INNER_COUNT = 11
+INNER_COUNT = 12
 
 
 def inner_rows(n_y, tile_first):
@@ -96,7 +96,7 @@
     fine = [(low + k, high - k) for k in (1, 1, 2, 2, 3)]
     start, one, integral = halves(low, high), halves(*fine[1]), halves(*fine[4])
     coarse = [clip(start, 2), clip(one, 1), clip(integral, 1), clip(integral, 0)]
-    return [*fine, *coarse, clip(inside(start), 1), clip(inside(one), 0)]
+    return [*fine, *coarse, clip(inside(start), 1), clip(inside(one), 0), clip(halves(*fine[3]), 0)]
 
 
 def inner_shapes(width, n_y, n_z, tile_first):
@@ -111,7 +111,7 @@
     items = []
     for i, ((low, high), rows, ref) in enumerate(zip(inner_rows(n_y, tile_first), values, refs)):
         for r in range(low, high):
-            ready = r + (0, 0, 1, 1, 2)[i] if i < 5 else 2 * r + (1, 1, 3, 3, 3, 3)[i - 5]
+            ready = r + (0, 0, 1, 1, 2)[i] if i < 5 else 2 * r + (1, 1, 3, 3, 3, 3, 2)[i - 5]
             items.append((ready, i, r, rows, ref, low))
     for _, _, r, rows, ref, low in sorted(items, key=lambda item: item[:3]):
         for field, value in enumerate(rows(r)):
@@ -181,6 +181,7 @@
     rest_zero, rest_one, rest_two = known_or(restricted(start)), known_or(restricted(node_one)), restricted(node_two)
     rest_integral = [known_or(restricted(quadrature(fresh, interval))) for interval in (0, 1)]
     rate_rest_zero, rate_rest_one = known_or(coarse(rest_zero)), known_or(coarse(rest_one))
+    rest_two = known_or(rest_two)
     coarse_start, rate_coarse_start = rest_zero, rate_rest_zero
 
     def coarse_stepped(state, rate, rest_rate, integral):
@@ -206,7 +207,7 @@
 
     nodes = corrected(node_one, coarse_one, rest_one), corrected(node_two, coarse_two, rest_two)
     fine_rows = (rate_zero, node_one, rate_one, node_two, rate_two)
-    return (rate_zero, *nodes), (*fine_rows, rest_zero, rest_one, *rest_integral, rate_rest_zero, rate_rest_one)
+    return (rate_zero, *nodes), (*fine_rows, rest_zero, rest_one, *rest_integral, rate_rest_zero, rate_rest_one, rest_two)
 
 
 def rows_of(ref, width, first):

time: 36.2 us -> 36.1 us (level)
  transfers between devices with their start and end apart: 12 -> 12, of which waited for: 5 -> 5; matrix products, arithmetic and copies ran while one was open for 0% -> 0% of each run, Pallas kernels for 6% -> 7%
where the time goes in v14:
time: 36.1 us; the launch traced here: 35.9 us
  starting transfers between devices  18.5 us (51%)
  waiting for transfers between devices  11.5 us (32%)
  Pallas kernels  4.93 us (14%)
  other arithmetic  0.87 us (2%)
    ppermute x12, starting transfers between devices, shifted(): return lax.ppermute(value, AXES, pairs)  18.5 us
    ppermute x12, waiting for transfers between devices, shifted(): return lax.ppermute(value, AXES, pairs)  11.5 us
    pallas_call x9, Pallas kernels, call(): pl.pallas_call(kernel, name=name, out_shape=[jax.ShapeDtypeStruct(shape,...  4.93 us
    select_n x1, other arithmetic, shards(): sent = jnp.where(place == n_tm - 1, initial_state, slice_guess[0])  0.86 us
  transfers between devices with their start and end apart: 12, of which 5 were waited for; matrix products, arithmetic and copies ran while one was open for 0% of the time, Pallas kernels for 7%

profile of v14, /device:TPU:0, one launch (start us, length us, event | category | flops | bytes accessed | tf_op | source)
XLA Modules:
  0.0 35.9 jit_solution(9116517610835802137)
XLA Ops:
  0.0 0.0 copy-start
  0.0 0.0 copy-start.1
  0.0 0.9 %bitcast_select_fusion = f32[2,4,16,128]{3,2,1,0:T(8,128)S(1)} fusion(f32[2,4,16,128]{3,2,1,0:T(8,128)} %param.4, f32[1,2,4,16,128]{4,3,2,1,0:T(8,128)} %param.5, pred[]{:T(512)S(6)} %eq.7), kind=kLoop, calls=%fused_computation.1 | loop fusion | flops 16384 | bytes 196609 | tf_op jit(solution)/shard_map/jit(_where)/select_n | solution.py:433
  0.9 0.0 copy-done
  0.9 0.0 copy-done.1
  0.9 2.5 %collective-permute-start.1 = (f32[4,64,128]{2,1,0:T(8,128)S(1)}, f32[4,64,128]{2,1,0:T(8,128)S(1)}, u32[]{:S(2)}, u32[]{:S(2)}) collective-permute-start(f32[4,64,128]{2,1,0:T(8,128)S(1)} %get-tuple-element.65.refs_1_), channel_id=1, source_target_pairs={{0,12},{1,13},{2,14},{3,15},{4,8},{5,9},{6,10},{7,11},{8,20},{9,21... | collective-permute-start | bytes 393224 | tf_op jit(solution)/shard_map/ppermute | solution.py:32
  3.4 2.7 %collective-permute-start.3 = (f32[168,128]{1,0:T(8,128)S(1)}, f32[168,128]{1,0:T(8,128)S(1)}, u32[]{:S(2)}, u32[]{:S(2)}) collective-permute-start(f32[168,128]{1,0:T(8,128)S(1)} %get-tuple-element.80), channel_id=1, source_target_pairs={{0,13},{1,14},{2,15},{3,12},{4,9},{5,10},{6,11},{7,8},{8,21},{9,22... | collective-permute-start | bytes 258056 | tf_op jit(solution)/shard_map/ppermute | solution.py:32
  6.1 1.1 %collective-permute-start.2 = (f32[168,128]{1,0:T(8,128)S(1)}, f32[168,128]{1,0:T(8,128)S(1)}, u32[]{:S(2)}, u32[]{:S(2)}) collective-permute-start(f32[168,128]{1,0:T(8,128)S(1)} %get-tuple-element.80), channel_id=1, source_target_pairs={{0,9},{1,10},{2,11},{3,8},{4,13},{5,14},{6,15},{7,12},{8,17},{9,18... | collective-permute-start | bytes 258056 | tf_op jit(solution)/shard_map/ppermute | solution.py:32
  7.3 0.5 %collective-permute-start = (f32[2,64,128]{2,1,0:T(8,128)S(1)}, f32[2,64,128]{2,1,0:T(8,128)S(1)}, u32[]{:S(2)}, u32[]{:S(2)}) collective-permute-start(f32[2,64,128]{2,1,0:T(8,128)S(1)} %get-tuple-element.64), channel_id=1, source_target_pairs={{0,8},{1,9},{2,10},{3,11},{4,12},{5,13},{6,14},{7,15},{8,16},{9,17... | collective-permute-start | bytes 196616 | tf_op jit(solution)/shard_map/ppermute | solution.py:32
  7.8 3.6 %collective-permute-done.refs_0_ = f32[2,64,128]{2,1,0:T(8,128)S(1)} collective-permute-done((f32[2,64,128]{2,1,0:T(8,128)S(1)}, f32[2,64,128]{2,1,0:T(8,128)S(1)}, u32[]{:S(2)}, u32[]{:S(2)}) %collective-permute-start) | collective-permute-done | bytes 65568 | tf_op jit(solution)/shard_map/ppermute | solution.py:32
  11.4 0.0 collective-permute-done.1.refs_2_
  11.4 0.4 %inner_first.1 = (f32[2,128,128]{2,1,0:T(8,128)S(1)}, f32[2,128,128]{2,1,0:T(8,128)S(1)}, f32[2,104,128]{2,1,0:T(8,128)S(1)}, f32[2,104,128]{2,1,0:T(8,128)S(1)}...) custom-call(f32[2,64,128]{2,1,0:T(8,128)S(1)} %collective-permute-do, ...), custom_call_target="tpu_custom_call" | custom-call | tf_op jit(solution)/shard_map/inner_first/pallas_call | solution.py:415
  11.9 0.0 collective-permute-done.3.refs_15_
  11.9 1.2 %collective-permute-done.2.refs_14_ = f32[168,128]{1,0:T(8,128)S(1)} collective-permute-done((f32[168,128]{1,0:T(8,128)S(1)}, f32[168,128]{1,0:T(8,128)S(1)}, u32[]{:S(2)}, u32[]{:S(2)}) %collective-permute-start.2) | collective-permute-done | bytes 86048 | tf_op jit(solution)/shard_map/ppermute | solution.py:32
  13.1 0.7 %first.1 = (f32[2,216,128]{2,1,0:T(8,128)S(1)}, f32[2,216,128]{2,1,0:T(8,128)S(1)}, f32[2,192,128]{2,1,0:T(8,128)S(1)}, f32[2,128,128]{2,1,0:T(8,128)S(1)}, f32[...) custom-call(f32[2,128,128]{2,1,0:T(8,128)S(1)} %get-tuple-element.66.refs_0_, ...), custom_call_target="tpu_custom_call" | custom-call | tf_op jit(solution)/shard_map/first/pallas_call | solution.py:415
  13.8 1.3 %collective-permute-start.4 = (f32[496,128]{1,0:T(8,128)S(1)}, f32[496,128]{1,0:T(8,128)S(1)}, u32[]{:S(2)}, u32[]{:S(2)}) collective-permute-start(f32[496,128]{1,0:T(8,128)S(1)} %get-tuple-element.83), channel_id=1, source_target_pairs={{0,3},{1,0},{2,1},{3,2},{4,7},{5,4},{6,5},{7,6},{8,11},{9,8},{10,9... | collective-permute-start | bytes 761864 | tf_op jit(solution)/shard_map/ppermute | solution.py:32
  15.1 0.0 collective-permute-start.5
  15.1 1.9 %collective-permute-start.6 = (f32[2,88,128]{2,1,0:T(8,128)S(1)}, f32[2,88,128]{2,1,0:T(8,128)S(1)}, u32[]{:S(2)}, u32[]{:S(2)}) collective-permute-start(f32[2,88,128]{2,1,0:T(8,128)S(1)} %get-tuple-element.101), channel_id=1, source_target_pairs={{0,11},{1,8},{2,9},{3,10},{4,15},{5,12},{6,13},{7,14},{8,19},{9,16... | collective-permute-start | bytes 270344 | tf_op jit(solution)/shard_map/ppermute | solution.py:32
  17.0 2.7 %collective-permute-done.5.got_ref.refs_14_ = f32[2,128,128]{2,1,0:T(8,128)S(1)} collective-permute-done((f32[2,128,128]{2,1,0:T(8,128)S(1)}, f32[2,128,128]{2,1,0:T(8,128)S(1)}, u32[]{:S(2)}, u32[]{:S(2)}) %collective-permute-start.5) | collective-permute-done | bytes 131104 | tf_op jit(solution)/shard_map/ppermute | solution.py:32
  19.7 0.7 %inner.2 = (f32[2,104,128]{2,1,0:T(8,128)S(1)}, f32[2,104,128]{2,1,0:T(8,128)S(1)}, f32[2,88,128]{2,1,0:T(8,128)S(1)}, f32[2,88,128]{2,1,0:T(8,128)S(1)}, f32[2,...) custom-call(s32[1]{0:T(128)} %bitcast.first_ref, ...), custom_call_target="tpu_custom_call" | custom-call | tf_op jit(solution)/shard_map/inner/pallas_call | solution.py:415
  20.5 2.3 %collective-permute-done.4.pair_edge.refs_16_.known_ref = f32[496,128]{1,0:T(8,128)S(1)} collective-permute-done((f32[496,128]{1,0:T(8,128)S(1)}, f32[496,128]{1,0:T(8,128)S(1)}, u32[]{:S(2)}, u32[]{:S(2)}) %collective-permute-start.4) | collective-permute-done | bytes 253984 | tf_op jit(solution)/shard_map/ppermute | solution.py:32
  22.8 0.2 second_rim.1
  23.0 0.0 collective-permute-done.6.refs_15_
  23.0 0.6 %second.1 = (f32[2,192,128]{2,1,0:T(8,128)S(1)}, f32[2,128,128]{2,1,0:T(8,128)S(1)}, f32[2,128,128]{2,1,0:T(8,128)S(1)}, f32[2,40,128]{2,1,0:T(8,128)S(1)}, f32[...) custom-call(s32[1]{0:T(128)} %bitcast.first_ref, ...), custom_call_target="tpu_custom_call" | custom-call | tf_op jit(solution)/shard_map/second/pallas_call | solution.py:415
  23.7 0.7 %collective-permute-start.7 = (f32[2,128,128]{2,1,0:T(8,128)S(1)}, f32[2,128,128]{2,1,0:T(8,128)S(1)}, u32[]{:S(2)}, u32[]{:S(2)}) collective-permute-start(f32[2,128,128]{2,1,0:T(8,128)S(1)} %get-tuple-element.104.two_ref), channel_id=1, source_target_pairs={{0,8},{1,9},{2,10},{3,11},{4,12},{5,13},{6,14},{7,15},{8,16},{9,17... | collective-permute-start | bytes 393224 | tf_op jit(solution)/shard_map/ppermute | solution.py:32
  24.4 0.0 collective-permute-start.8
  24.4 3.8 %collective-permute-start.9 = (f32[160,128]{1,0:T(8,128)S(1)}, f32[160,128]{1,0:T(8,128)S(1)}, u32[]{:S(2)}, u32[]{:S(2)}) collective-permute-start(f32[160,128]{1,0:T(8,128)S(1)} %get-tuple-element.118), channel_id=1, source_target_pairs={{0,3},{1,0},{2,1},{3,2},{4,7},{5,4},{6,5},{7,6},{8,11},{9,8},{10,9... | collective-permute-start | bytes 245768 | tf_op jit(solution)/shard_map/ppermute | solution.py:32
  28.2 0.0 collective-permute-start.10
  28.2 3.9 %collective-permute-start.11 = (f32[2,40,128]{2,1,0:T(8,128)S(1)}, f32[2,40,128]{2,1,0:T(8,128)S(1)}, u32[]{:S(2)}, u32[]{:S(2)}) collective-permute-start(f32[2,40,128]{2,1,0:T(8,128)S(1)} %get-tuple-element.122), channel_id=1, source_target_pairs={{0,11},{1,8},{2,9},{3,10},{4,15},{5,12},{6,13},{7,14},{8,19},{9,16... | collective-permute-start | bytes 122888 | tf_op jit(solution)/shard_map/ppermute | solution.py:32
  32.1 0.0 collective-permute-done.8.pair_low
  32.1 0.0 collective-permute-done.9.pair_high
  32.1 0.2 later_rim.1
  32.3 0.0 collective-permute-done.7.got_ref.refs_14_
  32.3 0.9 %inner.3 = (f32[2,112,128]{2,1,0:T(8,128)S(1)}, f32[2,112,128]{2,1,0:T(8,128)S(1)}, f32[2,96,128]{2,1,0:T(8,128)S(1)}, f32[2,96,128]{2,1,0:T(8,128)S(1)}, f32[2,...) custom-call(s32[1]{0:T(128)} %bitcast.first_ref, ...), custom_call_target="tpu_custom_call" | custom-call | tf_op jit(solution)/shard_map/inner/pallas_call | solution.py:415
  33.2 1.5 %collective-permute-done.10.refs_15_ = f32[2,40,128]{2,1,0:T(8,128)S(1)} collective-permute-done((f32[2,40,128]{2,1,0:T(8,128)S(1)}, f32[2,40,128]{2,1,0:T(8,128)S(1)}, u32[]{:S(2)}, u32[]{:S(2)}) %collective-permute-start.10) | collective-permute-done | bytes 40992 | tf_op jit(solution)/shard_map/ppermute | solution.py:32
  34.7 0.0 collective-permute-done.11.refs_16_
  34.7 1.2 %last.1 = f32[2,4,16,128]{3,2,1,0:T(8,128)} custom-call(s32[1]{0:T(128)} %bitcast.first_ref, f32[2,216,128]{2,1,0:T(8,128)S(1)} %get-tuple-element.81.start_ref, f32[2,216,128]{2,1,0:T(8,128)S(1)} %get-tuple-element.82.params_ref, f32[496,128]{1,0:T(8,128)S(1)} %collective-permute-done.4.pair_edge.refs_16_.known_ref, ...), custom_call_target="tpu_custom_call" | custom-call | tf_op jit(solution)/shard_map/last/pallas_call | solution.py:415
  (2 shorter events, 0.0 us)
Async XLA Ops:
  0.0 0.9 %copy-start = (f32[4,16,128]{2,1,0:T(8,128)S(1)}, f32[4,16,128]{2,1,0:T(8,128)}, u32[]{:S(2)}) copy-start(f32[4,16,128]{2,1,0:T(8,128)} %param.7) | copy-start | bytes 98308
  0.0 0.9 %copy-start.1 = (f32[4,16,128]{2,1,0:T(8,128)S(1)}, f32[4,16,128]{2,1,0:T(8,128)}, u32[]{:S(2)}) copy-start(f32[4,16,128]{2,1,0:T(8,128)} %param.6) | copy-start | bytes 98308
  0.9 10.5 %collective-permute-start.1 = (f32[4,64,128]{2,1,0:T(8,128)S(1)}, f32[4,64,128]{2,1,0:T(8,128)S(1)}, u32[]{:S(2)}, u32[]{:S(2)}) collective-permute-start(f32[4,64,128]{2,1,0:T(8,128)S(1)} %get-tuple-element.65.refs_1_), channel_id=1, source_target_pairs={{0,12},{1,13},{2,14},{3,15},{4,8},{5,9},{6,10},{7,11},{8,20},{9,21... | collective-permute-start | bytes 393224 | tf_op jit(solution)/shard_map/ppermute | solution.py:32
  3.4 8.5 %collective-permute-start.3 = (f32[168,128]{1,0:T(8,128)S(1)}, f32[168,128]{1,0:T(8,128)S(1)}, u32[]{:S(2)}, u32[]{:S(2)}) collective-permute-start(f32[168,128]{1,0:T(8,128)S(1)} %get-tuple-element.80), channel_id=1, source_target_pairs={{0,13},{1,14},{2,15},{3,12},{4,9},{5,10},{6,11},{7,8},{8,21},{9,22... | collective-permute-start | bytes 258056 | tf_op jit(solution)/shard_map/ppermute | solution.py:32
  6.1 7.0 %collective-permute-start.2 = (f32[168,128]{1,0:T(8,128)S(1)}, f32[168,128]{1,0:T(8,128)S(1)}, u32[]{:S(2)}, u32[]{:S(2)}) collective-permute-start(f32[168,128]{1,0:T(8,128)S(1)} %get-tuple-element.80), channel_id=1, source_target_pairs={{0,9},{1,10},{2,11},{3,8},{4,13},{5,14},{6,15},{7,12},{8,17},{9,18... | collective-permute-start | bytes 258056 | tf_op jit(solution)/shard_map/ppermute | solution.py:32
  7.3 4.2 %collective-permute-start = (f32[2,64,128]{2,1,0:T(8,128)S(1)}, f32[2,64,128]{2,1,0:T(8,128)S(1)}, u32[]{:S(2)}, u32[]{:S(2)}) collective-permute-start(f32[2,64,128]{2,1,0:T(8,128)S(1)} %get-tuple-element.64), channel_id=1, source_target_pairs={{0,8},{1,9},{2,10},{3,11},{4,12},{5,13},{6,14},{7,15},{8,16},{9,17... | collective-permute-start | bytes 196616 | tf_op jit(solution)/shard_map/ppermute | solution.py:32
  13.8 9.0 %collective-permute-start.4 = (f32[496,128]{1,0:T(8,128)S(1)}, f32[496,128]{1,0:T(8,128)S(1)}, u32[]{:S(2)}, u32[]{:S(2)}) collective-permute-start(f32[496,128]{1,0:T(8,128)S(1)} %get-tuple-element.83), channel_id=1, source_target_pairs={{0,3},{1,0},{2,1},{3,2},{4,7},{5,4},{6,5},{7,6},{8,11},{9,8},{10,9... | collective-permute-start | bytes 761864 | tf_op jit(solution)/shard_map/ppermute | solution.py:32
  15.1 4.6 %collective-permute-start.5 = (f32[2,128,128]{2,1,0:T(8,128)S(1)}, f32[2,128,128]{2,1,0:T(8,128)S(1)}, u32[]{:S(2)}, u32[]{:S(2)}) collective-permute-start(f32[2,128,128]{2,1,0:T(8,128)S(1)} %get-tuple-element.86.two_ref), channel_id=1, source_target_pairs={{0,8},{1,9},{2,10},{3,11},{4,12},{5,13},{6,14},{7,15},{8,16},{9,17... | collective-permute-start | bytes 393224 | tf_op jit(solution)/shard_map/ppermute | solution.py:32
  15.1 7.9 %collective-permute-start.6 = (f32[2,88,128]{2,1,0:T(8,128)S(1)}, f32[2,88,128]{2,1,0:T(8,128)S(1)}, u32[]{:S(2)}, u32[]{:S(2)}) collective-permute-start(f32[2,88,128]{2,1,0:T(8,128)S(1)} %get-tuple-element.101), channel_id=1, source_target_pairs={{0,11},{1,8},{2,9},{3,10},{4,15},{5,12},{6,13},{7,14},{8,19},{9,16... | collective-permute-start | bytes 270344 | tf_op jit(solution)/shard_map/ppermute | solution.py:32
  23.7 8.6 %collective-permute-start.7 = (f32[2,128,128]{2,1,0:T(8,128)S(1)}, f32[2,128,128]{2,1,0:T(8,128)S(1)}, u32[]{:S(2)}, u32[]{:S(2)}) collective-permute-start(f32[2,128,128]{2,1,0:T(8,128)S(1)} %get-tuple-element.104.two_ref), channel_id=1, source_target_pairs={{0,8},{1,9},{2,10},{3,11},{4,12},{5,13},{6,14},{7,15},{8,16},{9,17... | collective-permute-start | bytes 393224 | tf_op jit(solution)/shard_map/ppermute | solution.py:32
  24.4 7.7 %collective-permute-start.8 = (f32[160,128]{1,0:T(8,128)S(1)}, f32[160,128]{1,0:T(8,128)S(1)}, u32[]{:S(2)}, u32[]{:S(2)}) collective-permute-start(f32[160,128]{1,0:T(8,128)S(1)} %get-tuple-element.117), channel_id=1, source_target_pairs={{0,1},{1,2},{2,3},{3,0},{4,5},{5,6},{6,7},{7,4},{8,9},{9,10},{10,1... | collective-permute-start | bytes 245768 | tf_op jit(solution)/shard_map/ppermute | solution.py:32
  24.4 7.7 %collective-permute-start.9 = (f32[160,128]{1,0:T(8,128)S(1)}, f32[160,128]{1,0:T(8,128)S(1)}, u32[]{:S(2)}, u32[]{:S(2)}) collective-permute-start(f32[160,128]{1,0:T(8,128)S(1)} %get-tuple-element.118), channel_id=1, source_target_pairs={{0,3},{1,0},{2,1},{3,2},{4,7},{5,4},{6,5},{7,6},{8,11},{9,8},{10,9... | collective-permute-start | bytes 245768 | tf_op jit(solution)/shard_map/ppermute | solution.py:32
  28.2 6.5 %collective-permute-start.10 = (f32[2,40,128]{2,1,0:T(8,128)S(1)}, f32[2,40,128]{2,1,0:T(8,128)S(1)}, u32[]{:S(2)}, u32[]{:S(2)}) collective-permute-start(f32[2,40,128]{2,1,0:T(8,128)S(1)} %get-tuple-element.121), channel_id=1, source_target_pairs={{0,9},{1,10},{2,11},{3,8},{4,13},{5,14},{6,15},{7,12},{8,17},{9,18... | collective-permute-start | bytes 122888 | tf_op jit(solution)/shard_map/ppermute | solution.py:32
  28.2 6.5 %collective-permute-start.11 = (f32[2,40,128]{2,1,0:T(8,128)S(1)}, f32[2,40,128]{2,1,0:T(8,128)S(1)}, u32[]{:S(2)}, u32[]{:S(2)}) collective-permute-start(f32[2,40,128]{2,1,0:T(8,128)S(1)} %get-tuple-element.122), channel_id=1, source_target_pairs={{0,11},{1,8},{2,9},{3,10},{4,15},{5,12},{6,13},{7,14},{8,19},{9,16... | collective-permute-start | bytes 122888 | tf_op jit(solution)/shard_map/ppermute | solution.py:32
